TPU v7x, 32 devices: a whole 2x2x4 slice. The times are simulated.
32 devices in a mesh: grp: 4 (over y, x), blk: 8 (over z, core).
Axes of the slice: x: 2, y: 2, z: 4, core: 2. Of those that a mesh axis runs over, the one named last changes fastest.
Arguments:
- integrals: float32 [48, 1024, 1536], P('grp', 'blk'), may hold values from -0.9 to 0.9
- pair_lists: int32 [4, 2], P('grp'), may hold values from 0 to 48, as said below
- row_orbital: int32 [48], P('grp'), may hold values from 0 to 47, each once
- occ_energy: float32 [48], replicated, may hold values from -2 to -0.5
- vir_energy: float32 [1024], P('blk'), may hold values from 0.5 to 4
Outputs:
- three_index_density: float32 [48, 1024, 1536], P('grp', 'blk')
Inputs may be any that keep to these rules, and one draw needn't show every extreme that they name: `pair_lists`: entries are rows of the integrals, or 48 in unused slots; used slots come first; every group lists one to 2 rows, some group exactly one and some exactly 2; no two rows listed by one group are held by the same group (a group may list one of its own rows). `row_orbital`: each orbital stands in exactly one row.
All inputs are finite; a program needn't handle non-finite values.
Results may differ from a plain program's by a relative error of at most 0.0001.
Values sent between devices are 32-bit elements; how exact they have to be, the bound alone decides.
No kernel may reach another device: no remote copies, remote signals or barrier semaphores. Data moves between devices by JAX's collectives and lax.ppermute only.
A program may use at most 128 MiB of HBM per device.

v0:
```python
import jax
import jax.numpy as jnp
from jax import lax
from jax.sharding import PartitionSpec as P


def body(integrals, pair_lists, row_orbital, occ_energy, vir_energy):
    highest = lax.Precision.HIGHEST
    own_count, vir_width, aux_width = integrals.shape
    slot_count = pair_lists.shape[1]
    group_count = lax.axis_size("grp")
    group_place = lax.axis_index("grp")
    listed, orbitals = (
        lax.all_gather(pair_lists, "grp", axis=0, tiled=True),
        lax.all_gather(row_orbital, "grp", axis=0, tiled=True),
    )
    total_rows = orbitals.shape[0]
    columns = lax.broadcasted_iota(jnp.int32, (group_count, slot_count, total_rows), 2)
    matches = (listed[:, :, None] == columns).astype(jnp.float32)
    held_rows = lax.dynamic_slice_in_dim(matches, group_place * own_count, own_count, 2)
    selected = jnp.sum(held_rows, axis=1)
    outgoing = jnp.einsum("gr,rap->gap", selected, integrals, precision=highest)
    incoming = lax.all_to_all(outgoing, "grp", split_axis=0, concat_axis=0, tiled=True)
    own_match = lax.dynamic_index_in_dim(matches, group_place, 0, keepdims=False)
    owner_pick = jnp.sum(own_match.reshape(slot_count, group_count, own_count), axis=2)
    partner = jnp.einsum("js,sap->jap", owner_pick, incoming, precision=highest)
    orbital_ids = lax.broadcasted_iota(jnp.int32, (total_rows, occ_energy.shape[0]), 1)
    lookup = (orbitals[:, None] == orbital_ids).astype(jnp.float32)
    row_energy = jnp.dot(lookup, occ_energy, precision=highest)
    own_energy = lax.dynamic_slice_in_dim(row_energy, group_place * own_count, own_count, 0)
    partner_energy = jnp.dot(own_match, row_energy, precision=highest)
    vir_rows = vir_energy.reshape(1, vir_width)
    blocks = lax.all_gather(partner, "blk", axis=1, tiled=True)
    energies = lax.all_gather(vir_rows, "blk", axis=1, tiled=True)
    pair_block = jnp.einsum("iap,jbp->iajb", integrals, blocks, precision=highest)
    denominator = (
        own_energy[:, None, None, None]
        + partner_energy[None, None, :, None]
        - vir_energy[None, :, None, None]
        - energies[0][None, None, None, :]
    )
    amplitude = pair_block / denominator
    density_own = jnp.einsum("iajb,jbp->iap", amplitude, blocks, precision=highest)
    density_own, amplitudes = (density_own, amplitude)
    own_share = lax.psum_scatter(
        jnp.einsum("iajb,iap->bjp", amplitudes, integrals, precision=highest),
        "blk",
        scatter_dimension=0,
        tiled=True,
    )
    returning = jnp.einsum("bjp,js->bsp", own_share, owner_pick, precision=highest)
    arrived = lax.all_to_all(returning, "grp", split_axis=1, concat_axis=1, tiled=True)
    return density_own + jnp.einsum("sr,bsp->rbp", selected, arrived, precision=highest)


def solution(mesh):
    in_specs = (P("grp", "blk", None), P("grp", None), P("grp"), P(), P("blk"))
    out_specs = P("grp", "blk", None)
    return jax.shard_map(body, mesh=mesh, in_specs=in_specs, out_specs=out_specs, check_vma=False)
```

profile of v0, /device:TPU:0, one launch (start us, length us, event | category | flops | bytes accessed | tf_op | source)
XLA Modules:
  0.0 619.9 jit_solution(12099565835043440920)
XLA Ops:
  6.5 0.0 copy-start
  6.5 9.6 %all-gather.1 = s32[4,1,2]{2,1,0:T(1,128)S(1)} all-gather(s32[1,1,2]{2,1,0:T(1,128)} %bitcast.58), channel_id=1, replica_groups=mesh['grp'=4,'blk'=8] {'grp'}, dimensions={0}, use_global_device_ids=true | all-gather | bytes 40 | tf_op jit(solution)/shard_map/all_gather | solution.py:14
  16.1 0.1 iota_compare_fusion.2
  16.2 0.1 dynamic-slice_reduce_fusion
  16.3 15.8 %fusion = f32[4,128,1536]{2,0,1:T(4,128)S(1)} fusion(f32[12,128,1536]{2,1,0:T(8,128)} %param.5, f32[4,12]{1,0:T(4,128)S(1)} %dynamic-slice_reduce_fusion), kind=kOutput, calls=%fused_computation.1 | convolution fusion | flops 113246208 | bytes 12583104 | tf_op jit(solution)/shard_map/gr,rap->gap/dot_general | solution.py:22
  32.1 0.0 copy-start.4
  32.1 0.0 copy-start.3
  32.2 0.0 copy-start.2
  32.2 2.6 copy.21
  34.8 3.7 all-to-all-start
  38.5 0.0 all-gather.5.cloned.1.call-start
  38.6 0.1 reshape.48
  38.7 0.1 reduce_sum.18
  38.7 34.4 %all-to-all-done = f32[4,128,1536]{2,1,0:T(8,128)S(1)} async-done(((f32[4,128,1536]{2,1,0:T(8,128)}), f32[4,128,1536]{2,1,0:T(8,128)S(1)}, u32[]{:S(2)}, u32[]{:S(2)}) %all-to-all-start) | async-done | bytes 3145760 | tf_op jit(solution)/shard_map/all_to_all | solution.py:23
  73.1 7.2 %fusion.20 = f32[2,128,1536]{2,0,1:T(2,128)} fusion(f32[4,128,1536]{2,1,0:T(8,128)S(1)} %all-to-all-done, f32[2,4]{1,0:T(2,128)S(1)} %reduce_sum.18), kind=kOutput, calls=%fused_computation.15 | convolution fusion | flops 18874368 | bytes 4718624 | tf_op jit(solution)/shard_map/js,sap->jap/dot_general | solution.py:26
  80.3 0.0 slice-start
  80.3 0.0 all-gather.5.cloned.1.call-update
  80.3 0.0 reduce-scatter.2.cloned.1.call-start
  80.4 0.0 copy-done.4
  80.4 0.6 dynamic-slice
  81.5 0.0 copy-done.3
  81.5 0.2 dynamic-update-slice
  81.7 7.3 %all-reduce = s32[48]{0:T(128)S(1)} all-reduce(s32[48]{0:T(128)S(1)} %dynamic-update-slice), channel_id=1, replica_groups=mesh['grp'=4,'blk'=8] {'grp'}, use_global_device_ids=true, to_apply=%add | all-reduce | flops 48 | bytes 384
  89.1 0.0 copy-done
  89.1 0.2 fusion.24
  89.2 0.1 dynamic_slice.14
  89.3 0.0 copy-done.2
  89.3 12.3 %all-gather.2 = f32[8,1,128]{2,1,0:T(1,128)S(1)} all-gather(f32[1,1,128]{2,1,0:T(1,128)S(1)} %bitcast.57), channel_id=2, replica_groups=mesh['grp'=4,'blk'=8] {'blk'}, dimensions={0}, use_global_device_ids=true | all-gather | bytes 4608 | tf_op jit(solution)/shard_map/all_gather | solution.py:34
  101.7 0.1 convolution_bitcast_fusion
  101.8 0.1 broadcast_add_fusion
  101.8 0.1 broadcast_subtract_fusion
  101.9 95.6 %all-gather.5.cloned.1.call-done = f32[2,1024,1536]{2,0,1:T(2,128)} async-done(((f32[2,128,1536]{2,0,1:T(2,128)}), f32[2,1024,1536]{2,0,1:T(2,128)}) %all-gather.5.cloned.1.call-update) | async-done | bytes 12582928 | tf_op jit(solution)/shard_map/all_gather | solution.py:33
  197.5 0.0 slice-start.1
  197.5 0.0 slice-start.2
  197.5 72.1 %bitcast_divide_fusion = f32[12,128,2,1024]{1,3,0,2:T(8,128)} fusion(f32[12,128,1536]{2,1,0:T(8,128)} %param.5, f32[2,1024,1536,1]{2,0,1,3:T(2,128)} %bitcast.60, f32[1024]{0:T(1024)S(1)} %bitcast.56, f32[12,128,2]{1,0,2:T(8,128)S(1)} %broadcast_subtract_fusion), kind=kOutput, calls=%fused_computation | convolution fusion | flops 57988349952 | bytes 34619392 | tf_op jit(solution)/shard_map/iap,jbp->iajb/dot_general | solution.py:35
  269.6 0.0 slice-done
  269.6 0.0 slice-done.1
  269.6 0.0 slice-done.2
  269.7 78.6 %fusion.13 = f32[1024,2,1536]{2,0,1:T(8,128)} fusion(f32[12,128,2,1024]{1,3,0,2:T(8,128)} %bitcast_divide_fusion, f32[12,128,1536]{2,1,0:T(8,128)S(1)} %bitcast.53), kind=kOutput, calls=%fused_computation.11 | convolution fusion | flops 57982058496 | bytes 34603008 | tf_op jit(solution)/shard_map/iajb,iap->bjp/dot_general | solution.py:46
  348.3 0.0 reduce-scatter.2.cloned.1.call-update
  348.3 127.6 %reduce-scatter.2.cloned.1.call-done = f32[128,2,1536]{2,0,1:T(8,128)} async-done(((f32[1024,2,1536]{2,0,1:T(8,128)}), f32[128,2,1536]{2,0,1:T(8,128)}) %reduce-scatter.2.cloned.1.call-update) | async-done | bytes 1572880 | tf_op jit(solution)/shard_map/reduce_scatter | solution.py:45
  475.9 9.5 %fusion.22 = f32[4,128,1536]{2,0,1:T(4,128)S(1)} fusion(f32[128,2,1536]{2,0,1:T(8,128)} %reduce-scatter.2.cloned.1.call-done, f32[2,4]{1,0:T(2,128)S(1)} %reduce_sum.18), kind=kOutput, calls=%fused_computation.17 | convolution fusion | flops 18874368 | bytes 4718624 | tf_op jit(solution)/shard_map/bjp,js->bsp/dot_general | solution.py:51
  485.4 1.0 copy.51
  486.4 37.9 %all_to_all.10 = f32[128,4,1536]{2,0,1:T(8,128)S(1)} all-to-all(f32[128,4,1536]{2,0,1:T(8,128)S(1)} %bitcast.54), channel_id=1, replica_groups=mesh['grp'=4,'blk'=8] {'grp'}, dimensions={1} | all-to-all | bytes 6291456 | tf_op jit(solution)/shard_map/all_to_all | solution.py:52
  524.3 12.4 %fusion.18 = f32[12,128,1536]{2,0,1:T(8,128)S(1)} fusion(f32[128,4,1536]{2,0,1:T(8,128)S(1)} %all_to_all.10, f32[4,12]{1,0:T(4,128)S(1)} %dynamic-slice_reduce_fusion), kind=kOutput, calls=%fused_computation.13 | convolution fusion | flops 113246208 | bytes 12583104 | tf_op jit(solution)/shard_map/sr,bsp->rbp/dot_general | solution.py:53
  536.8 0.0 copy-start.1
  536.8 75.9 %bitcast_add_fusion = f32[12,128,1536]{2,1,0:T(8,128)} fusion(f32[12,128,1536]{2,0,1:T(8,128)S(1)} %fusion.18, f32[12,128,2,1024]{1,3,0,2:T(8,128)} %bitcast_divide_fusion, f32[2,1024,1536,1]{2,0,1,3:T(2,128)} %bitcast.61), kind=kOutput, calls=%fused_computation.7 | convolution fusion | flops 57984417792 | bytes 44040192 | tf_op jit(solution)/shard_map/iajb,jbp->iap/dot_general | solution.py:43
  612.7 0.0 copy-done.1
  (3 shorter events, 0.0 us)
Async XLA Ops:
  6.5 82.5 %copy-start = (f32[48]{0:T(128)S(1)}, f32[48]{0:T(128)}, u32[]{:S(2)}) copy-start(f32[48]{0:T(128)} %param.8) | copy-start | bytes 580
  32.1 48.2 %copy-start.4 = (u32[32]{0:T(128)S(1)}, u32[32]{0:T(128)}, u32[]{:S(2)}) copy-start(u32[32]{0:T(128)} %constant.21) | copy-start | bytes 388
  32.1 49.3 %copy-start.3 = (s32[12]{0:T(128)S(1)}, s32[12]{0:T(128)}, u32[]{:S(2)}) copy-start(s32[12]{0:T(128)} %param.7) | copy-start | bytes 148
  32.2 57.2 %copy-start.2 = (f32[128]{0:T(128)S(1)}, f32[128]{0:T(128)}, u32[]{:S(2)}) copy-start(f32[128]{0:T(128)} %param.9) | copy-start | bytes 1540
  34.8 38.3 %all-to-all-start = ((f32[4,128,1536]{2,1,0:T(8,128)}), f32[4,128,1536]{2,1,0:T(8,128)S(1)}, u32[]{:S(2)}, u32[]{:S(2)}) async-start(f32[4,128,1536]{2,1,0:T(8,128)} %copy.21), calls=%async_computation | async-start | bytes 6291456 | tf_op jit(solution)/shard_map/all_to_all | solution.py:23
  38.5 159.0 %all-gather.5.cloned.1.call-start = ((), (), s32[]{:S(2)}) async-start(), calls=%async_computation.3 | async-start | bytes 14155776 | tf_op jit(solution)/shard_map/all_gather | solution.py:33
  80.3 189.4 %slice-start = ((s8[9437184]{0:T(1024)(128)(4,1)}), s8[1048576]{0:T(1024)(128)(4,1)S(1)}, s32[]{:S(2)}) async-start(s8[9437184]{0:T(1024)(128)(4,1)} %bitcast.52), calls=%async_computation.5 | async-start | bytes 2097152
  80.3 395.6 %reduce-scatter.2.cloned.1.call-start = ((), (), s32[]{:S(2)}) async-start(), calls=%async_computation.4 | async-start | bytes 14155776 | tf_op jit(solution)/shard_map/reduce_scatter | solution.py:45
  197.5 72.1 %slice-start.1 = ((s8[9437184]{0:T(1024)(128)(4,1)}), s8[4194304]{0:T(1024)(128)(4,1)S(1)}, s32[]{:S(2)}) async-start(s8[9437184]{0:T(1024)(128)(4,1)} %bitcast.52), calls=%async_computation.6 | async-start | bytes 8388608
  197.5 72.1 %slice-start.2 = ((s8[9437184]{0:T(1024)(128)(4,1)}), s8[4194304]{0:T(1024)(128)(4,1)S(1)}, s32[]{:S(2)}) async-start(s8[9437184]{0:T(1024)(128)(4,1)} %bitcast.52), calls=%async_computation.7 | async-start | bytes 8388608
  536.8 76.0 %copy-start.1 = (f32[48]{0:T(128)S(1)}, f32[48]{0:T(128)}, u32[]{:S(2)}) copy-start(f32[48]{0:T(128)} %param.8) | copy-start | bytes 580
Sparse Core Ops, SparseCore 0:
  80.4 117.0 all-gather.4
  348.4 127.4 reduce-scatter.1
where the time goes:
time: 628 us; the launch traced here: 620 us
  matrix products  272 us (43%)
  waiting for transfers between devices  258 us (41%)
  blocking collectives  67.1 us (11%)
  between operations  14.5 us (2%)
    reduce_scatter x1, waiting for transfers between devices, body(): lax.psum_scatter(jnp.einsum('iajb,iap->bjp', amplitudes, integrals, preci...  128 us
    all_gather x1, waiting for transfers between devices, body(): blocks = lax.all_gather(partner, 'blk', axis=1, tiled=True)  95.6 us
    dot_general x1, matrix products, body(): jnp.einsum('iajb,iap->bjp', amplitudes, integrals, precision=highest)  78.6 us
    dot_general x1, matrix products, body(): jnp.einsum('iajb,jbp->iap', amplitude, blocks, precision=highest)  75.9 us
    dot_general x1, matrix products, body(): jnp.einsum('iap,jbp->iajb', integrals, blocks, precision=highest)  72.1 us
    all_to_all x1, blocking collectives, body(): lax.all_to_all(returning, 'grp', split_axis=1, concat_axis=1, tiled=True)  37.9 us
    all_to_all x1, waiting for transfers between devices, body(): lax.all_to_all(outgoing, 'grp', split_axis=0, concat_axis=0, tiled=True)  34.4 us
    dot_general x1, matrix products, body(): outgoing = jnp.einsum('gr,rap->gap', selected, integrals, precision=highest)  15.8 us
  transfers between devices with their start and end apart: 3, of which 3 were waited for; matrix products, arithmetic and copies ran while one was open for 0% of the time, Pallas kernels for 0%

commit v1 on v0

v1 whole, which is shorter than its diff:
```python
import functools

import jax
import jax.numpy as jnp
from jax import lax
from jax.experimental import pallas as pl
from jax.experimental.pallas import tpu as pltpu
from jax.sharding import PartitionSpec as P

PIECES = 2
CORES = 2
VMEM = 56 * 1024 * 1024


def split(x):
    high = x.astype(jnp.bfloat16)
    return high, (x - high.astype(jnp.float32)).astype(jnp.bfloat16)


def dot(a, b, contract):
    return lax.dot_general(a, b, ((contract[:1], contract[1:]), ((), ())), preferred_element_type=jnp.float32)


def block_rows(total, most):
    rows = most
    while total % rows:
        rows //= 2
    return rows


def split_kernel(x_ref, high_ref, low_ref):
    high, low = split(x_ref[...])
    high_ref[...] = high
    low_ref[...] = low


def split_rows(x):
    rows, width = x.shape
    step = block_rows(rows, 256)
    spec = pl.BlockSpec((step, width), lambda i: (i, 0))
    half = jax.ShapeDtypeStruct(x.shape, jnp.bfloat16)
    return pl.pallas_call(
        split_kernel,
        grid=(rows // step,),
        in_specs=[spec],
        out_specs=[spec, spec],
        out_shape=[half, half],
        cost_estimate=pl.CostEstimate(flops=2 * rows * width, bytes_accessed=8 * rows * width, transcendentals=0),
        compiler_params=pltpu.CompilerParams(vmem_limit_bytes=VMEM),
    )(x)


def unit_kernel(steps, chip_ref, own_high, own_low, sib_high, sib_low, row_ref, col_ref, *refs):
    parts = refs[:PIECES]
    t_high, t_low, r_high, r_low = refs[PIECES:PIECES + 4]
    grads = refs[PIECES + 4:2 * PIECES + 4]
    step = pl.program_id(0)
    width = parts[0].shape[0]

    @pl.when(step == 0)
    def _():
        for p in range(PIECES):
            high, low = split(parts[p][...])
            r_high[p * width:(p + 1) * width] = high
            r_low[p * width:(p + 1) * width] = low
            grads[p][...] = jnp.zeros_like(grads[p])

    def work(a_high_ref, a_low_ref):
        a_high = a_high_ref[...]
        a_low = a_low_ref[...]
        high, low = r_high[...], r_low[...]
        pair = dot(a_high, high, (1, 1)) + dot(a_high, low, (1, 1)) + dot(a_low, high, (1, 1))
        amplitude = pair / (row_ref[...] + col_ref[0])
        up, down = split(amplitude)
        t_high[...] = up
        t_low[...] = down
        up, down = split(amplitude.T)
        for p in range(PIECES):
            part = slice(p * width, (p + 1) * width)
            grads[p][...] += (
                dot(up[part], a_high, (1, 0)) + dot(down[part], a_high, (1, 0)) + dot(up[part], a_low, (1, 0))
            )

    @pl.when(step < steps)
    def _():
        work(own_high, own_low)

    @pl.when(step >= steps)
    def _():
        work(sib_high, sib_low)


def unit(chip, halves, row_energy, col_energy, parts):
    (own_high, own_low), (sib_high, sib_low) = halves
    rows, aux = own_high.shape
    step = block_rows(rows, 512)
    steps = rows // step
    part_rows = parts[0].shape[0]
    cols = part_rows * PIECES
    own = pl.BlockSpec((step, aux), lambda i, c: (jnp.minimum(i, steps - 1), 0))
    sib = pl.BlockSpec((step, aux), lambda i, c: (jnp.maximum(i - steps, 0), 0))
    whole = lambda shape: pl.BlockSpec(shape, lambda i, c: (0, 0))
    bf16 = lambda *shape: jax.ShapeDtypeStruct(shape, jnp.bfloat16)
    t_spec = pl.BlockSpec((step, cols), lambda i, c: (i, 0))
    outs = pl.pallas_call(
        functools.partial(unit_kernel, steps),
        grid_spec=pltpu.PrefetchScalarGridSpec(
            num_scalar_prefetch=1,
            grid=(2 * steps,),
            in_specs=[
                own, own, sib, sib,
                pl.BlockSpec((step, 1), lambda i, c: (i, 0)),
                pl.BlockSpec((1, 1, cols), lambda i, c: (c[0], 0, 0)),
            ] + [whole((part_rows, aux))] * PIECES,
            out_specs=[t_spec, t_spec, whole((cols, aux)), whole((cols, aux))] + [whole((part_rows, aux))] * PIECES,
        ),
        out_shape=[bf16(2 * rows, cols)] * 2 + [bf16(cols, aux)] * 2
        + [jax.ShapeDtypeStruct((part_rows, aux), jnp.float32)] * PIECES,
        cost_estimate=pl.CostEstimate(
            flops=24 * rows * aux * cols, bytes_accessed=8 * rows * aux + 16 * cols * aux, transcendentals=0
        ),
        compiler_params=pltpu.CompilerParams(vmem_limit_bytes=VMEM),
    )(chip, own_high, own_low, sib_high, sib_low, row_energy, col_energy, *parts)
    return outs[:4], outs[4:]


def forward_kernel(count, *refs):
    start = refs[:-1][4 * count:]
    total = start[0][...] if start else None
    for u in range(count):
        t_high, t_low, r_high, r_low = (ref[...] for ref in refs[4 * u:4 * u + 4])
        term = dot(t_high, r_high, (1, 0)) + dot(t_high, r_low, (1, 0)) + dot(t_low, r_high, (1, 0))
        total = term if total is None else total + term
    refs[-1][...] = total


def forward(half, units, start):
    rows = units[0][0].shape[0] // 2
    cols, aux = units[0][2].shape
    step = block_rows(rows, 256)
    steps = rows // step
    t_spec = pl.BlockSpec((step, cols), lambda i: (i + half * steps, 0))
    r_spec = pl.BlockSpec((cols, aux), lambda i: (0, 0))
    out_spec = pl.BlockSpec((step, aux), lambda i: (i, 0))
    operands = [x for one in units for x in one] + ([] if start is None else [start])
    return pl.pallas_call(
        functools.partial(forward_kernel, len(units)),
        grid=(steps,),
        in_specs=[t_spec, t_spec, r_spec, r_spec] * len(units) + [out_spec] * (start is not None),
        out_specs=out_spec,
        out_shape=jax.ShapeDtypeStruct((rows, aux), jnp.float32),
        cost_estimate=pl.CostEstimate(
            flops=6 * rows * aux * cols * len(units), bytes_accessed=8 * rows * aux, transcendentals=0
        ),
        compiler_params=pltpu.CompilerParams(vmem_limit_bytes=VMEM),
    )(*operands)


def ring_order(chips):
    return [0] + list(range(1, chips, 2)) + [z for z in range(chips - 1, 0, -1) if z % 2 == 0]


def body(integrals, pair_lists, row_orbital, occ_energy, vir_energy):
    own_count, width, aux = integrals.shape
    slots = pair_lists.shape[1]
    groups = lax.axis_size("grp")
    me = lax.axis_index("grp")
    place = lax.axis_index("blk")
    chips = lax.axis_size("blk") // CORES
    core = lax.rem(place, CORES)
    chip = lax.div(place, CORES)
    order = ring_order(chips)
    pairs = [
        (order[i] * CORES + c, order[(i + 1) % chips] * CORES + c) for i in range(chips) for c in range(CORES)
    ]
    swap = [(i, i ^ 1) for i in range(chips * CORES)]
    hop = lambda x: lax.ppermute(x, "blk", pairs)
    sibling = lambda x: lax.ppermute(x, "blk", swap)
    to_group = lambda x, k: lax.ppermute(x, "grp", [(g, g ^ k) for g in range(groups)])

    own_rows = integrals.reshape(own_count * width, aux)
    sib_rows = sibling(own_rows)

    picks = row_orbital[:, None] == lax.broadcasted_iota(jnp.int32, (own_count, occ_energy.shape[0]), 1)
    own_energy = jnp.sum(jnp.where(picks, occ_energy[None, :], 0.0), axis=1)
    packet = jnp.concatenate([pair_lists[0].astype(jnp.float32), own_energy])
    table = lax.all_gather(packet, "grp", axis=0)
    listed = table[:, :slots].astype(jnp.int32)
    row_energies = table[:, slots:].reshape(-1)
    holder = lax.div(listed, own_count)
    local = listed - holder * own_count
    mine = holder[me]

    rows_for = []
    asked_by = []
    for k in range(groups):
        asks = holder[me ^ k] == me
        asked_by.append(jnp.any(asks))
        rows_for.append(jnp.sum(jnp.where(asks, local[me ^ k], 0)))
    part_width = width // PIECES
    partners = []
    for p in range(PIECES):
        got = []
        for k in range(groups):
            block = lax.dynamic_slice(integrals, (rows_for[k], p * part_width, 0), (1, part_width, aux))[0]
            got.append(to_group(block, k) if k else block)
        chosen = []
        for s in range(slots):
            one = jnp.zeros((part_width, aux), jnp.float32)
            for k in range(groups):
                one = jnp.where(mine[s] == me ^ k, got[k], one)
            chosen.append(one)
        partners.append(jnp.concatenate(chosen, axis=0))

    virtual = lax.all_gather(vir_energy, "blk", axis=0)
    virtual = lax.dynamic_index_in_dim(virtual.reshape(chips, CORES, width), core, 1, keepdims=False)
    row_ids = lax.broadcasted_iota(jnp.int32, (slots, row_energies.shape[0]), 1)
    partner_energy = jnp.sum(jnp.where(listed[me][:, None] == row_ids, row_energies[None, :], 0.0), axis=1)
    col_energy = partner_energy[None, None, :, None] - virtual.reshape(chips, PIECES, 1, part_width)
    col_energy = col_energy.reshape(chips, 1, slots * width)
    sib_virtual = sibling(vir_energy)
    row_energy = own_energy[None, :, None] - jnp.stack([vir_energy, sib_virtual])[:, None, :]
    row_energy = row_energy.reshape(CORES * own_count * width, 1)

    halves = (split_rows(own_rows), split_rows(sib_rows))
    spot = sum(jnp.where(chip == z, i, 0) for i, z in enumerate(order))
    chip_at = lambda i: sum(jnp.where(i == j, z, 0) for j, z in enumerate(order))

    units = []
    grads = []
    parts = partners
    for s in range(chips):
        source = chip_at(lax.rem(spot - s + chips, chips)).astype(jnp.int32).reshape(1)
        one, grad = unit(source, halves, row_energy, col_energy, parts)
        units.append(one)
        grads.append(grad)
        if s < chips - 1:
            parts = [hop(x) for x in parts]

    shares = []
    for p in range(PIECES):
        total = grads[1][p]
        for s in range(2, chips + 1):
            total = hop(total) + grads[s % chips][p]
        shares.append(total.reshape(slots, part_width, aux))

    away = sibling(forward(1, units, None))
    density = forward(0, units, away).reshape(own_count, width, aux)
    for p in range(PIECES):
        for k in range(groups):
            back = jnp.zeros((part_width, aux), jnp.float32)
            for s in range(slots):
                back = jnp.where(mine[s] == me ^ k, shares[p][s], back)
            back = to_group(back, k) if k else back
            spot_of = (rows_for[k], p * part_width, 0)
            old = lax.dynamic_slice(density, spot_of, (1, part_width, aux))
            new = old + jnp.where(asked_by[k], back, 0.0)[None]
            density = lax.dynamic_update_slice(density, new, spot_of)
    return density


def solution(mesh):
    in_specs = (P("grp", "blk", None), P("grp", None), P("grp"), P(), P("blk"))
    out_specs = P("grp", "blk", None)
    return jax.shard_map(body, mesh=mesh, in_specs=in_specs, out_specs=out_specs, check_vma=False)
```

time: 628 us -> 476 us (0.76); the launches traced: 620 us -> 476 us
  matrix products: 272 us -> 0 us
  Pallas kernels: 0 us -> 209 us
  waiting for transfers between devices: 258 us -> 140 us
  other arithmetic: 0.4 us -> 25.9 us
  starting transfers between devices: 3.78 us -> 26.4 us
  blocking collectives: 67.1 us -> 47.8 us
  local copies, waits for them, and re-layouts: 4.66 us -> 12.7 us
    dot_general x9 -> x0, matrix products: 272 us -> none  [the longest x1 78.6 us: body(): jnp.einsum('iajb,iap->bjp', amplitudes, integrals, precision=highest)]
    pallas_call x0 -> x8, Pallas kernels: none -> 209 us  [the longest x4 150 us: unit(): pl.pallas_call(functools.partial(unit_kernel, steps), grid_spec=pltpu.Pre...]
    ppermute x0 -> x27, waiting for transfers between devices: none -> 140 us  [the longest x12 117 us: body(): hop = lambda x: lax.ppermute(x, 'blk', pairs)]
    reduce_scatter x1 -> x0, waiting for transfers between devices: 128 us -> none  [body(): lax.psum_scatter(jnp.einsum('iajb,iap->bjp', amplitudes, integrals, preci...]
    all_gather x1 -> x0, waiting for transfers between devices: 95.6 us -> none  [body(): blocks = lax.all_gather(partner, 'blk', axis=1, tiled=True)]
    all_to_all x1 -> x0, blocking collectives: 37.9 us -> none  [body(): lax.all_to_all(returning, 'grp', split_axis=1, concat_axis=1, tiled=True)]
    all_to_all x1 -> x0, waiting for transfers between devices: 34.4 us -> none  [body(): lax.all_to_all(outgoing, 'grp', split_axis=0, concat_axis=0, tiled=True)]
    ppermute x0 -> x27, starting transfers between devices: none -> 26.4 us  [the longest x12 14.5 us: body(): hop = lambda x: lax.ppermute(x, 'blk', pairs)]
  transfers between devices with their start and end apart: 3 -> 27, of which waited for: 3 -> 11; matrix products, arithmetic and copies ran while one was open for 0% -> 7% of each run, Pallas kernels for 0% -> 32%
where the time goes in v1:
time: 476 us
  Pallas kernels  209 us (44%)
  waiting for transfers between devices  140 us (29%)
  blocking collectives  47.8 us (10%)
  starting transfers between devices  26.4 us (6%)
  other arithmetic  25.9 us (5%)
  between operations  13.7 us (3%)
  local copies, waits for them, and re-layouts  12.7 us (3%)
    pallas_call x4, Pallas kernels, unit(): pl.pallas_call(functools.partial(unit_kernel, steps), grid_spec=pltpu.Pre...  150 us
    ppermute x12, waiting for transfers between devices, body(): hop = lambda x: lax.ppermute(x, 'blk', pairs)  117 us
    pallas_call x2, Pallas kernels, forward(): pl.pallas_call(functools.partial(forward_kernel, len(units)), grid=(steps...  41.4 us
    all_gather x1, blocking collectives, body(): virtual = lax.all_gather(vir_energy, 'blk', axis=0)  36.9 us
    ppermute x12, waiting for transfers between devices, body(): lax.ppermute(x, 'grp', [(g, g ^ k) for g in range(groups)])  23.3 us
    dynamic_update_slice x8, other arithmetic, body(): density = lax.dynamic_update_slice(density, new, spot_of)  19.6 us
    pallas_call x2, Pallas kernels, split_rows(): pl.pallas_call(split_kernel, grid=(rows // step,), in_specs=[spec], out_s...  17.3 us
    ppermute x12, starting transfers between devices, body(): hop = lambda x: lax.ppermute(x, 'blk', pairs)  14.5 us
  transfers between devices with their start and end apart: 27, of which 11 were waited for; matrix products, arithmetic and copies ran while one was open for 7% of the time, Pallas kernels for 32%

profile of v1, /device:TPU:0, one launch (start us, length us, event | category | flops | bytes accessed | tf_op | source)
XLA Modules:
  0.0 475.6 jit_solution(6374319593294226024)
XLA Ops:
  0.0 0.5 collective-permute-start
  0.5 1.2 dynamic-slice
  2.3 0.9 select_reduce_fusion
  3.2 0.7 convert_bitcast_fusion
  4.0 10.9 %all-reduce = f32[56]{0:T(128)S(1)} all-reduce(f32[56]{0:T(128)S(1)} %maximum_dynamic-update-slice_fusion), channel_id=2, replica_groups=mesh['grp'=4,'blk'=8] {'grp'}, use_global_device_ids=true, to_apply=%add | all-reduce | flops 56 | bytes 448
  15.0 0.7 compare_reduce_fusion.3
  15.8 0.7 fusion.20
  22.2 2.9 dynamic-slice_bitcast_fusion
  25.1 0.5 collective-permute-start.2
  25.6 0.2 collective-permute-start.3
  25.8 2.8 collective-permute-start.4
  28.6 0.5 collective-permute-start.5
  29.1 9.0 %collective-permute-done.2 = f32[64,1536]{1,0:T(8,128)S(1)} collective-permute-done((f32[64,1536]{1,0:T(8,128)S(1)}, f32[64,1536]{1,0:T(8,128)S(1)}, u32[]{:S(2)}, u32[]{:S(2)}) %collective-permute-start.2) | collective-permute-done | bytes 393248 | tf_op jit(solution)/shard_map/ppermute | solution.py:179
  38.0 0.2 collective-permute-start.6
  38.2 11.8 %collective-permute-done.3 = f32[64,1536]{1,0:T(8,128)S(1)} collective-permute-done((f32[64,1536]{1,0:T(8,128)S(1)}, f32[64,1536]{1,0:T(8,128)S(1)}, u32[]{:S(2)}, u32[]{:S(2)}) %collective-permute-start.3) | collective-permute-done | bytes 393248 | tf_op jit(solution)/shard_map/ppermute | solution.py:179
  51.3 0.6 fusion.23
  57.6 2.4 collective-permute-done.6
  60.1 1.4 fusion.11
  61.5 1.6 collective-permute-start.9
  63.2 2.6 collective-permute-start.8
  65.9 36.9 %all-gather.2 = f32[8,1,128]{2,1,0:T(1,128)S(1)} all-gather(f32[1,1,128]{2,1,0:T(1,128)S(1)} %bitcast.89), channel_id=3, replica_groups=mesh['grp'=4,'blk'=8] {'blk'}, dimensions={0}, use_global_device_ids=true | all-gather | bytes 4608 | tf_op jit(solution)/shard_map/all_gather | solution.py:215
  103.1 0.7 collective-permute-start.11
  103.9 1.6 collective-permute-start.10
  105.5 0.2 fusion.17
  105.8 0.6 broadcast_subtract_fusion.1.col_ref
  106.4 8.7 %shard_map.55 = (bf16[1536,1536]{1,0:T(8,128)(2,1)}, bf16[1536,1536]{1,0:T(8,128)(2,1)}) custom-call(f32[1536,1536]{1,0:T(8,128)} %bitcast.86), custom_call_target="tpu_custom_call" | custom-call | flops 4718592 | bytes 18874368 | tf_op jit(solution)/shard_map/pallas_call | solution.py:42
  115.2 2.7 sub.69.row_ref
  117.8 6.7 %collective-permute-done.11.refs_1_ = f32[128,1536]{1,0:T(8,128)} collective-permute-done((f32[128,1536]{1,0:T(8,128)S(1)}, f32[128,1536]{1,0:T(8,128)}, u32[]{:S(2)}, u32[]{:S(2)}) %collective-permute-start.11) | collective-permute-done | bytes 786464 | tf_op jit(solution)/shard_map/ppermute | solution.py:177
  124.6 16.8 %collective-permute-done.10.refs_0_ = f32[128,1536]{1,0:T(8,128)} collective-permute-done((f32[128,1536]{1,0:T(8,128)S(1)}, f32[128,1536]{1,0:T(8,128)}, u32[]{:S(2)}, u32[]{:S(2)}) %collective-permute-start.10) | collective-permute-done | bytes 786464 | tf_op jit(solution)/shard_map/ppermute | solution.py:177
  141.4 8.7 %shard_map.56 = (bf16[1536,1536]{1,0:T(8,128)(2,1)}, bf16[1536,1536]{1,0:T(8,128)(2,1)}) custom-call(f32[1536,1536]{1,0:T(8,128)} %collective-permute-done.x_ref), custom_call_target="tpu_custom_call" | custom-call | flops 4718592 | bytes 18874368 | tf_op jit(solution)/shard_map/pallas_call | solution.py:42
  150.1 37.5 %shard_map.57 = (bf16[3072,256]{1,0:T(8,128)(2,1)}, bf16[3072,256]{1,0:T(8,128)(2,1)}, bf16[256,1536]{1,0:T(8,128)(2,1)}, bf16[256,1536]{1,0:T(8,128)(2,1)}, f32[128,1536]{1,0:T(8,128)}, /*index=5*/f32[128,1536]{1,0:T(8,128)}) custom-call(s32[1]{0:T(128)} %bitcast.chip_ref, bf16[1536,1536]{1,0:T(8,128)(2,1)} %get-tuple-element.33.own_high, ...), custom_call_target="tpu_custom_call" | custom-call | flops 14495514624 | bytes 25165824 | tf_op jit(solution)/shard_map/pallas_call | solution.py:105
  187.6 37.7 %shard_map.59 = (bf16[3072,256]{1,0:T(8,128)(2,1)}, bf16[3072,256]{1,0:T(8,128)(2,1)}, bf16[256,1536]{1,0:T(8,128)(2,1)}, bf16[256,1536]{1,0:T(8,128)(2,1)}, f32[128,1536]{1,0:T(8,128)}, /*index=5*/f32[128,1536]{1,0:T(8,128)}) custom-call(s32[1]{0:T(128)} %bitcast.22.chip_ref, bf16[1536,1536]{1,0:T(8,128)(2,1)} %get-tuple-element.33.own_high, ...), custom_call_target="tpu_custom_call" | custom-call | flops 14495514624 | bytes 25165824 | tf_op jit(solution)/shard_map/pallas_call | solution.py:105
  225.3 37.5 %shard_map.58 = (bf16[3072,256]{1,0:T(8,128)(2,1)}, bf16[3072,256]{1,0:T(8,128)(2,1)}, bf16[256,1536]{1,0:T(8,128)(2,1)}, bf16[256,1536]{1,0:T(8,128)(2,1)}, f32[128,1536]{1,0:T(8,128)}, /*index=5*/f32[128,1536]{1,0:T(8,128)}) custom-call(s32[1]{0:T(128)} %bitcast.21.chip_ref, bf16[1536,1536]{1,0:T(8,128)(2,1)} %get-tuple-element.33.own_high, ...), custom_call_target="tpu_custom_call" | custom-call | flops 14495514624 | bytes 25165824 | tf_op jit(solution)/shard_map/pallas_call | solution.py:105
  262.8 0.9 copy-done.12
  263.7 0.3 copy-done.13
  264.0 37.7 %shard_map.60 = (bf16[3072,256]{1,0:T(8,128)(2,1)}, bf16[3072,256]{1,0:T(8,128)(2,1)}, bf16[256,1536]{1,0:T(8,128)(2,1)}, bf16[256,1536]{1,0:T(8,128)(2,1)}, f32[128,1536]{1,0:T(8,128)}, /*index=5*/f32[128,1536]{1,0:T(8,128)}) custom-call(s32[1]{0:T(128)} %bitcast.23.chip_ref, bf16[1536,1536]{1,0:T(8,128)(2,1)} %get-tuple-element.33.own_high, ...), custom_call_target="tpu_custom_call" | custom-call | flops 14495514624 | bytes 25165824 | tf_op jit(solution)/shard_map/pallas_call | solution.py:105
  301.7 20.5 %shard_map.61 = f32[1536,1536]{1,0:T(8,128)} custom-call(bf16[3072,256]{1,0:T(8,128)(2,1)} %get-tuple-element.37.refs_0_, bf16[3072,256]{1,0:T(8,128)(2,1)} %get-tuple-element.38.refs_1_, bf16[256,1536]{1,0:T(8,128)(2,1)} %get-tuple-element.39.refs_2_, bf16[256,1536]{1,0:T(8,128)(2,1)} %get-tuple-element.40.refs_3_, ...), custom_call_target="tpu_custom_call" | custom-call | flops 14495514624 | bytes 18874368 | tf_op jit(solution)/shard_map/pallas_call | solution.py:146
  322.4 2.3 collective-permute-start.15
  324.8 18.9 %collective-permute-done.15 = f32[128,1536]{1,0:T(8,128)S(1)} collective-permute-done((f32[128,1536]{1,0:T(8,128)S(1)}, f32[128,1536]{1,0:T(8,128)S(1)}, u32[]{:S(2)}, u32[]{:S(2)}) %collective-permute-start.15) | collective-permute-done | bytes 786464 | tf_op jit(solution)/shard_map/ppermute | solution.py:177
  343.8 1.4 collective-permute-start.16
  345.2 15.4 %collective-permute-done.21 = f32[128,1536]{1,0:T(8,128)S(1)} collective-permute-done((f32[128,1536]{1,0:T(8,128)S(1)}, f32[128,1536]{1,0:T(8,128)S(1)}, u32[]{:S(2)}, u32[]{:S(2)}) %collective-permute-start.21) | collective-permute-done | bytes 786464 | tf_op jit(solution)/shard_map/ppermute | solution.py:177
  360.7 1.4 collective-permute-start.22
  362.1 15.4 %collective-permute-done.16 = f32[128,1536]{1,0:T(8,128)S(1)} collective-permute-done((f32[128,1536]{1,0:T(8,128)S(1)}, f32[128,1536]{1,0:T(8,128)S(1)}, u32[]{:S(2)}, u32[]{:S(2)}) %collective-permute-start.16) | collective-permute-done | bytes 786464 | tf_op jit(solution)/shard_map/ppermute | solution.py:177
  377.5 1.4 collective-permute-start.17
  378.9 15.4 %collective-permute-done.22 = f32[128,1536]{1,0:T(8,128)S(1)} collective-permute-done((f32[128,1536]{1,0:T(8,128)S(1)}, f32[128,1536]{1,0:T(8,128)S(1)}, u32[]{:S(2)}, u32[]{:S(2)}) %collective-permute-start.22) | collective-permute-done | bytes 786464 | tf_op jit(solution)/shard_map/ppermute | solution.py:177
  394.4 1.4 collective-permute-start.23
  395.8 15.4 %collective-permute-done.17 = f32[128,1536]{1,0:T(8,128)S(1)} collective-permute-done((f32[128,1536]{1,0:T(8,128)S(1)}, f32[128,1536]{1,0:T(8,128)S(1)}, u32[]{:S(2)}, u32[]{:S(2)}) %collective-permute-start.17) | collective-permute-done | bytes 786464 | tf_op jit(solution)/shard_map/ppermute | solution.py:177
  411.4 1.1 collective-permute-start.18
  412.5 1.5 collective-permute-start.19
  413.9 1.0 collective-permute-start.20
  414.9 12.8 %collective-permute-done.23 = f32[128,1536]{1,0:T(8,128)S(1)} collective-permute-done((f32[128,1536]{1,0:T(8,128)S(1)}, f32[128,1536]{1,0:T(8,128)S(1)}, u32[]{:S(2)}, u32[]{:S(2)}) %collective-permute-start.23) | collective-permute-done | bytes 786464 | tf_op jit(solution)/shard_map/ppermute | solution.py:177
  428.0 1.1 collective-permute-start.24
  429.1 3.5 copy-done.9
  432.6 1.5 collective-permute-start.25
  434.1 20.9 %shard_map.62 = f32[1536,1536]{1,0:T(8,128)} custom-call(bf16[3072,256]{1,0:T(8,128)(2,1)} %get-tuple-element.37.refs_0_, bf16[3072,256]{1,0:T(8,128)(2,1)} %get-tuple-element.38.refs_1_, bf16[256,1536]{1,0:T(8,128)(2,1)} %get-tuple-element.39.refs_2_, bf16[256,1536]{1,0:T(8,128)(2,1)} %get-tuple-element.40.refs_3_, ...), custom_call_target="tpu_custom_call" | custom-call | flops 14495514624 | bytes 18874368 | tf_op jit(solution)/shard_map/pallas_call | solution.py:146
  455.0 2.5 fusion.7
  457.5 1.0 collective-permute-start.26
  458.4 2.4 fusion.6
  460.9 2.4 fusion.5
  463.3 2.4 fusion.4
  465.8 2.5 fusion.3
  468.3 2.5 fusion.2
  470.7 2.4 fusion.1
  473.2 2.4 fusion
  (77 shorter events, 2.0 us)
Async XLA Ops:
  0.0 65.8 %copy-start.8 = (f32[128]{0:T(128)S(1)}, f32[128]{0:T(128)}, u32[]{:S(2)}) copy-start(f32[128]{0:T(128)} %param.9) | copy-start | bytes 1540
  0.0 141.4 %collective-permute-start = (f32[1536,1536]{1,0:T(8,128)}, f32[1536,1536]{1,0:T(8,128)}, u32[]{:S(2)}, u32[]{:S(2)}) collective-permute-start(f32[1536,1536]{1,0:T(8,128)} %bitcast.85), channel_id=1, source_target_pairs={{0,1},{1,0},{2,3},{3,2},{4,5},{5,4},{6,7},{7,6},{8,9},{9,8},{10,11... | collective-permute-start | bytes 28311560 | tf_op jit(solution)/shard_map/ppermute | solution.py:178
  25.1 13.0 %collective-permute-start.2 = (f32[64,1536]{1,0:T(8,128)S(1)}, f32[64,1536]{1,0:T(8,128)S(1)}, u32[]{:S(2)}, u32[]{:S(2)}) collective-permute-start(f32[64,1536]{1,0:T(8,128)S(1)} %get-tuple-element.81), channel_id=1, source_target_pairs={{0,24},{8,16},{16,8},{24,0},{1,25},{9,17},{17,9},{25,1},{2,26},{10... | collective-permute-start | bytes 1179656 | tf_op jit(solution)/shard_map/ppermute | solution.py:179
  25.6 24.5 %collective-permute-start.3 = (f32[64,1536]{1,0:T(8,128)S(1)}, f32[64,1536]{1,0:T(8,128)S(1)}, u32[]{:S(2)}, u32[]{:S(2)}) collective-permute-start(f32[64,1536]{1,0:T(8,128)S(1)} %get-tuple-element.80), channel_id=1, source_target_pairs={{0,16},{8,24},{16,0},{24,8},{1,17},{9,25},{17,1},{25,9},{2,18},{10... | collective-permute-start | bytes 1179656 | tf_op jit(solution)/shard_map/ppermute | solution.py:179
  25.8 31.8 %collective-permute-start.4 = (f32[64,1536]{1,0:T(8,128)}, f32[64,1536]{1,0:T(8,128)S(1)}, u32[]{:S(2)}, u32[]{:S(2)}) collective-permute-start(f32[64,1536]{1,0:T(8,128)} %get-tuple-element.79), channel_id=1, source_target_pairs={{0,8},{8,0},{16,24},{24,16},{1,9},{9,1},{17,25},{25,17},{2,10},{10... | collective-permute-start | bytes 1179656 | tf_op jit(solution)/shard_map/ppermute | solution.py:179
  28.6 29.1 %collective-permute-start.5 = (f32[64,1536]{1,0:T(8,128)S(1)}, f32[64,1536]{1,0:T(8,128)S(1)}, u32[]{:S(2)}, u32[]{:S(2)}) collective-permute-start(f32[64,1536]{1,0:T(8,128)S(1)} %get-tuple-element.78), channel_id=1, source_target_pairs={{0,24},{8,16},{16,8},{24,0},{1,25},{9,17},{17,9},{25,1},{2,26},{10... | collective-permute-start | bytes 1179656 | tf_op jit(solution)/shard_map/ppermute | solution.py:179
  38.0 22.0 %collective-permute-start.6 = (f32[64,1536]{1,0:T(8,128)S(1)}, f32[64,1536]{1,0:T(8,128)S(1)}, u32[]{:S(2)}, u32[]{:S(2)}) collective-permute-start(f32[64,1536]{1,0:T(8,128)S(1)} %get-tuple-element.77), channel_id=1, source_target_pairs={{0,16},{8,24},{16,0},{24,8},{1,17},{9,25},{17,1},{25,9},{2,18},{10... | collective-permute-start | bytes 1179656 | tf_op jit(solution)/shard_map/ppermute | solution.py:179
  50.0 10.0 %collective-permute-start.7 = (f32[64,1536]{1,0:T(8,128)S(1)}, f32[64,1536]{1,0:T(8,128)S(1)}, u32[]{:S(2)}, u32[]{:S(2)}) collective-permute-start(f32[64,1536]{1,0:T(8,128)S(1)} %get-tuple-element.76), channel_id=1, source_target_pairs={{0,8},{8,0},{16,24},{24,16},{1,9},{9,1},{17,25},{25,17},{2,10},{10... | collective-permute-start | bytes 1179656 | tf_op jit(solution)/shard_map/ppermute | solution.py:179
  61.5 88.6 %copy-start = (f32[128,1536]{1,0:T(8,128)}, f32[128,1536]{1,0:T(8,128)S(1)}, u32[]{:S(2)}) copy-start(f32[128,1536]{1,0:T(8,128)S(1)} %pad_maximum_fusion.1.refs_1_) | copy-start | bytes 2359300
  61.5 41.6 %collective-permute-start.9 = (f32[128,1536]{1,0:T(8,128)S(1)}, f32[128,1536]{1,0:T(8,128)S(1)}, u32[]{:S(2)}, u32[]{:S(2)}) collective-permute-start(f32[128,1536]{1,0:T(8,128)S(1)} %pad_maximum_fusion.1.refs_1_), channel_id=1, source_target_pairs={{0,2},{1,3},{2,6},{3,7},{6,4},{7,5},{4,0},{5,1},{8,10},{9,11},{10,... | collective-permute-start | bytes 2359304 | tf_op jit(solution)/shard_map/ppermute | solution.py:177
  63.2 86.9 %copy-start.1 = (f32[128,1536]{1,0:T(8,128)}, f32[128,1536]{1,0:T(8,128)S(1)}, u32[]{:S(2)}) copy-start(f32[128,1536]{1,0:T(8,128)S(1)} %pad_maximum_fusion.refs_0_) | copy-start | bytes 2359300
  63.2 40.7 %collective-permute-start.8 = (f32[128,1536]{1,0:T(8,128)S(1)}, f32[128,1536]{1,0:T(8,128)S(1)}, u32[]{:S(2)}, u32[]{:S(2)}) collective-permute-start(f32[128,1536]{1,0:T(8,128)S(1)} %pad_maximum_fusion.refs_0_), channel_id=1, source_target_pairs={{0,2},{1,3},{2,6},{3,7},{6,4},{7,5},{4,0},{5,1},{8,10},{9,11},{10,... | collective-permute-start | bytes 2359304 | tf_op jit(solution)/shard_map/ppermute | solution.py:177
  65.8 49.2 %collective-permute-start.1 = (f32[128]{0:T(128)S(1)}, f32[128]{0:T(128)S(1)}, u32[]{:S(2)}, u32[]{:S(2)}) collective-permute-start(f32[128]{0:T(128)S(1)} %copy-done.8), channel_id=1, source_target_pairs={{0,1},{1,0},{2,3},{3,2},{4,5},{5,4},{6,7},{7,6},{8,9},{9,8},{10,11... | collective-permute-start | bytes 1544 | tf_op jit(solution)/shard_map/ppermute | solution.py:178
  103.1 47.0 %copy-start.10 = (f32[128,1536]{1,0:T(8,128)}, f32[128,1536]{1,0:T(8,128)S(1)}, u32[]{:S(2)}) copy-start(f32[128,1536]{1,0:T(8,128)S(1)} %collective-permute-done.9.refs_1_) | copy-start | bytes 2359300
  103.1 21.4 %collective-permute-start.11 = (f32[128,1536]{1,0:T(8,128)S(1)}, f32[128,1536]{1,0:T(8,128)}, u32[]{:S(2)}, u32[]{:S(2)}) collective-permute-start(f32[128,1536]{1,0:T(8,128)S(1)} %collective-permute-done.9.refs_1_), channel_id=1, source_target_pairs={{0,2},{1,3},{2,6},{3,7},{6,4},{7,5},{4,0},{5,1},{8,10},{9,11},{10,... | collective-permute-start | bytes 2359304 | tf_op jit(solution)/shard_map/ppermute | solution.py:177
  103.9 46.2 %copy-start.11 = (f32[128,1536]{1,0:T(8,128)}, f32[128,1536]{1,0:T(8,128)S(1)}, u32[]{:S(2)}) copy-start(f32[128,1536]{1,0:T(8,128)S(1)} %collective-permute-done.8.refs_0_) | copy-start | bytes 2359300
  103.9 37.5 %collective-permute-start.10 = (f32[128,1536]{1,0:T(8,128)S(1)}, f32[128,1536]{1,0:T(8,128)}, u32[]{:S(2)}, u32[]{:S(2)}) collective-permute-start(f32[128,1536]{1,0:T(8,128)S(1)} %collective-permute-done.8.refs_0_), channel_id=1, source_target_pairs={{0,2},{1,3},{2,6},{3,7},{6,4},{7,5},{4,0},{5,1},{8,10},{9,11},{10,... | collective-permute-start | bytes 2359304 | tf_op jit(solution)/shard_map/ppermute | solution.py:177
  124.6 138.2 %collective-permute-start.13 = (f32[128,1536]{1,0:T(8,128)}, f32[128,1536]{1,0:T(8,128)S(1)}, u32[]{:S(2)}, u32[]{:S(2)}) collective-permute-start(f32[128,1536]{1,0:T(8,128)} %collective-permute-done.11.refs_1_), channel_id=1, source_target_pairs={{0,2},{1,3},{2,6},{3,7},{6,4},{7,5},{4,0},{5,1},{8,10},{9,11},{10,... | collective-permute-start | bytes 2359304 | tf_op jit(solution)/shard_map/ppermute | solution.py:177
  141.4 121.4 %collective-permute-start.12 = (f32[128,1536]{1,0:T(8,128)}, f32[128,1536]{1,0:T(8,128)S(1)}, u32[]{:S(2)}, u32[]{:S(2)}) collective-permute-start(f32[128,1536]{1,0:T(8,128)} %collective-permute-done.10.refs_0_), channel_id=1, source_target_pairs={{0,2},{1,3},{2,6},{3,7},{6,4},{7,5},{4,0},{5,1},{8,10},{9,11},{10,... | collective-permute-start | bytes 2359304 | tf_op jit(solution)/shard_map/ppermute | solution.py:177
  262.8 0.9 copy-start.12
  262.8 1.2 copy-start.13
  301.7 20.7 %copy-start.15 = (f32[128,1536]{1,0:T(8,128)S(1)}, f32[128,1536]{1,0:T(8,128)}, u32[]{:S(2)}) copy-start(f32[128,1536]{1,0:T(8,128)} %get-tuple-element.53) | copy-start | bytes 2359300
  301.7 23.0 %copy-start.14 = (f32[128,1536]{1,0:T(8,128)S(1)}, f32[128,1536]{1,0:T(8,128)}, u32[]{:S(2)}) copy-start(f32[128,1536]{1,0:T(8,128)} %get-tuple-element.57) | copy-start | bytes 2359300
  301.7 42.0 %copy-start.6 = (f32[128,1536]{1,0:T(8,128)S(1)}, f32[128,1536]{1,0:T(8,128)}, u32[]{:S(2)}) copy-start(f32[128,1536]{1,0:T(8,128)} %get-tuple-element.54) | copy-start | bytes 2359300
  301.7 58.9 %copy-start.4 = (f32[128,1536]{1,0:T(8,128)S(1)}, f32[128,1536]{1,0:T(8,128)}, u32[]{:S(2)}) copy-start(f32[128,1536]{1,0:T(8,128)} %get-tuple-element.58) | copy-start | bytes 2359300
  301.7 75.7 %copy-start.7 = (f32[128,1536]{1,0:T(8,128)S(1)}, f32[128,1536]{1,0:T(8,128)}, u32[]{:S(2)}) copy-start(f32[128,1536]{1,0:T(8,128)} %get-tuple-element.55) | copy-start | bytes 2359300
  301.7 92.6 %copy-start.5 = (f32[128,1536]{1,0:T(8,128)S(1)}, f32[128,1536]{1,0:T(8,128)}, u32[]{:S(2)}) copy-start(f32[128,1536]{1,0:T(8,128)} %get-tuple-element.59) | copy-start | bytes 2359300
  322.3 88.9 %copy-start.3 = (f32[128,1536]{1,0:T(8,128)S(1)}, f32[128,1536]{1,0:T(8,128)}, u32[]{:S(2)}) copy-start(f32[128,1536]{1,0:T(8,128)} %get-tuple-element.56) | copy-start | bytes 2359300
  322.3 105.5 %copy-start.2 = (f32[128,1536]{1,0:T(8,128)S(1)}, f32[128,1536]{1,0:T(8,128)}, u32[]{:S(2)}) copy-start(f32[128,1536]{1,0:T(8,128)} %get-tuple-element.60) | copy-start | bytes 2359300
  322.3 106.8 %collective-permute-start.14 = (f32[1536,1536]{1,0:T(8,128)}, f32[1536,1536]{1,0:T(8,128)S(1)}, u32[]{:S(2)}, u32[]{:S(2)}) collective-permute-start(f32[1536,1536]{1,0:T(8,128)} %shard_map.61), channel_id=1, source_target_pairs={{0,1},{1,0},{2,3},{3,2},{4,5},{5,4},{6,7},{7,6},{8,9},{9,8},{10,11... | collective-permute-start | bytes 28311560 | tf_op jit(solution)/shard_map/ppermute | solution.py:178
  322.4 21.4 %collective-permute-start.15 = (f32[128,1536]{1,0:T(8,128)S(1)}, f32[128,1536]{1,0:T(8,128)S(1)}, u32[]{:S(2)}, u32[]{:S(2)}) collective-permute-start(f32[128,1536]{1,0:T(8,128)S(1)} %copy-done.15), channel_id=1, source_target_pairs={{0,2},{1,3},{2,6},{3,7},{6,4},{7,5},{4,0},{5,1},{8,10},{9,11},{10,... | collective-permute-start | bytes 2359304 | tf_op jit(solution)/shard_map/ppermute | solution.py:177
  324.7 35.9 %collective-permute-start.21 = (f32[128,1536]{1,0:T(8,128)S(1)}, f32[128,1536]{1,0:T(8,128)S(1)}, u32[]{:S(2)}, u32[]{:S(2)}) collective-permute-start(f32[128,1536]{1,0:T(8,128)S(1)} %copy-done.14), channel_id=1, source_target_pairs={{0,2},{1,3},{2,6},{3,7},{6,4},{7,5},{4,0},{5,1},{8,10},{9,11},{10,... | collective-permute-start | bytes 2359304 | tf_op jit(solution)/shard_map/ppermute | solution.py:177
  343.8 33.6 %collective-permute-start.16 = (f32[128,1536]{1,0:T(8,128)S(1)}, f32[128,1536]{1,0:T(8,128)S(1)}, u32[]{:S(2)}, u32[]{:S(2)}) collective-permute-start(f32[128,1536]{1,0:T(8,128)S(1)} %add.175), channel_id=1, source_target_pairs={{0,2},{1,3},{2,6},{3,7},{6,4},{7,5},{4,0},{5,1},{8,10},{9,11},{10,... | collective-permute-start | bytes 2359304 | tf_op jit(solution)/shard_map/ppermute | solution.py:177
  360.7 33.6 %collective-permute-start.22 = (f32[128,1536]{1,0:T(8,128)S(1)}, f32[128,1536]{1,0:T(8,128)S(1)}, u32[]{:S(2)}, u32[]{:S(2)}) collective-permute-start(f32[128,1536]{1,0:T(8,128)S(1)} %add.182), channel_id=1, source_target_pairs={{0,2},{1,3},{2,6},{3,7},{6,4},{7,5},{4,0},{5,1},{8,10},{9,11},{10,... | collective-permute-start | bytes 2359304 | tf_op jit(solution)/shard_map/ppermute | solution.py:177
  377.5 33.6 %collective-permute-start.17 = (f32[128,1536]{1,0:T(8,128)S(1)}, f32[128,1536]{1,0:T(8,128)S(1)}, u32[]{:S(2)}, u32[]{:S(2)}) collective-permute-start(f32[128,1536]{1,0:T(8,128)S(1)} %add.176), channel_id=1, source_target_pairs={{0,2},{1,3},{2,6},{3,7},{6,4},{7,5},{4,0},{5,1},{8,10},{9,11},{10,... | collective-permute-start | bytes 2359304 | tf_op jit(solution)/shard_map/ppermute | solution.py:177
  394.4 33.4 %collective-permute-start.23 = (f32[128,1536]{1,0:T(8,128)S(1)}, f32[128,1536]{1,0:T(8,128)S(1)}, u32[]{:S(2)}, u32[]{:S(2)}) collective-permute-start(f32[128,1536]{1,0:T(8,128)S(1)} %add.183), channel_id=1, source_target_pairs={{0,2},{1,3},{2,6},{3,7},{6,4},{7,5},{4,0},{5,1},{8,10},{9,11},{10,... | collective-permute-start | bytes 2359304 | tf_op jit(solution)/shard_map/ppermute | solution.py:177
  411.4 46.1 %collective-permute-start.18 = (f32[64,1536]{1,0:T(8,128)S(1)}, f32[64,1536]{1,0:T(8,128)S(1)}, u32[]{:S(2)}, u32[]{:S(2)}) collective-permute-start(f32[64,1536]{1,0:T(8,128)S(1)} %get-tuple-element.87), channel_id=1, source_target_pairs={{0,8},{8,0},{16,24},{24,16},{1,9},{9,1},{17,25},{25,17},{2,10},{10... | collective-permute-start | bytes 1179656 | tf_op jit(solution)/shard_map/ppermute | solution.py:179
  412.5 48.4 %collective-permute-start.19 = (f32[64,1536]{1,0:T(8,128)S(1)}, f32[64,1536]{1,0:T(8,128)S(1)}, u32[]{:S(2)}, u32[]{:S(2)}) collective-permute-start(f32[64,1536]{1,0:T(8,128)S(1)} %get-tuple-element.86), channel_id=1, source_target_pairs={{0,16},{8,24},{16,0},{24,8},{1,17},{9,25},{17,1},{25,9},{2,18},{10... | collective-permute-start | bytes 1179656 | tf_op jit(solution)/shard_map/ppermute | solution.py:179
  413.9 49.4 %collective-permute-start.20 = (f32[64,1536]{1,0:T(8,128)S(1)}, f32[64,1536]{1,0:T(8,128)S(1)}, u32[]{:S(2)}, u32[]{:S(2)}) collective-permute-start(f32[64,1536]{1,0:T(8,128)S(1)} %get-tuple-element.85), channel_id=1, source_target_pairs={{0,24},{8,16},{16,8},{24,0},{1,25},{9,17},{17,9},{25,1},{2,26},{10... | collective-permute-start | bytes 1179656 | tf_op jit(solution)/shard_map/ppermute | solution.py:179
  428.0 40.3 %collective-permute-start.24 = (f32[64,1536]{1,0:T(8,128)S(1)}, f32[64,1536]{1,0:T(8,128)S(1)}, u32[]{:S(2)}, u32[]{:S(2)}) collective-permute-start(f32[64,1536]{1,0:T(8,128)S(1)} %get-tuple-element.84), channel_id=1, source_target_pairs={{0,8},{8,0},{16,24},{24,16},{1,9},{9,1},{17,25},{25,17},{2,10},{10... | collective-permute-start | bytes 1179656 | tf_op jit(solution)/shard_map/ppermute | solution.py:179
  429.1 3.5 copy-start.9
  432.6 38.1 %collective-permute-start.25 = (f32[64,1536]{1,0:T(8,128)S(1)}, f32[64,1536]{1,0:T(8,128)S(1)}, u32[]{:S(2)}, u32[]{:S(2)}) collective-permute-start(f32[64,1536]{1,0:T(8,128)S(1)} %get-tuple-element.83), channel_id=1, source_target_pairs={{0,16},{8,24},{16,0},{24,8},{1,17},{9,25},{17,1},{25,9},{2,18},{10... | collective-permute-start | bytes 1179656 | tf_op jit(solution)/shard_map/ppermute | solution.py:179
  457.5 15.7 %collective-permute-start.26 = (f32[64,1536]{1,0:T(8,128)S(1)}, f32[64,1536]{1,0:T(8,128)S(1)}, u32[]{:S(2)}, u32[]{:S(2)}) collective-permute-start(f32[64,1536]{1,0:T(8,128)S(1)} %get-tuple-element.82), channel_id=1, source_target_pairs={{0,24},{8,16},{16,8},{24,0},{1,25},{9,17},{17,9},{25,1},{2,26},{10... | collective-permute-start | bytes 1179656 | tf_op jit(solution)/shard_map/ppermute | solution.py:179

commit v2 on v1

v2 whole, which is shorter than its diff:
```python
import functools

import jax
import jax.numpy as jnp
from jax import lax
from jax.experimental import pallas as pl
from jax.experimental.pallas import tpu as pltpu
from jax.sharding import PartitionSpec as P

PIECES = 2
CORES = 2
SCALE = 1
VMEM = 56 * 1024 * 1024
ANY = pl.BlockSpec(memory_space=pl.ANY)
SMEM = pl.BlockSpec(memory_space=pltpu.SMEM)
LOCAL = pl.BlockSpec(memory_space=pltpu.VMEM)
PARAMS = pltpu.CompilerParams(vmem_limit_bytes=VMEM)


def split(x):
    high = x.astype(jnp.bfloat16)
    return high, (x - high.astype(jnp.float32)).astype(jnp.bfloat16)


def dot(a, b, contract):
    return lax.dot_general(a, b, ((contract[:1], contract[1:]), ((), ())), preferred_element_type=jnp.float32)


def block_rows(total, most):
    rows = most
    while total % rows:
        rows //= 2
    return rows


def after(x, *others):
    return lax.optimization_barrier((x, others))[0]


def cost(flops, moved):
    return pl.CostEstimate(flops=flops // SCALE, bytes_accessed=moved // SCALE, transcendentals=0)


def split_kernel(x_ref, high_ref, low_ref):
    high_ref[...], low_ref[...] = split(x_ref[...])


def split_rows(x):
    rows, width = x.shape
    step = block_rows(rows, 256)
    spec = pl.BlockSpec((step, width), lambda i: (i, 0))
    half = jax.ShapeDtypeStruct(x.shape, jnp.bfloat16)
    return pl.pallas_call(
        split_kernel,
        grid=(rows // step,),
        in_specs=[spec],
        out_specs=[spec, spec],
        out_shape=[half, half],
        cost_estimate=cost(2 * rows * width, 8 * rows * width),
        compiler_params=PARAMS,
    )(x)


def asked_row(lists, me, slots, own_count):
    asked, row = False, 0
    for s in range(slots):
        entry = lists[s]
        hit = lax.div(entry, own_count) == me
        asked = jnp.logical_or(asked, hit)
        row = jnp.where(hit, entry - me * own_count, row)
    return asked, row


def slot_holder(lists, me, s, own_count):
    return lax.bitwise_xor(lax.div(lists[s], own_count), me)


def pick_kernel(groups, slots, own_count, first, me_ref, *refs):
    lists, x_ref, outs, sem = refs[:groups], refs[groups], refs[groups + 1:-1], refs[-1]
    rows = outs[0].shape[0]
    copies = []
    for k in range(1, groups):
        _, row = asked_row(lists[k], me_ref[0], slots, own_count)
        copies.append(pltpu.make_async_copy(x_ref.at[row, pl.ds(first, rows)], outs[k - 1], sem.at[k - 1]))
        copies[-1].start()
    for copy in copies:
        copy.wait()


def pick(me, lists, slots, integrals, first, rows):
    own_count, _, aux = integrals.shape
    groups = len(lists)
    return pl.pallas_call(
        functools.partial(pick_kernel, groups, slots, own_count, first),
        in_specs=[SMEM] * (groups + 1) + [ANY],
        out_specs=[LOCAL] * (groups - 1),
        out_shape=[jax.ShapeDtypeStruct((rows, aux), jnp.float32)] * (groups - 1),
        scratch_shapes=[pltpu.SemaphoreType.DMA((groups - 1,))],
        cost_estimate=cost(0, 8 * rows * aux * groups),
        compiler_params=PARAMS,
    )(me, *lists, integrals)


def choose_kernel(groups, slots, own_count, first, me_ref, lists, x_ref, *refs):
    got, out, sem = refs[:groups - 1], refs[groups - 1], refs[groups]
    rows = out.shape[0] // slots
    me = me_ref[0]
    for s in range(slots):
        k_of = slot_holder(lists, me, s, own_count)
        to = out.at[pl.ds(s * rows, rows)]
        row = jnp.clip(lists[s] - me * own_count, 0, own_count - 1)

        @pl.when(k_of == 0)
        def _():
            pltpu.make_async_copy(x_ref.at[row, pl.ds(first, rows)], to, sem.at[s]).start()

        for k in range(1, groups):
            @pl.when(k_of == k)
            def _():
                pltpu.make_async_copy(got[k - 1], to, sem.at[s]).start()

        @pl.when(k_of >= groups)
        def _():
            to[...] = jnp.zeros_like(to)

    for s in range(slots):
        @pl.when(slot_holder(lists, me, s, own_count) < groups)
        def _():
            pltpu.make_async_copy(got[0], out.at[pl.ds(s * rows, rows)], sem.at[s]).wait()


def choose(me, lists, slots, integrals, got, first):
    own_count, _, aux = integrals.shape
    rows = got[0].shape[0]
    groups = len(got) + 1
    return pl.pallas_call(
        functools.partial(choose_kernel, groups, slots, own_count, first),
        in_specs=[SMEM, SMEM] + [ANY] * groups,
        out_specs=LOCAL,
        out_shape=jax.ShapeDtypeStruct((slots * rows, aux), jnp.float32),
        scratch_shapes=[pltpu.SemaphoreType.DMA((slots,))],
        cost_estimate=cost(0, 8 * rows * aux * slots),
        compiler_params=PARAMS,
    )(me, lists, integrals, *got)


def back_kernel(groups, slots, own_count, me_ref, lists, share, *refs):
    outs, sem = refs[:-1], refs[-1]
    rows = outs[0].shape[0]
    copies = []
    for k in range(1, groups):
        slot = 0
        for s in range(slots):
            slot = jnp.where(slot_holder(lists, me_ref[0], s, own_count) == k, s, slot)
        start = pl.multiple_of(slot * rows, rows)
        copies.append(pltpu.make_async_copy(share.at[pl.ds(start, rows)], outs[k - 1], sem.at[k - 1]))
        copies[-1].start()
    for copy in copies:
        copy.wait()


def back(me, lists, slots, own_count, share, groups):
    rows, aux = share.shape[0] // slots, share.shape[1]
    return pl.pallas_call(
        functools.partial(back_kernel, groups, slots, own_count),
        in_specs=[SMEM, SMEM, ANY],
        out_specs=[LOCAL] * (groups - 1),
        out_shape=[jax.ShapeDtypeStruct((rows, aux), jnp.float32)] * (groups - 1),
        scratch_shapes=[pltpu.SemaphoreType.DMA((groups - 1,))],
        cost_estimate=cost(0, 8 * rows * aux * groups),
        compiler_params=PARAMS,
    )(me, lists, share)


def finish_kernel(groups, slots, own_count, first, me_ref, *refs):
    lists, share, arrived = refs[:groups], refs[groups], refs[groups + 1:2 * groups]
    _, density, held, added, sem_held, sem_added = refs[2 * groups:]
    rows = held.shape[1]
    me = me_ref[0]
    asked, places, heads = [], [], []
    for k in range(groups):
        is_asked, row = asked_row(lists[k], me, slots, own_count)
        head = k
        for j in range(k - 1, -1, -1):
            head = jnp.where(jnp.logical_and(asked[j], places[j] == row), j, head)
        asked.append(is_asked)
        places.append(row)
        heads.append(head)
    slot = 0
    for s in range(slots):
        slot = jnp.where(slot_holder(lists[0], me, s, own_count) == 0, s, slot)
    start = pl.multiple_of(slot * rows, rows)
    leads = [jnp.logical_and(asked[k], heads[k] == k) for k in range(groups)]
    source = [share.at[pl.ds(start, rows)]] + list(arrived)
    spots = [density.at[places[k], pl.ds(first, rows)] for k in range(groups)]
    reads = [pltpu.make_async_copy(spots[k], held.at[k], sem_held.at[k]) for k in range(groups)]
    terms = [pltpu.make_async_copy(source[k], added.at[k], sem_added.at[k]) for k in range(groups)]
    writes = [pltpu.make_async_copy(held.at[k], spots[k], sem_held.at[k]) for k in range(groups)]
    for k in range(groups):
        pl.when(leads[k])(reads[k].start)
        pl.when(asked[k])(terms[k].start)
    for k in range(groups):
        pl.when(leads[k])(reads[k].wait)
    for k in range(groups):
        @pl.when(asked[k])
        def _():
            terms[k].wait()
            held[heads[k]] = held[heads[k]] + added[k]
    for k in range(groups):
        pl.when(leads[k])(writes[k].start)
    for k in range(groups):
        pl.when(leads[k])(writes[k].wait)


def finish(me, lists, slots, share, arrived, density, first):
    own_count, _, aux = density.shape
    groups = len(lists)
    rows = share.shape[0] // slots
    return pl.pallas_call(
        functools.partial(finish_kernel, groups, slots, own_count, first),
        in_specs=[SMEM] * (groups + 1) + [ANY] * (groups + 1),
        out_specs=ANY,
        out_shape=jax.ShapeDtypeStruct(density.shape, jnp.float32),
        input_output_aliases={2 * groups + 1: 0},
        scratch_shapes=[
            pltpu.VMEM((groups, rows, aux), jnp.float32),
            pltpu.VMEM((groups, rows, aux), jnp.float32),
            pltpu.SemaphoreType.DMA((groups,)),
            pltpu.SemaphoreType.DMA((groups,)),
        ],
        cost_estimate=cost(0, 12 * rows * aux * groups),
        compiler_params=PARAMS,
    )(me, *lists, share, *arrived, density)


def unit_kernel(steps, own_high, own_low, sib_high, sib_low, row_ref, col_ref, *refs):
    parts = refs[:PIECES]
    t_high, t_low, r_high, r_low = refs[PIECES:PIECES + 4]
    grads = refs[PIECES + 4:2 * PIECES + 4]
    step = pl.program_id(0)
    width = parts[0].shape[0]

    @pl.when(step == 0)
    def _():
        for p in range(PIECES):
            part = slice(p * width, (p + 1) * width)
            r_high[part], r_low[part] = split(parts[p][...])
            grads[p][...] = jnp.zeros_like(grads[p])

    def work(a_high, a_low):
        high, low = r_high[...], r_low[...]
        pair = dot(high, a_high[...], (1, 1)) + dot(low, a_high[...], (1, 1)) + dot(high, a_low[...], (1, 1))
        up, down = split(pair / (row_ref[...] + col_ref[...]))
        t_high[...] = up
        t_low[...] = down
        term = dot(up, a_high[...], (1, 0)) + dot(down, a_high[...], (1, 0)) + dot(up, a_low[...], (1, 0))
        for p in range(PIECES):
            grads[p][...] += term[p * width:(p + 1) * width]

    @pl.when(step < steps)
    def _():
        work(own_high, own_low)

    @pl.when(step >= steps)
    def _():
        work(sib_high, sib_low)


def unit(halves, row_energy, col_energy, parts):
    (own_high, own_low), (sib_high, sib_low) = halves
    rows, aux = own_high.shape
    step = block_rows(rows, 512)
    steps = rows // step
    part_rows = parts[0].shape[0]
    cols = part_rows * PIECES
    own = pl.BlockSpec((step, aux), lambda i: (jnp.minimum(i, steps - 1), 0))
    sib = pl.BlockSpec((step, aux), lambda i: (jnp.maximum(i - steps, 0), 0))
    whole = lambda shape: pl.BlockSpec(shape, lambda i: (0, 0))
    bf16 = lambda *shape: jax.ShapeDtypeStruct(shape, jnp.bfloat16)
    t_spec = pl.BlockSpec((cols, step), lambda i: (0, i))
    outs = pl.pallas_call(
        functools.partial(unit_kernel, steps),
        grid=(2 * steps,),
        in_specs=[own, own, sib, sib, pl.BlockSpec((1, step), lambda i: (0, i)), whole((cols, 1))]
        + [whole((part_rows, aux))] * PIECES,
        out_specs=[t_spec, t_spec, whole((cols, aux)), whole((cols, aux))] + [whole((part_rows, aux))] * PIECES,
        out_shape=[bf16(cols, 2 * rows)] * 2 + [bf16(cols, aux)] * 2
        + [jax.ShapeDtypeStruct((part_rows, aux), jnp.float32)] * PIECES,
        cost_estimate=cost(24 * rows * aux * cols, 8 * rows * aux + 16 * cols * aux),
        compiler_params=PARAMS,
    )(own_high, own_low, sib_high, sib_low, row_energy, col_energy, *parts)
    return outs[:4], outs[4:]


def forward_kernel(count, spans, *refs):
    out = refs[-1]
    total = None
    for u in range(count):
        t_high, t_low, r_high, r_low = (ref[...] for ref in refs[4 * u:4 * u + 4])
        term = dot(t_high, r_high, (0, 0)) + dot(t_high, r_low, (0, 0)) + dot(t_low, r_high, (0, 0))
        total = term if total is None else total + term
    out[...] = total
    step = pl.program_id(0)
    for (begin, end), start in zip(spans, refs[4 * count:-1]):
        @pl.when(jnp.logical_and(step >= begin, step < end))
        def _():
            out[...] += start[...]


def forward(units, first, count, starts):
    cols, aux = units[0][2].shape
    step = block_rows(count, 256)
    steps = count // step
    spans = [(begin // step, (begin + rows.shape[0]) // step) for begin, rows in starts]
    t_spec = pl.BlockSpec((cols, step), lambda i: (0, i + first // step))
    r_spec = pl.BlockSpec((cols, aux), lambda i: (0, 0))
    out_spec = pl.BlockSpec((step, aux), lambda i: (i, 0))
    start_spec = lambda begin, end: pl.BlockSpec((step, aux), lambda i: (jnp.clip(i, begin, end - 1) - begin, 0))
    return pl.pallas_call(
        functools.partial(forward_kernel, len(units), spans),
        grid=(steps,),
        in_specs=[t_spec, t_spec, r_spec, r_spec] * len(units) + [start_spec(*span) for span in spans],
        out_specs=out_spec,
        out_shape=jax.ShapeDtypeStruct((count, aux), jnp.float32),
        cost_estimate=cost(6 * count * aux * cols * len(units), 8 * count * aux),
        compiler_params=PARAMS,
    )(*(x for one in units for x in one), *(rows for _, rows in starts))


def ring_order(chips):
    return [0] + list(range(1, chips, 2)) + [z for z in range(chips - 1, 0, -1) if z % 2 == 0]


def body(integrals, pair_lists, row_orbital, occ_energy, vir_energy):
    own_count, width, aux = integrals.shape
    slots = pair_lists.shape[1]
    groups = lax.axis_size("grp")
    me = lax.axis_index("grp")
    me_ref = me.astype(jnp.int32).reshape(1)
    chips = lax.axis_size("blk") // CORES
    order = ring_order(chips)
    ring = lambda s: [
        (order[i] * CORES + c, order[(i + s) % chips] * CORES + c) for i in range(chips) for c in range(CORES)
    ]
    swap = [(i, i ^ 1) for i in range(chips * CORES)]
    along = lambda x, s: lax.ppermute(x, "blk", ring(s))
    hop = lambda x: along(x, 1)
    sibling = lambda x: lax.ppermute(x, "blk", swap)
    to_group = lambda x, k: lax.ppermute(x, "grp", [(g, g ^ k) for g in range(groups)])

    packet = jnp.concatenate([pair_lists[0], row_orbital])
    packets = [packet] + [to_group(packet, k) for k in range(1, groups)]
    own_rows = integrals.reshape(own_count * width, aux)
    sib_rows = sibling(own_rows)

    part_width = width // PIECES
    blocks = [pick(me_ref, packets, slots, integrals, p * part_width, part_width) for p in range(PIECES)]

    own_half = split_rows(after(own_rows, *blocks[-1]))

    ids = lax.broadcasted_iota(jnp.int32, (groups, own_count, occ_energy.shape[0]), 2)
    orbitals = jnp.stack(packets)[:, slots:]
    row_energies = jnp.sum(jnp.where(orbitals[:, :, None] == ids, occ_energy, 0.0), axis=2)
    held_rows = lax.bitwise_xor(lax.broadcasted_iota(jnp.int32, (groups, own_count), 0), me) * own_count
    held_rows = held_rows + lax.broadcasted_iota(jnp.int32, (groups, own_count), 1)
    listed_here = pair_lists[0][:, None, None] == held_rows
    partner_energy = jnp.sum(jnp.where(listed_here, row_energies, 0.0), axis=(1, 2))
    sib_virtual = sibling(vir_energy)
    row_energy = row_energies[0][None, :, None] - jnp.stack([vir_energy, sib_virtual])[:, None, :]
    row_energy = row_energy.reshape(1, CORES * own_count * width)
    virtual = jnp.stack([vir_energy] + [along(vir_energy, s) for s in range(1, chips)])
    col_energy = partner_energy[None, None, :, None] - virtual.reshape(chips, PIECES, 1, part_width)
    col_energy = list(col_energy.reshape(chips, slots * width, 1))

    pieces = []
    for p in range(PIECES):
        sent = after(blocks[p], *got) if p else blocks[p]
        got = [to_group(block, k + 1) for k, block in enumerate(sent)]
        if p == 1:
            halves = (own_half, split_rows(after(sib_rows, pieces[0][0])))
        got = after(got, halves, row_energy, col_energy, pieces[-1][0]) if p else after(got, own_half)
        part = choose(me_ref, packet, slots, integrals, got, p * part_width)
        pieces.append([part, hop(part)])
        if p == 1:
            pieces[0][1] = after(pieces[0][1], halves)
    parts = [piece[0] for piece in pieces]
    first = [piece[1] for piece in pieces]

    units = []
    grads = []
    for s in range(chips):
        if s == 1:
            parts = first
        elif s:
            parts = [hop(x) for x in parts]
        ready = list(parts)
        if s == 0:
            ready[1] = after(ready[1], first[0])
        if s == 1:
            ready = after(ready, *grads[0])
        if s == chips - 1:
            totals = [hop(after(grad, parts[0], *grads[-1])) for grad in grads[1]]
        one, grad = unit(halves, row_energy, col_energy[s], ready)
        units.append(one)
        grads.append(grad)
    rows = own_count * width
    tail = block_rows(rows, 256)
    head = rows - tail
    aside = []
    for s in range(2, chips + 1):
        done = totals
        if s == 2:
            totals[0] = after(totals[0], *grads[-1])
        totals = [x + y for x, y in zip(totals, grads[s % chips])]
        if s == 2:
            aside.append(forward(after(units, *done), rows, rows // 2, []))
        if s == chips - 1:
            aside.append(forward(after(units, *done), rows + rows // 2, rows // 2, []))
        if s < chips:
            totals = [hop(x) for x in totals]

    known = [(0, sibling(aside[0])), (rows // 2, sibling(aside[1]))]
    density = forward(units, 0, rows, known).reshape(own_count, width, aux)
    arrived = None
    for p in range(PIECES):
        sent = back(me_ref, packet, slots, own_count, after(totals[p], density), groups)
        if arrived is not None:
            sent = after(sent, *arrived)
        arrived = [to_group(block, k + 1) for k, block in enumerate(sent)]
        density = finish(me_ref, packets, slots, totals[p], arrived, density, p * part_width)
    return density


def solution(mesh):
    in_specs = (P("grp", "blk", None), P("grp", None), P("grp"), P(), P("blk"))
    out_specs = P("grp", "blk", None)
    return jax.shard_map(body, mesh=mesh, in_specs=in_specs, out_specs=out_specs, check_vma=False)
```

time: 476 us -> 331 us (0.70)
  blocking collectives: 47.8 us -> 0 us
  waiting for transfers between devices: 140 us -> 93.1 us
  Pallas kernels: 209 us -> 180 us
  other arithmetic: 25.9 us -> 4.36 us
  between operations: 13.7 us -> 0.65 us
  starting transfers between devices: 26.4 us -> 38.2 us
    ppermute x12 -> x15, waiting for transfers between devices: 117 us -> 58.9 us  [body(): along = lambda x, s: lax.ppermute(x, 'blk', ring(s))]
    all_gather x1 -> x0, blocking collectives: 36.9 us -> none  [body(): virtual = lax.all_gather(vir_energy, 'blk', axis=0)]
    pallas_call x6 -> x15, Pallas kernels: 192 us -> 163 us  [the longest x4 91.6 us: unit(): pl.pallas_call(functools.partial(unit_kernel, steps), grid=(2 * steps,),...]
    dynamic_update_slice x8 -> x0, other arithmetic: 19.6 us -> none  [body(): density = lax.dynamic_update_slice(density, new, spot_of)]
    ppermute x12 -> x15, waiting for transfers between devices: 23.3 us -> 34.3 us  [body(): lax.ppermute(x, 'grp', [(g, g ^ k) for g in range(groups)])]
    unnamed x1 -> x0, blocking collectives: 10.9 us -> none
    ppermute x12 -> x15, starting transfers between devices: 11.3 us -> 18.2 us  [body(): lax.ppermute(x, 'grp', [(g, g ^ k) for g in range(groups)])]
    ppermute x12 -> x15, starting transfers between devices: 14.5 us -> 19.5 us  [body(): along = lambda x, s: lax.ppermute(x, 'blk', ring(s))]
  transfers between devices with their start and end apart: 27 -> 34, of which waited for: 11 -> 11; matrix products, arithmetic and copies ran while one was open for 7% -> 3% of each run, Pallas kernels for 32% -> 52%
where the time goes in v2:
time: 331 us; the launch traced here: 330 us
  Pallas kernels  180 us (54%)
  waiting for transfers between devices  93.1 us (28%)
  starting transfers between devices  38.2 us (12%)
  local copies, waits for them, and re-layouts  13.8 us (4%)
  other arithmetic  4.36 us (1%)
    pallas_call x4, Pallas kernels, unit(): pl.pallas_call(functools.partial(unit_kernel, steps), grid=(2 * steps,),...  91.6 us
    ppermute x15, waiting for transfers between devices, body(): along = lambda x, s: lax.ppermute(x, 'blk', ring(s))  58.9 us
    pallas_call x3, Pallas kernels, forward(): pl.pallas_call(functools.partial(forward_kernel, len(units), spans), grid...  47.6 us
    ppermute x15, waiting for transfers between devices, body(): lax.ppermute(x, 'grp', [(g, g ^ k) for g in range(groups)])  34.3 us
    ppermute x15, starting transfers between devices, body(): along = lambda x, s: lax.ppermute(x, 'blk', ring(s))  19.5 us
    ppermute x15, starting transfers between devices, body(): lax.ppermute(x, 'grp', [(g, g ^ k) for g in range(groups)])  18.2 us
    pallas_call x2, Pallas kernels, split_rows(): pl.pallas_call(split_kernel, grid=(rows // step,), in_specs=[spec], out_s...  17.3 us
    unnamed x74, local copies, waits for them, and re-layouts  8.33 us
  transfers between devices with their start and end apart: 34, of which 11 were waited for; matrix products, arithmetic and copies ran while one was open for 3% of the time, Pallas kernels for 52%

profile of v2, /device:TPU:0, one launch (start us, length us, event | category | flops | bytes accessed | tf_op | source)
XLA Modules:
  0.0 330.4 jit_solution(1980647422128798541)
XLA Ops:
  0.5 0.7 pad_add_fusion.1.refs_0_.lists
  1.2 2.5 collective-permute-start
  3.7 1.5 collective-permute-start.1
  5.2 2.0 collective-permute-start.8
  7.3 0.7 stack.47
  8.1 1.5 collective-permute-done.2.refs_3_
  10.2 3.1 shard_map.57
  13.9 1.0 collective-permute-start.5
  14.9 2.0 collective-permute-start.6
  16.9 0.7 pad_add_fusion
  18.1 3.7 %collective-permute-start.9 = (f32[128]{0:T(128)S(1)}, f32[128]{0:T(128)S(1)}, u32[]{:S(2)}, u32[]{:S(2)}) collective-permute-start(f32[128]{0:T(128)S(1)} %copy-done.24), channel_id=1, source_target_pairs={{0,6},{1,7},{2,4},{3,5},{6,0},{7,1},{4,2},{5,3},{8,14},{9,15},{10,... | collective-permute-start | bytes 1544 | tf_op jit(solution)/shard_map/ppermute | solution.py:346
  21.9 3.0 shard_map.55
  25.0 8.7 %shard_map.56 = (bf16[1536,1536]{1,0:T(8,128)(2,1)}, bf16[1536,1536]{1,0:T(8,128)(2,1)}) custom-call(f32[1536,1536]{1,0:T(8,128)} %bitcast.13), custom_call_target="tpu_custom_call" | custom-call | flops 4718592 | bytes 18874368 | tf_op jit(solution)/shard_map/pallas_call | solution.py:53
  34.0 0.7 copy-done.6
  35.0 2.7 shard_map.58.refs_0_
  37.7 2.1 collective-permute-start.11
  40.8 2.5 collective-permute-start.14
  44.4 0.8 copy.22.col_ref
  45.1 0.8 copy.20.col_ref
  45.9 0.8 copy.21.col_ref
  46.7 0.8 copy.23.col_ref
  47.5 8.7 %shard_map.59 = (bf16[1536,1536]{1,0:T(8,128)(2,1)}, bf16[1536,1536]{1,0:T(8,128)(2,1)}) custom-call(f32[1536,1536]{1,0:T(8,128)} %collective-permute-done.3.x_ref), custom_call_target="tpu_custom_call" | custom-call | flops 4718592 | bytes 18874368 | tf_op jit(solution)/shard_map/pallas_call | solution.py:53
  56.2 3.6 %collective-permute-done.14.refs_2_ = f32[64,1536]{1,0:T(8,128)S(1)} collective-permute-done((f32[64,1536]{1,0:T(8,128)S(1)}, f32[64,1536]{1,0:T(8,128)S(1)}, u32[]{:S(2)}, u32[]{:S(2)}) %collective-permute-start.14) | collective-permute-done | bytes 393248 | tf_op jit(solution)/shard_map/ppermute | solution.py:349
  59.8 0.8 copy-done.11
  60.6 2.6 shard_map.60.refs_1_
  63.2 0.6 collective-permute-start.15
  63.8 2.0 collective-permute-start.16
  65.8 22.9 %shard_map.61 = (bf16[256,3072]{1,0:T(8,128)(2,1)}, bf16[256,3072]{1,0:T(8,128)(2,1)}, bf16[256,1536]{1,0:T(8,128)(2,1)}, bf16[256,1536]{1,0:T(8,128)(2,1)}, f32[128,1536]{1,0:T(8,128)}, /*index=5*/f32[128,1536]{1,0:T(8,128)}) custom-call(bf16[1536,1536]{1,0:T(8,128)(2,1)} %get-tuple-element.104.own_high, bf16[1536,1536]{1,0:T(8,128)(2,1)} %get-tuple-element.105.own_low, ...), custom_call_target="tpu_custom_call" | custom-call | flops 14495514624 | bytes 25165824 | tf_op jit(solution)/shard_map/pallas_call | solution.py:281
  89.1 12.5 %collective-permute-done.16.refs_0_ = f32[128,1536]{1,0:T(8,128)S(1)} collective-permute-done((f32[128,1536]{1,0:T(8,128)S(1)}, f32[128,1536]{1,0:T(8,128)S(1)}, u32[]{:S(2)}, u32[]{:S(2)}) %collective-permute-start.16) | collective-permute-done | bytes 786464 | tf_op jit(solution)/shard_map/ppermute | solution.py:346
  101.7 23.1 %shard_map.62 = (bf16[256,3072]{1,0:T(8,128)(2,1)}, bf16[256,3072]{1,0:T(8,128)(2,1)}, bf16[256,1536]{1,0:T(8,128)(2,1)}, bf16[256,1536]{1,0:T(8,128)(2,1)}, f32[128,1536]{1,0:T(8,128)}, /*index=5*/f32[128,1536]{1,0:T(8,128)}) custom-call(bf16[1536,1536]{1,0:T(8,128)(2,1)} %get-tuple-element.104.own_high, bf16[1536,1536]{1,0:T(8,128)(2,1)} %get-tuple-element.105.own_low, ...), custom_call_target="tpu_custom_call" | custom-call | flops 14495514624 | bytes 25165824 | tf_op jit(solution)/shard_map/pallas_call | solution.py:281
  124.9 2.6 collective-permute-start.21
  127.4 22.8 %shard_map.63 = (bf16[256,3072]{1,0:T(8,128)(2,1)}, bf16[256,3072]{1,0:T(8,128)(2,1)}, bf16[256,1536]{1,0:T(8,128)(2,1)}, bf16[256,1536]{1,0:T(8,128)(2,1)}, f32[128,1536]{1,0:T(8,128)}, /*index=5*/f32[128,1536]{1,0:T(8,128)}) custom-call(bf16[1536,1536]{1,0:T(8,128)(2,1)} %get-tuple-element.104.own_high, bf16[1536,1536]{1,0:T(8,128)(2,1)} %get-tuple-element.105.own_low, ...), custom_call_target="tpu_custom_call" | custom-call | flops 14495514624 | bytes 25165824 | tf_op jit(solution)/shard_map/pallas_call | solution.py:281
  150.3 0.7 collective-permute-start.23
  151.0 1.7 collective-permute-start.19
  152.7 0.9 copy-done.33
  153.6 22.8 %shard_map.64 = (bf16[256,3072]{1,0:T(8,128)(2,1)}, bf16[256,3072]{1,0:T(8,128)(2,1)}, bf16[256,1536]{1,0:T(8,128)(2,1)}, bf16[256,1536]{1,0:T(8,128)(2,1)}, f32[128,1536]{1,0:T(8,128)}, /*index=5*/f32[128,1536]{1,0:T(8,128)}) custom-call(bf16[1536,1536]{1,0:T(8,128)(2,1)} %get-tuple-element.104.own_high, bf16[1536,1536]{1,0:T(8,128)(2,1)} %get-tuple-element.105.own_low, ...), custom_call_target="tpu_custom_call" | custom-call | flops 14495514624 | bytes 25165824 | tf_op jit(solution)/shard_map/pallas_call | solution.py:281
  176.5 0.7 collective-permute-start.24
  177.2 11.4 %collective-permute-done.19 = f32[128,1536]{1,0:T(8,128)S(1)} collective-permute-done((f32[128,1536]{1,0:T(8,128)S(1)}, f32[128,1536]{1,0:T(8,128)S(1)}, u32[]{:S(2)}, u32[]{:S(2)}) %collective-permute-start.19) | collective-permute-done | bytes 786464 | tf_op jit(solution)/shard_map/ppermute | solution.py:346
  188.9 12.5 %shard_map.65 = f32[768,1536]{1,0:T(8,128)} custom-call(bf16[256,3072]{1,0:T(8,128)(2,1)} %get-tuple-element.168.refs_0_, bf16[256,3072]{1,0:T(8,128)(2,1)} %get-tuple-element.169.refs_1_, bf16[256,1536]{1,0:T(8,128)(2,1)} %get-tuple-element.170.refs_2_, bf16[256,1536]{1,0:T(8,128)(2,1)} %get-tuple-element.171.refs_3_, ...), custom_call_target="tpu_custom_call" | custom-call | flops 7247757312 | bytes 9437184 | tf_op jit(solution)/shard_map/pallas_call | solution.py:319
  201.5 3.9 %collective-permute-done.24 = f32[128,1536]{1,0:T(8,128)S(1)} collective-permute-done((f32[128,1536]{1,0:T(8,128)S(1)}, f32[128,1536]{1,0:T(8,128)S(1)}, u32[]{:S(2)}, u32[]{:S(2)}) %collective-permute-start.24) | collective-permute-done | bytes 786464 | tf_op jit(solution)/shard_map/ppermute | solution.py:346
  205.4 12.6 %collective-permute-done.20 = f32[128,1536]{1,0:T(8,128)S(1)} collective-permute-done((f32[128,1536]{1,0:T(8,128)S(1)}, f32[128,1536]{1,0:T(8,128)S(1)}, u32[]{:S(2)}, u32[]{:S(2)}) %collective-permute-start.20) | collective-permute-done | bytes 786464 | tf_op jit(solution)/shard_map/ppermute | solution.py:346
  218.0 12.5 %shard_map.66 = f32[768,1536]{1,0:T(8,128)} custom-call(bf16[256,3072]{1,0:T(8,128)(2,1)} %get-tuple-element.168.refs_0_, bf16[256,3072]{1,0:T(8,128)(2,1)} %get-tuple-element.169.refs_1_, bf16[256,1536]{1,0:T(8,128)(2,1)} %get-tuple-element.170.refs_2_, bf16[256,1536]{1,0:T(8,128)(2,1)} %get-tuple-element.171.refs_3_, ...), custom_call_target="tpu_custom_call" | custom-call | flops 7247757312 | bytes 9437184 | tf_op jit(solution)/shard_map/pallas_call | solution.py:319
  230.9 2.6 collective-permute-start.22
  233.5 18.5 %collective-permute-done.25 = f32[128,1536]{1,0:T(8,128)S(1)} collective-permute-done((f32[128,1536]{1,0:T(8,128)S(1)}, f32[128,1536]{1,0:T(8,128)S(1)}, u32[]{:S(2)}, u32[]{:S(2)}) %collective-permute-start.25) | collective-permute-done | bytes 786464 | tf_op jit(solution)/shard_map/ppermute | solution.py:346
  252.0 1.0 add.31.share.refs_4_
  253.0 2.1 copy-done.25
  255.1 22.6 %shard_map.67 = f32[1536,1536]{1,0:T(8,128)} custom-call(bf16[256,3072]{1,0:T(8,128)(2,1)} %get-tuple-element.168.refs_0_, bf16[256,3072]{1,0:T(8,128)(2,1)} %get-tuple-element.169.refs_1_, bf16[256,1536]{1,0:T(8,128)(2,1)} %get-tuple-element.170.refs_2_, bf16[256,1536]{1,0:T(8,128)(2,1)} %get-tuple-element.171.refs_3_, ...), custom_call_target="tpu_custom_call" | custom-call | flops 14495514624 | bytes 18874368 | tf_op jit(solution)/shard_map/pallas_call | solution.py:319
  277.7 3.0 shard_map.68
  280.7 1.3 collective-permute-start.28
  282.5 1.8 collective-permute-start.30
  284.2 1.0 add.28.share.refs_4_
  285.3 7.7 %collective-permute-done.28.refs_5_ = f32[64,1536]{1,0:T(8,128)S(1)} collective-permute-done((f32[64,1536]{1,0:T(8,128)}, f32[64,1536]{1,0:T(8,128)S(1)}, u32[]{:S(2)}, u32[]{:S(2)}) %collective-permute-start.28) | collective-permute-done | bytes 393248 | tf_op jit(solution)/shard_map/ppermute | solution.py:349
  293.0 7.7 %collective-permute-done.29.refs_6_ = f32[64,1536]{1,0:T(8,128)S(1)} collective-permute-done((f32[64,1536]{1,0:T(8,128)}, f32[64,1536]{1,0:T(8,128)S(1)}, u32[]{:S(2)}, u32[]{:S(2)}) %collective-permute-start.29) | collective-permute-done | bytes 393248 | tf_op jit(solution)/shard_map/ppermute | solution.py:349
  300.7 0.7 copy-done.13
  301.4 0.8 copy-done.16
  302.2 3.1 shard_map.69.refs_8_
  305.3 3.1 shard_map.70
  308.8 1.2 collective-permute-start.32
  310.1 1.9 collective-permute-start.33
  312.0 8.8 %collective-permute-done.31.refs_5_ = f32[64,1536]{1,0:T(8,128)S(1)} collective-permute-done((f32[64,1536]{1,0:T(8,128)}, f32[64,1536]{1,0:T(8,128)S(1)}, u32[]{:S(2)}, u32[]{:S(2)}) %collective-permute-start.31) | collective-permute-done | bytes 393248 | tf_op jit(solution)/shard_map/ppermute | solution.py:349
  320.8 4.9 %collective-permute-done.32.refs_6_ = f32[64,1536]{1,0:T(8,128)S(1)} collective-permute-done((f32[64,1536]{1,0:T(8,128)}, f32[64,1536]{1,0:T(8,128)S(1)}, u32[]{:S(2)}, u32[]{:S(2)}) %collective-permute-start.32) | collective-permute-done | bytes 393248 | tf_op jit(solution)/shard_map/ppermute | solution.py:349
  325.6 0.7 copy-done.15
  326.4 0.8 copy-done.17
  327.1 3.1 shard_map.71
  (129 shorter events, 7.3 us)
Async XLA Ops:
  0.0 47.5 %collective-permute-start.3 = (f32[1536,1536]{1,0:T(8,128)}, f32[1536,1536]{1,0:T(8,128)}, u32[]{:S(2)}, u32[]{:S(2)}) collective-permute-start(f32[1536,1536]{1,0:T(8,128)} %bitcast.12), channel_id=1, source_target_pairs={{0,1},{1,0},{2,3},{3,2},{4,5},{5,4},{6,7},{7,6},{8,9},{9,8},{10,11... | collective-permute-start | bytes 28311560 | tf_op jit(solution)/shard_map/ppermute | solution.py:348
  1.2 8.5 %copy-start.18 = (s32[14]{0:T(128)}, s32[14]{0:T(128)S(1)}, u32[]{:S(2)}) copy-start(s32[14]{0:T(128)S(1)} %pad_add_fusion.1.refs_0_.lists) | copy-start | bytes 172
  1.2 6.9 %collective-permute-start = (s32[14]{0:T(128)S(1)}, s32[14]{0:T(128)S(1)}, u32[]{:S(2)}, u32[]{:S(2)}) collective-permute-start(s32[14]{0:T(128)S(1)} %pad_add_fusion.1.refs_0_.lists), channel_id=1, source_target_pairs={{0,8},{8,0},{16,24},{24,16},{1,9},{9,1},{17,25},{25,17},{2,10},{10... | collective-permute-start | bytes 176 | tf_op jit(solution)/shard_map/ppermute | solution.py:349
  3.7 4.4 %collective-permute-start.1 = (s32[14]{0:T(128)S(1)}, s32[14]{0:T(128)S(1)}, u32[]{:S(2)}, u32[]{:S(2)}) collective-permute-start(s32[14]{0:T(128)S(1)} %pad_add_fusion.1.refs_0_.lists), channel_id=1, source_target_pairs={{0,16},{8,24},{16,0},{24,8},{1,17},{9,25},{17,1},{25,9},{2,18},{10... | collective-permute-start | bytes 176 | tf_op jit(solution)/shard_map/ppermute | solution.py:349
  5.2 4.4 %collective-permute-start.2 = (s32[14]{0:T(128)S(1)}, s32[14]{0:T(128)S(1)}, u32[]{:S(2)}, u32[]{:S(2)}) collective-permute-start(s32[14]{0:T(128)S(1)} %pad_add_fusion.1.refs_0_.lists), channel_id=1, source_target_pairs={{0,24},{8,16},{16,8},{24,0},{1,25},{9,17},{17,9},{25,1},{2,26},{10... | collective-permute-start | bytes 176 | tf_op jit(solution)/shard_map/ppermute | solution.py:349
  5.2 12.9 %collective-permute-start.8 = (f32[128]{0:T(128)}, f32[128]{0:T(128)S(1)}, u32[]{:S(2)}, u32[]{:S(2)}) collective-permute-start(f32[128]{0:T(128)} %param.9), channel_id=1, source_target_pairs={{0,2},{1,3},{2,6},{3,7},{6,4},{7,5},{4,0},{5,1},{8,10},{9,11},{10,... | collective-permute-start | bytes 1544 | tf_op jit(solution)/shard_map/ppermute | solution.py:346
  8.1 1.6 copy-start.19
  8.1 1.6 copy-start.20
  10.2 7.6 %copy-start.22 = (f32[48]{0:T(128)S(1)}, f32[48]{0:T(128)}, u32[]{:S(2)}) copy-start(f32[48]{0:T(128)} %param.8) | copy-start | bytes 580
  10.2 7.8 %copy-start.23 = (s32[1,2]{1,0:T(1,128)S(1)}, s32[1,2]{1,0:T(1,128)}, u32[]{:S(2)}) copy-start(s32[1,2]{1,0:T(1,128)} %param.6) | copy-start | bytes 28
  10.2 8.0 %copy-start.24 = (f32[128]{0:T(128)S(1)}, f32[128]{0:T(128)}, u32[]{:S(2)}) copy-start(f32[128]{0:T(128)} %param.9) | copy-start | bytes 1540
  13.3 20.7 %collective-permute-start.4 = (f32[64,1536]{1,0:T(8,128)}, f32[64,1536]{1,0:T(8,128)S(1)}, u32[]{:S(2)}, u32[]{:S(2)}) collective-permute-start(f32[64,1536]{1,0:T(8,128)} %get-tuple-element.106), channel_id=1, source_target_pairs={{0,8},{8,0},{16,24},{24,16},{1,9},{9,1},{17,25},{25,17},{2,10},{10... | collective-permute-start | bytes 1179656 | tf_op jit(solution)/shard_map/ppermute | solution.py:349
  13.9 20.1 %collective-permute-start.5 = (f32[64,1536]{1,0:T(8,128)}, f32[64,1536]{1,0:T(8,128)S(1)}, u32[]{:S(2)}, u32[]{:S(2)}) collective-permute-start(f32[64,1536]{1,0:T(8,128)} %get-tuple-element.107), channel_id=1, source_target_pairs={{0,16},{8,24},{16,0},{24,8},{1,17},{9,25},{17,1},{25,9},{2,18},{10... | collective-permute-start | bytes 1179656 | tf_op jit(solution)/shard_map/ppermute | solution.py:349
  14.9 19.1 %collective-permute-start.6 = (f32[64,1536]{1,0:T(8,128)}, f32[64,1536]{1,0:T(8,128)S(1)}, u32[]{:S(2)}, u32[]{:S(2)}) collective-permute-start(f32[64,1536]{1,0:T(8,128)} %get-tuple-element.108), channel_id=1, source_target_pairs={{0,24},{8,16},{16,8},{24,0},{1,25},{9,17},{17,9},{25,1},{2,26},{10... | collective-permute-start | bytes 1179656 | tf_op jit(solution)/shard_map/ppermute | solution.py:349
  18.1 6.8 %collective-permute-start.9 = (f32[128]{0:T(128)S(1)}, f32[128]{0:T(128)S(1)}, u32[]{:S(2)}, u32[]{:S(2)}) collective-permute-start(f32[128]{0:T(128)S(1)} %copy-done.24), channel_id=1, source_target_pairs={{0,6},{1,7},{2,4},{3,5},{6,0},{7,1},{4,2},{5,3},{8,14},{9,15},{10,... | collective-permute-start | bytes 1544 | tf_op jit(solution)/shard_map/ppermute | solution.py:346
  25.0 8.9 %collective-permute-start.10 = (f32[128]{0:T(128)S(1)}, f32[128]{0:T(128)S(1)}, u32[]{:S(2)}, u32[]{:S(2)}) collective-permute-start(f32[128]{0:T(128)S(1)} %copy-done.24), channel_id=1, source_target_pairs={{0,4},{1,5},{2,0},{3,1},{6,2},{7,3},{4,6},{5,7},{8,12},{9,13},{10,... | collective-permute-start | bytes 1544 | tf_op jit(solution)/shard_map/ppermute | solution.py:346
  33.9 7.0 %collective-permute-start.7 = (f32[128]{0:T(128)S(1)}, f32[128]{0:T(128)S(1)}, u32[]{:S(2)}, u32[]{:S(2)}) collective-permute-start(f32[128]{0:T(128)S(1)} %copy-done.24), channel_id=1, source_target_pairs={{0,1},{1,0},{2,3},{3,2},{4,5},{5,4},{6,7},{7,6},{8,9},{9,8},{10,11... | collective-permute-start | bytes 1544 | tf_op jit(solution)/shard_map/ppermute | solution.py:348
  34.0 0.9 copy-start.7
  34.0 1.0 copy-start.8
  35.0 4.8 %copy-start.36 = (f32[64,1536]{1,0:T(8,128)S(1)}, f32[64,1536]{1,0:T(8,128)}, u32[]{:S(2)}) copy-start(f32[64,1536]{1,0:T(8,128)} %get-tuple-element.116) | copy-start | bytes 1179652
  35.0 5.4 %copy-start.35 = (f32[64,1536]{1,0:T(8,128)S(1)}, f32[64,1536]{1,0:T(8,128)}, u32[]{:S(2)}) copy-start(f32[64,1536]{1,0:T(8,128)} %get-tuple-element.117) | copy-start | bytes 1179652
  35.0 5.9 %copy-start.34 = (f32[64,1536]{1,0:T(8,128)S(1)}, f32[64,1536]{1,0:T(8,128)}, u32[]{:S(2)}) copy-start(f32[64,1536]{1,0:T(8,128)} %get-tuple-element.118) | copy-start | bytes 1179652
  37.7 26.1 %collective-permute-start.11 = (f32[128,1536]{1,0:T(8,128)}, f32[128,1536]{1,0:T(8,128)S(1)}, u32[]{:S(2)}, u32[]{:S(2)}) collective-permute-start(f32[128,1536]{1,0:T(8,128)} %shard_map.58.refs_0_), channel_id=1, source_target_pairs={{0,2},{1,3},{2,6},{3,7},{6,4},{7,5},{4,0},{5,1},{8,10},{9,11},{10,... | collective-permute-start | bytes 2359304 | tf_op jit(solution)/shard_map/ppermute | solution.py:346
  39.8 16.4 %collective-permute-start.12 = (f32[64,1536]{1,0:T(8,128)S(1)}, f32[64,1536]{1,0:T(8,128)S(1)}, u32[]{:S(2)}, u32[]{:S(2)}) collective-permute-start(f32[64,1536]{1,0:T(8,128)S(1)} %copy-done.36), channel_id=1, source_target_pairs={{0,8},{8,0},{16,24},{24,16},{1,9},{9,1},{17,25},{25,17},{2,10},{10... | collective-permute-start | bytes 1179656 | tf_op jit(solution)/shard_map/ppermute | solution.py:349
  40.4 15.8 %collective-permute-start.13 = (f32[64,1536]{1,0:T(8,128)S(1)}, f32[64,1536]{1,0:T(8,128)S(1)}, u32[]{:S(2)}, u32[]{:S(2)}) collective-permute-start(f32[64,1536]{1,0:T(8,128)S(1)} %copy-done.35), channel_id=1, source_target_pairs={{0,16},{8,24},{16,0},{24,8},{1,17},{9,25},{17,1},{25,9},{2,18},{10... | collective-permute-start | bytes 1179656 | tf_op jit(solution)/shard_map/ppermute | solution.py:349
  40.8 19.0 %collective-permute-start.14 = (f32[64,1536]{1,0:T(8,128)S(1)}, f32[64,1536]{1,0:T(8,128)S(1)}, u32[]{:S(2)}, u32[]{:S(2)}) collective-permute-start(f32[64,1536]{1,0:T(8,128)S(1)} %copy-done.34), channel_id=1, source_target_pairs={{0,24},{8,16},{16,8},{24,0},{1,25},{9,17},{17,9},{25,1},{2,26},{10... | collective-permute-start | bytes 1179656 | tf_op jit(solution)/shard_map/ppermute | solution.py:349
  56.2 3.6 %copy-start.9 = (f32[64,1536]{1,0:T(8,128)}, f32[64,1536]{1,0:T(8,128)S(1)}, u32[]{:S(2)}) copy-start(f32[64,1536]{1,0:T(8,128)S(1)} %collective-permute-done.12.refs_0_) | copy-start | bytes 1179652
  56.2 3.6 %copy-start.10 = (f32[64,1536]{1,0:T(8,128)}, f32[64,1536]{1,0:T(8,128)S(1)}, u32[]{:S(2)}) copy-start(f32[64,1536]{1,0:T(8,128)S(1)} %collective-permute-done.13.refs_1_) | copy-start | bytes 1179652
  63.2 25.6 %collective-permute-start.15 = (f32[128,1536]{1,0:T(8,128)}, f32[128,1536]{1,0:T(8,128)S(1)}, u32[]{:S(2)}, u32[]{:S(2)}) collective-permute-start(f32[128,1536]{1,0:T(8,128)} %shard_map.60.refs_1_), channel_id=1, source_target_pairs={{0,2},{1,3},{2,6},{3,7},{6,4},{7,5},{4,0},{5,1},{8,10},{9,11},{10,... | collective-permute-start | bytes 2359304 | tf_op jit(solution)/shard_map/ppermute | solution.py:346
  63.8 24.9 %copy-start.26 = (f32[128,1536]{1,0:T(8,128)}, f32[128,1536]{1,0:T(8,128)S(1)}, u32[]{:S(2)}) copy-start(f32[128,1536]{1,0:T(8,128)S(1)} %collective-permute-done.11.refs_0_) | copy-start | bytes 2359300
  63.8 37.8 %collective-permute-start.16 = (f32[128,1536]{1,0:T(8,128)S(1)}, f32[128,1536]{1,0:T(8,128)S(1)}, u32[]{:S(2)}, u32[]{:S(2)}) collective-permute-start(f32[128,1536]{1,0:T(8,128)S(1)} %collective-permute-done.11.refs_0_), channel_id=1, source_target_pairs={{0,2},{1,3},{2,6},{3,7},{6,4},{7,5},{4,0},{5,1},{8,10},{9,11},{10,... | collective-permute-start | bytes 2359304 | tf_op jit(solution)/shard_map/ppermute | solution.py:346
  88.7 12.9 %copy-start.32 = (f32[128,1536]{1,0:T(8,128)}, f32[128,1536]{1,0:T(8,128)S(1)}, u32[]{:S(2)}) copy-start(f32[128,1536]{1,0:T(8,128)S(1)} %collective-permute-done.15.refs_1_) | copy-start | bytes 2359300
  88.8 36.1 %collective-permute-start.18 = (f32[128,1536]{1,0:T(8,128)S(1)}, f32[128,1536]{1,0:T(8,128)S(1)}, u32[]{:S(2)}, u32[]{:S(2)}) collective-permute-start(f32[128,1536]{1,0:T(8,128)S(1)} %collective-permute-done.15.refs_1_), channel_id=1, source_target_pairs={{0,2},{1,3},{2,6},{3,7},{6,4},{7,5},{4,0},{5,1},{8,10},{9,11},{10,... | collective-permute-start | bytes 2359304 | tf_op jit(solution)/shard_map/ppermute | solution.py:346
  101.7 23.2 %copy-start.30 = (f32[128,1536]{1,0:T(8,128)}, f32[128,1536]{1,0:T(8,128)S(1)}, u32[]{:S(2)}) copy-start(f32[128,1536]{1,0:T(8,128)S(1)} %collective-permute-done.16.refs_0_) | copy-start | bytes 2359300
  101.7 48.6 %collective-permute-start.17 = (f32[128,1536]{1,0:T(8,128)S(1)}, f32[128,1536]{1,0:T(8,128)S(1)}, u32[]{:S(2)}, u32[]{:S(2)}) collective-permute-start(f32[128,1536]{1,0:T(8,128)S(1)} %collective-permute-done.16.refs_0_), channel_id=1, source_target_pairs={{0,2},{1,3},{2,6},{3,7},{6,4},{7,5},{4,0},{5,1},{8,10},{9,11},{10,... | collective-permute-start | bytes 2359304 | tf_op jit(solution)/shard_map/ppermute | solution.py:346
  124.8 25.4 %copy-start.28 = (f32[128,1536]{1,0:T(8,128)S(1)}, f32[128,1536]{1,0:T(8,128)}, u32[]{:S(2)}) copy-start(f32[128,1536]{1,0:T(8,128)} %get-tuple-element.133) | copy-start | bytes 2359300
  124.8 26.1 %copy-start.27 = (f32[128,1536]{1,0:T(8,128)S(1)}, f32[128,1536]{1,0:T(8,128)}, u32[]{:S(2)}) copy-start(f32[128,1536]{1,0:T(8,128)} %get-tuple-element.130) | copy-start | bytes 2359300
  124.8 2.6 copy-start.31
  124.9 27.8 %collective-permute-start.21 = (f32[128,1536]{1,0:T(8,128)S(1)}, f32[128,1536]{1,0:T(8,128)S(1)}, u32[]{:S(2)}, u32[]{:S(2)}) collective-permute-start(f32[128,1536]{1,0:T(8,128)S(1)} %collective-permute-done.18.refs_1_), channel_id=1, source_target_pairs={{0,2},{1,3},{2,6},{3,7},{6,4},{7,5},{4,0},{5,1},{8,10},{9,11},{10,... | collective-permute-start | bytes 2359304 | tf_op jit(solution)/shard_map/ppermute | solution.py:346
  150.2 2.4 copy-start.29
  150.3 26.1 %collective-permute-start.23 = (f32[128,1536]{1,0:T(8,128)S(1)}, f32[128,1536]{1,0:T(8,128)S(1)}, u32[]{:S(2)}, u32[]{:S(2)}) collective-permute-start(f32[128,1536]{1,0:T(8,128)S(1)} %copy-done.28), channel_id=1, source_target_pairs={{0,2},{1,3},{2,6},{3,7},{6,4},{7,5},{4,0},{5,1},{8,10},{9,11},{10,... | collective-permute-start | bytes 2359304 | tf_op jit(solution)/shard_map/ppermute | solution.py:346
  151.0 25.4 %copy-start.5 = (f32[128,1536]{1,0:T(8,128)S(1)}, f32[128,1536]{1,0:T(8,128)}, u32[]{:S(2)}) copy-start(f32[128,1536]{1,0:T(8,128)} %get-tuple-element.128) | copy-start | bytes 2359300
  151.0 37.6 %copy-start.4 = (f32[128,1536]{1,0:T(8,128)S(1)}, f32[128,1536]{1,0:T(8,128)}, u32[]{:S(2)}) copy-start(f32[128,1536]{1,0:T(8,128)} %get-tuple-element.129) | copy-start | bytes 2359300
  151.0 37.6 %collective-permute-start.19 = (f32[128,1536]{1,0:T(8,128)S(1)}, f32[128,1536]{1,0:T(8,128)S(1)}, u32[]{:S(2)}, u32[]{:S(2)}) collective-permute-start(f32[128,1536]{1,0:T(8,128)S(1)} %copy-done.27), channel_id=1, source_target_pairs={{0,2},{1,3},{2,6},{3,7},{6,4},{7,5},{4,0},{5,1},{8,10},{9,11},{10,... | collective-permute-start | bytes 2359304 | tf_op jit(solution)/shard_map/ppermute | solution.py:346
  152.7 0.9 copy-start.33
  176.5 28.9 %collective-permute-start.24 = (f32[128,1536]{1,0:T(8,128)S(1)}, f32[128,1536]{1,0:T(8,128)S(1)}, u32[]{:S(2)}, u32[]{:S(2)}) collective-permute-start(f32[128,1536]{1,0:T(8,128)S(1)} %add.29), channel_id=1, source_target_pairs={{0,2},{1,3},{2,6},{3,7},{6,4},{7,5},{4,0},{5,1},{8,10},{9,11},{10,... | collective-permute-start | bytes 2359304 | tf_op jit(solution)/shard_map/ppermute | solution.py:346
  188.6 29.4 %collective-permute-start.20 = (f32[128,1536]{1,0:T(8,128)S(1)}, f32[128,1536]{1,0:T(8,128)S(1)}, u32[]{:S(2)}, u32[]{:S(2)}) collective-permute-start(f32[128,1536]{1,0:T(8,128)S(1)} %add.26), channel_id=1, source_target_pairs={{0,2},{1,3},{2,6},{3,7},{6,4},{7,5},{4,0},{5,1},{8,10},{9,11},{10,... | collective-permute-start | bytes 2359304 | tf_op jit(solution)/shard_map/ppermute | solution.py:346
  201.4 29.1 %copy-start.3 = (f32[128,1536]{1,0:T(8,128)S(1)}, f32[128,1536]{1,0:T(8,128)}, u32[]{:S(2)}) copy-start(f32[128,1536]{1,0:T(8,128)} %get-tuple-element.134) | copy-start | bytes 2359300
  201.5 29.3 %copy-start.2 = (f32[128,1536]{1,0:T(8,128)S(1)}, f32[128,1536]{1,0:T(8,128)}, u32[]{:S(2)}) copy-start(f32[128,1536]{1,0:T(8,128)} %get-tuple-element.131) | copy-start | bytes 2359300
  201.5 51.5 %collective-permute-start.26 = (f32[768,1536]{1,0:T(8,128)}, f32[768,1536]{1,0:T(8,128)}, u32[]{:S(2)}, u32[]{:S(2)}) collective-permute-start(f32[768,1536]{1,0:T(8,128)} %shard_map.65), channel_id=1, source_target_pairs={{0,1},{1,0},{2,3},{3,2},{4,5},{5,4},{6,7},{7,6},{8,9},{9,8},{10,11... | collective-permute-start | bytes 14155784 | tf_op jit(solution)/shard_map/ppermute | solution.py:348
  230.5 21.5 %copy-start.1 = (f32[128,1536]{1,0:T(8,128)S(1)}, f32[128,1536]{1,0:T(8,128)}, u32[]{:S(2)}) copy-start(f32[128,1536]{1,0:T(8,128)} %get-tuple-element.123) | copy-start | bytes 2359300
  230.5 22.5 %collective-permute-start.27 = (f32[768,1536]{1,0:T(8,128)}, f32[768,1536]{1,0:T(8,128)S(1)}, u32[]{:S(2)}, u32[]{:S(2)}) collective-permute-start(f32[768,1536]{1,0:T(8,128)} %shard_map.66), channel_id=1, source_target_pairs={{0,1},{1,0},{2,3},{3,2},{4,5},{5,4},{6,7},{7,6},{8,9},{9,8},{10,11... | collective-permute-start | bytes 14155784 | tf_op jit(solution)/shard_map/ppermute | solution.py:348
  230.7 21.3 %collective-permute-start.25 = (f32[128,1536]{1,0:T(8,128)S(1)}, f32[128,1536]{1,0:T(8,128)S(1)}, u32[]{:S(2)}, u32[]{:S(2)}) collective-permute-start(f32[128,1536]{1,0:T(8,128)S(1)} %add.30), channel_id=1, source_target_pairs={{0,2},{1,3},{2,6},{3,7},{6,4},{7,5},{4,0},{5,1},{8,10},{9,11},{10,... | collective-permute-start | bytes 2359304 | tf_op jit(solution)/shard_map/ppermute | solution.py:346
  230.9 53.4 %collective-permute-start.22 = (f32[128,1536]{1,0:T(8,128)S(1)}, f32[128,1536]{1,0:T(8,128)S(1)}, u32[]{:S(2)}, u32[]{:S(2)}) collective-permute-start(f32[128,1536]{1,0:T(8,128)S(1)} %add.27), channel_id=1, source_target_pairs={{0,2},{1,3},{2,6},{3,7},{6,4},{7,5},{4,0},{5,1},{8,10},{9,11},{10,... | collective-permute-start | bytes 2359304 | tf_op jit(solution)/shard_map/ppermute | solution.py:346
  253.0 31.3 %copy-start = (f32[128,1536]{1,0:T(8,128)S(1)}, f32[128,1536]{1,0:T(8,128)}, u32[]{:S(2)}) copy-start(f32[128,1536]{1,0:T(8,128)} %get-tuple-element.124) | copy-start | bytes 2359300
  253.0 2.1 copy-start.25
  280.7 12.3 %collective-permute-start.28 = (f32[64,1536]{1,0:T(8,128)}, f32[64,1536]{1,0:T(8,128)S(1)}, u32[]{:S(2)}, u32[]{:S(2)}) collective-permute-start(f32[64,1536]{1,0:T(8,128)} %get-tuple-element.185), channel_id=1, source_target_pairs={{0,8},{8,0},{16,24},{24,16},{1,9},{9,1},{17,25},{25,17},{2,10},{10... | collective-permute-start | bytes 1179656 | tf_op jit(solution)/shard_map/ppermute | solution.py:349
  282.0 18.7 %collective-permute-start.29 = (f32[64,1536]{1,0:T(8,128)}, f32[64,1536]{1,0:T(8,128)S(1)}, u32[]{:S(2)}, u32[]{:S(2)}) collective-permute-start(f32[64,1536]{1,0:T(8,128)} %get-tuple-element.186), channel_id=1, source_target_pairs={{0,16},{8,24},{16,0},{24,8},{1,17},{9,25},{17,1},{25,9},{2,18},{10... | collective-permute-start | bytes 1179656 | tf_op jit(solution)/shard_map/ppermute | solution.py:349
  282.5 18.2 %collective-permute-start.30 = (f32[64,1536]{1,0:T(8,128)}, f32[64,1536]{1,0:T(8,128)S(1)}, u32[]{:S(2)}, u32[]{:S(2)}) collective-permute-start(f32[64,1536]{1,0:T(8,128)} %get-tuple-element.187), channel_id=1, source_target_pairs={{0,24},{8,16},{16,8},{24,0},{1,25},{9,17},{17,9},{25,1},{2,26},{10... | collective-permute-start | bytes 1179656 | tf_op jit(solution)/shard_map/ppermute | solution.py:349
  293.0 7.7 %copy-start.12 = (f32[64,1536]{1,0:T(8,128)}, f32[64,1536]{1,0:T(8,128)S(1)}, u32[]{:S(2)}) copy-start(f32[64,1536]{1,0:T(8,128)S(1)} %collective-permute-done.28.refs_5_) | copy-start | bytes 1179652
  308.4 12.3 %collective-permute-start.31 = (f32[64,1536]{1,0:T(8,128)}, f32[64,1536]{1,0:T(8,128)S(1)}, u32[]{:S(2)}, u32[]{:S(2)}) collective-permute-start(f32[64,1536]{1,0:T(8,128)} %get-tuple-element.192), channel_id=1, source_target_pairs={{0,8},{8,0},{16,24},{24,16},{1,9},{9,1},{17,25},{25,17},{2,10},{10... | collective-permute-start | bytes 1179656 | tf_op jit(solution)/shard_map/ppermute | solution.py:349
  308.8 16.8 %collective-permute-start.32 = (f32[64,1536]{1,0:T(8,128)}, f32[64,1536]{1,0:T(8,128)S(1)}, u32[]{:S(2)}, u32[]{:S(2)}) collective-permute-start(f32[64,1536]{1,0:T(8,128)} %get-tuple-element.193), channel_id=1, source_target_pairs={{0,16},{8,24},{16,0},{24,8},{1,17},{9,25},{17,1},{25,9},{2,18},{10... | collective-permute-start | bytes 1179656 | tf_op jit(solution)/shard_map/ppermute | solution.py:349
  310.1 15.5 %collective-permute-start.33 = (f32[64,1536]{1,0:T(8,128)}, f32[64,1536]{1,0:T(8,128)S(1)}, u32[]{:S(2)}, u32[]{:S(2)}) collective-permute-start(f32[64,1536]{1,0:T(8,128)} %get-tuple-element.194), channel_id=1, source_target_pairs={{0,24},{8,16},{16,8},{24,0},{1,25},{9,17},{17,9},{25,1},{2,26},{10... | collective-permute-start | bytes 1179656 | tf_op jit(solution)/shard_map/ppermute | solution.py:349
  320.7 4.9 %copy-start.14 = (f32[64,1536]{1,0:T(8,128)}, f32[64,1536]{1,0:T(8,128)S(1)}, u32[]{:S(2)}) copy-start(f32[64,1536]{1,0:T(8,128)S(1)} %collective-permute-done.31.refs_5_) | copy-start | bytes 1179652
  (7 other events, 5.0 us)

commit v3 on v2

--- a/solution.py
+++ b/solution.py
@@ -374,7 +374,7 @@
 
     pieces = []
     for p in range(PIECES):
-        sent = after(blocks[p], *got) if p else blocks[p]
+        sent = blocks[p]
         got = [to_group(block, k + 1) for k, block in enumerate(sent)]
         if p == 1:
             halves = (own_half, split_rows(after(sib_rows, pieces[0][0])))
@@ -404,8 +404,11 @@
         units.append(one)
         grads.append(grad)
     rows = own_count * width
-    tail = block_rows(rows, 256)
-    head = rows - tail
+    step = block_rows(rows, 256)
+    last = rows - step
+    middle = 0
+    last = rows // 2
+    cuts = [(0, last), (last, rows)]
     aside = []
     for s in range(2, chips + 1):
         done = totals
@@ -413,19 +416,20 @@
             totals[0] = after(totals[0], *grads[-1])
         totals = [x + y for x, y in zip(totals, grads[s % chips])]
         if s == 2:
-            aside.append(forward(after(units, *done), rows, rows // 2, []))
+            aside.append(forward(after(units, *done), rows, last, []))
         if s == chips - 1:
-            aside.append(forward(after(units, *done), rows + rows // 2, rows // 2, []))
+            most = forward(after(units[:-1], done[0], aside[0]), rows + last, rows - last, [])
+            ready = after(units, most, *done)
+            aside.append(forward(ready[-1:], rows + last, rows - last, [(0, most)]))
         if s < chips:
             totals = [hop(x) for x in totals]
 
-    known = [(0, sibling(aside[0])), (rows // 2, sibling(aside[1]))]
-    density = forward(units, 0, rows, known).reshape(own_count, width, aux)
-    arrived = None
+    early = forward(after(units[:-1], aside[1]), 0, rows, [])
+    known = [(0, early)] + [(begin, sibling(x)) for (begin, _), x in zip(cuts, aside)]
+    density = forward(units[-1:], 0, rows, known).reshape(own_count, width, aux)
     for p in range(PIECES):
-        sent = back(me_ref, packet, slots, own_count, after(totals[p], density), groups)
-        if arrived is not None:
-            sent = after(sent, *arrived)
+        share = after(totals[p], known, *(arrived if p else []))
+        sent = back(me_ref, packet, slots, own_count, share, groups)
         arrived = [to_group(block, k + 1) for k, block in enumerate(sent)]
         density = finish(me_ref, packets, slots, totals[p], arrived, density, p * part_width)
     return density

time: 331 us -> 301 us (0.909)
  waiting for transfers between devices: 93.1 us -> 48.3 us
  Pallas kernels: 180 us -> 195 us
    ppermute x15, waiting for transfers between devices: 34.3 us -> 9.42 us  [body(): lax.ppermute(x, 'grp', [(g, g ^ k) for g in range(groups)])]
    ppermute x15, waiting for transfers between devices: 58.9 us -> 38.9 us  [body(): along = lambda x, s: lax.ppermute(x, 'blk', ring(s))]
    pallas_call x3 -> x5, Pallas kernels: 47.6 us -> 61.9 us  [forward(): pl.pallas_call(functools.partial(forward_kernel, len(units), spans), grid...]
    unnamed x74 -> x72, local copies, waits for them, and re-layouts: 8.33 us -> 4.97 us
  transfers between devices with their start and end apart: 34 -> 34, of which waited for: 11 -> 10; matrix products, arithmetic and copies ran while one was open for 3% -> 4% of each run, Pallas kernels for 52% -> 63%
where the time goes in v3:
time: 301 us; the launch traced here: 300 us
  Pallas kernels  195 us (65%)
  waiting for transfers between devices  48.3 us (16%)
  starting transfers between devices  38.3 us (13%)
  local copies, waits for them, and re-layouts  10.5 us (3%)
  other arithmetic  7.25 us (2%)
    pallas_call x4, Pallas kernels, unit(): pl.pallas_call(functools.partial(unit_kernel, steps), grid=(2 * steps,),...  91.6 us
    pallas_call x5, Pallas kernels, forward(): pl.pallas_call(functools.partial(forward_kernel, len(units), spans), grid...  61.9 us
    ppermute x15, waiting for transfers between devices, body(): along = lambda x, s: lax.ppermute(x, 'blk', ring(s))  38.9 us
    ppermute x15, starting transfers between devices, body(): lax.ppermute(x, 'grp', [(g, g ^ k) for g in range(groups)])  19.3 us
    ppermute x15, starting transfers between devices, body(): along = lambda x, s: lax.ppermute(x, 'blk', ring(s))  18.4 us
    pallas_call x2, Pallas kernels, split_rows(): pl.pallas_call(split_kernel, grid=(rows // step,), in_specs=[spec], out_s...  17.4 us
    ppermute x15, waiting for transfers between devices, body(): lax.ppermute(x, 'grp', [(g, g ^ k) for g in range(groups)])  9.42 us
    pallas_call x2, Pallas kernels, back(): pl.pallas_call(functools.partial(back_kernel, groups, slots, own_count),...  6.94 us
  transfers between devices with their start and end apart: 34, of which 10 were waited for; matrix products, arithmetic and copies ran while one was open for 4% of the time, Pallas kernels for 63%

profile of v3, /device:TPU:0, one launch (start us, length us, event | category | flops | bytes accessed | tf_op | source)
XLA Modules:
  0.0 300.4 jit_solution(16604812405140545288)
XLA Ops:
  0.5 0.7 pad_add_fusion.1.refs_0_.lists
  1.2 2.5 collective-permute-start
  3.7 1.5 collective-permute-start.1
  5.2 2.0 collective-permute-start.8
  7.3 0.7 stack.47
  8.1 1.5 collective-permute-done.2.refs_3_
  10.2 3.1 %shard_map.57 = (f32[64,1536]{1,0:T(8,128)}, f32[64,1536]{1,0:T(8,128)}, f32[64,1536]{1,0:T(8,128)}) custom-call(s32[1]{0:T(128)} %bitcast.me_ref, s32[14]{0:T(128)} %copy-done.19, s32[14]{0:T(128)} %copy-done.20, s32[14]{0:T(128)} %copy-done.21, s32[14]{0:T(128)} %copy-done.22, f32[12,128,1536]{2,1,0:T(8,128)} %x_ref.3), custom_call_target="tpu_custom_call" | custom-call | bytes 3145728 | tf_op jit(solution)/shard_map/pallas_call | solution.py:93
  13.9 1.1 collective-permute-start.5
  15.1 1.9 collective-permute-start.6
  16.9 0.7 pad_add_fusion
  18.2 3.7 %collective-permute-start.9 = (f32[128]{0:T(128)S(1)}, f32[128]{0:T(128)S(1)}, u32[]{:S(2)}, u32[]{:S(2)}) collective-permute-start(f32[128]{0:T(128)S(1)} %copy-done.25), channel_id=1, source_target_pairs={{0,6},{1,7},{2,4},{3,5},{6,0},{7,1},{4,2},{5,3},{8,14},{9,15},{10,... | collective-permute-start | bytes 1544 | tf_op jit(solution)/shard_map/ppermute | solution.py:346
  22.0 3.0 %shard_map.55 = (f32[64,1536]{1,0:T(8,128)}, f32[64,1536]{1,0:T(8,128)}, f32[64,1536]{1,0:T(8,128)}) custom-call(s32[1]{0:T(128)} %bitcast.me_ref, s32[14]{0:T(128)} %copy-done.19, s32[14]{0:T(128)} %copy-done.20, s32[14]{0:T(128)} %copy-done.21, s32[14]{0:T(128)} %copy-done.22, f32[12,128,1536]{2,1,0:T(8,128)} %x_ref.3), custom_call_target="tpu_custom_call" | custom-call | bytes 3145728 | tf_op jit(solution)/shard_map/pallas_call | solution.py:93
  25.1 8.7 %shard_map.56 = (bf16[1536,1536]{1,0:T(8,128)(2,1)}, bf16[1536,1536]{1,0:T(8,128)(2,1)}) custom-call(f32[1536,1536]{1,0:T(8,128)} %bitcast.13), custom_call_target="tpu_custom_call" | custom-call | flops 4718592 | bytes 18874368 | tf_op jit(solution)/shard_map/pallas_call | solution.py:53
  34.7 1.7 collective-permute-start.13
  36.4 0.7 copy-done.10
  37.1 2.7 shard_map.58.refs_0_
  39.8 1.2 collective-permute-start.11
  41.1 2.4 collective-permute-start.14
  44.5 0.8 copy.22.col_ref
  45.3 0.8 copy.20.col_ref
  46.1 0.8 copy.21.col_ref
  46.9 0.8 copy.23.col_ref
  47.7 8.7 %shard_map.59 = (bf16[1536,1536]{1,0:T(8,128)(2,1)}, bf16[1536,1536]{1,0:T(8,128)(2,1)}) custom-call(f32[1536,1536]{1,0:T(8,128)} %collective-permute-done.3.x_ref), custom_call_target="tpu_custom_call" | custom-call | flops 4718592 | bytes 18874368 | tf_op jit(solution)/shard_map/pallas_call | solution.py:53
  56.4 0.7 copy-done.8
  57.5 2.6 shard_map.60.refs_1_
  60.1 0.7 collective-permute-start.15
  60.8 2.0 collective-permute-start.16
  62.8 22.8 %shard_map.61 = (bf16[256,3072]{1,0:T(8,128)(2,1)}, bf16[256,3072]{1,0:T(8,128)(2,1)}, bf16[256,1536]{1,0:T(8,128)(2,1)}, bf16[256,1536]{1,0:T(8,128)(2,1)}, f32[128,1536]{1,0:T(8,128)}, /*index=5*/f32[128,1536]{1,0:T(8,128)}) custom-call(bf16[1536,1536]{1,0:T(8,128)(2,1)} %get-tuple-element.110.own_high, bf16[1536,1536]{1,0:T(8,128)(2,1)} %get-tuple-element.111.own_low, ...), custom_call_target="tpu_custom_call" | custom-call | flops 14495514624 | bytes 25165824 | tf_op jit(solution)/shard_map/pallas_call | solution.py:281
  86.0 12.5 %collective-permute-done.16.refs_0_ = f32[128,1536]{1,0:T(8,128)S(1)} collective-permute-done((f32[128,1536]{1,0:T(8,128)S(1)}, f32[128,1536]{1,0:T(8,128)S(1)}, u32[]{:S(2)}, u32[]{:S(2)}) %collective-permute-start.16) | collective-permute-done | bytes 786464 | tf_op jit(solution)/shard_map/ppermute | solution.py:346
  98.6 23.1 %shard_map.62 = (bf16[256,3072]{1,0:T(8,128)(2,1)}, bf16[256,3072]{1,0:T(8,128)(2,1)}, bf16[256,1536]{1,0:T(8,128)(2,1)}, bf16[256,1536]{1,0:T(8,128)(2,1)}, f32[128,1536]{1,0:T(8,128)}, /*index=5*/f32[128,1536]{1,0:T(8,128)}) custom-call(bf16[1536,1536]{1,0:T(8,128)(2,1)} %get-tuple-element.110.own_high, bf16[1536,1536]{1,0:T(8,128)(2,1)} %get-tuple-element.111.own_low, ...), custom_call_target="tpu_custom_call" | custom-call | flops 14495514624 | bytes 25165824 | tf_op jit(solution)/shard_map/pallas_call | solution.py:281
  121.7 2.6 collective-permute-start.21
  124.4 22.9 %shard_map.63 = (bf16[256,3072]{1,0:T(8,128)(2,1)}, bf16[256,3072]{1,0:T(8,128)(2,1)}, bf16[256,1536]{1,0:T(8,128)(2,1)}, bf16[256,1536]{1,0:T(8,128)(2,1)}, f32[128,1536]{1,0:T(8,128)}, /*index=5*/f32[128,1536]{1,0:T(8,128)}) custom-call(bf16[1536,1536]{1,0:T(8,128)(2,1)} %get-tuple-element.110.own_high, bf16[1536,1536]{1,0:T(8,128)(2,1)} %get-tuple-element.111.own_low, ...), custom_call_target="tpu_custom_call" | custom-call | flops 14495514624 | bytes 25165824 | tf_op jit(solution)/shard_map/pallas_call | solution.py:281
  148.0 1.6 collective-permute-start.19
  149.6 0.9 copy-done.33
  150.5 22.8 %shard_map.64 = (bf16[256,3072]{1,0:T(8,128)(2,1)}, bf16[256,3072]{1,0:T(8,128)(2,1)}, bf16[256,1536]{1,0:T(8,128)(2,1)}, bf16[256,1536]{1,0:T(8,128)(2,1)}, f32[128,1536]{1,0:T(8,128)}, /*index=5*/f32[128,1536]{1,0:T(8,128)}) custom-call(bf16[1536,1536]{1,0:T(8,128)(2,1)} %get-tuple-element.110.own_high, bf16[1536,1536]{1,0:T(8,128)(2,1)} %get-tuple-element.111.own_low, ...), custom_call_target="tpu_custom_call" | custom-call | flops 14495514624 | bytes 25165824 | tf_op jit(solution)/shard_map/pallas_call | solution.py:281
  173.5 0.7 collective-permute-start.24
  174.2 11.4 %collective-permute-done.19 = f32[128,1536]{1,0:T(8,128)S(1)} collective-permute-done((f32[128,1536]{1,0:T(8,128)S(1)}, f32[128,1536]{1,0:T(8,128)S(1)}, u32[]{:S(2)}, u32[]{:S(2)}) %collective-permute-start.19) | collective-permute-done | bytes 786464 | tf_op jit(solution)/shard_map/ppermute | solution.py:346
  185.6 1.0 add.26
  186.5 12.5 %shard_map.65 = f32[768,1536]{1,0:T(8,128)} custom-call(bf16[256,3072]{1,0:T(8,128)(2,1)} %get-tuple-element.187.refs_0_, bf16[256,3072]{1,0:T(8,128)(2,1)} %get-tuple-element.188.refs_1_, bf16[256,1536]{1,0:T(8,128)(2,1)} %get-tuple-element.189.refs_2_, bf16[256,1536]{1,0:T(8,128)(2,1)} %get-tuple-element.190.refs_3_, ...), custom_call_target="tpu_custom_call" | custom-call | flops 7247757312 | bytes 9437184 | tf_op jit(solution)/shard_map/pallas_call | solution.py:319
  199.1 3.3 %collective-permute-done.24 = f32[128,1536]{1,0:T(8,128)S(1)} collective-permute-done((f32[128,1536]{1,0:T(8,128)S(1)}, f32[128,1536]{1,0:T(8,128)S(1)}, u32[]{:S(2)}, u32[]{:S(2)}) %collective-permute-start.24) | collective-permute-done | bytes 786464 | tf_op jit(solution)/shard_map/ppermute | solution.py:346
  202.4 10.1 %shard_map.66.refs_4_ = f32[768,1536]{1,0:T(8,128)} custom-call(bf16[256,3072]{1,0:T(8,128)(2,1)} %get-tuple-element.187.refs_0_, bf16[256,3072]{1,0:T(8,128)(2,1)} %get-tuple-element.188.refs_1_, bf16[256,1536]{1,0:T(8,128)(2,1)} %get-tuple-element.189.refs_2_, bf16[256,1536]{1,0:T(8,128)(2,1)} %get-tuple-element.190.refs_3_, ...), custom_call_target="tpu_custom_call" | custom-call | flops 5435817984 | bytes 9437184 | tf_op jit(solution)/shard_map/pallas_call | solution.py:319
  212.6 2.3 collective-permute-done.20
  214.9 7.7 %shard_map.67 = f32[768,1536]{1,0:T(8,128)} custom-call(bf16[256,3072]{1,0:T(8,128)(2,1)} %get-tuple-element.183.refs_12_.refs_0_, bf16[256,3072]{1,0:T(8,128)(2,1)} %get-tuple-element.184.refs_13_.refs_1_, bf16[256,1536]{1,0:T(8,128)(2,1)} %get-tuple-element.185.refs_14_.refs_2_, bf16[256,1536]{1,0:T(8,128)(2,1)} %get-tuple-element.186.refs_15_.refs_3_, ...), custom_call_target="tpu_custom_call" | custom-call | flops 1811939328 | bytes 9437184 | tf_op jit(solution)/shard_map/pallas_call | solution.py:319
  222.6 1.0 add.30
  223.6 2.7 collective-permute-start.22
  226.4 16.2 %shard_map.68.refs_4_ = f32[1536,1536]{1,0:T(8,128)} custom-call(bf16[256,3072]{1,0:T(8,128)(2,1)} %get-tuple-element.187.refs_0_, bf16[256,3072]{1,0:T(8,128)(2,1)} %get-tuple-element.188.refs_1_, bf16[256,1536]{1,0:T(8,128)(2,1)} %get-tuple-element.189.refs_2_, bf16[256,1536]{1,0:T(8,128)(2,1)} %get-tuple-element.190.refs_3_, ...), custom_call_target="tpu_custom_call" | custom-call | flops 10871635968 | bytes 18874368 | tf_op jit(solution)/shard_map/pallas_call | solution.py:319
  242.6 2.5 collective-permute-done.27
  245.1 2.1 add.31.share.refs_4_
  247.2 3.8 %shard_map.69 = (f32[64,1536]{1,0:T(8,128)}, f32[64,1536]{1,0:T(8,128)}, f32[64,1536]{1,0:T(8,128)}) custom-call(s32[1]{0:T(128)} %bitcast.me_ref, s32[14]{0:T(128)} %copy-done.19, f32[128,1536]{1,0:T(8,128)} %add.31.share.refs_4_), custom_call_target="tpu_custom_call" | custom-call | bytes 3145728 | tf_op jit(solution)/shard_map/pallas_call | solution.py:164
  251.6 0.8 collective-permute-start.29
  252.4 2.2 collective-permute-start.30
  254.6 6.8 %collective-permute-done.22 = f32[128,1536]{1,0:T(8,128)S(1)} collective-permute-done((f32[128,1536]{1,0:T(8,128)S(1)}, f32[128,1536]{1,0:T(8,128)S(1)}, u32[]{:S(2)}, u32[]{:S(2)}) %collective-permute-start.22) | collective-permute-done | bytes 786464 | tf_op jit(solution)/shard_map/ppermute | solution.py:346
  261.4 1.0 add.28.share.refs_4_
  262.5 0.9 collective-permute-done.28.refs_5_
  263.6 6.7 %collective-permute-done.30.refs_7_ = f32[64,1536]{1,0:T(8,128)S(1)} collective-permute-done((f32[64,1536]{1,0:T(8,128)}, f32[64,1536]{1,0:T(8,128)S(1)}, u32[]{:S(2)}, u32[]{:S(2)}) %collective-permute-start.30) | collective-permute-done | bytes 393248 | tf_op jit(solution)/shard_map/ppermute | solution.py:349
  270.3 3.1 %shard_map.70 = (f32[64,1536]{1,0:T(8,128)}, f32[64,1536]{1,0:T(8,128)}, f32[64,1536]{1,0:T(8,128)}) custom-call(s32[1]{0:T(128)} %bitcast.me_ref, s32[14]{0:T(128)} %copy-done.19, f32[128,1536]{1,0:T(8,128)} %add.28.share.refs_4_), custom_call_target="tpu_custom_call" | custom-call | bytes 3145728 | tf_op jit(solution)/shard_map/pallas_call | solution.py:164
  273.4 1.6 collective-permute-start.31
  275.0 0.8 collective-permute-start.32
  275.8 1.2 collective-permute-start.33
  277.0 15.3 %shard_map.71 = f32[1536,1536]{1,0:T(8,128)} custom-call(bf16[256,3072]{1,0:T(8,128)(2,1)} %get-tuple-element.183.refs_12_.refs_0_, bf16[256,3072]{1,0:T(8,128)(2,1)} %get-tuple-element.184.refs_13_.refs_1_, bf16[256,1536]{1,0:T(8,128)(2,1)} %get-tuple-element.185.refs_14_.refs_2_, bf16[256,1536]{1,0:T(8,128)(2,1)} %get-tuple-element.186.refs_15_.refs_3_, ...), custom_call_target="tpu_custom_call" | custom-call | flops 3623878656 | bytes 18874368 | tf_op jit(solution)/shard_map/pallas_call | solution.py:319
  292.3 3.1 %shard_map.72.refs_8_ = f32[12,128,1536]{2,1,0:T(8,128)} custom-call(s32[1]{0:T(128)} %bitcast.me_ref, s32[14]{0:T(128)} %copy-done.19, s32[14]{0:T(128)} %copy-done.20, s32[14]{0:T(128)} %copy-done.21, s32[14]{0:T(128)} %copy-done.22, f32[128,1536]{1,0:T(8,128)} %add.31.share.refs_4_, f32[64,1536]{1,0:T(8,128)} %copy-done.13, ...), custom_call_target="tpu_custom_call", output_to_operand_aliasing={{}: (9, {})} | custom-call | bytes 4718592 | tf_op jit(solution)/shard_map/pallas_call | solution.py:219
  295.5 0.7 copy-done.16
  296.4 0.7 copy-done.18
  297.1 3.1 %shard_map.73 = f32[12,128,1536]{2,1,0:T(8,128)} custom-call(s32[1]{0:T(128)} %bitcast.me_ref, s32[14]{0:T(128)} %copy-done.19, s32[14]{0:T(128)} %copy-done.20, s32[14]{0:T(128)} %copy-done.21, s32[14]{0:T(128)} %copy-done.22, f32[128,1536]{1,0:T(8,128)} %add.28.share.refs_4_, f32[64,1536]{1,0:T(8,128)} %copy-done.16, ...), custom_call_target="tpu_custom_call", output_to_operand_aliasing={{}: (9, {})} | custom-call | bytes 4718592 | tf_op jit(solution)/shard_map/pallas_call | solution.py:219
  (129 shorter events, 7.1 us)
Async XLA Ops:
  0.0 47.7 %collective-permute-start.3 = (f32[1536,1536]{1,0:T(8,128)}, f32[1536,1536]{1,0:T(8,128)}, u32[]{:S(2)}, u32[]{:S(2)}) collective-permute-start(f32[1536,1536]{1,0:T(8,128)} %bitcast.12), channel_id=1, source_target_pairs={{0,1},{1,0},{2,3},{3,2},{4,5},{5,4},{6,7},{7,6},{8,9},{9,8},{10,11... | collective-permute-start | bytes 28311560 | tf_op jit(solution)/shard_map/ppermute | solution.py:348
  1.2 8.5 %copy-start.19 = (s32[14]{0:T(128)}, s32[14]{0:T(128)S(1)}, u32[]{:S(2)}) copy-start(s32[14]{0:T(128)S(1)} %pad_add_fusion.1.refs_0_.lists) | copy-start | bytes 172
  1.2 6.9 %collective-permute-start = (s32[14]{0:T(128)S(1)}, s32[14]{0:T(128)S(1)}, u32[]{:S(2)}, u32[]{:S(2)}) collective-permute-start(s32[14]{0:T(128)S(1)} %pad_add_fusion.1.refs_0_.lists), channel_id=1, source_target_pairs={{0,8},{8,0},{16,24},{24,16},{1,9},{9,1},{17,25},{25,17},{2,10},{10... | collective-permute-start | bytes 176 | tf_op jit(solution)/shard_map/ppermute | solution.py:349
  3.7 4.4 %collective-permute-start.1 = (s32[14]{0:T(128)S(1)}, s32[14]{0:T(128)S(1)}, u32[]{:S(2)}, u32[]{:S(2)}) collective-permute-start(s32[14]{0:T(128)S(1)} %pad_add_fusion.1.refs_0_.lists), channel_id=1, source_target_pairs={{0,16},{8,24},{16,0},{24,8},{1,17},{9,25},{17,1},{25,9},{2,18},{10... | collective-permute-start | bytes 176 | tf_op jit(solution)/shard_map/ppermute | solution.py:349
  5.2 4.4 %collective-permute-start.2 = (s32[14]{0:T(128)S(1)}, s32[14]{0:T(128)S(1)}, u32[]{:S(2)}, u32[]{:S(2)}) collective-permute-start(s32[14]{0:T(128)S(1)} %pad_add_fusion.1.refs_0_.lists), channel_id=1, source_target_pairs={{0,24},{8,16},{16,8},{24,0},{1,25},{9,17},{17,9},{25,1},{2,26},{10... | collective-permute-start | bytes 176 | tf_op jit(solution)/shard_map/ppermute | solution.py:349
  5.2 13.0 %collective-permute-start.8 = (f32[128]{0:T(128)}, f32[128]{0:T(128)S(1)}, u32[]{:S(2)}, u32[]{:S(2)}) collective-permute-start(f32[128]{0:T(128)} %param.9), channel_id=1, source_target_pairs={{0,2},{1,3},{2,6},{3,7},{6,4},{7,5},{4,0},{5,1},{8,10},{9,11},{10,... | collective-permute-start | bytes 1544 | tf_op jit(solution)/shard_map/ppermute | solution.py:346
  8.1 1.6 copy-start.20
  8.1 1.6 copy-start.21
  10.2 7.6 %copy-start.23 = (f32[48]{0:T(128)S(1)}, f32[48]{0:T(128)}, u32[]{:S(2)}) copy-start(f32[48]{0:T(128)} %param.8) | copy-start | bytes 580
  10.2 7.8 %copy-start.24 = (s32[1,2]{1,0:T(1,128)S(1)}, s32[1,2]{1,0:T(1,128)}, u32[]{:S(2)}) copy-start(s32[1,2]{1,0:T(1,128)} %param.6) | copy-start | bytes 28
  10.2 8.0 %copy-start.25 = (f32[128]{0:T(128)S(1)}, f32[128]{0:T(128)}, u32[]{:S(2)}) copy-start(f32[128]{0:T(128)} %param.9) | copy-start | bytes 1540
  13.4 20.7 %collective-permute-start.4 = (f32[64,1536]{1,0:T(8,128)}, f32[64,1536]{1,0:T(8,128)S(1)}, u32[]{:S(2)}, u32[]{:S(2)}) collective-permute-start(f32[64,1536]{1,0:T(8,128)} %get-tuple-element.112), channel_id=1, source_target_pairs={{0,8},{8,0},{16,24},{24,16},{1,9},{9,1},{17,25},{25,17},{2,10},{10... | collective-permute-start | bytes 1179656 | tf_op jit(solution)/shard_map/ppermute | solution.py:349
  13.9 20.7 %collective-permute-start.5 = (f32[64,1536]{1,0:T(8,128)}, f32[64,1536]{1,0:T(8,128)S(1)}, u32[]{:S(2)}, u32[]{:S(2)}) collective-permute-start(f32[64,1536]{1,0:T(8,128)} %get-tuple-element.113), channel_id=1, source_target_pairs={{0,16},{8,24},{16,0},{24,8},{1,17},{9,25},{17,1},{25,9},{2,18},{10... | collective-permute-start | bytes 1179656 | tf_op jit(solution)/shard_map/ppermute | solution.py:349
  15.1 21.3 %collective-permute-start.6 = (f32[64,1536]{1,0:T(8,128)}, f32[64,1536]{1,0:T(8,128)S(1)}, u32[]{:S(2)}, u32[]{:S(2)}) collective-permute-start(f32[64,1536]{1,0:T(8,128)} %get-tuple-element.114), channel_id=1, source_target_pairs={{0,24},{8,16},{16,8},{24,0},{1,25},{9,17},{17,9},{25,1},{2,26},{10... | collective-permute-start | bytes 1179656 | tf_op jit(solution)/shard_map/ppermute | solution.py:349
  18.2 6.8 %collective-permute-start.9 = (f32[128]{0:T(128)S(1)}, f32[128]{0:T(128)S(1)}, u32[]{:S(2)}, u32[]{:S(2)}) collective-permute-start(f32[128]{0:T(128)S(1)} %copy-done.25), channel_id=1, source_target_pairs={{0,6},{1,7},{2,4},{3,5},{6,0},{7,1},{4,2},{5,3},{8,14},{9,15},{10,... | collective-permute-start | bytes 1544 | tf_op jit(solution)/shard_map/ppermute | solution.py:346
  25.1 9.6 %copy-start.35 = (f32[64,1536]{1,0:T(8,128)S(1)}, f32[64,1536]{1,0:T(8,128)}, u32[]{:S(2)}) copy-start(f32[64,1536]{1,0:T(8,128)} %get-tuple-element.107) | copy-start | bytes 1179652
  25.1 8.9 %collective-permute-start.10 = (f32[128]{0:T(128)S(1)}, f32[128]{0:T(128)S(1)}, u32[]{:S(2)}, u32[]{:S(2)}) collective-permute-start(f32[128]{0:T(128)S(1)} %copy-done.25), channel_id=1, source_target_pairs={{0,4},{1,5},{2,0},{3,1},{6,2},{7,3},{4,6},{5,7},{8,12},{9,13},{10,... | collective-permute-start | bytes 1544 | tf_op jit(solution)/shard_map/ppermute | solution.py:346
  34.0 7.1 %collective-permute-start.7 = (f32[128]{0:T(128)S(1)}, f32[128]{0:T(128)S(1)}, u32[]{:S(2)}, u32[]{:S(2)}) collective-permute-start(f32[128]{0:T(128)S(1)} %copy-done.25), channel_id=1, source_target_pairs={{0,1},{1,0},{2,3},{3,2},{4,5},{5,4},{6,7},{7,6},{8,9},{9,8},{10,11... | collective-permute-start | bytes 1544 | tf_op jit(solution)/shard_map/ppermute | solution.py:348
  34.1 2.3 copy-start.7
  34.1 22.3 %collective-permute-start.12 = (f32[64,1536]{1,0:T(8,128)}, f32[64,1536]{1,0:T(8,128)S(1)}, u32[]{:S(2)}, u32[]{:S(2)}) collective-permute-start(f32[64,1536]{1,0:T(8,128)} %get-tuple-element.106), channel_id=1, source_target_pairs={{0,8},{8,0},{16,24},{24,16},{1,9},{9,1},{17,25},{25,17},{2,10},{10... | collective-permute-start | bytes 1179656 | tf_op jit(solution)/shard_map/ppermute | solution.py:349
  34.7 1.7 copy-start.9
  34.7 21.7 %collective-permute-start.13 = (f32[64,1536]{1,0:T(8,128)S(1)}, f32[64,1536]{1,0:T(8,128)S(1)}, u32[]{:S(2)}, u32[]{:S(2)}) collective-permute-start(f32[64,1536]{1,0:T(8,128)S(1)} %copy-done.35), channel_id=1, source_target_pairs={{0,16},{8,24},{16,0},{24,8},{1,17},{9,25},{17,1},{25,9},{2,18},{10... | collective-permute-start | bytes 1179656 | tf_op jit(solution)/shard_map/ppermute | solution.py:349
  37.1 4.0 %copy-start.34 = (f32[64,1536]{1,0:T(8,128)S(1)}, f32[64,1536]{1,0:T(8,128)}, u32[]{:S(2)}) copy-start(f32[64,1536]{1,0:T(8,128)} %get-tuple-element.108) | copy-start | bytes 1179652
  39.8 20.9 %collective-permute-start.11 = (f32[128,1536]{1,0:T(8,128)}, f32[128,1536]{1,0:T(8,128)S(1)}, u32[]{:S(2)}, u32[]{:S(2)}) collective-permute-start(f32[128,1536]{1,0:T(8,128)} %shard_map.58.refs_0_), channel_id=1, source_target_pairs={{0,2},{1,3},{2,6},{3,7},{6,4},{7,5},{4,0},{5,1},{8,10},{9,11},{10,... | collective-permute-start | bytes 2359304 | tf_op jit(solution)/shard_map/ppermute | solution.py:346
  41.1 15.3 %collective-permute-start.14 = (f32[64,1536]{1,0:T(8,128)S(1)}, f32[64,1536]{1,0:T(8,128)S(1)}, u32[]{:S(2)}, u32[]{:S(2)}) collective-permute-start(f32[64,1536]{1,0:T(8,128)S(1)} %copy-done.34), channel_id=1, source_target_pairs={{0,24},{8,16},{16,8},{24,0},{1,25},{9,17},{17,9},{25,1},{2,26},{10... | collective-permute-start | bytes 1179656 | tf_op jit(solution)/shard_map/ppermute | solution.py:349
  56.4 0.9 copy-start.11
  56.4 1.0 copy-start.12
  60.1 25.6 %collective-permute-start.15 = (f32[128,1536]{1,0:T(8,128)}, f32[128,1536]{1,0:T(8,128)S(1)}, u32[]{:S(2)}, u32[]{:S(2)}) collective-permute-start(f32[128,1536]{1,0:T(8,128)} %shard_map.60.refs_1_), channel_id=1, source_target_pairs={{0,2},{1,3},{2,6},{3,7},{6,4},{7,5},{4,0},{5,1},{8,10},{9,11},{10,... | collective-permute-start | bytes 2359304 | tf_op jit(solution)/shard_map/ppermute | solution.py:346
  60.8 24.9 %copy-start.26 = (f32[128,1536]{1,0:T(8,128)}, f32[128,1536]{1,0:T(8,128)S(1)}, u32[]{:S(2)}) copy-start(f32[128,1536]{1,0:T(8,128)S(1)} %collective-permute-done.11.refs_0_) | copy-start | bytes 2359300
  60.8 37.8 %collective-permute-start.16 = (f32[128,1536]{1,0:T(8,128)S(1)}, f32[128,1536]{1,0:T(8,128)S(1)}, u32[]{:S(2)}, u32[]{:S(2)}) collective-permute-start(f32[128,1536]{1,0:T(8,128)S(1)} %collective-permute-done.11.refs_0_), channel_id=1, source_target_pairs={{0,2},{1,3},{2,6},{3,7},{6,4},{7,5},{4,0},{5,1},{8,10},{9,11},{10,... | collective-permute-start | bytes 2359304 | tf_op jit(solution)/shard_map/ppermute | solution.py:346
  85.6 12.9 %copy-start.32 = (f32[128,1536]{1,0:T(8,128)}, f32[128,1536]{1,0:T(8,128)S(1)}, u32[]{:S(2)}) copy-start(f32[128,1536]{1,0:T(8,128)S(1)} %collective-permute-done.15.refs_1_) | copy-start | bytes 2359300
  85.7 36.1 %collective-permute-start.18 = (f32[128,1536]{1,0:T(8,128)S(1)}, f32[128,1536]{1,0:T(8,128)S(1)}, u32[]{:S(2)}, u32[]{:S(2)}) collective-permute-start(f32[128,1536]{1,0:T(8,128)S(1)} %collective-permute-done.15.refs_1_), channel_id=1, source_target_pairs={{0,2},{1,3},{2,6},{3,7},{6,4},{7,5},{4,0},{5,1},{8,10},{9,11},{10,... | collective-permute-start | bytes 2359304 | tf_op jit(solution)/shard_map/ppermute | solution.py:346
  98.6 23.1 %copy-start.30 = (f32[128,1536]{1,0:T(8,128)}, f32[128,1536]{1,0:T(8,128)S(1)}, u32[]{:S(2)}) copy-start(f32[128,1536]{1,0:T(8,128)S(1)} %collective-permute-done.16.refs_0_) | copy-start | bytes 2359300
  98.6 48.7 %collective-permute-start.17 = (f32[128,1536]{1,0:T(8,128)S(1)}, f32[128,1536]{1,0:T(8,128)S(1)}, u32[]{:S(2)}, u32[]{:S(2)}) collective-permute-start(f32[128,1536]{1,0:T(8,128)S(1)} %collective-permute-done.16.refs_0_), channel_id=1, source_target_pairs={{0,2},{1,3},{2,6},{3,7},{6,4},{7,5},{4,0},{5,1},{8,10},{9,11},{10,... | collective-permute-start | bytes 2359304 | tf_op jit(solution)/shard_map/ppermute | solution.py:346
  121.7 25.6 %copy-start.28 = (f32[128,1536]{1,0:T(8,128)S(1)}, f32[128,1536]{1,0:T(8,128)}, u32[]{:S(2)}) copy-start(f32[128,1536]{1,0:T(8,128)} %get-tuple-element.152) | copy-start | bytes 2359300
  121.7 26.3 %copy-start.27 = (f32[128,1536]{1,0:T(8,128)S(1)}, f32[128,1536]{1,0:T(8,128)}, u32[]{:S(2)}) copy-start(f32[128,1536]{1,0:T(8,128)} %get-tuple-element.133) | copy-start | bytes 2359300
  121.7 2.6 copy-start.31
  121.7 27.9 %collective-permute-start.21 = (f32[128,1536]{1,0:T(8,128)S(1)}, f32[128,1536]{1,0:T(8,128)S(1)}, u32[]{:S(2)}, u32[]{:S(2)}) collective-permute-start(f32[128,1536]{1,0:T(8,128)S(1)} %collective-permute-done.18.refs_1_), channel_id=1, source_target_pairs={{0,2},{1,3},{2,6},{3,7},{6,4},{7,5},{4,0},{5,1},{8,10},{9,11},{10,... | collective-permute-start | bytes 2359304 | tf_op jit(solution)/shard_map/ppermute | solution.py:346
  147.3 2.4 copy-start.29
  147.3 26.1 %collective-permute-start.23 = (f32[128,1536]{1,0:T(8,128)S(1)}, f32[128,1536]{1,0:T(8,128)S(1)}, u32[]{:S(2)}, u32[]{:S(2)}) collective-permute-start(f32[128,1536]{1,0:T(8,128)S(1)} %copy-done.28), channel_id=1, source_target_pairs={{0,2},{1,3},{2,6},{3,7},{6,4},{7,5},{4,0},{5,1},{8,10},{9,11},{10,... | collective-permute-start | bytes 2359304 | tf_op jit(solution)/shard_map/ppermute | solution.py:346
  148.0 25.4 %copy-start.6 = (f32[128,1536]{1,0:T(8,128)S(1)}, f32[128,1536]{1,0:T(8,128)}, u32[]{:S(2)}) copy-start(f32[128,1536]{1,0:T(8,128)} %get-tuple-element.131) | copy-start | bytes 2359300
  148.0 37.6 %copy-start.5 = (f32[128,1536]{1,0:T(8,128)S(1)}, f32[128,1536]{1,0:T(8,128)}, u32[]{:S(2)}) copy-start(f32[128,1536]{1,0:T(8,128)} %get-tuple-element.132) | copy-start | bytes 2359300
  148.0 37.6 %collective-permute-start.19 = (f32[128,1536]{1,0:T(8,128)S(1)}, f32[128,1536]{1,0:T(8,128)S(1)}, u32[]{:S(2)}, u32[]{:S(2)}) collective-permute-start(f32[128,1536]{1,0:T(8,128)S(1)} %copy-done.27), channel_id=1, source_target_pairs={{0,2},{1,3},{2,6},{3,7},{6,4},{7,5},{4,0},{5,1},{8,10},{9,11},{10,... | collective-permute-start | bytes 2359304 | tf_op jit(solution)/shard_map/ppermute | solution.py:346
  149.6 0.9 copy-start.33
  173.5 28.9 %collective-permute-start.24 = (f32[128,1536]{1,0:T(8,128)S(1)}, f32[128,1536]{1,0:T(8,128)S(1)}, u32[]{:S(2)}, u32[]{:S(2)}) collective-permute-start(f32[128,1536]{1,0:T(8,128)S(1)} %add.29), channel_id=1, source_target_pairs={{0,2},{1,3},{2,6},{3,7},{6,4},{7,5},{4,0},{5,1},{8,10},{9,11},{10,... | collective-permute-start | bytes 2359304 | tf_op jit(solution)/shard_map/ppermute | solution.py:346
  186.5 28.3 %collective-permute-start.20 = (f32[128,1536]{1,0:T(8,128)}, f32[128,1536]{1,0:T(8,128)S(1)}, u32[]{:S(2)}, u32[]{:S(2)}) collective-permute-start(f32[128,1536]{1,0:T(8,128)} %add.26), channel_id=1, source_target_pairs={{0,2},{1,3},{2,6},{3,7},{6,4},{7,5},{4,0},{5,1},{8,10},{9,11},{10,... | collective-permute-start | bytes 2359304 | tf_op jit(solution)/shard_map/ppermute | solution.py:346
  199.0 48.2 %collective-permute-start.25 = (f32[768,1536]{1,0:T(8,128)}, f32[768,1536]{1,0:T(8,128)S(1)}, u32[]{:S(2)}, u32[]{:S(2)}) collective-permute-start(f32[768,1536]{1,0:T(8,128)} %shard_map.65), channel_id=1, source_target_pairs={{0,1},{1,0},{2,3},{3,2},{4,5},{5,4},{6,7},{7,6},{8,9},{9,8},{10,11... | collective-permute-start | bytes 14155784 | tf_op jit(solution)/shard_map/ppermute | solution.py:348
  212.6 10.0 %copy-start.4 = (f32[128,1536]{1,0:T(8,128)S(1)}, f32[128,1536]{1,0:T(8,128)}, u32[]{:S(2)}) copy-start(f32[128,1536]{1,0:T(8,128)} %get-tuple-element.153) | copy-start | bytes 2359300
  212.6 11.0 %copy-start.3 = (f32[128,1536]{1,0:T(8,128)S(1)}, f32[128,1536]{1,0:T(8,128)}, u32[]{:S(2)}) copy-start(f32[128,1536]{1,0:T(8,128)} %get-tuple-element.134) | copy-start | bytes 2359300
  222.5 24.7 %collective-permute-start.26 = (f32[768,1536]{1,0:T(8,128)}, f32[768,1536]{1,0:T(8,128)}, u32[]{:S(2)}, u32[]{:S(2)}) collective-permute-start(f32[768,1536]{1,0:T(8,128)} %shard_map.67), channel_id=1, source_target_pairs={{0,1},{1,0},{2,3},{3,2},{4,5},{5,4},{6,7},{7,6},{8,9},{9,8},{10,11... | collective-permute-start | bytes 14155784 | tf_op jit(solution)/shard_map/ppermute | solution.py:348
  223.5 21.6 %collective-permute-start.27 = (f32[128,1536]{1,0:T(8,128)}, f32[128,1536]{1,0:T(8,128)}, u32[]{:S(2)}, u32[]{:S(2)}) collective-permute-start(f32[128,1536]{1,0:T(8,128)} %add.30), channel_id=1, source_target_pairs={{0,2},{1,3},{2,6},{3,7},{6,4},{7,5},{4,0},{5,1},{8,10},{9,11},{10,... | collective-permute-start | bytes 2359304 | tf_op jit(solution)/shard_map/ppermute | solution.py:346
  223.6 21.5 %copy-start.2 = (f32[128,1536]{1,0:T(8,128)S(1)}, f32[128,1536]{1,0:T(8,128)}, u32[]{:S(2)}) copy-start(f32[128,1536]{1,0:T(8,128)} %get-tuple-element.126) | copy-start | bytes 2359300
  223.6 37.8 %copy-start.1 = (f32[128,1536]{1,0:T(8,128)S(1)}, f32[128,1536]{1,0:T(8,128)}, u32[]{:S(2)}) copy-start(f32[128,1536]{1,0:T(8,128)} %get-tuple-element.127) | copy-start | bytes 2359300
  223.6 37.8 %collective-permute-start.22 = (f32[128,1536]{1,0:T(8,128)S(1)}, f32[128,1536]{1,0:T(8,128)S(1)}, u32[]{:S(2)}, u32[]{:S(2)}) collective-permute-start(f32[128,1536]{1,0:T(8,128)S(1)} %add.27), channel_id=1, source_target_pairs={{0,2},{1,3},{2,6},{3,7},{6,4},{7,5},{4,0},{5,1},{8,10},{9,11},{10,... | collective-permute-start | bytes 2359304 | tf_op jit(solution)/shard_map/ppermute | solution.py:346
  247.2 29.8 %copy-start = (f32[768,1536]{1,0:T(8,128)}, f32[768,1536]{1,0:T(8,128)S(1)}, u32[]{:S(2)}) copy-start(f32[768,1536]{1,0:T(8,128)S(1)} %collective-permute-done.25.refs_5_) | copy-start | bytes 14155780
  251.0 12.3 %collective-permute-start.28 = (f32[64,1536]{1,0:T(8,128)}, f32[64,1536]{1,0:T(8,128)S(1)}, u32[]{:S(2)}, u32[]{:S(2)}) collective-permute-start(f32[64,1536]{1,0:T(8,128)} %get-tuple-element.200), channel_id=1, source_target_pairs={{0,8},{8,0},{16,24},{24,16},{1,9},{9,1},{17,25},{25,17},{2,10},{10... | collective-permute-start | bytes 1179656 | tf_op jit(solution)/shard_map/ppermute | solution.py:349
  251.6 12.0 %collective-permute-start.29 = (f32[64,1536]{1,0:T(8,128)}, f32[64,1536]{1,0:T(8,128)S(1)}, u32[]{:S(2)}, u32[]{:S(2)}) collective-permute-start(f32[64,1536]{1,0:T(8,128)} %get-tuple-element.201), channel_id=1, source_target_pairs={{0,16},{8,24},{16,0},{24,8},{1,17},{9,25},{17,1},{25,9},{2,18},{10... | collective-permute-start | bytes 1179656 | tf_op jit(solution)/shard_map/ppermute | solution.py:349
  252.4 17.9 %collective-permute-start.30 = (f32[64,1536]{1,0:T(8,128)}, f32[64,1536]{1,0:T(8,128)S(1)}, u32[]{:S(2)}, u32[]{:S(2)}) collective-permute-start(f32[64,1536]{1,0:T(8,128)} %get-tuple-element.202), channel_id=1, source_target_pairs={{0,24},{8,16},{16,8},{24,0},{1,25},{9,17},{17,9},{25,1},{2,26},{10... | collective-permute-start | bytes 1179656 | tf_op jit(solution)/shard_map/ppermute | solution.py:349
  263.4 28.9 %copy-start.13 = (f32[64,1536]{1,0:T(8,128)}, f32[64,1536]{1,0:T(8,128)S(1)}, u32[]{:S(2)}) copy-start(f32[64,1536]{1,0:T(8,128)S(1)} %collective-permute-done.28.refs_5_) | copy-start | bytes 1179652
  263.6 28.7 %copy-start.14 = (f32[64,1536]{1,0:T(8,128)}, f32[64,1536]{1,0:T(8,128)S(1)}, u32[]{:S(2)}) copy-start(f32[64,1536]{1,0:T(8,128)S(1)} %collective-permute-done.29.refs_6_) | copy-start | bytes 1179652
  270.3 22.0 %copy-start.15 = (f32[64,1536]{1,0:T(8,128)}, f32[64,1536]{1,0:T(8,128)S(1)}, u32[]{:S(2)}) copy-start(f32[64,1536]{1,0:T(8,128)S(1)} %collective-permute-done.30.refs_7_) | copy-start | bytes 1179652
  273.4 22.0 %collective-permute-start.31 = (f32[64,1536]{1,0:T(8,128)}, f32[64,1536]{1,0:T(8,128)S(1)}, u32[]{:S(2)}, u32[]{:S(2)}) collective-permute-start(f32[64,1536]{1,0:T(8,128)} %get-tuple-element.204), channel_id=1, source_target_pairs={{0,8},{8,0},{16,24},{24,16},{1,9},{9,1},{17,25},{25,17},{2,10},{10... | collective-permute-start | bytes 1179656 | tf_op jit(solution)/shard_map/ppermute | solution.py:349
  275.0 20.4 %collective-permute-start.32 = (f32[64,1536]{1,0:T(8,128)}, f32[64,1536]{1,0:T(8,128)S(1)}, u32[]{:S(2)}, u32[]{:S(2)}) collective-permute-start(f32[64,1536]{1,0:T(8,128)} %get-tuple-element.205), channel_id=1, source_target_pairs={{0,16},{8,24},{16,0},{24,8},{1,17},{9,25},{17,1},{25,9},{2,18},{10... | collective-permute-start | bytes 1179656 | tf_op jit(solution)/shard_map/ppermute | solution.py:349
  275.8 19.7 %collective-permute-start.33 = (f32[64,1536]{1,0:T(8,128)}, f32[64,1536]{1,0:T(8,128)S(1)}, u32[]{:S(2)}, u32[]{:S(2)}) collective-permute-start(f32[64,1536]{1,0:T(8,128)} %get-tuple-element.206), channel_id=1, source_target_pairs={{0,24},{8,16},{16,8},{24,0},{1,25},{9,17},{17,9},{25,1},{2,26},{10... | collective-permute-start | bytes 1179656 | tf_op jit(solution)/shard_map/ppermute | solution.py:349
  (6 other events, 4.5 us)

commit v4 on v3

--- a/solution.py
+++ b/solution.py
@@ -368,7 +368,9 @@
     sib_virtual = sibling(vir_energy)
     row_energy = row_energies[0][None, :, None] - jnp.stack([vir_energy, sib_virtual])[:, None, :]
     row_energy = row_energy.reshape(1, CORES * own_count * width)
-    virtual = jnp.stack([vir_energy] + [along(vir_energy, s) for s in range(1, chips)])
+    virtual = [vir_energy] + [along(vir_energy, s) for s in range(1, chips)]
+    early_energies = [sib_virtual] + virtual[1:]
+    virtual = jnp.stack(virtual)
     col_energy = partner_energy[None, None, :, None] - virtual.reshape(chips, PIECES, 1, part_width)
     col_energy = list(col_energy.reshape(chips, slots * width, 1))
 
@@ -378,7 +380,7 @@
         got = [to_group(block, k + 1) for k, block in enumerate(sent)]
         if p == 1:
             halves = (own_half, split_rows(after(sib_rows, pieces[0][0])))
-        got = after(got, halves, row_energy, col_energy, pieces[-1][0]) if p else after(got, own_half)
+        got = after(got, halves, row_energy, col_energy, pieces[-1][0]) if p else after(got, own_half, early_energies)
         part = choose(me_ref, packet, slots, integrals, got, p * part_width)
         pieces.append([part, hop(part)])
         if p == 1:
@@ -427,8 +429,9 @@
     early = forward(after(units[:-1], aside[1]), 0, rows, [])
     known = [(0, early)] + [(begin, sibling(x)) for (begin, _), x in zip(cuts, aside)]
     density = forward(units[-1:], 0, rows, known).reshape(own_count, width, aux)
+    product = density
     for p in range(PIECES):
-        share = after(totals[p], known, *(arrived if p else []))
+        share = after(totals[p], known, *([product] + arrived if p else []))
         sent = back(me_ref, packet, slots, own_count, share, groups)
         arrived = [to_group(block, k + 1) for k, block in enumerate(sent)]
         density = finish(me_ref, packets, slots, totals[p], arrived, density, p * part_width)

time: 301 us -> 306 us (1.017)
  waiting for transfers between devices: 48.3 us -> 53.8 us
    ppermute x15, waiting for transfers between devices: 9.42 us -> 14.9 us  [body(): lax.ppermute(x, 'grp', [(g, g ^ k) for g in range(groups)])]
  transfers between devices with their start and end apart: 34 -> 34, of which waited for: 10 -> 11; matrix products, arithmetic and copies ran while one was open for 4% -> 4% of each run, Pallas kernels for 63% -> 62%
where the time goes in v4:
time: 306 us
  Pallas kernels  196 us (64%)
  waiting for transfers between devices  53.8 us (18%)
  starting transfers between devices  38.4 us (13%)
  local copies, waits for them, and re-layouts  10.4 us (3%)
  other arithmetic  7.27 us (2%)
    pallas_call x4, Pallas kernels, unit(): pl.pallas_call(functools.partial(unit_kernel, steps), grid=(2 * steps,),...  91.8 us
    pallas_call x5, Pallas kernels, forward(): pl.pallas_call(functools.partial(forward_kernel, len(units), spans), grid...  61.9 us
    ppermute x15, waiting for transfers between devices, body(): along = lambda x, s: lax.ppermute(x, 'blk', ring(s))  37.9 us
    ppermute x15, starting transfers between devices, body(): along = lambda x, s: lax.ppermute(x, 'blk', ring(s))  19.6 us
    ppermute x15, starting transfers between devices, body(): lax.ppermute(x, 'grp', [(g, g ^ k) for g in range(groups)])  18.3 us
    pallas_call x2, Pallas kernels, split_rows(): pl.pallas_call(split_kernel, grid=(rows // step,), in_specs=[spec], out_s...  17.4 us
    ppermute x15, waiting for transfers between devices, body(): lax.ppermute(x, 'grp', [(g, g ^ k) for g in range(groups)])  14.9 us
    pallas_call x2, Pallas kernels, back(): pl.pallas_call(functools.partial(back_kernel, groups, slots, own_count),...  6.93 us
  transfers between devices with their start and end apart: 34, of which 11 were waited for; matrix products, arithmetic and copies ran while one was open for 4% of the time, Pallas kernels for 62%

profile of v4, /device:TPU:0, one launch (start us, length us, event | category | flops | bytes accessed | tf_op | source)
XLA Modules:
  0.0 306.0 jit_solution(17949493855780818913)
XLA Ops:
  0.5 0.7 pad_add_fusion.1.refs_0_.lists
  1.2 2.5 collective-permute-start
  3.7 1.5 collective-permute-start.1
  5.2 2.0 collective-permute-start.8
  7.3 0.7 stack.47
  8.1 1.5 collective-permute-done.2.refs_3_
  10.2 3.2 %shard_map.57 = (f32[64,1536]{1,0:T(8,128)}, f32[64,1536]{1,0:T(8,128)}, f32[64,1536]{1,0:T(8,128)}) custom-call(s32[1]{0:T(128)} %bitcast.me_ref, s32[14]{0:T(128)} %copy-done.19, s32[14]{0:T(128)} %copy-done.20, s32[14]{0:T(128)} %copy-done.21, s32[14]{0:T(128)} %copy-done.22, f32[12,128,1536]{2,1,0:T(8,128)} %x_ref.3), custom_call_target="tpu_custom_call" | custom-call | bytes 3145728 | tf_op jit(solution)/shard_map/pallas_call | solution.py:93
  14.0 1.1 collective-permute-start.5
  15.1 1.9 collective-permute-start.6
  18.3 3.7 %collective-permute-start.9 = (f32[128]{0:T(128)S(1)}, f32[128]{0:T(128)S(1)}, u32[]{:S(2)}, u32[]{:S(2)}) collective-permute-start(f32[128]{0:T(128)S(1)} %copy-done.25), channel_id=1, source_target_pairs={{0,6},{1,7},{2,4},{3,5},{6,0},{7,1},{4,2},{5,3},{8,14},{9,15},{10,... | collective-permute-start | bytes 1544 | tf_op jit(solution)/shard_map/ppermute | solution.py:346
  22.0 3.0 shard_map.55
  25.1 8.7 %shard_map.56 = (bf16[1536,1536]{1,0:T(8,128)(2,1)}, bf16[1536,1536]{1,0:T(8,128)(2,1)}) custom-call(f32[1536,1536]{1,0:T(8,128)} %bitcast.13), custom_call_target="tpu_custom_call" | custom-call | flops 4718592 | bytes 18874368 | tf_op jit(solution)/shard_map/pallas_call | solution.py:53
  34.1 1.0 collective-permute-done.7
  35.7 1.6 collective-permute-start.13
  37.3 1.5 collective-permute-start.14
  38.8 0.7 copy-done.9
  39.5 2.6 shard_map.58.refs_0_
  42.1 2.0 collective-permute-start.11
  45.2 0.8 copy.22.col_ref
  46.0 0.8 copy.20.col_ref
  46.8 0.8 copy.21.col_ref
  47.6 0.8 copy.23.col_ref
  48.4 8.7 %shard_map.59 = (bf16[1536,1536]{1,0:T(8,128)(2,1)}, bf16[1536,1536]{1,0:T(8,128)(2,1)}) custom-call(f32[1536,1536]{1,0:T(8,128)} %collective-permute-done.3.x_ref), custom_call_target="tpu_custom_call" | custom-call | flops 4718592 | bytes 18874368 | tf_op jit(solution)/shard_map/pallas_call | solution.py:53
  57.2 0.7 copy-done.10
  58.1 2.6 shard_map.60.refs_1_
  60.7 0.7 collective-permute-start.15
  62.1 1.4 collective-permute-start.16
  63.5 22.8 %shard_map.61 = (bf16[256,3072]{1,0:T(8,128)(2,1)}, bf16[256,3072]{1,0:T(8,128)(2,1)}, bf16[256,1536]{1,0:T(8,128)(2,1)}, bf16[256,1536]{1,0:T(8,128)(2,1)}, f32[128,1536]{1,0:T(8,128)}, /*index=5*/f32[128,1536]{1,0:T(8,128)}) custom-call(bf16[1536,1536]{1,0:T(8,128)(2,1)} %get-tuple-element.110.own_high, bf16[1536,1536]{1,0:T(8,128)(2,1)} %get-tuple-element.111.own_low, ...), custom_call_target="tpu_custom_call" | custom-call | flops 14495514624 | bytes 25165824 | tf_op jit(solution)/shard_map/pallas_call | solution.py:281
  86.3 1.3 collective-permute-start.18
  87.6 11.6 %collective-permute-done.16.refs_0_ = f32[128,1536]{1,0:T(8,128)S(1)} collective-permute-done((f32[128,1536]{1,0:T(8,128)S(1)}, f32[128,1536]{1,0:T(8,128)S(1)}, u32[]{:S(2)}, u32[]{:S(2)}) %collective-permute-start.16) | collective-permute-done | bytes 786464 | tf_op jit(solution)/shard_map/ppermute | solution.py:346
  99.2 23.2 %shard_map.62 = (bf16[256,3072]{1,0:T(8,128)(2,1)}, bf16[256,3072]{1,0:T(8,128)(2,1)}, bf16[256,1536]{1,0:T(8,128)(2,1)}, bf16[256,1536]{1,0:T(8,128)(2,1)}, f32[128,1536]{1,0:T(8,128)}, /*index=5*/f32[128,1536]{1,0:T(8,128)}) custom-call(bf16[1536,1536]{1,0:T(8,128)(2,1)} %get-tuple-element.110.own_high, bf16[1536,1536]{1,0:T(8,128)(2,1)} %get-tuple-element.111.own_low, ...), custom_call_target="tpu_custom_call" | custom-call | flops 14495514624 | bytes 25165824 | tf_op jit(solution)/shard_map/pallas_call | solution.py:281
  122.5 2.8 collective-permute-start.21
  125.2 23.0 %shard_map.63 = (bf16[256,3072]{1,0:T(8,128)(2,1)}, bf16[256,3072]{1,0:T(8,128)(2,1)}, bf16[256,1536]{1,0:T(8,128)(2,1)}, bf16[256,1536]{1,0:T(8,128)(2,1)}, f32[128,1536]{1,0:T(8,128)}, /*index=5*/f32[128,1536]{1,0:T(8,128)}) custom-call(bf16[1536,1536]{1,0:T(8,128)(2,1)} %get-tuple-element.110.own_high, bf16[1536,1536]{1,0:T(8,128)(2,1)} %get-tuple-element.111.own_low, ...), custom_call_target="tpu_custom_call" | custom-call | flops 14495514624 | bytes 25165824 | tf_op jit(solution)/shard_map/pallas_call | solution.py:281
  148.9 1.6 collective-permute-start.19
  150.5 0.9 copy-done.33
  151.4 22.9 %shard_map.64 = (bf16[256,3072]{1,0:T(8,128)(2,1)}, bf16[256,3072]{1,0:T(8,128)(2,1)}, bf16[256,1536]{1,0:T(8,128)(2,1)}, bf16[256,1536]{1,0:T(8,128)(2,1)}, f32[128,1536]{1,0:T(8,128)}, /*index=5*/f32[128,1536]{1,0:T(8,128)}) custom-call(bf16[1536,1536]{1,0:T(8,128)(2,1)} %get-tuple-element.110.own_high, bf16[1536,1536]{1,0:T(8,128)(2,1)} %get-tuple-element.111.own_low, ...), custom_call_target="tpu_custom_call" | custom-call | flops 14495514624 | bytes 25165824 | tf_op jit(solution)/shard_map/pallas_call | solution.py:281
  175.1 11.4 %collective-permute-done.19 = f32[128,1536]{1,0:T(8,128)S(1)} collective-permute-done((f32[128,1536]{1,0:T(8,128)S(1)}, f32[128,1536]{1,0:T(8,128)S(1)}, u32[]{:S(2)}, u32[]{:S(2)}) %collective-permute-start.19) | collective-permute-done | bytes 786464 | tf_op jit(solution)/shard_map/ppermute | solution.py:346
  186.5 1.0 add.26
  187.5 12.5 %shard_map.65 = f32[768,1536]{1,0:T(8,128)} custom-call(bf16[256,3072]{1,0:T(8,128)(2,1)} %get-tuple-element.187.refs_0_, bf16[256,3072]{1,0:T(8,128)(2,1)} %get-tuple-element.188.refs_1_, bf16[256,1536]{1,0:T(8,128)(2,1)} %get-tuple-element.189.refs_2_, bf16[256,1536]{1,0:T(8,128)(2,1)} %get-tuple-element.190.refs_3_, ...), custom_call_target="tpu_custom_call" | custom-call | flops 7247757312 | bytes 9437184 | tf_op jit(solution)/shard_map/pallas_call | solution.py:319
  200.0 3.3 %collective-permute-done.24 = f32[128,1536]{1,0:T(8,128)S(1)} collective-permute-done((f32[128,1536]{1,0:T(8,128)S(1)}, f32[128,1536]{1,0:T(8,128)S(1)}, u32[]{:S(2)}, u32[]{:S(2)}) %collective-permute-start.24) | collective-permute-done | bytes 786464 | tf_op jit(solution)/shard_map/ppermute | solution.py:346
  203.3 10.1 %shard_map.66.refs_4_ = f32[768,1536]{1,0:T(8,128)} custom-call(bf16[256,3072]{1,0:T(8,128)(2,1)} %get-tuple-element.187.refs_0_, bf16[256,3072]{1,0:T(8,128)(2,1)} %get-tuple-element.188.refs_1_, bf16[256,1536]{1,0:T(8,128)(2,1)} %get-tuple-element.189.refs_2_, bf16[256,1536]{1,0:T(8,128)(2,1)} %get-tuple-element.190.refs_3_, ...), custom_call_target="tpu_custom_call" | custom-call | flops 5435817984 | bytes 9437184 | tf_op jit(solution)/shard_map/pallas_call | solution.py:319
  213.5 1.7 collective-permute-done.20
  215.2 7.7 %shard_map.67 = f32[768,1536]{1,0:T(8,128)} custom-call(bf16[256,3072]{1,0:T(8,128)(2,1)} %get-tuple-element.183.refs_12_.refs_0_, bf16[256,3072]{1,0:T(8,128)(2,1)} %get-tuple-element.184.refs_13_.refs_1_, bf16[256,1536]{1,0:T(8,128)(2,1)} %get-tuple-element.185.refs_14_.refs_2_, bf16[256,1536]{1,0:T(8,128)(2,1)} %get-tuple-element.186.refs_15_.refs_3_, ...), custom_call_target="tpu_custom_call" | custom-call | flops 1811939328 | bytes 9437184 | tf_op jit(solution)/shard_map/pallas_call | solution.py:319
  222.9 1.0 add.30
  224.0 2.8 collective-permute-start.22
  226.8 16.2 %shard_map.68.refs_4_ = f32[1536,1536]{1,0:T(8,128)} custom-call(bf16[256,3072]{1,0:T(8,128)(2,1)} %get-tuple-element.187.refs_0_, bf16[256,3072]{1,0:T(8,128)(2,1)} %get-tuple-element.188.refs_1_, bf16[256,1536]{1,0:T(8,128)(2,1)} %get-tuple-element.189.refs_2_, bf16[256,1536]{1,0:T(8,128)(2,1)} %get-tuple-element.190.refs_3_, ...), custom_call_target="tpu_custom_call" | custom-call | flops 10871635968 | bytes 18874368 | tf_op jit(solution)/shard_map/pallas_call | solution.py:319
  243.0 2.4 collective-permute-done.27
  245.4 2.1 add.31.share.refs_4_
  247.6 3.8 %shard_map.70 = (f32[64,1536]{1,0:T(8,128)}, f32[64,1536]{1,0:T(8,128)}, f32[64,1536]{1,0:T(8,128)}) custom-call(s32[1]{0:T(128)} %bitcast.me_ref, s32[14]{0:T(128)} %copy-done.19, f32[128,1536]{1,0:T(8,128)} %add.31.share.refs_4_), custom_call_target="tpu_custom_call" | custom-call | bytes 3145728 | tf_op jit(solution)/shard_map/pallas_call | solution.py:164
  251.4 0.8 collective-permute-start.28
  252.2 0.8 collective-permute-start.29
  253.0 1.9 collective-permute-start.30
  255.0 6.8 %collective-permute-done.22 = f32[128,1536]{1,0:T(8,128)S(1)} collective-permute-done((f32[128,1536]{1,0:T(8,128)S(1)}, f32[128,1536]{1,0:T(8,128)S(1)}, u32[]{:S(2)}, u32[]{:S(2)}) %collective-permute-start.22) | collective-permute-done | bytes 786464 | tf_op jit(solution)/shard_map/ppermute | solution.py:346
  261.8 1.0 add.28.share.refs_4_
  262.8 15.3 %shard_map.69 = f32[1536,1536]{1,0:T(8,128)} custom-call(bf16[256,3072]{1,0:T(8,128)(2,1)} %get-tuple-element.183.refs_12_.refs_0_, bf16[256,3072]{1,0:T(8,128)(2,1)} %get-tuple-element.184.refs_13_.refs_1_, bf16[256,1536]{1,0:T(8,128)(2,1)} %get-tuple-element.185.refs_14_.refs_2_, bf16[256,1536]{1,0:T(8,128)(2,1)} %get-tuple-element.186.refs_15_.refs_3_, ...), custom_call_target="tpu_custom_call" | custom-call | flops 3623878656 | bytes 18874368 | tf_op jit(solution)/shard_map/pallas_call | solution.py:319
  278.2 3.1 %shard_map.71 = (f32[64,1536]{1,0:T(8,128)}, f32[64,1536]{1,0:T(8,128)}, f32[64,1536]{1,0:T(8,128)}) custom-call(s32[1]{0:T(128)} %bitcast.me_ref, s32[14]{0:T(128)} %copy-done.19, f32[128,1536]{1,0:T(8,128)} %add.28.share.refs_4_), custom_call_target="tpu_custom_call" | custom-call | bytes 3145728 | tf_op jit(solution)/shard_map/pallas_call | solution.py:164
  281.3 0.8 collective-permute-start.31
  282.8 2.0 collective-permute-start.33
  284.9 3.1 %shard_map.72.refs_8_ = f32[12,128,1536]{2,1,0:T(8,128)} custom-call(s32[1]{0:T(128)} %bitcast.me_ref, s32[14]{0:T(128)} %copy-done.19, s32[14]{0:T(128)} %copy-done.20, s32[14]{0:T(128)} %copy-done.21, s32[14]{0:T(128)} %copy-done.22, f32[128,1536]{1,0:T(8,128)} %add.31.share.refs_4_, f32[64,1536]{1,0:T(8,128)} %copy-done.13, ...), custom_call_target="tpu_custom_call", output_to_operand_aliasing={{}: (9, {})} | custom-call | bytes 4718592 | tf_op jit(solution)/shard_map/pallas_call | solution.py:219
  288.0 5.6 %collective-permute-done.31.refs_5_ = f32[64,1536]{1,0:T(8,128)S(1)} collective-permute-done((f32[64,1536]{1,0:T(8,128)}, f32[64,1536]{1,0:T(8,128)S(1)}, u32[]{:S(2)}, u32[]{:S(2)}) %collective-permute-start.31) | collective-permute-done | bytes 393248 | tf_op jit(solution)/shard_map/ppermute | solution.py:349
  293.6 7.6 %collective-permute-done.32.refs_6_ = f32[64,1536]{1,0:T(8,128)S(1)} collective-permute-done((f32[64,1536]{1,0:T(8,128)}, f32[64,1536]{1,0:T(8,128)S(1)}, u32[]{:S(2)}, u32[]{:S(2)}) %collective-permute-start.32) | collective-permute-done | bytes 393248 | tf_op jit(solution)/shard_map/ppermute | solution.py:349
  301.3 0.7 copy-done.17
  302.0 0.8 copy-done.18
  302.8 3.1 %shard_map.73 = f32[12,128,1536]{2,1,0:T(8,128)} custom-call(s32[1]{0:T(128)} %bitcast.me_ref, s32[14]{0:T(128)} %copy-done.19, s32[14]{0:T(128)} %copy-done.20, s32[14]{0:T(128)} %copy-done.21, s32[14]{0:T(128)} %copy-done.22, f32[128,1536]{1,0:T(8,128)} %add.28.share.refs_4_, f32[64,1536]{1,0:T(8,128)} %copy-done.16, ...), custom_call_target="tpu_custom_call", output_to_operand_aliasing={{}: (9, {})} | custom-call | bytes 4718592 | tf_op jit(solution)/shard_map/pallas_call | solution.py:219
  (129 shorter events, 8.4 us)
Async XLA Ops:
  0.0 48.4 %collective-permute-start.3 = (f32[1536,1536]{1,0:T(8,128)}, f32[1536,1536]{1,0:T(8,128)}, u32[]{:S(2)}, u32[]{:S(2)}) collective-permute-start(f32[1536,1536]{1,0:T(8,128)} %bitcast.12), channel_id=1, source_target_pairs={{0,1},{1,0},{2,3},{3,2},{4,5},{5,4},{6,7},{7,6},{8,9},{9,8},{10,11... | collective-permute-start | bytes 28311560 | tf_op jit(solution)/shard_map/ppermute | solution.py:348
  1.2 8.5 %copy-start.19 = (s32[14]{0:T(128)}, s32[14]{0:T(128)S(1)}, u32[]{:S(2)}) copy-start(s32[14]{0:T(128)S(1)} %pad_add_fusion.1.refs_0_.lists) | copy-start | bytes 172
  1.2 6.9 %collective-permute-start = (s32[14]{0:T(128)S(1)}, s32[14]{0:T(128)S(1)}, u32[]{:S(2)}, u32[]{:S(2)}) collective-permute-start(s32[14]{0:T(128)S(1)} %pad_add_fusion.1.refs_0_.lists), channel_id=1, source_target_pairs={{0,8},{8,0},{16,24},{24,16},{1,9},{9,1},{17,25},{25,17},{2,10},{10... | collective-permute-start | bytes 176 | tf_op jit(solution)/shard_map/ppermute | solution.py:349
  3.7 4.4 %collective-permute-start.1 = (s32[14]{0:T(128)S(1)}, s32[14]{0:T(128)S(1)}, u32[]{:S(2)}, u32[]{:S(2)}) collective-permute-start(s32[14]{0:T(128)S(1)} %pad_add_fusion.1.refs_0_.lists), channel_id=1, source_target_pairs={{0,16},{8,24},{16,0},{24,8},{1,17},{9,25},{17,1},{25,9},{2,18},{10... | collective-permute-start | bytes 176 | tf_op jit(solution)/shard_map/ppermute | solution.py:349
  5.2 4.4 %collective-permute-start.2 = (s32[14]{0:T(128)S(1)}, s32[14]{0:T(128)S(1)}, u32[]{:S(2)}, u32[]{:S(2)}) collective-permute-start(s32[14]{0:T(128)S(1)} %pad_add_fusion.1.refs_0_.lists), channel_id=1, source_target_pairs={{0,24},{8,16},{16,8},{24,0},{1,25},{9,17},{17,9},{25,1},{2,26},{10... | collective-permute-start | bytes 176 | tf_op jit(solution)/shard_map/ppermute | solution.py:349
  5.2 13.0 %collective-permute-start.8 = (f32[128]{0:T(128)}, f32[128]{0:T(128)S(1)}, u32[]{:S(2)}, u32[]{:S(2)}) collective-permute-start(f32[128]{0:T(128)} %param.9), channel_id=1, source_target_pairs={{0,2},{1,3},{2,6},{3,7},{6,4},{7,5},{4,0},{5,1},{8,10},{9,11},{10,... | collective-permute-start | bytes 1544 | tf_op jit(solution)/shard_map/ppermute | solution.py:346
  8.1 1.6 copy-start.20
  8.1 1.6 copy-start.21
  10.2 7.6 %copy-start.23 = (f32[48]{0:T(128)S(1)}, f32[48]{0:T(128)}, u32[]{:S(2)}) copy-start(f32[48]{0:T(128)} %param.8) | copy-start | bytes 580
  10.2 7.8 %copy-start.24 = (s32[1,2]{1,0:T(1,128)S(1)}, s32[1,2]{1,0:T(1,128)}, u32[]{:S(2)}) copy-start(s32[1,2]{1,0:T(1,128)} %param.6) | copy-start | bytes 28
  10.2 8.0 %copy-start.25 = (f32[128]{0:T(128)S(1)}, f32[128]{0:T(128)}, u32[]{:S(2)}) copy-start(f32[128]{0:T(128)} %param.9) | copy-start | bytes 1540
  13.4 22.3 %collective-permute-start.4 = (f32[64,1536]{1,0:T(8,128)}, f32[64,1536]{1,0:T(8,128)S(1)}, u32[]{:S(2)}, u32[]{:S(2)}) collective-permute-start(f32[64,1536]{1,0:T(8,128)} %get-tuple-element.112), channel_id=1, source_target_pairs={{0,8},{8,0},{16,24},{24,16},{1,9},{9,1},{17,25},{25,17},{2,10},{10... | collective-permute-start | bytes 1179656 | tf_op jit(solution)/shard_map/ppermute | solution.py:349
  14.0 23.3 %collective-permute-start.5 = (f32[64,1536]{1,0:T(8,128)}, f32[64,1536]{1,0:T(8,128)S(1)}, u32[]{:S(2)}, u32[]{:S(2)}) collective-permute-start(f32[64,1536]{1,0:T(8,128)} %get-tuple-element.113), channel_id=1, source_target_pairs={{0,16},{8,24},{16,0},{24,8},{1,17},{9,25},{17,1},{25,9},{2,18},{10... | collective-permute-start | bytes 1179656 | tf_op jit(solution)/shard_map/ppermute | solution.py:349
  15.1 23.7 %collective-permute-start.6 = (f32[64,1536]{1,0:T(8,128)}, f32[64,1536]{1,0:T(8,128)S(1)}, u32[]{:S(2)}, u32[]{:S(2)}) collective-permute-start(f32[64,1536]{1,0:T(8,128)} %get-tuple-element.114), channel_id=1, source_target_pairs={{0,24},{8,16},{16,8},{24,0},{1,25},{9,17},{17,9},{25,1},{2,26},{10... | collective-permute-start | bytes 1179656 | tf_op jit(solution)/shard_map/ppermute | solution.py:349
  18.3 6.8 %collective-permute-start.9 = (f32[128]{0:T(128)S(1)}, f32[128]{0:T(128)S(1)}, u32[]{:S(2)}, u32[]{:S(2)}) collective-permute-start(f32[128]{0:T(128)S(1)} %copy-done.25), channel_id=1, source_target_pairs={{0,6},{1,7},{2,4},{3,5},{6,0},{7,1},{4,2},{5,3},{8,14},{9,15},{10,... | collective-permute-start | bytes 1544 | tf_op jit(solution)/shard_map/ppermute | solution.py:346
  25.0 10.7 %copy-start.35 = (f32[64,1536]{1,0:T(8,128)S(1)}, f32[64,1536]{1,0:T(8,128)}, u32[]{:S(2)}) copy-start(f32[64,1536]{1,0:T(8,128)} %get-tuple-element.107) | copy-start | bytes 1179652
  25.0 12.3 %copy-start.34 = (f32[64,1536]{1,0:T(8,128)S(1)}, f32[64,1536]{1,0:T(8,128)}, u32[]{:S(2)}) copy-start(f32[64,1536]{1,0:T(8,128)} %get-tuple-element.108) | copy-start | bytes 1179652
  25.1 9.0 %collective-permute-start.10 = (f32[128]{0:T(128)S(1)}, f32[128]{0:T(128)S(1)}, u32[]{:S(2)}, u32[]{:S(2)}) collective-permute-start(f32[128]{0:T(128)S(1)} %copy-done.25), channel_id=1, source_target_pairs={{0,4},{1,5},{2,0},{3,1},{6,2},{7,3},{4,6},{5,7},{8,12},{9,13},{10,... | collective-permute-start | bytes 1544 | tf_op jit(solution)/shard_map/ppermute | solution.py:346
  34.0 1.1 collective-permute-start.7
  35.2 22.0 %collective-permute-start.12 = (f32[64,1536]{1,0:T(8,128)}, f32[64,1536]{1,0:T(8,128)S(1)}, u32[]{:S(2)}, u32[]{:S(2)}) collective-permute-start(f32[64,1536]{1,0:T(8,128)} %get-tuple-element.106), channel_id=1, source_target_pairs={{0,8},{8,0},{16,24},{24,16},{1,9},{9,1},{17,25},{25,17},{2,10},{10... | collective-permute-start | bytes 1179656 | tf_op jit(solution)/shard_map/ppermute | solution.py:349
  35.7 3.1 %copy-start.7 = (f32[64,1536]{1,0:T(8,128)}, f32[64,1536]{1,0:T(8,128)S(1)}, u32[]{:S(2)}) copy-start(f32[64,1536]{1,0:T(8,128)S(1)} %collective-permute-done.4.refs_0_) | copy-start | bytes 1179652
  35.7 21.4 %collective-permute-start.13 = (f32[64,1536]{1,0:T(8,128)S(1)}, f32[64,1536]{1,0:T(8,128)S(1)}, u32[]{:S(2)}, u32[]{:S(2)}) collective-permute-start(f32[64,1536]{1,0:T(8,128)S(1)} %copy-done.35), channel_id=1, source_target_pairs={{0,16},{8,24},{16,0},{24,8},{1,17},{9,25},{17,1},{25,9},{2,18},{10... | collective-permute-start | bytes 1179656 | tf_op jit(solution)/shard_map/ppermute | solution.py:349
  37.3 1.5 copy-start.8
  37.3 19.8 %collective-permute-start.14 = (f32[64,1536]{1,0:T(8,128)S(1)}, f32[64,1536]{1,0:T(8,128)S(1)}, u32[]{:S(2)}, u32[]{:S(2)}) collective-permute-start(f32[64,1536]{1,0:T(8,128)S(1)} %copy-done.34), channel_id=1, source_target_pairs={{0,24},{8,16},{16,8},{24,0},{1,25},{9,17},{17,9},{25,1},{2,26},{10... | collective-permute-start | bytes 1179656 | tf_op jit(solution)/shard_map/ppermute | solution.py:349
  42.1 20.0 %collective-permute-start.11 = (f32[128,1536]{1,0:T(8,128)}, f32[128,1536]{1,0:T(8,128)S(1)}, u32[]{:S(2)}, u32[]{:S(2)}) collective-permute-start(f32[128,1536]{1,0:T(8,128)} %shard_map.58.refs_0_), channel_id=1, source_target_pairs={{0,2},{1,3},{2,6},{3,7},{6,4},{7,5},{4,0},{5,1},{8,10},{9,11},{10,... | collective-permute-start | bytes 2359304 | tf_op jit(solution)/shard_map/ppermute | solution.py:346
  57.1 0.9 copy-start.11
  57.2 1.0 copy-start.12
  60.7 25.6 %collective-permute-start.15 = (f32[128,1536]{1,0:T(8,128)}, f32[128,1536]{1,0:T(8,128)S(1)}, u32[]{:S(2)}, u32[]{:S(2)}) collective-permute-start(f32[128,1536]{1,0:T(8,128)} %shard_map.60.refs_1_), channel_id=1, source_target_pairs={{0,2},{1,3},{2,6},{3,7},{6,4},{7,5},{4,0},{5,1},{8,10},{9,11},{10,... | collective-permute-start | bytes 2359304 | tf_op jit(solution)/shard_map/ppermute | solution.py:346
  62.1 24.2 %copy-start.26 = (f32[128,1536]{1,0:T(8,128)}, f32[128,1536]{1,0:T(8,128)S(1)}, u32[]{:S(2)}) copy-start(f32[128,1536]{1,0:T(8,128)S(1)} %collective-permute-done.11.refs_0_) | copy-start | bytes 2359300
  62.1 37.1 %collective-permute-start.16 = (f32[128,1536]{1,0:T(8,128)S(1)}, f32[128,1536]{1,0:T(8,128)S(1)}, u32[]{:S(2)}, u32[]{:S(2)}) collective-permute-start(f32[128,1536]{1,0:T(8,128)S(1)} %collective-permute-done.11.refs_0_), channel_id=1, source_target_pairs={{0,2},{1,3},{2,6},{3,7},{6,4},{7,5},{4,0},{5,1},{8,10},{9,11},{10,... | collective-permute-start | bytes 2359304 | tf_op jit(solution)/shard_map/ppermute | solution.py:346
  86.3 12.9 %copy-start.32 = (f32[128,1536]{1,0:T(8,128)}, f32[128,1536]{1,0:T(8,128)S(1)}, u32[]{:S(2)}) copy-start(f32[128,1536]{1,0:T(8,128)S(1)} %collective-permute-done.15.refs_1_) | copy-start | bytes 2359300
  86.3 36.1 %collective-permute-start.18 = (f32[128,1536]{1,0:T(8,128)S(1)}, f32[128,1536]{1,0:T(8,128)S(1)}, u32[]{:S(2)}, u32[]{:S(2)}) collective-permute-start(f32[128,1536]{1,0:T(8,128)S(1)} %collective-permute-done.15.refs_1_), channel_id=1, source_target_pairs={{0,2},{1,3},{2,6},{3,7},{6,4},{7,5},{4,0},{5,1},{8,10},{9,11},{10,... | collective-permute-start | bytes 2359304 | tf_op jit(solution)/shard_map/ppermute | solution.py:346
  99.2 23.2 %copy-start.30 = (f32[128,1536]{1,0:T(8,128)}, f32[128,1536]{1,0:T(8,128)S(1)}, u32[]{:S(2)}) copy-start(f32[128,1536]{1,0:T(8,128)S(1)} %collective-permute-done.16.refs_0_) | copy-start | bytes 2359300
  99.2 49.0 %collective-permute-start.17 = (f32[128,1536]{1,0:T(8,128)S(1)}, f32[128,1536]{1,0:T(8,128)S(1)}, u32[]{:S(2)}, u32[]{:S(2)}) collective-permute-start(f32[128,1536]{1,0:T(8,128)S(1)} %collective-permute-done.16.refs_0_), channel_id=1, source_target_pairs={{0,2},{1,3},{2,6},{3,7},{6,4},{7,5},{4,0},{5,1},{8,10},{9,11},{10,... | collective-permute-start | bytes 2359304 | tf_op jit(solution)/shard_map/ppermute | solution.py:346
  122.4 25.8 %copy-start.28 = (f32[128,1536]{1,0:T(8,128)S(1)}, f32[128,1536]{1,0:T(8,128)}, u32[]{:S(2)}) copy-start(f32[128,1536]{1,0:T(8,128)} %get-tuple-element.152) | copy-start | bytes 2359300
  122.4 26.5 %copy-start.27 = (f32[128,1536]{1,0:T(8,128)S(1)}, f32[128,1536]{1,0:T(8,128)}, u32[]{:S(2)}) copy-start(f32[128,1536]{1,0:T(8,128)} %get-tuple-element.133) | copy-start | bytes 2359300
  122.5 2.8 copy-start.31
  122.5 28.0 %collective-permute-start.21 = (f32[128,1536]{1,0:T(8,128)S(1)}, f32[128,1536]{1,0:T(8,128)S(1)}, u32[]{:S(2)}, u32[]{:S(2)}) collective-permute-start(f32[128,1536]{1,0:T(8,128)S(1)} %collective-permute-done.18.refs_1_), channel_id=1, source_target_pairs={{0,2},{1,3},{2,6},{3,7},{6,4},{7,5},{4,0},{5,1},{8,10},{9,11},{10,... | collective-permute-start | bytes 2359304 | tf_op jit(solution)/shard_map/ppermute | solution.py:346
  148.2 2.3 copy-start.29
  148.2 26.1 %collective-permute-start.23 = (f32[128,1536]{1,0:T(8,128)S(1)}, f32[128,1536]{1,0:T(8,128)S(1)}, u32[]{:S(2)}, u32[]{:S(2)}) collective-permute-start(f32[128,1536]{1,0:T(8,128)S(1)} %copy-done.28), channel_id=1, source_target_pairs={{0,2},{1,3},{2,6},{3,7},{6,4},{7,5},{4,0},{5,1},{8,10},{9,11},{10,... | collective-permute-start | bytes 2359304 | tf_op jit(solution)/shard_map/ppermute | solution.py:346
  148.9 25.4 %copy-start.6 = (f32[128,1536]{1,0:T(8,128)S(1)}, f32[128,1536]{1,0:T(8,128)}, u32[]{:S(2)}) copy-start(f32[128,1536]{1,0:T(8,128)} %get-tuple-element.131) | copy-start | bytes 2359300
  148.9 37.6 %copy-start.5 = (f32[128,1536]{1,0:T(8,128)S(1)}, f32[128,1536]{1,0:T(8,128)}, u32[]{:S(2)}) copy-start(f32[128,1536]{1,0:T(8,128)} %get-tuple-element.132) | copy-start | bytes 2359300
  148.9 37.6 %collective-permute-start.19 = (f32[128,1536]{1,0:T(8,128)S(1)}, f32[128,1536]{1,0:T(8,128)S(1)}, u32[]{:S(2)}, u32[]{:S(2)}) collective-permute-start(f32[128,1536]{1,0:T(8,128)S(1)} %copy-done.27), channel_id=1, source_target_pairs={{0,2},{1,3},{2,6},{3,7},{6,4},{7,5},{4,0},{5,1},{8,10},{9,11},{10,... | collective-permute-start | bytes 2359304 | tf_op jit(solution)/shard_map/ppermute | solution.py:346
  174.4 28.9 %collective-permute-start.24 = (f32[128,1536]{1,0:T(8,128)S(1)}, f32[128,1536]{1,0:T(8,128)S(1)}, u32[]{:S(2)}, u32[]{:S(2)}) collective-permute-start(f32[128,1536]{1,0:T(8,128)S(1)} %add.29), channel_id=1, source_target_pairs={{0,2},{1,3},{2,6},{3,7},{6,4},{7,5},{4,0},{5,1},{8,10},{9,11},{10,... | collective-permute-start | bytes 2359304 | tf_op jit(solution)/shard_map/ppermute | solution.py:346
  187.5 27.8 %collective-permute-start.20 = (f32[128,1536]{1,0:T(8,128)}, f32[128,1536]{1,0:T(8,128)S(1)}, u32[]{:S(2)}, u32[]{:S(2)}) collective-permute-start(f32[128,1536]{1,0:T(8,128)} %add.26), channel_id=1, source_target_pairs={{0,2},{1,3},{2,6},{3,7},{6,4},{7,5},{4,0},{5,1},{8,10},{9,11},{10,... | collective-permute-start | bytes 2359304 | tf_op jit(solution)/shard_map/ppermute | solution.py:346
  200.0 47.6 %collective-permute-start.25 = (f32[768,1536]{1,0:T(8,128)}, f32[768,1536]{1,0:T(8,128)S(1)}, u32[]{:S(2)}, u32[]{:S(2)}) collective-permute-start(f32[768,1536]{1,0:T(8,128)} %shard_map.65), channel_id=1, source_target_pairs={{0,1},{1,0},{2,3},{3,2},{4,5},{5,4},{6,7},{7,6},{8,9},{9,8},{10,11... | collective-permute-start | bytes 14155784 | tf_op jit(solution)/shard_map/ppermute | solution.py:348
  213.5 9.4 %copy-start.4 = (f32[128,1536]{1,0:T(8,128)S(1)}, f32[128,1536]{1,0:T(8,128)}, u32[]{:S(2)}) copy-start(f32[128,1536]{1,0:T(8,128)} %get-tuple-element.153) | copy-start | bytes 2359300
  213.5 10.4 %copy-start.3 = (f32[128,1536]{1,0:T(8,128)S(1)}, f32[128,1536]{1,0:T(8,128)}, u32[]{:S(2)}) copy-start(f32[128,1536]{1,0:T(8,128)} %get-tuple-element.134) | copy-start | bytes 2359300
  222.9 24.7 %collective-permute-start.26 = (f32[768,1536]{1,0:T(8,128)}, f32[768,1536]{1,0:T(8,128)}, u32[]{:S(2)}, u32[]{:S(2)}) collective-permute-start(f32[768,1536]{1,0:T(8,128)} %shard_map.67), channel_id=1, source_target_pairs={{0,1},{1,0},{2,3},{3,2},{4,5},{5,4},{6,7},{7,6},{8,9},{9,8},{10,11... | collective-permute-start | bytes 14155784 | tf_op jit(solution)/shard_map/ppermute | solution.py:348
  223.9 21.6 %collective-permute-start.27 = (f32[128,1536]{1,0:T(8,128)}, f32[128,1536]{1,0:T(8,128)}, u32[]{:S(2)}, u32[]{:S(2)}) collective-permute-start(f32[128,1536]{1,0:T(8,128)} %add.30), channel_id=1, source_target_pairs={{0,2},{1,3},{2,6},{3,7},{6,4},{7,5},{4,0},{5,1},{8,10},{9,11},{10,... | collective-permute-start | bytes 2359304 | tf_op jit(solution)/shard_map/ppermute | solution.py:346
  224.0 21.5 %copy-start.2 = (f32[128,1536]{1,0:T(8,128)S(1)}, f32[128,1536]{1,0:T(8,128)}, u32[]{:S(2)}) copy-start(f32[128,1536]{1,0:T(8,128)} %get-tuple-element.126) | copy-start | bytes 2359300
  224.0 37.8 %copy-start.1 = (f32[128,1536]{1,0:T(8,128)S(1)}, f32[128,1536]{1,0:T(8,128)}, u32[]{:S(2)}) copy-start(f32[128,1536]{1,0:T(8,128)} %get-tuple-element.127) | copy-start | bytes 2359300
  224.0 37.8 %collective-permute-start.22 = (f32[128,1536]{1,0:T(8,128)S(1)}, f32[128,1536]{1,0:T(8,128)S(1)}, u32[]{:S(2)}, u32[]{:S(2)}) collective-permute-start(f32[128,1536]{1,0:T(8,128)S(1)} %add.27), channel_id=1, source_target_pairs={{0,2},{1,3},{2,6},{3,7},{6,4},{7,5},{4,0},{5,1},{8,10},{9,11},{10,... | collective-permute-start | bytes 2359304 | tf_op jit(solution)/shard_map/ppermute | solution.py:346
  247.6 15.3 %copy-start = (f32[768,1536]{1,0:T(8,128)}, f32[768,1536]{1,0:T(8,128)S(1)}, u32[]{:S(2)}) copy-start(f32[768,1536]{1,0:T(8,128)S(1)} %collective-permute-done.25.refs_5_) | copy-start | bytes 14155780
  251.4 26.7 %collective-permute-start.28 = (f32[64,1536]{1,0:T(8,128)}, f32[64,1536]{1,0:T(8,128)S(1)}, u32[]{:S(2)}, u32[]{:S(2)}) collective-permute-start(f32[64,1536]{1,0:T(8,128)} %get-tuple-element.200), channel_id=1, source_target_pairs={{0,8},{8,0},{16,24},{24,16},{1,9},{9,1},{17,25},{25,17},{2,10},{10... | collective-permute-start | bytes 1179656 | tf_op jit(solution)/shard_map/ppermute | solution.py:349
  252.2 25.9 %collective-permute-start.29 = (f32[64,1536]{1,0:T(8,128)}, f32[64,1536]{1,0:T(8,128)S(1)}, u32[]{:S(2)}, u32[]{:S(2)}) collective-permute-start(f32[64,1536]{1,0:T(8,128)} %get-tuple-element.201), channel_id=1, source_target_pairs={{0,16},{8,24},{16,0},{24,8},{1,17},{9,25},{17,1},{25,9},{2,18},{10... | collective-permute-start | bytes 1179656 | tf_op jit(solution)/shard_map/ppermute | solution.py:349
  253.0 25.2 %collective-permute-start.30 = (f32[64,1536]{1,0:T(8,128)}, f32[64,1536]{1,0:T(8,128)S(1)}, u32[]{:S(2)}, u32[]{:S(2)}) collective-permute-start(f32[64,1536]{1,0:T(8,128)} %get-tuple-element.202), channel_id=1, source_target_pairs={{0,24},{8,16},{16,8},{24,0},{1,25},{9,17},{17,9},{25,1},{2,26},{10... | collective-permute-start | bytes 1179656 | tf_op jit(solution)/shard_map/ppermute | solution.py:349
  278.1 6.7 %copy-start.13 = (f32[64,1536]{1,0:T(8,128)}, f32[64,1536]{1,0:T(8,128)S(1)}, u32[]{:S(2)}) copy-start(f32[64,1536]{1,0:T(8,128)S(1)} %collective-permute-done.28.refs_5_) | copy-start | bytes 1179652
  278.2 6.7 %copy-start.14 = (f32[64,1536]{1,0:T(8,128)}, f32[64,1536]{1,0:T(8,128)S(1)}, u32[]{:S(2)}) copy-start(f32[64,1536]{1,0:T(8,128)S(1)} %collective-permute-done.29.refs_6_) | copy-start | bytes 1179652
  278.2 6.7 %copy-start.15 = (f32[64,1536]{1,0:T(8,128)}, f32[64,1536]{1,0:T(8,128)S(1)}, u32[]{:S(2)}) copy-start(f32[64,1536]{1,0:T(8,128)S(1)} %collective-permute-done.30.refs_7_) | copy-start | bytes 1179652
  281.3 12.3 %collective-permute-start.31 = (f32[64,1536]{1,0:T(8,128)}, f32[64,1536]{1,0:T(8,128)S(1)}, u32[]{:S(2)}, u32[]{:S(2)}) collective-permute-start(f32[64,1536]{1,0:T(8,128)} %get-tuple-element.204), channel_id=1, source_target_pairs={{0,8},{8,0},{16,24},{24,16},{1,9},{9,1},{17,25},{25,17},{2,10},{10... | collective-permute-start | bytes 1179656 | tf_op jit(solution)/shard_map/ppermute | solution.py:349
  282.1 19.1 %collective-permute-start.32 = (f32[64,1536]{1,0:T(8,128)}, f32[64,1536]{1,0:T(8,128)S(1)}, u32[]{:S(2)}, u32[]{:S(2)}) collective-permute-start(f32[64,1536]{1,0:T(8,128)} %get-tuple-element.205), channel_id=1, source_target_pairs={{0,16},{8,24},{16,0},{24,8},{1,17},{9,25},{17,1},{25,9},{2,18},{10... | collective-permute-start | bytes 1179656 | tf_op jit(solution)/shard_map/ppermute | solution.py:349
  282.8 18.4 %collective-permute-start.33 = (f32[64,1536]{1,0:T(8,128)}, f32[64,1536]{1,0:T(8,128)S(1)}, u32[]{:S(2)}, u32[]{:S(2)}) collective-permute-start(f32[64,1536]{1,0:T(8,128)} %get-tuple-element.206), channel_id=1, source_target_pairs={{0,24},{8,16},{16,8},{24,0},{1,25},{9,17},{17,9},{25,1},{2,26},{10... | collective-permute-start | bytes 1179656 | tf_op jit(solution)/shard_map/ppermute | solution.py:349
  293.6 7.7 %copy-start.16 = (f32[64,1536]{1,0:T(8,128)}, f32[64,1536]{1,0:T(8,128)S(1)}, u32[]{:S(2)}) copy-start(f32[64,1536]{1,0:T(8,128)S(1)} %collective-permute-done.31.refs_5_) | copy-start | bytes 1179652
  (6 other events, 4.5 us)

commit v5 on v4

--- a/solution.py
+++ b/solution.py
@@ -172,9 +172,11 @@
     )(me, lists, share)
 
 
-def finish_kernel(groups, slots, own_count, first, me_ref, *refs):
-    lists, share, arrived = refs[:groups], refs[groups], refs[groups + 1:2 * groups]
-    _, density, held, added, sem_held, sem_added = refs[2 * groups:]
+def finish_kernel(groups, slots, own_count, me_ref, *refs):
+    lists, refs = refs[:groups], refs[groups:]
+    shares, refs = refs[:PIECES], refs[PIECES:]
+    arrived = refs[:PIECES * (groups - 1)]
+    _, density, held, added, sem_held, sem_added = refs[PIECES * (groups - 1):]
     rows = held.shape[1]
     me = me_ref[0]
     asked, places, heads = [], [], []
@@ -191,46 +193,47 @@
         slot = jnp.where(slot_holder(lists[0], me, s, own_count) == 0, s, slot)
     start = pl.multiple_of(slot * rows, rows)
     leads = [jnp.logical_and(asked[k], heads[k] == k) for k in range(groups)]
-    source = [share.at[pl.ds(start, rows)]] + list(arrived)
-    spots = [density.at[places[k], pl.ds(first, rows)] for k in range(groups)]
-    reads = [pltpu.make_async_copy(spots[k], held.at[k], sem_held.at[k]) for k in range(groups)]
-    terms = [pltpu.make_async_copy(source[k], added.at[k], sem_added.at[k]) for k in range(groups)]
-    writes = [pltpu.make_async_copy(held.at[k], spots[k], sem_held.at[k]) for k in range(groups)]
-    for k in range(groups):
-        pl.when(leads[k])(reads[k].start)
-        pl.when(asked[k])(terms[k].start)
-    for k in range(groups):
-        pl.when(leads[k])(reads[k].wait)
-    for k in range(groups):
+    every = [(p, k) for p in range(PIECES) for k in range(groups)]
+    reads, terms, writes = {}, {}, {}
+    for n, (p, k) in enumerate(every):
+        source = arrived[p * (groups - 1) + k - 1] if k else shares[p].at[pl.ds(start, rows)]
+        spot = density.at[places[k], pl.ds(p * rows, rows)]
+        reads[p, k] = pltpu.make_async_copy(spot, held.at[n], sem_held.at[n])
+        writes[p, k] = pltpu.make_async_copy(held.at[n], spot, sem_held.at[n])
+        terms[p, k] = pltpu.make_async_copy(source, added.at[n], sem_added.at[n])
+    for p, k in every:
+        pl.when(leads[k])(reads[p, k].start)
+        pl.when(asked[k])(terms[p, k].start)
+    for p, k in every:
+        pl.when(leads[k])(reads[p, k].wait)
+    for n, (p, k) in enumerate(every):
         @pl.when(asked[k])
         def _():
-            terms[k].wait()
-            held[heads[k]] = held[heads[k]] + added[k]
-    for k in range(groups):
-        pl.when(leads[k])(writes[k].start)
-    for k in range(groups):
-        pl.when(leads[k])(writes[k].wait)
-
-
-def finish(me, lists, slots, share, arrived, density, first):
+            terms[p, k].wait()
+            held[p * groups + heads[k]] = held[p * groups + heads[k]] + added[n]
+    for p, k in every:
+        pl.when(leads[k])(writes[p, k].start)
+    for p, k in every:
+        pl.when(leads[k])(writes[p, k].wait)
+
+
+def finish(me, lists, slots, shares, arrived, density):
     own_count, _, aux = density.shape
     groups = len(lists)
-    rows = share.shape[0] // slots
-    return pl.pallas_call(
-        functools.partial(finish_kernel, groups, slots, own_count, first),
-        in_specs=[SMEM] * (groups + 1) + [ANY] * (groups + 1),
+    rows = shares[0].shape[0] // slots
+    blocks = [block for piece in arrived for block in piece]
+    operands = [me, *lists, *shares, *blocks, density]
+    return pl.pallas_call(
+        functools.partial(finish_kernel, groups, slots, own_count),
+        in_specs=[SMEM] * (groups + 1) + [ANY] * (PIECES + len(blocks) + 1),
         out_specs=ANY,
         out_shape=jax.ShapeDtypeStruct(density.shape, jnp.float32),
-        input_output_aliases={2 * groups + 1: 0},
-        scratch_shapes=[
-            pltpu.VMEM((groups, rows, aux), jnp.float32),
-            pltpu.VMEM((groups, rows, aux), jnp.float32),
-            pltpu.SemaphoreType.DMA((groups,)),
-            pltpu.SemaphoreType.DMA((groups,)),
-        ],
-        cost_estimate=cost(0, 12 * rows * aux * groups),
-        compiler_params=PARAMS,
-    )(me, *lists, share, *arrived, density)
+        input_output_aliases={len(operands) - 1: 0},
+        scratch_shapes=[pltpu.VMEM((PIECES * groups, rows, aux), jnp.float32)] * 2
+        + [pltpu.SemaphoreType.DMA((PIECES * groups,))] * 2,
+        cost_estimate=cost(0, 12 * rows * aux * groups * PIECES),
+        compiler_params=PARAMS,
+    )(*operands)
 
 
 def unit_kernel(steps, own_high, own_low, sib_high, sib_low, row_ref, col_ref, *refs):
@@ -380,7 +383,7 @@
         got = [to_group(block, k + 1) for k, block in enumerate(sent)]
         if p == 1:
             halves = (own_half, split_rows(after(sib_rows, pieces[0][0])))
-        got = after(got, halves, row_energy, col_energy, pieces[-1][0]) if p else after(got, own_half, early_energies)
+        got = after(got, halves, pieces[-1][0]) if p else after(got, own_half, early_energies)
         part = choose(me_ref, packet, slots, integrals, got, p * part_width)
         pieces.append([part, hop(part)])
         if p == 1:
@@ -429,13 +432,12 @@
     early = forward(after(units[:-1], aside[1]), 0, rows, [])
     known = [(0, early)] + [(begin, sibling(x)) for (begin, _), x in zip(cuts, aside)]
     density = forward(units[-1:], 0, rows, known).reshape(own_count, width, aux)
-    product = density
+    arrived = []
     for p in range(PIECES):
-        share = after(totals[p], known, *([product] + arrived if p else []))
+        share = after(totals[p], known, *(arrived[-1] if p else []))
         sent = back(me_ref, packet, slots, own_count, share, groups)
-        arrived = [to_group(block, k + 1) for k, block in enumerate(sent)]
-        density = finish(me_ref, packets, slots, totals[p], arrived, density, p * part_width)
-    return density
+        arrived.append([to_group(block, k + 1) for k, block in enumerate(sent)])
+    return finish(me_ref, packets, slots, totals, arrived, density)
 
 
 def solution(mesh):

time: 306 us -> 298 us (0.974); the launches traced: 306 us -> 295 us
  waiting for transfers between devices: 53.8 us -> 47.3 us
  Pallas kernels: 196 us -> 191 us
    ppermute x15, waiting for transfers between devices: 14.9 us -> 9.42 us  [body(): lax.ppermute(x, 'grp', [(g, g ^ k) for g in range(groups)])]
    pallas_call x2 -> x1, Pallas kernels: 6.2 us -> 0.94 us  [finish(): pl.pallas_call(functools.partial(finish_kernel, groups, slots, own_count)...]
  transfers between devices with their start and end apart: 34 -> 34, of which waited for: 11 -> 12; matrix products, arithmetic and copies ran while one was open for 4% -> 4% of each run, Pallas kernels for 62% -> 63%
where the time goes in v5:
time: 298 us; the launch traced here: 295 us
  Pallas kernels  191 us (64%)
  waiting for transfers between devices  47.3 us (16%)
  starting transfers between devices  39.8 us (13%)
  local copies, waits for them, and re-layouts  9.43 us (3%)
  other arithmetic  7.25 us (2%)
    pallas_call x4, Pallas kernels, unit(): pl.pallas_call(functools.partial(unit_kernel, steps), grid=(2 * steps,),...  91.6 us
    pallas_call x5, Pallas kernels, forward(): pl.pallas_call(functools.partial(forward_kernel, len(units), spans), grid...  61.9 us
    ppermute x15, waiting for transfers between devices, body(): along = lambda x, s: lax.ppermute(x, 'blk', ring(s))  36.8 us
    ppermute x15, starting transfers between devices, body(): along = lambda x, s: lax.ppermute(x, 'blk', ring(s))  20.9 us
    ppermute x15, starting transfers between devices, body(): lax.ppermute(x, 'grp', [(g, g ^ k) for g in range(groups)])  18.3 us
    pallas_call x2, Pallas kernels, split_rows(): pl.pallas_call(split_kernel, grid=(rows // step,), in_specs=[spec], out_s...  17.4 us
    ppermute x15, waiting for transfers between devices, body(): lax.ppermute(x, 'grp', [(g, g ^ k) for g in range(groups)])  9.42 us
    pallas_call x2, Pallas kernels, back(): pl.pallas_call(functools.partial(back_kernel, groups, slots, own_count),...  6.92 us
  transfers between devices with their start and end apart: 34, of which 12 were waited for; matrix products, arithmetic and copies ran while one was open for 4% of the time, Pallas kernels for 63%

profile of v5, /device:TPU:0, one launch (start us, length us, event | category | flops | bytes accessed | tf_op | source)
XLA Modules:
  0.0 294.9 jit_solution(2503945612318272297)
XLA Ops:
  0.5 0.7 pad_add_fusion.1.refs_0_.lists
  1.2 2.5 collective-permute-start
  3.7 1.5 collective-permute-start.1
  5.2 2.0 collective-permute-start.8
  7.3 0.7 stack.47
  8.1 1.5 collective-permute-done.2.refs_3_
  10.2 3.3 %shard_map.57 = (f32[64,1536]{1,0:T(8,128)}, f32[64,1536]{1,0:T(8,128)}, f32[64,1536]{1,0:T(8,128)}) custom-call(s32[1]{0:T(128)} %bitcast.me_ref, s32[14]{0:T(128)} %copy-done.19, s32[14]{0:T(128)} %copy-done.20, s32[14]{0:T(128)} %copy-done.21, s32[14]{0:T(128)} %copy-done.22, f32[12,128,1536]{2,1,0:T(8,128)} %x_ref.3), custom_call_target="tpu_custom_call" | custom-call | bytes 3145728 | tf_op jit(solution)/shard_map/pallas_call | solution.py:93
  14.1 0.9 collective-permute-start.5
  14.9 2.2 collective-permute-start.6
  17.1 0.7 pad_add_fusion
  18.4 3.7 %collective-permute-start.9 = (f32[128]{0:T(128)S(1)}, f32[128]{0:T(128)S(1)}, u32[]{:S(2)}, u32[]{:S(2)}) collective-permute-start(f32[128]{0:T(128)S(1)} %copy-done.25), channel_id=1, source_target_pairs={{0,6},{1,7},{2,4},{3,5},{6,0},{7,1},{4,2},{5,3},{8,14},{9,15},{10,... | collective-permute-start | bytes 1544 | tf_op jit(solution)/shard_map/ppermute | solution.py:349
  22.2 3.1 %shard_map.55 = (f32[64,1536]{1,0:T(8,128)}, f32[64,1536]{1,0:T(8,128)}, f32[64,1536]{1,0:T(8,128)}) custom-call(s32[1]{0:T(128)} %bitcast.me_ref, s32[14]{0:T(128)} %copy-done.19, s32[14]{0:T(128)} %copy-done.20, s32[14]{0:T(128)} %copy-done.21, s32[14]{0:T(128)} %copy-done.22, f32[12,128,1536]{2,1,0:T(8,128)} %x_ref.3), custom_call_target="tpu_custom_call" | custom-call | bytes 3145728 | tf_op jit(solution)/shard_map/pallas_call | solution.py:93
  25.4 8.7 %shard_map.56 = (bf16[1536,1536]{1,0:T(8,128)(2,1)}, bf16[1536,1536]{1,0:T(8,128)(2,1)}) custom-call(f32[1536,1536]{1,0:T(8,128)} %bitcast.13), custom_call_target="tpu_custom_call" | custom-call | flops 4718592 | bytes 18874368 | tf_op jit(solution)/shard_map/pallas_call | solution.py:53
  34.4 1.0 collective-permute-done.7
  35.8 1.3 collective-permute-start.13
  37.0 2.0 collective-permute-start.14
  39.1 0.7 copy-done.9
  39.8 2.7 shard_map.58.refs_0_
  42.5 2.0 collective-permute-start.11
  44.5 0.8 unstack.34.col_ref
  46.0 0.8 unstack.33.col_ref
  46.8 0.8 unstack.32.col_ref
  47.6 0.8 unstack.35.col_ref
  48.4 8.7 %shard_map.59 = (bf16[1536,1536]{1,0:T(8,128)(2,1)}, bf16[1536,1536]{1,0:T(8,128)(2,1)}) custom-call(f32[1536,1536]{1,0:T(8,128)} %collective-permute-done.3.x_ref), custom_call_target="tpu_custom_call" | custom-call | flops 4718592 | bytes 18874368 | tf_op jit(solution)/shard_map/pallas_call | solution.py:53
  57.2 0.7 copy-done.10
  58.2 2.7 shard_map.60.refs_1_
  60.9 0.6 collective-permute-start.15
  61.6 0.9 collective-permute-done.11.refs_0_
  62.5 1.1 collective-permute-start.16
  63.6 22.8 %shard_map.61 = (bf16[256,3072]{1,0:T(8,128)(2,1)}, bf16[256,3072]{1,0:T(8,128)(2,1)}, bf16[256,1536]{1,0:T(8,128)(2,1)}, bf16[256,1536]{1,0:T(8,128)(2,1)}, f32[128,1536]{1,0:T(8,128)}, /*index=5*/f32[128,1536]{1,0:T(8,128)}) custom-call(bf16[1536,1536]{1,0:T(8,128)(2,1)} %get-tuple-element.110.own_high, bf16[1536,1536]{1,0:T(8,128)(2,1)} %get-tuple-element.111.own_low, ...), custom_call_target="tpu_custom_call" | custom-call | flops 14495514624 | bytes 25165824 | tf_op jit(solution)/shard_map/pallas_call | solution.py:284
  86.4 1.5 collective-permute-start.18
  87.9 11.5 %collective-permute-done.16.refs_0_ = f32[128,1536]{1,0:T(8,128)S(1)} collective-permute-done((f32[128,1536]{1,0:T(8,128)S(1)}, f32[128,1536]{1,0:T(8,128)S(1)}, u32[]{:S(2)}, u32[]{:S(2)}) %collective-permute-start.16) | collective-permute-done | bytes 786464 | tf_op jit(solution)/shard_map/ppermute | solution.py:349
  99.4 23.1 %shard_map.62 = (bf16[256,3072]{1,0:T(8,128)(2,1)}, bf16[256,3072]{1,0:T(8,128)(2,1)}, bf16[256,1536]{1,0:T(8,128)(2,1)}, bf16[256,1536]{1,0:T(8,128)(2,1)}, f32[128,1536]{1,0:T(8,128)}, /*index=5*/f32[128,1536]{1,0:T(8,128)}) custom-call(bf16[1536,1536]{1,0:T(8,128)(2,1)} %get-tuple-element.110.own_high, bf16[1536,1536]{1,0:T(8,128)(2,1)} %get-tuple-element.111.own_low, ...), custom_call_target="tpu_custom_call" | custom-call | flops 14495514624 | bytes 25165824 | tf_op jit(solution)/shard_map/pallas_call | solution.py:284
  122.6 2.6 collective-permute-start.20
  125.2 22.9 %shard_map.63 = (bf16[256,3072]{1,0:T(8,128)(2,1)}, bf16[256,3072]{1,0:T(8,128)(2,1)}, bf16[256,1536]{1,0:T(8,128)(2,1)}, bf16[256,1536]{1,0:T(8,128)(2,1)}, f32[128,1536]{1,0:T(8,128)}, /*index=5*/f32[128,1536]{1,0:T(8,128)}) custom-call(bf16[1536,1536]{1,0:T(8,128)(2,1)} %get-tuple-element.110.own_high, bf16[1536,1536]{1,0:T(8,128)(2,1)} %get-tuple-element.111.own_low, ...), custom_call_target="tpu_custom_call" | custom-call | flops 14495514624 | bytes 25165824 | tf_op jit(solution)/shard_map/pallas_call | solution.py:284
  148.1 0.7 collective-permute-start.23
  148.8 1.7 collective-permute-start.19
  150.5 0.9 copy-done.33
  151.4 22.8 %shard_map.64 = (bf16[256,3072]{1,0:T(8,128)(2,1)}, bf16[256,3072]{1,0:T(8,128)(2,1)}, bf16[256,1536]{1,0:T(8,128)(2,1)}, bf16[256,1536]{1,0:T(8,128)(2,1)}, f32[128,1536]{1,0:T(8,128)}, /*index=5*/f32[128,1536]{1,0:T(8,128)}) custom-call(bf16[1536,1536]{1,0:T(8,128)(2,1)} %get-tuple-element.110.own_high, bf16[1536,1536]{1,0:T(8,128)(2,1)} %get-tuple-element.111.own_low, ...), custom_call_target="tpu_custom_call" | custom-call | flops 14495514624 | bytes 25165824 | tf_op jit(solution)/shard_map/pallas_call | solution.py:284
  174.2 8.3 %collective-permute-done.19 = f32[128,1536]{1,0:T(8,128)S(1)} collective-permute-done((f32[128,1536]{1,0:T(8,128)S(1)}, f32[128,1536]{1,0:T(8,128)S(1)}, u32[]{:S(2)}, u32[]{:S(2)}) %collective-permute-start.19) | collective-permute-done | bytes 786464 | tf_op jit(solution)/shard_map/ppermute | solution.py:349
  182.8 1.0 add.29
  183.7 2.3 collective-permute-start.24
  186.0 12.5 %shard_map.65 = f32[768,1536]{1,0:T(8,128)} custom-call(bf16[256,3072]{1,0:T(8,128)(2,1)} %get-tuple-element.187.refs_0_, bf16[256,3072]{1,0:T(8,128)(2,1)} %get-tuple-element.188.refs_1_, bf16[256,1536]{1,0:T(8,128)(2,1)} %get-tuple-element.189.refs_2_, bf16[256,1536]{1,0:T(8,128)(2,1)} %get-tuple-element.190.refs_3_, ...), custom_call_target="tpu_custom_call" | custom-call | flops 7247757312 | bytes 9437184 | tf_op jit(solution)/shard_map/pallas_call | solution.py:322
  198.6 5.5 %collective-permute-done.21 = f32[128,1536]{1,0:T(8,128)S(1)} collective-permute-done((f32[128,1536]{1,0:T(8,128)S(1)}, f32[128,1536]{1,0:T(8,128)S(1)}, u32[]{:S(2)}, u32[]{:S(2)}) %collective-permute-start.21) | collective-permute-done | bytes 786464 | tf_op jit(solution)/shard_map/ppermute | solution.py:349
  204.1 10.1 %shard_map.66.refs_4_ = f32[768,1536]{1,0:T(8,128)} custom-call(bf16[256,3072]{1,0:T(8,128)(2,1)} %get-tuple-element.187.refs_0_, bf16[256,3072]{1,0:T(8,128)(2,1)} %get-tuple-element.188.refs_1_, bf16[256,1536]{1,0:T(8,128)(2,1)} %get-tuple-element.189.refs_2_, bf16[256,1536]{1,0:T(8,128)(2,1)} %get-tuple-element.190.refs_3_, ...), custom_call_target="tpu_custom_call" | custom-call | flops 5435817984 | bytes 9437184 | tf_op jit(solution)/shard_map/pallas_call | solution.py:322
  214.2 1.2 collective-permute-done.24
  215.4 7.7 %shard_map.67 = f32[768,1536]{1,0:T(8,128)} custom-call(bf16[256,3072]{1,0:T(8,128)(2,1)} %get-tuple-element.183.refs_12_.refs_0_, bf16[256,3072]{1,0:T(8,128)(2,1)} %get-tuple-element.184.refs_13_.refs_1_, bf16[256,1536]{1,0:T(8,128)(2,1)} %get-tuple-element.185.refs_14_.refs_2_, bf16[256,1536]{1,0:T(8,128)(2,1)} %get-tuple-element.186.refs_15_.refs_3_, ...), custom_call_target="tpu_custom_call" | custom-call | flops 1811939328 | bytes 9437184 | tf_op jit(solution)/shard_map/pallas_call | solution.py:322
  223.1 1.0 add.27
  224.2 2.7 collective-permute-start.25
  226.9 16.2 %shard_map.68.refs_4_ = f32[1536,1536]{1,0:T(8,128)} custom-call(bf16[256,3072]{1,0:T(8,128)(2,1)} %get-tuple-element.187.refs_0_, bf16[256,3072]{1,0:T(8,128)(2,1)} %get-tuple-element.188.refs_1_, bf16[256,1536]{1,0:T(8,128)(2,1)} %get-tuple-element.189.refs_2_, bf16[256,1536]{1,0:T(8,128)(2,1)} %get-tuple-element.190.refs_3_, ...), custom_call_target="tpu_custom_call" | custom-call | flops 10871635968 | bytes 18874368 | tf_op jit(solution)/shard_map/pallas_call | solution.py:322
  243.1 2.5 collective-permute-done.22
  245.6 2.1 add.28.share.refs_4_
  247.8 3.9 %shard_map.69 = (f32[64,1536]{1,0:T(8,128)}, f32[64,1536]{1,0:T(8,128)}, f32[64,1536]{1,0:T(8,128)}) custom-call(s32[1]{0:T(128)} %bitcast.me_ref, s32[14]{0:T(128)} %copy-done.19, f32[128,1536]{1,0:T(8,128)} %add.28.share.refs_4_), custom_call_target="tpu_custom_call" | custom-call | bytes 3145728 | tf_op jit(solution)/shard_map/pallas_call | solution.py:164
  252.6 2.6 collective-permute-start.30
  255.2 6.8 %collective-permute-done.25 = f32[128,1536]{1,0:T(8,128)S(1)} collective-permute-done((f32[128,1536]{1,0:T(8,128)S(1)}, f32[128,1536]{1,0:T(8,128)S(1)}, u32[]{:S(2)}, u32[]{:S(2)}) %collective-permute-start.25) | collective-permute-done | bytes 786464 | tf_op jit(solution)/shard_map/ppermute | solution.py:349
  262.0 1.0 add.31.share.refs_5_
  263.0 0.9 collective-permute-done.28.refs_6_
  264.0 6.8 %collective-permute-done.29.refs_7_ = f32[64,1536]{1,0:T(8,128)S(1)} collective-permute-done((f32[64,1536]{1,0:T(8,128)}, f32[64,1536]{1,0:T(8,128)S(1)}, u32[]{:S(2)}, u32[]{:S(2)}) %collective-permute-start.29) | collective-permute-done | bytes 393248 | tf_op jit(solution)/shard_map/ppermute | solution.py:352
  270.8 3.1 %shard_map.70 = (f32[64,1536]{1,0:T(8,128)}, f32[64,1536]{1,0:T(8,128)}, f32[64,1536]{1,0:T(8,128)}) custom-call(s32[1]{0:T(128)} %bitcast.me_ref, s32[14]{0:T(128)} %copy-done.19, f32[128,1536]{1,0:T(8,128)} %add.31.share.refs_5_), custom_call_target="tpu_custom_call" | custom-call | bytes 3145728 | tf_op jit(solution)/shard_map/pallas_call | solution.py:164
  273.8 1.7 collective-permute-start.31
  275.9 1.5 collective-permute-start.33
  277.4 15.3 %shard_map.71 = f32[1536,1536]{1,0:T(8,128)} custom-call(bf16[256,3072]{1,0:T(8,128)(2,1)} %get-tuple-element.183.refs_12_.refs_0_, bf16[256,3072]{1,0:T(8,128)(2,1)} %get-tuple-element.184.refs_13_.refs_1_, bf16[256,1536]{1,0:T(8,128)(2,1)} %get-tuple-element.185.refs_14_.refs_2_, bf16[256,1536]{1,0:T(8,128)(2,1)} %get-tuple-element.186.refs_15_.refs_3_, ...), custom_call_target="tpu_custom_call" | custom-call | flops 3623878656 | bytes 18874368 | tf_op jit(solution)/shard_map/pallas_call | solution.py:322
  292.9 0.6 copy-done.16
  293.8 0.9 shard_map.72
  (124 shorter events, 6.2 us)
Async XLA Ops:
  0.0 48.4 %collective-permute-start.3 = (f32[1536,1536]{1,0:T(8,128)}, f32[1536,1536]{1,0:T(8,128)}, u32[]{:S(2)}, u32[]{:S(2)}) collective-permute-start(f32[1536,1536]{1,0:T(8,128)} %bitcast.12), channel_id=1, source_target_pairs={{0,1},{1,0},{2,3},{3,2},{4,5},{5,4},{6,7},{7,6},{8,9},{9,8},{10,11... | collective-permute-start | bytes 28311560 | tf_op jit(solution)/shard_map/ppermute | solution.py:351
  1.2 8.5 %copy-start.19 = (s32[14]{0:T(128)}, s32[14]{0:T(128)S(1)}, u32[]{:S(2)}) copy-start(s32[14]{0:T(128)S(1)} %pad_add_fusion.1.refs_0_.lists) | copy-start | bytes 172
  1.2 6.9 %collective-permute-start = (s32[14]{0:T(128)S(1)}, s32[14]{0:T(128)S(1)}, u32[]{:S(2)}, u32[]{:S(2)}) collective-permute-start(s32[14]{0:T(128)S(1)} %pad_add_fusion.1.refs_0_.lists), channel_id=1, source_target_pairs={{0,8},{8,0},{16,24},{24,16},{1,9},{9,1},{17,25},{25,17},{2,10},{10... | collective-permute-start | bytes 176 | tf_op jit(solution)/shard_map/ppermute | solution.py:352
  3.7 4.4 %collective-permute-start.1 = (s32[14]{0:T(128)S(1)}, s32[14]{0:T(128)S(1)}, u32[]{:S(2)}, u32[]{:S(2)}) collective-permute-start(s32[14]{0:T(128)S(1)} %pad_add_fusion.1.refs_0_.lists), channel_id=1, source_target_pairs={{0,16},{8,24},{16,0},{24,8},{1,17},{9,25},{17,1},{25,9},{2,18},{10... | collective-permute-start | bytes 176 | tf_op jit(solution)/shard_map/ppermute | solution.py:352
  5.2 4.4 %collective-permute-start.2 = (s32[14]{0:T(128)S(1)}, s32[14]{0:T(128)S(1)}, u32[]{:S(2)}, u32[]{:S(2)}) collective-permute-start(s32[14]{0:T(128)S(1)} %pad_add_fusion.1.refs_0_.lists), channel_id=1, source_target_pairs={{0,24},{8,16},{16,8},{24,0},{1,25},{9,17},{17,9},{25,1},{2,26},{10... | collective-permute-start | bytes 176 | tf_op jit(solution)/shard_map/ppermute | solution.py:352
  5.2 13.2 %collective-permute-start.8 = (f32[128]{0:T(128)}, f32[128]{0:T(128)S(1)}, u32[]{:S(2)}, u32[]{:S(2)}) collective-permute-start(f32[128]{0:T(128)} %param.9), channel_id=1, source_target_pairs={{0,2},{1,3},{2,6},{3,7},{6,4},{7,5},{4,0},{5,1},{8,10},{9,11},{10,... | collective-permute-start | bytes 1544 | tf_op jit(solution)/shard_map/ppermute | solution.py:349
  8.1 1.6 copy-start.20
  8.1 1.6 copy-start.21
  10.2 7.8 %copy-start.23 = (f32[48]{0:T(128)S(1)}, f32[48]{0:T(128)}, u32[]{:S(2)}) copy-start(f32[48]{0:T(128)} %param.8) | copy-start | bytes 580
  10.2 8.0 %copy-start.24 = (s32[1,2]{1,0:T(1,128)S(1)}, s32[1,2]{1,0:T(1,128)}, u32[]{:S(2)}) copy-start(s32[1,2]{1,0:T(1,128)} %param.6) | copy-start | bytes 28
  10.2 8.2 %copy-start.25 = (f32[128]{0:T(128)S(1)}, f32[128]{0:T(128)}, u32[]{:S(2)}) copy-start(f32[128]{0:T(128)} %param.9) | copy-start | bytes 1540
  13.6 22.2 %collective-permute-start.4 = (f32[64,1536]{1,0:T(8,128)}, f32[64,1536]{1,0:T(8,128)S(1)}, u32[]{:S(2)}, u32[]{:S(2)}) collective-permute-start(f32[64,1536]{1,0:T(8,128)} %get-tuple-element.112), channel_id=1, source_target_pairs={{0,8},{8,0},{16,24},{24,16},{1,9},{9,1},{17,25},{25,17},{2,10},{10... | collective-permute-start | bytes 1179656 | tf_op jit(solution)/shard_map/ppermute | solution.py:352
  14.1 22.9 %collective-permute-start.5 = (f32[64,1536]{1,0:T(8,128)}, f32[64,1536]{1,0:T(8,128)S(1)}, u32[]{:S(2)}, u32[]{:S(2)}) collective-permute-start(f32[64,1536]{1,0:T(8,128)} %get-tuple-element.113), channel_id=1, source_target_pairs={{0,16},{8,24},{16,0},{24,8},{1,17},{9,25},{17,1},{25,9},{2,18},{10... | collective-permute-start | bytes 1179656 | tf_op jit(solution)/shard_map/ppermute | solution.py:352
  14.9 24.1 %collective-permute-start.6 = (f32[64,1536]{1,0:T(8,128)}, f32[64,1536]{1,0:T(8,128)S(1)}, u32[]{:S(2)}, u32[]{:S(2)}) collective-permute-start(f32[64,1536]{1,0:T(8,128)} %get-tuple-element.114), channel_id=1, source_target_pairs={{0,24},{8,16},{16,8},{24,0},{1,25},{9,17},{17,9},{25,1},{2,26},{10... | collective-permute-start | bytes 1179656 | tf_op jit(solution)/shard_map/ppermute | solution.py:352
  18.4 6.9 %collective-permute-start.9 = (f32[128]{0:T(128)S(1)}, f32[128]{0:T(128)S(1)}, u32[]{:S(2)}, u32[]{:S(2)}) collective-permute-start(f32[128]{0:T(128)S(1)} %copy-done.25), channel_id=1, source_target_pairs={{0,6},{1,7},{2,4},{3,5},{6,0},{7,1},{4,2},{5,3},{8,14},{9,15},{10,... | collective-permute-start | bytes 1544 | tf_op jit(solution)/shard_map/ppermute | solution.py:349
  25.3 10.5 %copy-start.35 = (f32[64,1536]{1,0:T(8,128)S(1)}, f32[64,1536]{1,0:T(8,128)}, u32[]{:S(2)}) copy-start(f32[64,1536]{1,0:T(8,128)} %get-tuple-element.107) | copy-start | bytes 1179652
  25.3 11.7 %copy-start.34 = (f32[64,1536]{1,0:T(8,128)S(1)}, f32[64,1536]{1,0:T(8,128)}, u32[]{:S(2)}) copy-start(f32[64,1536]{1,0:T(8,128)} %get-tuple-element.108) | copy-start | bytes 1179652
  25.3 9.0 %collective-permute-start.10 = (f32[128]{0:T(128)S(1)}, f32[128]{0:T(128)S(1)}, u32[]{:S(2)}, u32[]{:S(2)}) collective-permute-start(f32[128]{0:T(128)S(1)} %copy-done.25), channel_id=1, source_target_pairs={{0,4},{1,5},{2,0},{3,1},{6,2},{7,3},{4,6},{5,7},{8,12},{9,13},{10,... | collective-permute-start | bytes 1544 | tf_op jit(solution)/shard_map/ppermute | solution.py:349
  34.3 1.1 collective-permute-start.7
  35.4 21.7 %collective-permute-start.12 = (f32[64,1536]{1,0:T(8,128)}, f32[64,1536]{1,0:T(8,128)S(1)}, u32[]{:S(2)}, u32[]{:S(2)}) collective-permute-start(f32[64,1536]{1,0:T(8,128)} %get-tuple-element.106), channel_id=1, source_target_pairs={{0,8},{8,0},{16,24},{24,16},{1,9},{9,1},{17,25},{25,17},{2,10},{10... | collective-permute-start | bytes 1179656 | tf_op jit(solution)/shard_map/ppermute | solution.py:352
  35.8 3.3 %copy-start.7 = (f32[64,1536]{1,0:T(8,128)}, f32[64,1536]{1,0:T(8,128)S(1)}, u32[]{:S(2)}) copy-start(f32[64,1536]{1,0:T(8,128)S(1)} %collective-permute-done.4.refs_0_) | copy-start | bytes 1179652
  35.8 21.4 %collective-permute-start.13 = (f32[64,1536]{1,0:T(8,128)S(1)}, f32[64,1536]{1,0:T(8,128)S(1)}, u32[]{:S(2)}, u32[]{:S(2)}) collective-permute-start(f32[64,1536]{1,0:T(8,128)S(1)} %copy-done.35), channel_id=1, source_target_pairs={{0,16},{8,24},{16,0},{24,8},{1,17},{9,25},{17,1},{25,9},{2,18},{10... | collective-permute-start | bytes 1179656 | tf_op jit(solution)/shard_map/ppermute | solution.py:352
  37.0 2.0 copy-start.8
  37.0 20.1 %collective-permute-start.14 = (f32[64,1536]{1,0:T(8,128)S(1)}, f32[64,1536]{1,0:T(8,128)S(1)}, u32[]{:S(2)}, u32[]{:S(2)}) collective-permute-start(f32[64,1536]{1,0:T(8,128)S(1)} %copy-done.34), channel_id=1, source_target_pairs={{0,24},{8,16},{16,8},{24,0},{1,25},{9,17},{17,9},{25,1},{2,26},{10... | collective-permute-start | bytes 1179656 | tf_op jit(solution)/shard_map/ppermute | solution.py:352
  42.5 20.0 %collective-permute-start.11 = (f32[128,1536]{1,0:T(8,128)}, f32[128,1536]{1,0:T(8,128)S(1)}, u32[]{:S(2)}, u32[]{:S(2)}) collective-permute-start(f32[128,1536]{1,0:T(8,128)} %shard_map.58.refs_0_), channel_id=1, source_target_pairs={{0,2},{1,3},{2,6},{3,7},{6,4},{7,5},{4,0},{5,1},{8,10},{9,11},{10,... | collective-permute-start | bytes 2359304 | tf_op jit(solution)/shard_map/ppermute | solution.py:349
  57.1 0.9 copy-start.11
  57.1 1.0 copy-start.12
  60.9 25.5 %collective-permute-start.15 = (f32[128,1536]{1,0:T(8,128)}, f32[128,1536]{1,0:T(8,128)S(1)}, u32[]{:S(2)}, u32[]{:S(2)}) collective-permute-start(f32[128,1536]{1,0:T(8,128)} %shard_map.60.refs_1_), channel_id=1, source_target_pairs={{0,2},{1,3},{2,6},{3,7},{6,4},{7,5},{4,0},{5,1},{8,10},{9,11},{10,... | collective-permute-start | bytes 2359304 | tf_op jit(solution)/shard_map/ppermute | solution.py:349
  62.5 23.9 %copy-start.26 = (f32[128,1536]{1,0:T(8,128)}, f32[128,1536]{1,0:T(8,128)S(1)}, u32[]{:S(2)}) copy-start(f32[128,1536]{1,0:T(8,128)S(1)} %collective-permute-done.11.refs_0_) | copy-start | bytes 2359300
  62.5 36.9 %collective-permute-start.16 = (f32[128,1536]{1,0:T(8,128)S(1)}, f32[128,1536]{1,0:T(8,128)S(1)}, u32[]{:S(2)}, u32[]{:S(2)}) collective-permute-start(f32[128,1536]{1,0:T(8,128)S(1)} %collective-permute-done.11.refs_0_), channel_id=1, source_target_pairs={{0,2},{1,3},{2,6},{3,7},{6,4},{7,5},{4,0},{5,1},{8,10},{9,11},{10,... | collective-permute-start | bytes 2359304 | tf_op jit(solution)/shard_map/ppermute | solution.py:349
  86.4 13.0 %copy-start.32 = (f32[128,1536]{1,0:T(8,128)}, f32[128,1536]{1,0:T(8,128)S(1)}, u32[]{:S(2)}) copy-start(f32[128,1536]{1,0:T(8,128)S(1)} %collective-permute-done.15.refs_1_) | copy-start | bytes 2359300
  86.4 36.1 %collective-permute-start.18 = (f32[128,1536]{1,0:T(8,128)S(1)}, f32[128,1536]{1,0:T(8,128)S(1)}, u32[]{:S(2)}, u32[]{:S(2)}) collective-permute-start(f32[128,1536]{1,0:T(8,128)S(1)} %collective-permute-done.15.refs_1_), channel_id=1, source_target_pairs={{0,2},{1,3},{2,6},{3,7},{6,4},{7,5},{4,0},{5,1},{8,10},{9,11},{10,... | collective-permute-start | bytes 2359304 | tf_op jit(solution)/shard_map/ppermute | solution.py:349
  99.4 23.1 %copy-start.30 = (f32[128,1536]{1,0:T(8,128)}, f32[128,1536]{1,0:T(8,128)S(1)}, u32[]{:S(2)}) copy-start(f32[128,1536]{1,0:T(8,128)S(1)} %collective-permute-done.16.refs_0_) | copy-start | bytes 2359300
  99.4 48.6 %collective-permute-start.17 = (f32[128,1536]{1,0:T(8,128)S(1)}, f32[128,1536]{1,0:T(8,128)S(1)}, u32[]{:S(2)}, u32[]{:S(2)}) collective-permute-start(f32[128,1536]{1,0:T(8,128)S(1)} %collective-permute-done.16.refs_0_), channel_id=1, source_target_pairs={{0,2},{1,3},{2,6},{3,7},{6,4},{7,5},{4,0},{5,1},{8,10},{9,11},{10,... | collective-permute-start | bytes 2359304 | tf_op jit(solution)/shard_map/ppermute | solution.py:349
  122.5 25.5 %copy-start.27 = (f32[128,1536]{1,0:T(8,128)S(1)}, f32[128,1536]{1,0:T(8,128)}, u32[]{:S(2)}) copy-start(f32[128,1536]{1,0:T(8,128)} %get-tuple-element.138) | copy-start | bytes 2359300
  122.5 26.2 %copy-start.28 = (f32[128,1536]{1,0:T(8,128)S(1)}, f32[128,1536]{1,0:T(8,128)}, u32[]{:S(2)}) copy-start(f32[128,1536]{1,0:T(8,128)} %get-tuple-element.133) | copy-start | bytes 2359300
  122.6 2.6 copy-start.31
  122.6 27.9 %collective-permute-start.20 = (f32[128,1536]{1,0:T(8,128)S(1)}, f32[128,1536]{1,0:T(8,128)S(1)}, u32[]{:S(2)}, u32[]{:S(2)}) collective-permute-start(f32[128,1536]{1,0:T(8,128)S(1)} %collective-permute-done.18.refs_1_), channel_id=1, source_target_pairs={{0,2},{1,3},{2,6},{3,7},{6,4},{7,5},{4,0},{5,1},{8,10},{9,11},{10,... | collective-permute-start | bytes 2359304 | tf_op jit(solution)/shard_map/ppermute | solution.py:349
  148.0 2.4 copy-start.29
  148.1 34.7 %collective-permute-start.23 = (f32[128,1536]{1,0:T(8,128)S(1)}, f32[128,1536]{1,0:T(8,128)S(1)}, u32[]{:S(2)}, u32[]{:S(2)}) collective-permute-start(f32[128,1536]{1,0:T(8,128)S(1)} %copy-done.27), channel_id=1, source_target_pairs={{0,2},{1,3},{2,6},{3,7},{6,4},{7,5},{4,0},{5,1},{8,10},{9,11},{10,... | collective-permute-start | bytes 2359304 | tf_op jit(solution)/shard_map/ppermute | solution.py:349
  148.7 33.8 %copy-start.6 = (f32[128,1536]{1,0:T(8,128)S(1)}, f32[128,1536]{1,0:T(8,128)}, u32[]{:S(2)}) copy-start(f32[128,1536]{1,0:T(8,128)} %get-tuple-element.131) | copy-start | bytes 2359300
  148.8 34.0 %copy-start.5 = (f32[128,1536]{1,0:T(8,128)S(1)}, f32[128,1536]{1,0:T(8,128)}, u32[]{:S(2)}) copy-start(f32[128,1536]{1,0:T(8,128)} %get-tuple-element.132) | copy-start | bytes 2359300
  148.8 33.8 %collective-permute-start.19 = (f32[128,1536]{1,0:T(8,128)S(1)}, f32[128,1536]{1,0:T(8,128)S(1)}, u32[]{:S(2)}, u32[]{:S(2)}) collective-permute-start(f32[128,1536]{1,0:T(8,128)S(1)} %copy-done.28), channel_id=1, source_target_pairs={{0,2},{1,3},{2,6},{3,7},{6,4},{7,5},{4,0},{5,1},{8,10},{9,11},{10,... | collective-permute-start | bytes 2359304 | tf_op jit(solution)/shard_map/ppermute | solution.py:349
  150.5 0.9 copy-start.33
  182.6 21.4 %collective-permute-start.21 = (f32[128,1536]{1,0:T(8,128)S(1)}, f32[128,1536]{1,0:T(8,128)S(1)}, u32[]{:S(2)}, u32[]{:S(2)}) collective-permute-start(f32[128,1536]{1,0:T(8,128)S(1)} %add.26), channel_id=1, source_target_pairs={{0,2},{1,3},{2,6},{3,7},{6,4},{7,5},{4,0},{5,1},{8,10},{9,11},{10,... | collective-permute-start | bytes 2359304 | tf_op jit(solution)/shard_map/ppermute | solution.py:349
  183.7 31.7 %collective-permute-start.24 = (f32[128,1536]{1,0:T(8,128)}, f32[128,1536]{1,0:T(8,128)S(1)}, u32[]{:S(2)}, u32[]{:S(2)}) collective-permute-start(f32[128,1536]{1,0:T(8,128)} %add.29), channel_id=1, source_target_pairs={{0,2},{1,3},{2,6},{3,7},{6,4},{7,5},{4,0},{5,1},{8,10},{9,11},{10,... | collective-permute-start | bytes 2359304 | tf_op jit(solution)/shard_map/ppermute | solution.py:349
  198.5 49.3 %collective-permute-start.26 = (f32[768,1536]{1,0:T(8,128)}, f32[768,1536]{1,0:T(8,128)S(1)}, u32[]{:S(2)}, u32[]{:S(2)}) collective-permute-start(f32[768,1536]{1,0:T(8,128)} %shard_map.65), channel_id=1, source_target_pairs={{0,1},{1,0},{2,3},{3,2},{4,5},{5,4},{6,7},{7,6},{8,9},{9,8},{10,11... | collective-permute-start | bytes 14155784 | tf_op jit(solution)/shard_map/ppermute | solution.py:351
  214.2 8.9 %copy-start.4 = (f32[128,1536]{1,0:T(8,128)S(1)}, f32[128,1536]{1,0:T(8,128)}, u32[]{:S(2)}) copy-start(f32[128,1536]{1,0:T(8,128)} %get-tuple-element.134) | copy-start | bytes 2359300
  214.2 9.9 %copy-start.3 = (f32[128,1536]{1,0:T(8,128)S(1)}, f32[128,1536]{1,0:T(8,128)}, u32[]{:S(2)}) copy-start(f32[128,1536]{1,0:T(8,128)} %get-tuple-element.135) | copy-start | bytes 2359300
  223.1 24.7 %collective-permute-start.27 = (f32[768,1536]{1,0:T(8,128)}, f32[768,1536]{1,0:T(8,128)}, u32[]{:S(2)}, u32[]{:S(2)}) collective-permute-start(f32[768,1536]{1,0:T(8,128)} %shard_map.67), channel_id=1, source_target_pairs={{0,1},{1,0},{2,3},{3,2},{4,5},{5,4},{6,7},{7,6},{8,9},{9,8},{10,11... | collective-permute-start | bytes 14155784 | tf_op jit(solution)/shard_map/ppermute | solution.py:351
  224.1 21.6 %collective-permute-start.22 = (f32[128,1536]{1,0:T(8,128)}, f32[128,1536]{1,0:T(8,128)}, u32[]{:S(2)}, u32[]{:S(2)}) collective-permute-start(f32[128,1536]{1,0:T(8,128)} %add.27), channel_id=1, source_target_pairs={{0,2},{1,3},{2,6},{3,7},{6,4},{7,5},{4,0},{5,1},{8,10},{9,11},{10,... | collective-permute-start | bytes 2359304 | tf_op jit(solution)/shard_map/ppermute | solution.py:349
  224.2 21.5 %copy-start.2 = (f32[128,1536]{1,0:T(8,128)S(1)}, f32[128,1536]{1,0:T(8,128)}, u32[]{:S(2)}) copy-start(f32[128,1536]{1,0:T(8,128)} %get-tuple-element.126) | copy-start | bytes 2359300
  224.2 37.8 %copy-start.1 = (f32[128,1536]{1,0:T(8,128)S(1)}, f32[128,1536]{1,0:T(8,128)}, u32[]{:S(2)}) copy-start(f32[128,1536]{1,0:T(8,128)} %get-tuple-element.127) | copy-start | bytes 2359300
  224.2 37.8 %collective-permute-start.25 = (f32[128,1536]{1,0:T(8,128)S(1)}, f32[128,1536]{1,0:T(8,128)S(1)}, u32[]{:S(2)}, u32[]{:S(2)}) collective-permute-start(f32[128,1536]{1,0:T(8,128)S(1)} %add.30), channel_id=1, source_target_pairs={{0,2},{1,3},{2,6},{3,7},{6,4},{7,5},{4,0},{5,1},{8,10},{9,11},{10,... | collective-permute-start | bytes 2359304 | tf_op jit(solution)/shard_map/ppermute | solution.py:349
  247.7 29.6 %copy-start = (f32[768,1536]{1,0:T(8,128)}, f32[768,1536]{1,0:T(8,128)S(1)}, u32[]{:S(2)}) copy-start(f32[768,1536]{1,0:T(8,128)S(1)} %collective-permute-done.26.refs_5_) | copy-start | bytes 14155780
  251.6 12.3 %collective-permute-start.28 = (f32[64,1536]{1,0:T(8,128)}, f32[64,1536]{1,0:T(8,128)S(1)}, u32[]{:S(2)}, u32[]{:S(2)}) collective-permute-start(f32[64,1536]{1,0:T(8,128)} %get-tuple-element.200), channel_id=1, source_target_pairs={{0,8},{8,0},{16,24},{24,16},{1,9},{9,1},{17,25},{25,17},{2,10},{10... | collective-permute-start | bytes 1179656 | tf_op jit(solution)/shard_map/ppermute | solution.py:352
  252.0 18.7 %collective-permute-start.29 = (f32[64,1536]{1,0:T(8,128)}, f32[64,1536]{1,0:T(8,128)S(1)}, u32[]{:S(2)}, u32[]{:S(2)}) collective-permute-start(f32[64,1536]{1,0:T(8,128)} %get-tuple-element.201), channel_id=1, source_target_pairs={{0,16},{8,24},{16,0},{24,8},{1,17},{9,25},{17,1},{25,9},{2,18},{10... | collective-permute-start | bytes 1179656 | tf_op jit(solution)/shard_map/ppermute | solution.py:352
  252.6 18.2 %collective-permute-start.30 = (f32[64,1536]{1,0:T(8,128)}, f32[64,1536]{1,0:T(8,128)S(1)}, u32[]{:S(2)}, u32[]{:S(2)}) collective-permute-start(f32[64,1536]{1,0:T(8,128)} %get-tuple-element.202), channel_id=1, source_target_pairs={{0,24},{8,16},{16,8},{24,0},{1,25},{9,17},{17,9},{25,1},{2,26},{10... | collective-permute-start | bytes 1179656 | tf_op jit(solution)/shard_map/ppermute | solution.py:352
  263.9 28.8 %copy-start.13 = (f32[64,1536]{1,0:T(8,128)}, f32[64,1536]{1,0:T(8,128)S(1)}, u32[]{:S(2)}) copy-start(f32[64,1536]{1,0:T(8,128)S(1)} %collective-permute-done.28.refs_6_) | copy-start | bytes 1179652
  270.8 22.0 %copy-start.14 = (f32[64,1536]{1,0:T(8,128)}, f32[64,1536]{1,0:T(8,128)S(1)}, u32[]{:S(2)}) copy-start(f32[64,1536]{1,0:T(8,128)S(1)} %collective-permute-done.29.refs_7_) | copy-start | bytes 1179652
  270.8 22.0 %copy-start.15 = (f32[64,1536]{1,0:T(8,128)}, f32[64,1536]{1,0:T(8,128)S(1)}, u32[]{:S(2)}) copy-start(f32[64,1536]{1,0:T(8,128)S(1)} %collective-permute-done.30.refs_8_) | copy-start | bytes 1179652
  273.8 18.9 %collective-permute-start.31 = (f32[64,1536]{1,0:T(8,128)}, f32[64,1536]{1,0:T(8,128)S(1)}, u32[]{:S(2)}, u32[]{:S(2)}) collective-permute-start(f32[64,1536]{1,0:T(8,128)} %get-tuple-element.204), channel_id=1, source_target_pairs={{0,8},{8,0},{16,24},{24,16},{1,9},{9,1},{17,25},{25,17},{2,10},{10... | collective-permute-start | bytes 1179656 | tf_op jit(solution)/shard_map/ppermute | solution.py:352
  275.6 17.2 %collective-permute-start.32 = (f32[64,1536]{1,0:T(8,128)}, f32[64,1536]{1,0:T(8,128)S(1)}, u32[]{:S(2)}, u32[]{:S(2)}) collective-permute-start(f32[64,1536]{1,0:T(8,128)} %get-tuple-element.205), channel_id=1, source_target_pairs={{0,16},{8,24},{16,0},{24,8},{1,17},{9,25},{17,1},{25,9},{2,18},{10... | collective-permute-start | bytes 1179656 | tf_op jit(solution)/shard_map/ppermute | solution.py:352
  275.9 17.0 %collective-permute-start.33 = (f32[64,1536]{1,0:T(8,128)}, f32[64,1536]{1,0:T(8,128)S(1)}, u32[]{:S(2)}, u32[]{:S(2)}) collective-permute-start(f32[64,1536]{1,0:T(8,128)} %get-tuple-element.206), channel_id=1, source_target_pairs={{0,24},{8,16},{16,8},{24,0},{1,25},{9,17},{17,9},{25,1},{2,26},{10... | collective-permute-start | bytes 1179656 | tf_op jit(solution)/shard_map/ppermute | solution.py:352
  (6 other events, 4.7 us)

commit v6 on v5

--- a/solution.py
+++ b/solution.py
@@ -397,7 +397,7 @@
         if s == 1:
             parts = first
         elif s:
-            parts = [hop(x) for x in parts]
+            parts = [hop(after(x, *grads[1]) if s == 3 and p == 0 else x) for p, x in enumerate(parts)]
         ready = list(parts)
         if s == 0:
             ready[1] = after(ready[1], first[0])

time: 298 us -> 300 us (level)
  transfers between devices with their start and end apart: 34 -> 34, of which waited for: 12 -> 12; matrix products, arithmetic and copies ran while one was open for 4% -> 4% of each run, Pallas kernels for 63% -> 62%
where the time goes in v6:
time: 300 us
  Pallas kernels  193 us (64%)
  waiting for transfers between devices  48.8 us (16%)
  starting transfers between devices  39.8 us (13%)
  local copies, waits for them, and re-layouts  10.4 us (3%)
  other arithmetic  7.25 us (2%)
    pallas_call x4, Pallas kernels, unit(): pl.pallas_call(functools.partial(unit_kernel, steps), grid=(2 * steps,),...  91.3 us
    pallas_call x5, Pallas kernels, forward(): pl.pallas_call(functools.partial(forward_kernel, len(units), spans), grid...  61.9 us
    ppermute x15, waiting for transfers between devices, body(): along = lambda x, s: lax.ppermute(x, 'blk', ring(s))  38.1 us
    ppermute x15, starting transfers between devices, body(): along = lambda x, s: lax.ppermute(x, 'blk', ring(s))  20.9 us
    ppermute x15, starting transfers between devices, body(): lax.ppermute(x, 'grp', [(g, g ^ k) for g in range(groups)])  18.3 us
    pallas_call x2, Pallas kernels, split_rows(): pl.pallas_call(split_kernel, grid=(rows // step,), in_specs=[spec], out_s...  17.4 us
    ppermute x15, waiting for transfers between devices, body(): lax.ppermute(x, 'grp', [(g, g ^ k) for g in range(groups)])  9.68 us
    pallas_call x2, Pallas kernels, back(): pl.pallas_call(functools.partial(back_kernel, groups, slots, own_count),...  7.03 us
  transfers between devices with their start and end apart: 34, of which 12 were waited for; matrix products, arithmetic and copies ran while one was open for 4% of the time, Pallas kernels for 62%

profile of v6, /device:TPU:0, one launch (start us, length us, event | category | flops | bytes accessed | tf_op | source)
XLA Modules:
  0.0 299.7 jit_solution(11549831841443185000)
XLA Ops:
  0.5 0.7 pad_add_fusion.1.refs_0_.lists
  1.2 2.5 collective-permute-start
  3.7 1.5 collective-permute-start.1
  5.2 2.0 collective-permute-start.8
  8.1 1.5 collective-permute-done.2.refs_3_
  10.2 3.1 %shard_map.57 = (f32[64,1536]{1,0:T(8,128)}, f32[64,1536]{1,0:T(8,128)}, f32[64,1536]{1,0:T(8,128)}) custom-call(s32[1]{0:T(128)} %bitcast.me_ref, s32[14]{0:T(128)} %copy-done.19, s32[14]{0:T(128)} %copy-done.20, s32[14]{0:T(128)} %copy-done.21, s32[14]{0:T(128)} %copy-done.22, f32[12,128,1536]{2,1,0:T(8,128)} %x_ref.3), custom_call_target="tpu_custom_call" | custom-call | bytes 3145728 | tf_op jit(solution)/shard_map/pallas_call | solution.py:93
  14.0 0.9 collective-permute-start.5
  14.9 2.0 collective-permute-start.6
  18.2 3.7 %collective-permute-start.9 = (f32[128]{0:T(128)S(1)}, f32[128]{0:T(128)S(1)}, u32[]{:S(2)}, u32[]{:S(2)}) collective-permute-start(f32[128]{0:T(128)S(1)} %copy-done.25), channel_id=1, source_target_pairs={{0,6},{1,7},{2,4},{3,5},{6,0},{7,1},{4,2},{5,3},{8,14},{9,15},{10,... | collective-permute-start | bytes 1544 | tf_op jit(solution)/shard_map/ppermute | solution.py:349
  22.0 3.0 shard_map.55
  25.1 8.7 %shard_map.56 = (bf16[1536,1536]{1,0:T(8,128)(2,1)}, bf16[1536,1536]{1,0:T(8,128)(2,1)}) custom-call(f32[1536,1536]{1,0:T(8,128)} %bitcast.13), custom_call_target="tpu_custom_call" | custom-call | flops 4718592 | bytes 18874368 | tf_op jit(solution)/shard_map/pallas_call | solution.py:53
  34.1 1.0 collective-permute-done.7
  35.7 1.3 collective-permute-start.13
  37.0 1.7 collective-permute-start.14
  38.8 0.7 copy-done.9
  39.5 2.6 shard_map.58.refs_0_
  42.1 2.0 collective-permute-start.11
  44.1 0.8 unstack.34.col_ref
  45.6 0.8 unstack.33.col_ref
  46.4 0.8 unstack.32.col_ref
  47.2 0.8 unstack.35.col_ref
  48.0 8.7 %shard_map.59 = (bf16[1536,1536]{1,0:T(8,128)(2,1)}, bf16[1536,1536]{1,0:T(8,128)(2,1)}) custom-call(f32[1536,1536]{1,0:T(8,128)} %collective-permute-done.3.x_ref), custom_call_target="tpu_custom_call" | custom-call | flops 4718592 | bytes 18874368 | tf_op jit(solution)/shard_map/pallas_call | solution.py:53
  57.8 2.6 shard_map.60.refs_1_
  60.4 0.7 collective-permute-start.15
  61.1 0.9 collective-permute-done.11.refs_0_
  62.1 1.1 collective-permute-start.16
  63.1 22.8 %shard_map.61 = (bf16[256,3072]{1,0:T(8,128)(2,1)}, bf16[256,3072]{1,0:T(8,128)(2,1)}, bf16[256,1536]{1,0:T(8,128)(2,1)}, bf16[256,1536]{1,0:T(8,128)(2,1)}, f32[128,1536]{1,0:T(8,128)}, /*index=5*/f32[128,1536]{1,0:T(8,128)}) custom-call(bf16[1536,1536]{1,0:T(8,128)(2,1)} %get-tuple-element.111.own_high, bf16[1536,1536]{1,0:T(8,128)(2,1)} %get-tuple-element.112.own_low, ...), custom_call_target="tpu_custom_call" | custom-call | flops 14495514624 | bytes 25165824 | tf_op jit(solution)/shard_map/pallas_call | solution.py:284
  86.0 1.6 collective-permute-start.18
  87.6 22.8 %shard_map.62 = (bf16[256,3072]{1,0:T(8,128)(2,1)}, bf16[256,3072]{1,0:T(8,128)(2,1)}, bf16[256,1536]{1,0:T(8,128)(2,1)}, bf16[256,1536]{1,0:T(8,128)(2,1)}, f32[128,1536]{1,0:T(8,128)}, /*index=5*/f32[128,1536]{1,0:T(8,128)}) custom-call(bf16[1536,1536]{1,0:T(8,128)(2,1)} %get-tuple-element.111.own_high, bf16[1536,1536]{1,0:T(8,128)(2,1)} %get-tuple-element.112.own_low, ...), custom_call_target="tpu_custom_call" | custom-call | flops 14495514624 | bytes 25165824 | tf_op jit(solution)/shard_map/pallas_call | solution.py:284
  110.5 1.5 collective-permute-start.17
  112.0 3.6 %collective-permute-done.18.refs_1_ = f32[128,1536]{1,0:T(8,128)S(1)} collective-permute-done((f32[128,1536]{1,0:T(8,128)S(1)}, f32[128,1536]{1,0:T(8,128)S(1)}, u32[]{:S(2)}, u32[]{:S(2)}) %collective-permute-start.18) | collective-permute-done | bytes 786464 | tf_op jit(solution)/shard_map/ppermute | solution.py:349
  115.6 0.9 copy-done.31
  116.5 22.9 %shard_map.63 = (bf16[256,3072]{1,0:T(8,128)(2,1)}, bf16[256,3072]{1,0:T(8,128)(2,1)}, bf16[256,1536]{1,0:T(8,128)(2,1)}, bf16[256,1536]{1,0:T(8,128)(2,1)}, f32[128,1536]{1,0:T(8,128)}, /*index=5*/f32[128,1536]{1,0:T(8,128)}) custom-call(bf16[1536,1536]{1,0:T(8,128)(2,1)} %get-tuple-element.111.own_high, bf16[1536,1536]{1,0:T(8,128)(2,1)} %get-tuple-element.112.own_low, ...), custom_call_target="tpu_custom_call" | custom-call | flops 14495514624 | bytes 25165824 | tf_op jit(solution)/shard_map/pallas_call | solution.py:284
  139.4 2.0 collective-permute-start.23
  141.4 0.9 collective-permute-start.19
  142.3 7.0 %collective-permute-done.20.refs_1_ = f32[128,1536]{1,0:T(8,128)S(1)} collective-permute-done((f32[128,1536]{1,0:T(8,128)S(1)}, f32[128,1536]{1,0:T(8,128)S(1)}, u32[]{:S(2)}, u32[]{:S(2)}) %collective-permute-start.20) | collective-permute-done | bytes 786464 | tf_op jit(solution)/shard_map/ppermute | solution.py:349
  149.3 0.9 copy-done.33
  150.2 22.8 %shard_map.64 = (bf16[256,3072]{1,0:T(8,128)(2,1)}, bf16[256,3072]{1,0:T(8,128)(2,1)}, bf16[256,1536]{1,0:T(8,128)(2,1)}, bf16[256,1536]{1,0:T(8,128)(2,1)}, f32[128,1536]{1,0:T(8,128)}, /*index=5*/f32[128,1536]{1,0:T(8,128)}) custom-call(bf16[1536,1536]{1,0:T(8,128)(2,1)} %get-tuple-element.111.own_high, bf16[1536,1536]{1,0:T(8,128)(2,1)} %get-tuple-element.112.own_low, ...), custom_call_target="tpu_custom_call" | custom-call | flops 14495514624 | bytes 25165824 | tf_op jit(solution)/shard_map/pallas_call | solution.py:284
  173.1 8.1 %collective-permute-done.19 = f32[128,1536]{1,0:T(8,128)S(1)} collective-permute-done((f32[128,1536]{1,0:T(8,128)S(1)}, f32[128,1536]{1,0:T(8,128)S(1)}, u32[]{:S(2)}, u32[]{:S(2)}) %collective-permute-start.19) | collective-permute-done | bytes 786464 | tf_op jit(solution)/shard_map/ppermute | solution.py:349
  181.4 1.0 add.29
  182.3 2.7 collective-permute-start.24
  185.0 12.5 %shard_map.65 = f32[768,1536]{1,0:T(8,128)} custom-call(bf16[256,3072]{1,0:T(8,128)(2,1)} %get-tuple-element.189.refs_0_, bf16[256,3072]{1,0:T(8,128)(2,1)} %get-tuple-element.190.refs_1_, bf16[256,1536]{1,0:T(8,128)(2,1)} %get-tuple-element.191.refs_2_, bf16[256,1536]{1,0:T(8,128)(2,1)} %get-tuple-element.192.refs_3_, ...), custom_call_target="tpu_custom_call" | custom-call | flops 7247757312 | bytes 9437184 | tf_op jit(solution)/shard_map/pallas_call | solution.py:322
  197.6 5.1 %collective-permute-done.21 = f32[128,1536]{1,0:T(8,128)S(1)} collective-permute-done((f32[128,1536]{1,0:T(8,128)S(1)}, f32[128,1536]{1,0:T(8,128)S(1)}, u32[]{:S(2)}, u32[]{:S(2)}) %collective-permute-start.21) | collective-permute-done | bytes 786464 | tf_op jit(solution)/shard_map/ppermute | solution.py:349
  202.7 10.1 %shard_map.66.refs_4_ = f32[768,1536]{1,0:T(8,128)} custom-call(bf16[256,3072]{1,0:T(8,128)(2,1)} %get-tuple-element.189.refs_0_, bf16[256,3072]{1,0:T(8,128)(2,1)} %get-tuple-element.190.refs_1_, bf16[256,1536]{1,0:T(8,128)(2,1)} %get-tuple-element.191.refs_2_, bf16[256,1536]{1,0:T(8,128)(2,1)} %get-tuple-element.192.refs_3_, ...), custom_call_target="tpu_custom_call" | custom-call | flops 5435817984 | bytes 9437184 | tf_op jit(solution)/shard_map/pallas_call | solution.py:322
  212.9 3.9 %collective-permute-done.24 = f32[128,1536]{1,0:T(8,128)S(1)} collective-permute-done((f32[128,1536]{1,0:T(8,128)}, f32[128,1536]{1,0:T(8,128)S(1)}, u32[]{:S(2)}, u32[]{:S(2)}) %collective-permute-start.24) | collective-permute-done | bytes 786464 | tf_op jit(solution)/shard_map/ppermute | solution.py:349
  216.8 7.7 %shard_map.67 = f32[768,1536]{1,0:T(8,128)} custom-call(bf16[256,3072]{1,0:T(8,128)(2,1)} %get-tuple-element.185.refs_12_.refs_0_, bf16[256,3072]{1,0:T(8,128)(2,1)} %get-tuple-element.186.refs_13_.refs_1_, bf16[256,1536]{1,0:T(8,128)(2,1)} %get-tuple-element.187.refs_14_.refs_2_, bf16[256,1536]{1,0:T(8,128)(2,1)} %get-tuple-element.188.refs_15_.refs_3_, ...), custom_call_target="tpu_custom_call" | custom-call | flops 1811939328 | bytes 9437184 | tf_op jit(solution)/shard_map/pallas_call | solution.py:322
  224.5 1.0 add.27
  225.6 2.6 collective-permute-start.25
  228.2 16.2 %shard_map.68.refs_4_ = f32[1536,1536]{1,0:T(8,128)} custom-call(bf16[256,3072]{1,0:T(8,128)(2,1)} %get-tuple-element.189.refs_0_, bf16[256,3072]{1,0:T(8,128)(2,1)} %get-tuple-element.190.refs_1_, bf16[256,1536]{1,0:T(8,128)(2,1)} %get-tuple-element.191.refs_2_, bf16[256,1536]{1,0:T(8,128)(2,1)} %get-tuple-element.192.refs_3_, ...), custom_call_target="tpu_custom_call" | custom-call | flops 10871635968 | bytes 18874368 | tf_op jit(solution)/shard_map/pallas_call | solution.py:322
  244.4 2.6 collective-permute-done.22
  247.0 2.1 add.28.share.refs_4_
  249.1 3.9 %shard_map.69 = (f32[64,1536]{1,0:T(8,128)}, f32[64,1536]{1,0:T(8,128)}, f32[64,1536]{1,0:T(8,128)}) custom-call(s32[1]{0:T(128)} %bitcast.me_ref, s32[14]{0:T(128)} %copy-done.19, f32[128,1536]{1,0:T(8,128)} %add.28.share.refs_4_), custom_call_target="tpu_custom_call" | custom-call | bytes 3145728 | tf_op jit(solution)/shard_map/pallas_call | solution.py:164
  253.0 0.8 collective-permute-start.28
  254.1 2.4 collective-permute-start.30
  256.6 6.8 %collective-permute-done.25 = f32[128,1536]{1,0:T(8,128)S(1)} collective-permute-done((f32[128,1536]{1,0:T(8,128)S(1)}, f32[128,1536]{1,0:T(8,128)S(1)}, u32[]{:S(2)}, u32[]{:S(2)}) %collective-permute-start.25) | collective-permute-done | bytes 786464 | tf_op jit(solution)/shard_map/ppermute | solution.py:349
  263.4 1.0 add.31.share.refs_5_
  264.4 0.9 collective-permute-done.28.refs_6_
  265.3 7.2 %collective-permute-done.29.refs_7_ = f32[64,1536]{1,0:T(8,128)S(1)} collective-permute-done((f32[64,1536]{1,0:T(8,128)}, f32[64,1536]{1,0:T(8,128)S(1)}, u32[]{:S(2)}, u32[]{:S(2)}) %collective-permute-start.29) | collective-permute-done | bytes 393248 | tf_op jit(solution)/shard_map/ppermute | solution.py:352
  272.5 3.2 %shard_map.70 = (f32[64,1536]{1,0:T(8,128)}, f32[64,1536]{1,0:T(8,128)}, f32[64,1536]{1,0:T(8,128)}) custom-call(s32[1]{0:T(128)} %bitcast.me_ref, s32[14]{0:T(128)} %copy-done.19, f32[128,1536]{1,0:T(8,128)} %add.31.share.refs_5_), custom_call_target="tpu_custom_call" | custom-call | bytes 3145728 | tf_op jit(solution)/shard_map/pallas_call | solution.py:164
  275.7 1.3 collective-permute-start.31
  277.0 0.8 collective-permute-start.32
  277.7 1.5 collective-permute-start.33
  279.2 15.3 %shard_map.71 = f32[1536,1536]{1,0:T(8,128)} custom-call(bf16[256,3072]{1,0:T(8,128)(2,1)} %get-tuple-element.185.refs_12_.refs_0_, bf16[256,3072]{1,0:T(8,128)(2,1)} %get-tuple-element.186.refs_13_.refs_1_, bf16[256,1536]{1,0:T(8,128)(2,1)} %get-tuple-element.187.refs_14_.refs_2_, bf16[256,1536]{1,0:T(8,128)(2,1)} %get-tuple-element.188.refs_15_.refs_3_, ...), custom_call_target="tpu_custom_call" | custom-call | flops 3623878656 | bytes 18874368 | tf_op jit(solution)/shard_map/pallas_call | solution.py:322
  295.6 3.9 %shard_map.72 = f32[12,128,1536]{2,1,0:T(8,128)} custom-call(s32[1]{0:T(128)} %bitcast.me_ref, s32[14]{0:T(128)} %copy-done.19, s32[14]{0:T(128)} %copy-done.20, s32[14]{0:T(128)} %copy-done.21, s32[14]{0:T(128)} %copy-done.22, f32[128,1536]{1,0:T(8,128)} %add.28.share.refs_4_, f32[128,1536]{1,0:T(8,128)} %add.31.share.refs_5_, ...), custom_call_target="tpu_custom_call", output_to_operand_aliasing={{}: (13, {})} | custom-call | bytes 9437184 | tf_op jit(solution)/shard_map/pallas_call | solution.py:226
  (124 shorter events, 8.3 us)
Async XLA Ops:
  0.0 48.0 %collective-permute-start.3 = (f32[1536,1536]{1,0:T(8,128)}, f32[1536,1536]{1,0:T(8,128)}, u32[]{:S(2)}, u32[]{:S(2)}) collective-permute-start(f32[1536,1536]{1,0:T(8,128)} %bitcast.12), channel_id=1, source_target_pairs={{0,1},{1,0},{2,3},{3,2},{4,5},{5,4},{6,7},{7,6},{8,9},{9,8},{10,11... | collective-permute-start | bytes 28311560 | tf_op jit(solution)/shard_map/ppermute | solution.py:351
  1.2 8.5 %copy-start.19 = (s32[14]{0:T(128)}, s32[14]{0:T(128)S(1)}, u32[]{:S(2)}) copy-start(s32[14]{0:T(128)S(1)} %pad_add_fusion.1.refs_0_.lists) | copy-start | bytes 172
  1.2 6.9 %collective-permute-start = (s32[14]{0:T(128)S(1)}, s32[14]{0:T(128)S(1)}, u32[]{:S(2)}, u32[]{:S(2)}) collective-permute-start(s32[14]{0:T(128)S(1)} %pad_add_fusion.1.refs_0_.lists), channel_id=1, source_target_pairs={{0,8},{8,0},{16,24},{24,16},{1,9},{9,1},{17,25},{25,17},{2,10},{10... | collective-permute-start | bytes 176 | tf_op jit(solution)/shard_map/ppermute | solution.py:352
  3.7 4.4 %collective-permute-start.1 = (s32[14]{0:T(128)S(1)}, s32[14]{0:T(128)S(1)}, u32[]{:S(2)}, u32[]{:S(2)}) collective-permute-start(s32[14]{0:T(128)S(1)} %pad_add_fusion.1.refs_0_.lists), channel_id=1, source_target_pairs={{0,16},{8,24},{16,0},{24,8},{1,17},{9,25},{17,1},{25,9},{2,18},{10... | collective-permute-start | bytes 176 | tf_op jit(solution)/shard_map/ppermute | solution.py:352
  5.2 4.4 %collective-permute-start.2 = (s32[14]{0:T(128)S(1)}, s32[14]{0:T(128)S(1)}, u32[]{:S(2)}, u32[]{:S(2)}) collective-permute-start(s32[14]{0:T(128)S(1)} %pad_add_fusion.1.refs_0_.lists), channel_id=1, source_target_pairs={{0,24},{8,16},{16,8},{24,0},{1,25},{9,17},{17,9},{25,1},{2,26},{10... | collective-permute-start | bytes 176 | tf_op jit(solution)/shard_map/ppermute | solution.py:352
  5.2 13.0 %collective-permute-start.8 = (f32[128]{0:T(128)}, f32[128]{0:T(128)S(1)}, u32[]{:S(2)}, u32[]{:S(2)}) collective-permute-start(f32[128]{0:T(128)} %param.9), channel_id=1, source_target_pairs={{0,2},{1,3},{2,6},{3,7},{6,4},{7,5},{4,0},{5,1},{8,10},{9,11},{10,... | collective-permute-start | bytes 1544 | tf_op jit(solution)/shard_map/ppermute | solution.py:349
  8.1 1.6 copy-start.20
  8.1 1.6 copy-start.21
  10.2 7.6 %copy-start.23 = (f32[48]{0:T(128)S(1)}, f32[48]{0:T(128)}, u32[]{:S(2)}) copy-start(f32[48]{0:T(128)} %param.8) | copy-start | bytes 580
  10.2 7.8 %copy-start.24 = (s32[1,2]{1,0:T(1,128)S(1)}, s32[1,2]{1,0:T(1,128)}, u32[]{:S(2)}) copy-start(s32[1,2]{1,0:T(1,128)} %param.6) | copy-start | bytes 28
  10.2 8.0 %copy-start.25 = (f32[128]{0:T(128)S(1)}, f32[128]{0:T(128)}, u32[]{:S(2)}) copy-start(f32[128]{0:T(128)} %param.9) | copy-start | bytes 1540
  13.4 22.3 %collective-permute-start.4 = (f32[64,1536]{1,0:T(8,128)}, f32[64,1536]{1,0:T(8,128)S(1)}, u32[]{:S(2)}, u32[]{:S(2)}) collective-permute-start(f32[64,1536]{1,0:T(8,128)} %get-tuple-element.113), channel_id=1, source_target_pairs={{0,8},{8,0},{16,24},{24,16},{1,9},{9,1},{17,25},{25,17},{2,10},{10... | collective-permute-start | bytes 1179656 | tf_op jit(solution)/shard_map/ppermute | solution.py:352
  14.0 23.0 %collective-permute-start.5 = (f32[64,1536]{1,0:T(8,128)}, f32[64,1536]{1,0:T(8,128)S(1)}, u32[]{:S(2)}, u32[]{:S(2)}) collective-permute-start(f32[64,1536]{1,0:T(8,128)} %get-tuple-element.114), channel_id=1, source_target_pairs={{0,16},{8,24},{16,0},{24,8},{1,17},{9,25},{17,1},{25,9},{2,18},{10... | collective-permute-start | bytes 1179656 | tf_op jit(solution)/shard_map/ppermute | solution.py:352
  14.9 23.8 %collective-permute-start.6 = (f32[64,1536]{1,0:T(8,128)}, f32[64,1536]{1,0:T(8,128)S(1)}, u32[]{:S(2)}, u32[]{:S(2)}) collective-permute-start(f32[64,1536]{1,0:T(8,128)} %get-tuple-element.115), channel_id=1, source_target_pairs={{0,24},{8,16},{16,8},{24,0},{1,25},{9,17},{17,9},{25,1},{2,26},{10... | collective-permute-start | bytes 1179656 | tf_op jit(solution)/shard_map/ppermute | solution.py:352
  18.2 6.8 %collective-permute-start.9 = (f32[128]{0:T(128)S(1)}, f32[128]{0:T(128)S(1)}, u32[]{:S(2)}, u32[]{:S(2)}) collective-permute-start(f32[128]{0:T(128)S(1)} %copy-done.25), channel_id=1, source_target_pairs={{0,6},{1,7},{2,4},{3,5},{6,0},{7,1},{4,2},{5,3},{8,14},{9,15},{10,... | collective-permute-start | bytes 1544 | tf_op jit(solution)/shard_map/ppermute | solution.py:349
  25.0 10.7 %copy-start.35 = (f32[64,1536]{1,0:T(8,128)S(1)}, f32[64,1536]{1,0:T(8,128)}, u32[]{:S(2)}) copy-start(f32[64,1536]{1,0:T(8,128)} %get-tuple-element.108) | copy-start | bytes 1179652
  25.0 12.0 %copy-start.34 = (f32[64,1536]{1,0:T(8,128)S(1)}, f32[64,1536]{1,0:T(8,128)}, u32[]{:S(2)}) copy-start(f32[64,1536]{1,0:T(8,128)} %get-tuple-element.109) | copy-start | bytes 1179652
  25.0 9.0 %collective-permute-start.10 = (f32[128]{0:T(128)S(1)}, f32[128]{0:T(128)S(1)}, u32[]{:S(2)}, u32[]{:S(2)}) collective-permute-start(f32[128]{0:T(128)S(1)} %copy-done.25), channel_id=1, source_target_pairs={{0,4},{1,5},{2,0},{3,1},{6,2},{7,3},{4,6},{5,7},{8,12},{9,13},{10,... | collective-permute-start | bytes 1544 | tf_op jit(solution)/shard_map/ppermute | solution.py:349
  34.0 1.1 collective-permute-start.7
  35.1 21.6 %collective-permute-start.12 = (f32[64,1536]{1,0:T(8,128)}, f32[64,1536]{1,0:T(8,128)S(1)}, u32[]{:S(2)}, u32[]{:S(2)}) collective-permute-start(f32[64,1536]{1,0:T(8,128)} %get-tuple-element.107), channel_id=1, source_target_pairs={{0,8},{8,0},{16,24},{24,16},{1,9},{9,1},{17,25},{25,17},{2,10},{10... | collective-permute-start | bytes 1179656 | tf_op jit(solution)/shard_map/ppermute | solution.py:352
  35.7 3.1 %copy-start.7 = (f32[64,1536]{1,0:T(8,128)}, f32[64,1536]{1,0:T(8,128)S(1)}, u32[]{:S(2)}) copy-start(f32[64,1536]{1,0:T(8,128)S(1)} %collective-permute-done.4.refs_0_) | copy-start | bytes 1179652
  35.7 21.0 %collective-permute-start.13 = (f32[64,1536]{1,0:T(8,128)S(1)}, f32[64,1536]{1,0:T(8,128)S(1)}, u32[]{:S(2)}, u32[]{:S(2)}) collective-permute-start(f32[64,1536]{1,0:T(8,128)S(1)} %copy-done.35), channel_id=1, source_target_pairs={{0,16},{8,24},{16,0},{24,8},{1,17},{9,25},{17,1},{25,9},{2,18},{10... | collective-permute-start | bytes 1179656 | tf_op jit(solution)/shard_map/ppermute | solution.py:352
  37.0 1.8 copy-start.8
  37.0 19.7 %collective-permute-start.14 = (f32[64,1536]{1,0:T(8,128)S(1)}, f32[64,1536]{1,0:T(8,128)S(1)}, u32[]{:S(2)}, u32[]{:S(2)}) collective-permute-start(f32[64,1536]{1,0:T(8,128)S(1)} %copy-done.34), channel_id=1, source_target_pairs={{0,24},{8,16},{16,8},{24,0},{1,25},{9,17},{17,9},{25,1},{2,26},{10... | collective-permute-start | bytes 1179656 | tf_op jit(solution)/shard_map/ppermute | solution.py:352
  42.1 20.0 %collective-permute-start.11 = (f32[128,1536]{1,0:T(8,128)}, f32[128,1536]{1,0:T(8,128)S(1)}, u32[]{:S(2)}, u32[]{:S(2)}) collective-permute-start(f32[128,1536]{1,0:T(8,128)} %shard_map.58.refs_0_), channel_id=1, source_target_pairs={{0,2},{1,3},{2,6},{3,7},{6,4},{7,5},{4,0},{5,1},{8,10},{9,11},{10,... | collective-permute-start | bytes 2359304 | tf_op jit(solution)/shard_map/ppermute | solution.py:349
  56.7 0.9 copy-start.11
  56.7 1.0 copy-start.12
  60.4 25.6 %collective-permute-start.15 = (f32[128,1536]{1,0:T(8,128)}, f32[128,1536]{1,0:T(8,128)S(1)}, u32[]{:S(2)}, u32[]{:S(2)}) collective-permute-start(f32[128,1536]{1,0:T(8,128)} %shard_map.60.refs_1_), channel_id=1, source_target_pairs={{0,2},{1,3},{2,6},{3,7},{6,4},{7,5},{4,0},{5,1},{8,10},{9,11},{10,... | collective-permute-start | bytes 2359304 | tf_op jit(solution)/shard_map/ppermute | solution.py:349
  62.1 23.9 %copy-start.26 = (f32[128,1536]{1,0:T(8,128)}, f32[128,1536]{1,0:T(8,128)S(1)}, u32[]{:S(2)}) copy-start(f32[128,1536]{1,0:T(8,128)S(1)} %collective-permute-done.11.refs_0_) | copy-start | bytes 2359300
  62.1 48.4 %collective-permute-start.16 = (f32[128,1536]{1,0:T(8,128)S(1)}, f32[128,1536]{1,0:T(8,128)S(1)}, u32[]{:S(2)}, u32[]{:S(2)}) collective-permute-start(f32[128,1536]{1,0:T(8,128)S(1)} %collective-permute-done.11.refs_0_), channel_id=1, source_target_pairs={{0,2},{1,3},{2,6},{3,7},{6,4},{7,5},{4,0},{5,1},{8,10},{9,11},{10,... | collective-permute-start | bytes 2359304 | tf_op jit(solution)/shard_map/ppermute | solution.py:349
  86.0 1.6 copy-start.32
  86.0 29.6 %collective-permute-start.18 = (f32[128,1536]{1,0:T(8,128)S(1)}, f32[128,1536]{1,0:T(8,128)S(1)}, u32[]{:S(2)}, u32[]{:S(2)}) collective-permute-start(f32[128,1536]{1,0:T(8,128)S(1)} %collective-permute-done.15.refs_1_), channel_id=1, source_target_pairs={{0,2},{1,3},{2,6},{3,7},{6,4},{7,5},{4,0},{5,1},{8,10},{9,11},{10,... | collective-permute-start | bytes 2359304 | tf_op jit(solution)/shard_map/ppermute | solution.py:349
  110.4 5.2 %copy-start.29 = (f32[128,1536]{1,0:T(8,128)}, f32[128,1536]{1,0:T(8,128)S(1)}, u32[]{:S(2)}) copy-start(f32[128,1536]{1,0:T(8,128)S(1)} %collective-permute-done.16.refs_0_) | copy-start | bytes 2359300
  110.4 28.9 %copy-start.27 = (f32[128,1536]{1,0:T(8,128)S(1)}, f32[128,1536]{1,0:T(8,128)}, u32[]{:S(2)}) copy-start(f32[128,1536]{1,0:T(8,128)} %get-tuple-element.140) | copy-start | bytes 2359300
  110.4 31.0 %copy-start.28 = (f32[128,1536]{1,0:T(8,128)S(1)}, f32[128,1536]{1,0:T(8,128)}, u32[]{:S(2)}) copy-start(f32[128,1536]{1,0:T(8,128)} %get-tuple-element.136) | copy-start | bytes 2359300
  110.5 28.9 %collective-permute-start.17 = (f32[128,1536]{1,0:T(8,128)S(1)}, f32[128,1536]{1,0:T(8,128)S(1)}, u32[]{:S(2)}, u32[]{:S(2)}) collective-permute-start(f32[128,1536]{1,0:T(8,128)S(1)} %collective-permute-done.16.refs_0_), channel_id=1, source_target_pairs={{0,2},{1,3},{2,6},{3,7},{6,4},{7,5},{4,0},{5,1},{8,10},{9,11},{10,... | collective-permute-start | bytes 2359304 | tf_op jit(solution)/shard_map/ppermute | solution.py:349
  115.6 33.7 %collective-permute-start.20 = (f32[128,1536]{1,0:T(8,128)S(1)}, f32[128,1536]{1,0:T(8,128)S(1)}, u32[]{:S(2)}, u32[]{:S(2)}) collective-permute-start(f32[128,1536]{1,0:T(8,128)S(1)} %collective-permute-done.18.refs_1_), channel_id=1, source_target_pairs={{0,2},{1,3},{2,6},{3,7},{6,4},{7,5},{4,0},{5,1},{8,10},{9,11},{10,... | collective-permute-start | bytes 2359304 | tf_op jit(solution)/shard_map/ppermute | solution.py:349
  139.4 9.9 %copy-start.30 = (f32[128,1536]{1,0:T(8,128)}, f32[128,1536]{1,0:T(8,128)S(1)}, u32[]{:S(2)}) copy-start(f32[128,1536]{1,0:T(8,128)S(1)} %collective-permute-done.17.refs_0_) | copy-start | bytes 2359300
  139.4 41.8 %copy-start.6 = (f32[128,1536]{1,0:T(8,128)S(1)}, f32[128,1536]{1,0:T(8,128)}, u32[]{:S(2)}) copy-start(f32[128,1536]{1,0:T(8,128)} %get-tuple-element.134) | copy-start | bytes 2359300
  139.4 42.0 %copy-start.5 = (f32[128,1536]{1,0:T(8,128)S(1)}, f32[128,1536]{1,0:T(8,128)}, u32[]{:S(2)}) copy-start(f32[128,1536]{1,0:T(8,128)} %get-tuple-element.135) | copy-start | bytes 2359300
  139.4 41.9 %collective-permute-start.23 = (f32[128,1536]{1,0:T(8,128)S(1)}, f32[128,1536]{1,0:T(8,128)S(1)}, u32[]{:S(2)}, u32[]{:S(2)}) collective-permute-start(f32[128,1536]{1,0:T(8,128)S(1)} %copy-done.27), channel_id=1, source_target_pairs={{0,2},{1,3},{2,6},{3,7},{6,4},{7,5},{4,0},{5,1},{8,10},{9,11},{10,... | collective-permute-start | bytes 2359304 | tf_op jit(solution)/shard_map/ppermute | solution.py:349
  141.4 39.8 %collective-permute-start.19 = (f32[128,1536]{1,0:T(8,128)S(1)}, f32[128,1536]{1,0:T(8,128)S(1)}, u32[]{:S(2)}, u32[]{:S(2)}) collective-permute-start(f32[128,1536]{1,0:T(8,128)S(1)} %copy-done.28), channel_id=1, source_target_pairs={{0,2},{1,3},{2,6},{3,7},{6,4},{7,5},{4,0},{5,1},{8,10},{9,11},{10,... | collective-permute-start | bytes 2359304 | tf_op jit(solution)/shard_map/ppermute | solution.py:349
  149.3 0.9 copy-start.33
  181.3 21.4 %collective-permute-start.21 = (f32[128,1536]{1,0:T(8,128)S(1)}, f32[128,1536]{1,0:T(8,128)S(1)}, u32[]{:S(2)}, u32[]{:S(2)}) collective-permute-start(f32[128,1536]{1,0:T(8,128)S(1)} %add.26), channel_id=1, source_target_pairs={{0,2},{1,3},{2,6},{3,7},{6,4},{7,5},{4,0},{5,1},{8,10},{9,11},{10,... | collective-permute-start | bytes 2359304 | tf_op jit(solution)/shard_map/ppermute | solution.py:349
  182.3 34.5 %collective-permute-start.24 = (f32[128,1536]{1,0:T(8,128)}, f32[128,1536]{1,0:T(8,128)S(1)}, u32[]{:S(2)}, u32[]{:S(2)}) collective-permute-start(f32[128,1536]{1,0:T(8,128)} %add.29), channel_id=1, source_target_pairs={{0,2},{1,3},{2,6},{3,7},{6,4},{7,5},{4,0},{5,1},{8,10},{9,11},{10,... | collective-permute-start | bytes 2359304 | tf_op jit(solution)/shard_map/ppermute | solution.py:349
  197.5 51.6 %collective-permute-start.26 = (f32[768,1536]{1,0:T(8,128)}, f32[768,1536]{1,0:T(8,128)S(1)}, u32[]{:S(2)}, u32[]{:S(2)}) collective-permute-start(f32[768,1536]{1,0:T(8,128)} %shard_map.65), channel_id=1, source_target_pairs={{0,1},{1,0},{2,3},{3,2},{4,5},{5,4},{6,7},{7,6},{8,9},{9,8},{10,11... | collective-permute-start | bytes 14155784 | tf_op jit(solution)/shard_map/ppermute | solution.py:351
  212.9 11.6 %copy-start.4 = (f32[128,1536]{1,0:T(8,128)S(1)}, f32[128,1536]{1,0:T(8,128)}, u32[]{:S(2)}) copy-start(f32[128,1536]{1,0:T(8,128)} %get-tuple-element.137) | copy-start | bytes 2359300
  212.9 12.6 %copy-start.3 = (f32[128,1536]{1,0:T(8,128)S(1)}, f32[128,1536]{1,0:T(8,128)}, u32[]{:S(2)}) copy-start(f32[128,1536]{1,0:T(8,128)} %get-tuple-element.138) | copy-start | bytes 2359300
  224.5 24.7 %collective-permute-start.27 = (f32[768,1536]{1,0:T(8,128)}, f32[768,1536]{1,0:T(8,128)}, u32[]{:S(2)}, u32[]{:S(2)}) collective-permute-start(f32[768,1536]{1,0:T(8,128)} %shard_map.67), channel_id=1, source_target_pairs={{0,1},{1,0},{2,3},{3,2},{4,5},{5,4},{6,7},{7,6},{8,9},{9,8},{10,11... | collective-permute-start | bytes 14155784 | tf_op jit(solution)/shard_map/ppermute | solution.py:351
  225.5 21.6 %collective-permute-start.22 = (f32[128,1536]{1,0:T(8,128)}, f32[128,1536]{1,0:T(8,128)}, u32[]{:S(2)}, u32[]{:S(2)}) collective-permute-start(f32[128,1536]{1,0:T(8,128)} %add.27), channel_id=1, source_target_pairs={{0,2},{1,3},{2,6},{3,7},{6,4},{7,5},{4,0},{5,1},{8,10},{9,11},{10,... | collective-permute-start | bytes 2359304 | tf_op jit(solution)/shard_map/ppermute | solution.py:349
  225.6 21.5 %copy-start.2 = (f32[128,1536]{1,0:T(8,128)S(1)}, f32[128,1536]{1,0:T(8,128)}, u32[]{:S(2)}) copy-start(f32[128,1536]{1,0:T(8,128)} %get-tuple-element.127) | copy-start | bytes 2359300
  225.6 37.8 %copy-start.1 = (f32[128,1536]{1,0:T(8,128)S(1)}, f32[128,1536]{1,0:T(8,128)}, u32[]{:S(2)}) copy-start(f32[128,1536]{1,0:T(8,128)} %get-tuple-element.128) | copy-start | bytes 2359300
  225.6 37.8 %collective-permute-start.25 = (f32[128,1536]{1,0:T(8,128)S(1)}, f32[128,1536]{1,0:T(8,128)S(1)}, u32[]{:S(2)}, u32[]{:S(2)}) collective-permute-start(f32[128,1536]{1,0:T(8,128)S(1)} %add.30), channel_id=1, source_target_pairs={{0,2},{1,3},{2,6},{3,7},{6,4},{7,5},{4,0},{5,1},{8,10},{9,11},{10,... | collective-permute-start | bytes 2359304 | tf_op jit(solution)/shard_map/ppermute | solution.py:349
  249.1 30.1 %copy-start = (f32[768,1536]{1,0:T(8,128)}, f32[768,1536]{1,0:T(8,128)S(1)}, u32[]{:S(2)}) copy-start(f32[768,1536]{1,0:T(8,128)S(1)} %collective-permute-done.26.refs_5_) | copy-start | bytes 14155780
  253.0 12.3 %collective-permute-start.28 = (f32[64,1536]{1,0:T(8,128)}, f32[64,1536]{1,0:T(8,128)S(1)}, u32[]{:S(2)}, u32[]{:S(2)}) collective-permute-start(f32[64,1536]{1,0:T(8,128)} %get-tuple-element.202), channel_id=1, source_target_pairs={{0,8},{8,0},{16,24},{24,16},{1,9},{9,1},{17,25},{25,17},{2,10},{10... | collective-permute-start | bytes 1179656 | tf_op jit(solution)/shard_map/ppermute | solution.py:352
  253.8 18.7 %collective-permute-start.29 = (f32[64,1536]{1,0:T(8,128)}, f32[64,1536]{1,0:T(8,128)S(1)}, u32[]{:S(2)}, u32[]{:S(2)}) collective-permute-start(f32[64,1536]{1,0:T(8,128)} %get-tuple-element.203), channel_id=1, source_target_pairs={{0,16},{8,24},{16,0},{24,8},{1,17},{9,25},{17,1},{25,9},{2,18},{10... | collective-permute-start | bytes 1179656 | tf_op jit(solution)/shard_map/ppermute | solution.py:352
  254.1 18.4 %collective-permute-start.30 = (f32[64,1536]{1,0:T(8,128)}, f32[64,1536]{1,0:T(8,128)S(1)}, u32[]{:S(2)}, u32[]{:S(2)}) collective-permute-start(f32[64,1536]{1,0:T(8,128)} %get-tuple-element.204), channel_id=1, source_target_pairs={{0,24},{8,16},{16,8},{24,0},{1,25},{9,17},{17,9},{25,1},{2,26},{10... | collective-permute-start | bytes 1179656 | tf_op jit(solution)/shard_map/ppermute | solution.py:352
  265.3 29.2 %copy-start.13 = (f32[64,1536]{1,0:T(8,128)}, f32[64,1536]{1,0:T(8,128)S(1)}, u32[]{:S(2)}) copy-start(f32[64,1536]{1,0:T(8,128)S(1)} %collective-permute-done.28.refs_6_) | copy-start | bytes 1179652
  272.5 22.1 %copy-start.14 = (f32[64,1536]{1,0:T(8,128)}, f32[64,1536]{1,0:T(8,128)S(1)}, u32[]{:S(2)}) copy-start(f32[64,1536]{1,0:T(8,128)S(1)} %collective-permute-done.29.refs_7_) | copy-start | bytes 1179652
  272.5 22.1 %copy-start.15 = (f32[64,1536]{1,0:T(8,128)}, f32[64,1536]{1,0:T(8,128)S(1)}, u32[]{:S(2)}) copy-start(f32[64,1536]{1,0:T(8,128)S(1)} %collective-permute-done.30.refs_8_) | copy-start | bytes 1179652
  275.7 18.9 %collective-permute-start.31 = (f32[64,1536]{1,0:T(8,128)}, f32[64,1536]{1,0:T(8,128)S(1)}, u32[]{:S(2)}, u32[]{:S(2)}) collective-permute-start(f32[64,1536]{1,0:T(8,128)} %get-tuple-element.206), channel_id=1, source_target_pairs={{0,8},{8,0},{16,24},{24,16},{1,9},{9,1},{17,25},{25,17},{2,10},{10... | collective-permute-start | bytes 1179656 | tf_op jit(solution)/shard_map/ppermute | solution.py:352
  277.0 17.7 %collective-permute-start.32 = (f32[64,1536]{1,0:T(8,128)}, f32[64,1536]{1,0:T(8,128)S(1)}, u32[]{:S(2)}, u32[]{:S(2)}) collective-permute-start(f32[64,1536]{1,0:T(8,128)} %get-tuple-element.207), channel_id=1, source_target_pairs={{0,16},{8,24},{16,0},{24,8},{1,17},{9,25},{17,1},{25,9},{2,18},{10... | collective-permute-start | bytes 1179656 | tf_op jit(solution)/shard_map/ppermute | solution.py:352
  277.7 16.9 %collective-permute-start.33 = (f32[64,1536]{1,0:T(8,128)}, f32[64,1536]{1,0:T(8,128)S(1)}, u32[]{:S(2)}, u32[]{:S(2)}) collective-permute-start(f32[64,1536]{1,0:T(8,128)} %get-tuple-element.208), channel_id=1, source_target_pairs={{0,24},{8,16},{16,8},{24,0},{1,25},{9,17},{17,9},{25,1},{2,26},{10... | collective-permute-start | bytes 1179656 | tf_op jit(solution)/shard_map/ppermute | solution.py:352
  294.6 1.0 copy-start.18
  (6 other events, 4.6 us)

commit v7 on v5

--- a/solution.py
+++ b/solution.py
@@ -1,4 +1,5 @@
 import functools
+import math
 
 import jax
 import jax.numpy as jnp
@@ -295,24 +296,32 @@
     return outs[:4], outs[4:]
 
 
-def forward_kernel(count, spans, *refs):
+def forward_term(refs):
+    t_high, t_low, r_high, r_low = (ref[...] for ref in refs)
+    return dot(t_high, r_high, (0, 0)) + dot(t_high, r_low, (0, 0)) + dot(t_low, r_high, (0, 0))
+
+
+def forward_kernel(count, spans, partial, *refs):
     out = refs[-1]
     total = None
-    for u in range(count):
-        t_high, t_low, r_high, r_low = (ref[...] for ref in refs[4 * u:4 * u + 4])
-        term = dot(t_high, r_high, (0, 0)) + dot(t_high, r_low, (0, 0)) + dot(t_low, r_high, (0, 0))
+    for u in range(count - partial):
+        term = forward_term(refs[4 * u:4 * u + 4])
         total = term if total is None else total + term
     out[...] = total
     step = pl.program_id(0)
+    if partial:
+        @pl.when(step < pl.num_programs(0) - 1)
+        def _():
+            out[...] += forward_term(refs[4 * (count - 1):4 * count])
     for (begin, end), start in zip(spans, refs[4 * count:-1]):
         @pl.when(jnp.logical_and(step >= begin, step < end))
         def _():
             out[...] += start[...]
 
 
-def forward(units, first, count, starts):
+def forward(units, first, count, starts, partial=False):
     cols, aux = units[0][2].shape
-    step = block_rows(count, 256)
+    step = block_rows(math.gcd(count, *(begin for begin, _ in starts), *(rows.shape[0] for _, rows in starts)), 256)
     steps = count // step
     spans = [(begin // step, (begin + rows.shape[0]) // step) for begin, rows in starts]
     t_spec = pl.BlockSpec((cols, step), lambda i: (0, i + first // step))
@@ -320,7 +329,7 @@
     out_spec = pl.BlockSpec((step, aux), lambda i: (i, 0))
     start_spec = lambda begin, end: pl.BlockSpec((step, aux), lambda i: (jnp.clip(i, begin, end - 1) - begin, 0))
     return pl.pallas_call(
-        functools.partial(forward_kernel, len(units), spans),
+        functools.partial(forward_kernel, len(units), spans, partial),
         grid=(steps,),
         in_specs=[t_spec, t_spec, r_spec, r_spec] * len(units) + [start_spec(*span) for span in spans],
         out_specs=out_spec,
@@ -328,6 +337,30 @@
         cost_estimate=cost(6 * count * aux * cols * len(units), 8 * count * aux),
         compiler_params=PARAMS,
     )(*(x for one in units for x in one), *(rows for _, rows in starts))
+
+
+def complete_kernel(t_high, t_low, r_high, r_low, known, out):
+    out[...] = known[...] + forward_term((t_high, t_low, r_high, r_low))
+
+
+def complete(unit_parts, first, known):
+    cols, aux = unit_parts[2].shape
+    count = known.shape[0]
+    step = block_rows(count, 256)
+    last = count // step - 1
+    t_spec = pl.BlockSpec((cols, step), lambda i: (0, first // step + last))
+    r_spec = pl.BlockSpec((cols, aux), lambda i: (0, 0))
+    block = pl.BlockSpec((step, aux), lambda i: (last, 0))
+    return pl.pallas_call(
+        complete_kernel,
+        grid=(1,),
+        in_specs=[t_spec, t_spec, r_spec, r_spec, block],
+        out_specs=block,
+        out_shape=jax.ShapeDtypeStruct(known.shape, jnp.float32),
+        input_output_aliases={4: 0},
+        cost_estimate=cost(6 * count * aux * cols, 8 * count * aux),
+        compiler_params=PARAMS,
+    )(*unit_parts, known)
 
 
 def ring_order(chips):
@@ -423,9 +456,8 @@
         if s == 2:
             aside.append(forward(after(units, *done), rows, last, []))
         if s == chips - 1:
-            most = forward(after(units[:-1], done[0], aside[0]), rows + last, rows - last, [])
-            ready = after(units, most, *done)
-            aside.append(forward(ready[-1:], rows + last, rows - last, [(0, most)]))
+            most = forward(after(units, done[0], aside[0]), rows + last, rows - last, [], partial=True)
+            aside.append(complete(after(units[-1], most, *done), rows + last, most))
         if s < chips:
             totals = [hop(x) for x in totals]
 

time: 298 us -> 295 us (0.990); the launches traced: 295 us -> 295 us
  transfers between devices with their start and end apart: 34 -> 34, of which waited for: 12 -> 10; matrix products, arithmetic and copies ran while one was open for 4% -> 4% of each run, Pallas kernels for 63% -> 63%
where the time goes in v7:
time: 295 us
  Pallas kernels  192 us (65%)
  waiting for transfers between devices  46.8 us (16%)
  starting transfers between devices  39.5 us (13%)
  local copies, waits for them, and re-layouts  9.52 us (3%)
  other arithmetic  7.27 us (2%)
    pallas_call x4, Pallas kernels, unit(): pl.pallas_call(functools.partial(unit_kernel, steps), grid=(2 * steps,),...  91.6 us
    pallas_call x4, Pallas kernels, forward(): pl.pallas_call(functools.partial(forward_kernel, len(units), spans, parti...  56.4 us
    ppermute x15, waiting for transfers between devices, body(): along = lambda x, s: lax.ppermute(x, 'blk', ring(s))  36 us
    ppermute x15, starting transfers between devices, body(): along = lambda x, s: lax.ppermute(x, 'blk', ring(s))  20.6 us
    ppermute x15, starting transfers between devices, body(): lax.ppermute(x, 'grp', [(g, g ^ k) for g in range(groups)])  18.3 us
    pallas_call x2, Pallas kernels, split_rows(): pl.pallas_call(split_kernel, grid=(rows // step,), in_specs=[spec], out_s...  17.4 us
    ppermute x15, waiting for transfers between devices, body(): lax.ppermute(x, 'grp', [(g, g ^ k) for g in range(groups)])  9.75 us
    pallas_call x2, Pallas kernels, back(): pl.pallas_call(functools.partial(back_kernel, groups, slots, own_count),...  7.03 us
  transfers between devices with their start and end apart: 34, of which 10 were waited for; matrix products, arithmetic and copies ran while one was open for 4% of the time, Pallas kernels for 63%

profile of v7, /device:TPU:0, one launch (start us, length us, event | category | flops | bytes accessed | tf_op | source)
XLA Modules:
  0.0 295.3 jit_solution(4111955070569587163)
XLA Ops:
  0.5 0.7 pad_add_fusion.1.refs_0_.lists
  1.2 2.5 collective-permute-start
  3.7 1.5 collective-permute-start.1
  5.2 2.0 collective-permute-start.8
  7.3 0.7 stack.47
  8.1 1.5 collective-permute-done.2.refs_3_
  10.2 3.1 %shard_map.57 = (f32[64,1536]{1,0:T(8,128)}, f32[64,1536]{1,0:T(8,128)}, f32[64,1536]{1,0:T(8,128)}) custom-call(s32[1]{0:T(128)} %bitcast.me_ref, s32[14]{0:T(128)} %copy-done.19, s32[14]{0:T(128)} %copy-done.20, s32[14]{0:T(128)} %copy-done.21, s32[14]{0:T(128)} %copy-done.22, f32[12,128,1536]{2,1,0:T(8,128)} %x_ref.3), custom_call_target="tpu_custom_call" | custom-call | bytes 3145728 | tf_op jit(solution)/shard_map/pallas_call | solution.py:94
  14.0 1.1 collective-permute-start.5
  15.1 1.8 collective-permute-start.6
  16.9 0.7 pad_add_fusion
  18.2 3.7 %collective-permute-start.9 = (f32[128]{0:T(128)S(1)}, f32[128]{0:T(128)S(1)}, u32[]{:S(2)}, u32[]{:S(2)}) collective-permute-start(f32[128]{0:T(128)S(1)} %copy-done.25), channel_id=1, source_target_pairs={{0,6},{1,7},{2,4},{3,5},{6,0},{7,1},{4,2},{5,3},{8,14},{9,15},{10,... | collective-permute-start | bytes 1544 | tf_op jit(solution)/shard_map/ppermute | solution.py:382
  22.0 3.0 %shard_map.55 = (f32[64,1536]{1,0:T(8,128)}, f32[64,1536]{1,0:T(8,128)}, f32[64,1536]{1,0:T(8,128)}) custom-call(s32[1]{0:T(128)} %bitcast.me_ref, s32[14]{0:T(128)} %copy-done.19, s32[14]{0:T(128)} %copy-done.20, s32[14]{0:T(128)} %copy-done.21, s32[14]{0:T(128)} %copy-done.22, f32[12,128,1536]{2,1,0:T(8,128)} %x_ref.3), custom_call_target="tpu_custom_call" | custom-call | bytes 3145728 | tf_op jit(solution)/shard_map/pallas_call | solution.py:94
  25.1 8.7 %shard_map.56 = (bf16[1536,1536]{1,0:T(8,128)(2,1)}, bf16[1536,1536]{1,0:T(8,128)(2,1)}) custom-call(f32[1536,1536]{1,0:T(8,128)} %bitcast.13), custom_call_target="tpu_custom_call" | custom-call | flops 4718592 | bytes 18874368 | tf_op jit(solution)/shard_map/pallas_call | solution.py:54
  34.1 1.0 collective-permute-done.7
  35.7 1.6 collective-permute-start.13
  37.3 1.4 collective-permute-start.14
  38.8 0.7 copy-done.9
  39.5 2.6 shard_map.58.refs_0_
  42.1 2.0 collective-permute-start.11
  44.1 0.8 unstack.34.col_ref
  45.6 0.8 unstack.33.col_ref
  46.4 0.8 unstack.32.col_ref
  47.2 0.8 unstack.35.col_ref
  48.0 8.7 %shard_map.59 = (bf16[1536,1536]{1,0:T(8,128)(2,1)}, bf16[1536,1536]{1,0:T(8,128)(2,1)}) custom-call(f32[1536,1536]{1,0:T(8,128)} %collective-permute-done.3.x_ref), custom_call_target="tpu_custom_call" | custom-call | flops 4718592 | bytes 18874368 | tf_op jit(solution)/shard_map/pallas_call | solution.py:54
  56.7 0.7 copy-done.10
  57.8 2.6 shard_map.60.refs_1_
  60.4 0.7 collective-permute-start.15
  61.1 0.9 collective-permute-done.11.refs_0_
  62.1 1.1 collective-permute-start.16
  63.1 22.8 %shard_map.61 = (bf16[256,3072]{1,0:T(8,128)(2,1)}, bf16[256,3072]{1,0:T(8,128)(2,1)}, bf16[256,1536]{1,0:T(8,128)(2,1)}, bf16[256,1536]{1,0:T(8,128)(2,1)}, f32[128,1536]{1,0:T(8,128)}, /*index=5*/f32[128,1536]{1,0:T(8,128)}) custom-call(bf16[1536,1536]{1,0:T(8,128)(2,1)} %get-tuple-element.114.own_high, bf16[1536,1536]{1,0:T(8,128)(2,1)} %get-tuple-element.115.own_low, ...), custom_call_target="tpu_custom_call" | custom-call | flops 14495514624 | bytes 25165824 | tf_op jit(solution)/shard_map/pallas_call | solution.py:285
  86.0 1.6 collective-permute-start.18
  87.6 11.3 %collective-permute-done.16.refs_0_ = f32[128,1536]{1,0:T(8,128)S(1)} collective-permute-done((f32[128,1536]{1,0:T(8,128)S(1)}, f32[128,1536]{1,0:T(8,128)S(1)}, u32[]{:S(2)}, u32[]{:S(2)}) %collective-permute-start.16) | collective-permute-done | bytes 786464 | tf_op jit(solution)/shard_map/ppermute | solution.py:382
  98.9 23.1 %shard_map.62 = (bf16[256,3072]{1,0:T(8,128)(2,1)}, bf16[256,3072]{1,0:T(8,128)(2,1)}, bf16[256,1536]{1,0:T(8,128)(2,1)}, bf16[256,1536]{1,0:T(8,128)(2,1)}, f32[128,1536]{1,0:T(8,128)}, /*index=5*/f32[128,1536]{1,0:T(8,128)}) custom-call(bf16[1536,1536]{1,0:T(8,128)(2,1)} %get-tuple-element.114.own_high, bf16[1536,1536]{1,0:T(8,128)(2,1)} %get-tuple-element.115.own_low, ...), custom_call_target="tpu_custom_call" | custom-call | flops 14495514624 | bytes 25165824 | tf_op jit(solution)/shard_map/pallas_call | solution.py:285
  122.0 2.7 collective-permute-start.20
  124.7 22.9 %shard_map.63 = (bf16[256,3072]{1,0:T(8,128)(2,1)}, bf16[256,3072]{1,0:T(8,128)(2,1)}, bf16[256,1536]{1,0:T(8,128)(2,1)}, bf16[256,1536]{1,0:T(8,128)(2,1)}, f32[128,1536]{1,0:T(8,128)}, /*index=5*/f32[128,1536]{1,0:T(8,128)}) custom-call(bf16[1536,1536]{1,0:T(8,128)(2,1)} %get-tuple-element.114.own_high, bf16[1536,1536]{1,0:T(8,128)(2,1)} %get-tuple-element.115.own_low, ...), custom_call_target="tpu_custom_call" | custom-call | flops 14495514624 | bytes 25165824 | tf_op jit(solution)/shard_map/pallas_call | solution.py:285
  148.3 1.6 collective-permute-start.19
  149.9 0.9 copy-done.33
  150.8 22.8 %shard_map.64 = (bf16[256,3072]{1,0:T(8,128)(2,1)}, bf16[256,3072]{1,0:T(8,128)(2,1)}, bf16[256,1536]{1,0:T(8,128)(2,1)}, bf16[256,1536]{1,0:T(8,128)(2,1)}, f32[128,1536]{1,0:T(8,128)}, /*index=5*/f32[128,1536]{1,0:T(8,128)}) custom-call(bf16[1536,1536]{1,0:T(8,128)(2,1)} %get-tuple-element.114.own_high, bf16[1536,1536]{1,0:T(8,128)(2,1)} %get-tuple-element.115.own_low, ...), custom_call_target="tpu_custom_call" | custom-call | flops 14495514624 | bytes 25165824 | tf_op jit(solution)/shard_map/pallas_call | solution.py:285
  173.7 8.4 %collective-permute-done.19 = f32[128,1536]{1,0:T(8,128)S(1)} collective-permute-done((f32[128,1536]{1,0:T(8,128)S(1)}, f32[128,1536]{1,0:T(8,128)S(1)}, u32[]{:S(2)}, u32[]{:S(2)}) %collective-permute-start.19) | collective-permute-done | bytes 786464 | tf_op jit(solution)/shard_map/ppermute | solution.py:382
  182.6 1.0 add.29
  183.6 1.9 collective-permute-start.24
  185.5 12.5 %shard_map.65 = f32[768,1536]{1,0:T(8,128)} custom-call(bf16[256,3072]{1,0:T(8,128)(2,1)} %get-tuple-element.195.refs_0_, bf16[256,3072]{1,0:T(8,128)(2,1)} %get-tuple-element.196.refs_1_, bf16[256,1536]{1,0:T(8,128)(2,1)} %get-tuple-element.197.refs_2_, bf16[256,1536]{1,0:T(8,128)(2,1)} %get-tuple-element.198.refs_3_, ...), custom_call_target="tpu_custom_call" | custom-call | flops 7247757312 | bytes 9437184 | tf_op jit(solution)/shard_map/pallas_call | solution.py:331
  198.0 5.6 %collective-permute-done.21 = f32[128,1536]{1,0:T(8,128)S(1)} collective-permute-done((f32[128,1536]{1,0:T(8,128)S(1)}, f32[128,1536]{1,0:T(8,128)S(1)}, u32[]{:S(2)}, u32[]{:S(2)}) %collective-permute-start.21) | collective-permute-done | bytes 786464 | tf_op jit(solution)/shard_map/ppermute | solution.py:382
  203.6 12.3 %shard_map.66.known = f32[768,1536]{1,0:T(8,128)} custom-call(bf16[256,3072]{1,0:T(8,128)(2,1)} %get-tuple-element.195.refs_0_, bf16[256,3072]{1,0:T(8,128)(2,1)} %get-tuple-element.196.refs_1_, bf16[256,1536]{1,0:T(8,128)(2,1)} %get-tuple-element.197.refs_2_, bf16[256,1536]{1,0:T(8,128)(2,1)} %get-tuple-element.198.refs_3_, ...), custom_call_target="tpu_custom_call" | custom-call | flops 7247757312 | bytes 9437184 | tf_op jit(solution)/shard_map/pallas_call | solution.py:331
  216.0 4.1 %shard_map.67 = f32[768,1536]{1,0:T(8,128)} custom-call(bf16[256,3072]{1,0:T(8,128)(2,1)} %get-tuple-element.191.refs_12_.t_high.refs_0_, bf16[256,3072]{1,0:T(8,128)(2,1)} %get-tuple-element.192.refs_13_.t_low.refs_1_, bf16[256,1536]{1,0:T(8,128)(2,1)} %get-tuple-element.193.refs_14_.r_high.refs_2_, ...), custom_call_target="tpu_custom_call", output_to_operand_aliasing={{}: (4, {})} | custom-call | flops 1811939328 | bytes 9437184 | tf_op jit(solution)/shard_map/pallas_call | solution.py:354
  220.0 1.0 add.27
  221.1 2.3 collective-permute-start.25
  223.4 16.2 %shard_map.68.refs_4_ = f32[1536,1536]{1,0:T(8,128)} custom-call(bf16[256,3072]{1,0:T(8,128)(2,1)} %get-tuple-element.195.refs_0_, bf16[256,3072]{1,0:T(8,128)(2,1)} %get-tuple-element.196.refs_1_, bf16[256,1536]{1,0:T(8,128)(2,1)} %get-tuple-element.197.refs_2_, bf16[256,1536]{1,0:T(8,128)(2,1)} %get-tuple-element.198.refs_3_, ...), custom_call_target="tpu_custom_call" | custom-call | flops 10871635968 | bytes 18874368 | tf_op jit(solution)/shard_map/pallas_call | solution.py:331
  239.6 2.9 collective-permute-done.22
  242.6 2.1 add.28.share.refs_4_
  244.7 3.9 %shard_map.69 = (f32[64,1536]{1,0:T(8,128)}, f32[64,1536]{1,0:T(8,128)}, f32[64,1536]{1,0:T(8,128)}) custom-call(s32[1]{0:T(128)} %bitcast.me_ref, s32[14]{0:T(128)} %copy-done.19, f32[128,1536]{1,0:T(8,128)} %add.28.share.refs_4_), custom_call_target="tpu_custom_call" | custom-call | bytes 3145728 | tf_op jit(solution)/shard_map/pallas_call | solution.py:165
  248.5 0.9 collective-permute-start.28
  249.4 0.7 collective-permute-start.29
  250.1 2.0 collective-permute-start.30
  252.1 6.8 %collective-permute-done.25 = f32[128,1536]{1,0:T(8,128)S(1)} collective-permute-done((f32[128,1536]{1,0:T(8,128)S(1)}, f32[128,1536]{1,0:T(8,128)S(1)}, u32[]{:S(2)}, u32[]{:S(2)}) %collective-permute-start.25) | collective-permute-done | bytes 786464 | tf_op jit(solution)/shard_map/ppermute | solution.py:382
  258.9 1.0 add.31.share.refs_5_
  259.9 0.9 collective-permute-done.28.refs_6_
  260.9 7.2 %collective-permute-done.29.refs_7_ = f32[64,1536]{1,0:T(8,128)S(1)} collective-permute-done((f32[64,1536]{1,0:T(8,128)}, f32[64,1536]{1,0:T(8,128)S(1)}, u32[]{:S(2)}, u32[]{:S(2)}) %collective-permute-start.29) | collective-permute-done | bytes 393248 | tf_op jit(solution)/shard_map/ppermute | solution.py:385
  268.1 3.2 %shard_map.70 = (f32[64,1536]{1,0:T(8,128)}, f32[64,1536]{1,0:T(8,128)}, f32[64,1536]{1,0:T(8,128)}) custom-call(s32[1]{0:T(128)} %bitcast.me_ref, s32[14]{0:T(128)} %copy-done.19, f32[128,1536]{1,0:T(8,128)} %add.31.share.refs_5_), custom_call_target="tpu_custom_call" | custom-call | bytes 3145728 | tf_op jit(solution)/shard_map/pallas_call | solution.py:165
  271.3 1.2 collective-permute-start.31
  273.0 1.9 collective-permute-start.33
  274.9 15.3 %shard_map.71 = f32[1536,1536]{1,0:T(8,128)} custom-call(bf16[256,3072]{1,0:T(8,128)(2,1)} %get-tuple-element.191.refs_12_.t_high.refs_0_, bf16[256,3072]{1,0:T(8,128)(2,1)} %get-tuple-element.192.refs_13_.t_low.refs_1_, bf16[256,1536]{1,0:T(8,128)(2,1)} %get-tuple-element.193.refs_14_.r_high.refs_2_, ...), custom_call_target="tpu_custom_call" | custom-call | flops 3623878656 | bytes 18874368 | tf_op jit(solution)/shard_map/pallas_call | solution.py:331
  290.3 0.7 copy-done.16
  291.2 3.9 %shard_map.72 = f32[12,128,1536]{2,1,0:T(8,128)} custom-call(s32[1]{0:T(128)} %bitcast.me_ref, s32[14]{0:T(128)} %copy-done.19, s32[14]{0:T(128)} %copy-done.20, s32[14]{0:T(128)} %copy-done.21, s32[14]{0:T(128)} %copy-done.22, f32[128,1536]{1,0:T(8,128)} %add.28.share.refs_4_, f32[128,1536]{1,0:T(8,128)} %add.31.share.refs_5_, ...), custom_call_target="tpu_custom_call", output_to_operand_aliasing={{}: (13, {})} | custom-call | bytes 9437184 | tf_op jit(solution)/shard_map/pallas_call | solution.py:227
  (124 shorter events, 6.6 us)
Async XLA Ops:
  0.0 48.0 %collective-permute-start.3 = (f32[1536,1536]{1,0:T(8,128)}, f32[1536,1536]{1,0:T(8,128)}, u32[]{:S(2)}, u32[]{:S(2)}) collective-permute-start(f32[1536,1536]{1,0:T(8,128)} %bitcast.12), channel_id=1, source_target_pairs={{0,1},{1,0},{2,3},{3,2},{4,5},{5,4},{6,7},{7,6},{8,9},{9,8},{10,11... | collective-permute-start | bytes 28311560 | tf_op jit(solution)/shard_map/ppermute | solution.py:384
  1.2 8.5 %copy-start.19 = (s32[14]{0:T(128)}, s32[14]{0:T(128)S(1)}, u32[]{:S(2)}) copy-start(s32[14]{0:T(128)S(1)} %pad_add_fusion.1.refs_0_.lists) | copy-start | bytes 172
  1.2 6.9 %collective-permute-start = (s32[14]{0:T(128)S(1)}, s32[14]{0:T(128)S(1)}, u32[]{:S(2)}, u32[]{:S(2)}) collective-permute-start(s32[14]{0:T(128)S(1)} %pad_add_fusion.1.refs_0_.lists), channel_id=1, source_target_pairs={{0,8},{8,0},{16,24},{24,16},{1,9},{9,1},{17,25},{25,17},{2,10},{10... | collective-permute-start | bytes 176 | tf_op jit(solution)/shard_map/ppermute | solution.py:385
  3.7 4.4 %collective-permute-start.1 = (s32[14]{0:T(128)S(1)}, s32[14]{0:T(128)S(1)}, u32[]{:S(2)}, u32[]{:S(2)}) collective-permute-start(s32[14]{0:T(128)S(1)} %pad_add_fusion.1.refs_0_.lists), channel_id=1, source_target_pairs={{0,16},{8,24},{16,0},{24,8},{1,17},{9,25},{17,1},{25,9},{2,18},{10... | collective-permute-start | bytes 176 | tf_op jit(solution)/shard_map/ppermute | solution.py:385
  5.2 4.4 %collective-permute-start.2 = (s32[14]{0:T(128)S(1)}, s32[14]{0:T(128)S(1)}, u32[]{:S(2)}, u32[]{:S(2)}) collective-permute-start(s32[14]{0:T(128)S(1)} %pad_add_fusion.1.refs_0_.lists), channel_id=1, source_target_pairs={{0,24},{8,16},{16,8},{24,0},{1,25},{9,17},{17,9},{25,1},{2,26},{10... | collective-permute-start | bytes 176 | tf_op jit(solution)/shard_map/ppermute | solution.py:385
  5.2 13.0 %collective-permute-start.8 = (f32[128]{0:T(128)}, f32[128]{0:T(128)S(1)}, u32[]{:S(2)}, u32[]{:S(2)}) collective-permute-start(f32[128]{0:T(128)} %param.9), channel_id=1, source_target_pairs={{0,2},{1,3},{2,6},{3,7},{6,4},{7,5},{4,0},{5,1},{8,10},{9,11},{10,... | collective-permute-start | bytes 1544 | tf_op jit(solution)/shard_map/ppermute | solution.py:382
  8.1 1.6 copy-start.20
  8.1 1.6 copy-start.21
  10.2 7.6 %copy-start.23 = (f32[48]{0:T(128)S(1)}, f32[48]{0:T(128)}, u32[]{:S(2)}) copy-start(f32[48]{0:T(128)} %param.8) | copy-start | bytes 580
  10.2 7.8 %copy-start.24 = (s32[1,2]{1,0:T(1,128)S(1)}, s32[1,2]{1,0:T(1,128)}, u32[]{:S(2)}) copy-start(s32[1,2]{1,0:T(1,128)} %param.6) | copy-start | bytes 28
  10.2 8.0 %copy-start.25 = (f32[128]{0:T(128)S(1)}, f32[128]{0:T(128)}, u32[]{:S(2)}) copy-start(f32[128]{0:T(128)} %param.9) | copy-start | bytes 1540
  13.4 22.3 %collective-permute-start.4 = (f32[64,1536]{1,0:T(8,128)}, f32[64,1536]{1,0:T(8,128)S(1)}, u32[]{:S(2)}, u32[]{:S(2)}) collective-permute-start(f32[64,1536]{1,0:T(8,128)} %get-tuple-element.116), channel_id=1, source_target_pairs={{0,8},{8,0},{16,24},{24,16},{1,9},{9,1},{17,25},{25,17},{2,10},{10... | collective-permute-start | bytes 1179656 | tf_op jit(solution)/shard_map/ppermute | solution.py:385
  14.0 23.3 %collective-permute-start.5 = (f32[64,1536]{1,0:T(8,128)}, f32[64,1536]{1,0:T(8,128)S(1)}, u32[]{:S(2)}, u32[]{:S(2)}) collective-permute-start(f32[64,1536]{1,0:T(8,128)} %get-tuple-element.117), channel_id=1, source_target_pairs={{0,16},{8,24},{16,0},{24,8},{1,17},{9,25},{17,1},{25,9},{2,18},{10... | collective-permute-start | bytes 1179656 | tf_op jit(solution)/shard_map/ppermute | solution.py:385
  15.1 23.6 %collective-permute-start.6 = (f32[64,1536]{1,0:T(8,128)}, f32[64,1536]{1,0:T(8,128)S(1)}, u32[]{:S(2)}, u32[]{:S(2)}) collective-permute-start(f32[64,1536]{1,0:T(8,128)} %get-tuple-element.118), channel_id=1, source_target_pairs={{0,24},{8,16},{16,8},{24,0},{1,25},{9,17},{17,9},{25,1},{2,26},{10... | collective-permute-start | bytes 1179656 | tf_op jit(solution)/shard_map/ppermute | solution.py:385
  18.2 6.8 %collective-permute-start.9 = (f32[128]{0:T(128)S(1)}, f32[128]{0:T(128)S(1)}, u32[]{:S(2)}, u32[]{:S(2)}) collective-permute-start(f32[128]{0:T(128)S(1)} %copy-done.25), channel_id=1, source_target_pairs={{0,6},{1,7},{2,4},{3,5},{6,0},{7,1},{4,2},{5,3},{8,14},{9,15},{10,... | collective-permute-start | bytes 1544 | tf_op jit(solution)/shard_map/ppermute | solution.py:382
  25.0 10.7 %copy-start.35 = (f32[64,1536]{1,0:T(8,128)S(1)}, f32[64,1536]{1,0:T(8,128)}, u32[]{:S(2)}) copy-start(f32[64,1536]{1,0:T(8,128)} %get-tuple-element.111) | copy-start | bytes 1179652
  25.0 12.3 %copy-start.34 = (f32[64,1536]{1,0:T(8,128)S(1)}, f32[64,1536]{1,0:T(8,128)}, u32[]{:S(2)}) copy-start(f32[64,1536]{1,0:T(8,128)} %get-tuple-element.112) | copy-start | bytes 1179652
  25.0 9.0 %collective-permute-start.10 = (f32[128]{0:T(128)S(1)}, f32[128]{0:T(128)S(1)}, u32[]{:S(2)}, u32[]{:S(2)}) collective-permute-start(f32[128]{0:T(128)S(1)} %copy-done.25), channel_id=1, source_target_pairs={{0,4},{1,5},{2,0},{3,1},{6,2},{7,3},{4,6},{5,7},{8,12},{9,13},{10,... | collective-permute-start | bytes 1544 | tf_op jit(solution)/shard_map/ppermute | solution.py:382
  34.0 1.1 collective-permute-start.7
  35.1 21.6 %collective-permute-start.12 = (f32[64,1536]{1,0:T(8,128)}, f32[64,1536]{1,0:T(8,128)S(1)}, u32[]{:S(2)}, u32[]{:S(2)}) collective-permute-start(f32[64,1536]{1,0:T(8,128)} %get-tuple-element.110), channel_id=1, source_target_pairs={{0,8},{8,0},{16,24},{24,16},{1,9},{9,1},{17,25},{25,17},{2,10},{10... | collective-permute-start | bytes 1179656 | tf_op jit(solution)/shard_map/ppermute | solution.py:385
  35.7 3.1 %copy-start.7 = (f32[64,1536]{1,0:T(8,128)}, f32[64,1536]{1,0:T(8,128)S(1)}, u32[]{:S(2)}) copy-start(f32[64,1536]{1,0:T(8,128)S(1)} %collective-permute-done.4.refs_0_) | copy-start | bytes 1179652
  35.7 21.0 %collective-permute-start.13 = (f32[64,1536]{1,0:T(8,128)S(1)}, f32[64,1536]{1,0:T(8,128)S(1)}, u32[]{:S(2)}, u32[]{:S(2)}) collective-permute-start(f32[64,1536]{1,0:T(8,128)S(1)} %copy-done.35), channel_id=1, source_target_pairs={{0,16},{8,24},{16,0},{24,8},{1,17},{9,25},{17,1},{25,9},{2,18},{10... | collective-permute-start | bytes 1179656 | tf_op jit(solution)/shard_map/ppermute | solution.py:385
  37.3 1.5 copy-start.8
  37.3 19.4 %collective-permute-start.14 = (f32[64,1536]{1,0:T(8,128)S(1)}, f32[64,1536]{1,0:T(8,128)S(1)}, u32[]{:S(2)}, u32[]{:S(2)}) collective-permute-start(f32[64,1536]{1,0:T(8,128)S(1)} %copy-done.34), channel_id=1, source_target_pairs={{0,24},{8,16},{16,8},{24,0},{1,25},{9,17},{17,9},{25,1},{2,26},{10... | collective-permute-start | bytes 1179656 | tf_op jit(solution)/shard_map/ppermute | solution.py:385
  42.1 20.0 %collective-permute-start.11 = (f32[128,1536]{1,0:T(8,128)}, f32[128,1536]{1,0:T(8,128)S(1)}, u32[]{:S(2)}, u32[]{:S(2)}) collective-permute-start(f32[128,1536]{1,0:T(8,128)} %shard_map.58.refs_0_), channel_id=1, source_target_pairs={{0,2},{1,3},{2,6},{3,7},{6,4},{7,5},{4,0},{5,1},{8,10},{9,11},{10,... | collective-permute-start | bytes 2359304 | tf_op jit(solution)/shard_map/ppermute | solution.py:382
  56.7 0.9 copy-start.11
  56.7 1.0 copy-start.12
  60.4 25.6 %collective-permute-start.15 = (f32[128,1536]{1,0:T(8,128)}, f32[128,1536]{1,0:T(8,128)S(1)}, u32[]{:S(2)}, u32[]{:S(2)}) collective-permute-start(f32[128,1536]{1,0:T(8,128)} %shard_map.60.refs_1_), channel_id=1, source_target_pairs={{0,2},{1,3},{2,6},{3,7},{6,4},{7,5},{4,0},{5,1},{8,10},{9,11},{10,... | collective-permute-start | bytes 2359304 | tf_op jit(solution)/shard_map/ppermute | solution.py:382
  62.1 23.9 %copy-start.26 = (f32[128,1536]{1,0:T(8,128)}, f32[128,1536]{1,0:T(8,128)S(1)}, u32[]{:S(2)}) copy-start(f32[128,1536]{1,0:T(8,128)S(1)} %collective-permute-done.11.refs_0_) | copy-start | bytes 2359300
  62.1 36.8 %collective-permute-start.16 = (f32[128,1536]{1,0:T(8,128)S(1)}, f32[128,1536]{1,0:T(8,128)S(1)}, u32[]{:S(2)}, u32[]{:S(2)}) collective-permute-start(f32[128,1536]{1,0:T(8,128)S(1)} %collective-permute-done.11.refs_0_), channel_id=1, source_target_pairs={{0,2},{1,3},{2,6},{3,7},{6,4},{7,5},{4,0},{5,1},{8,10},{9,11},{10,... | collective-permute-start | bytes 2359304 | tf_op jit(solution)/shard_map/ppermute | solution.py:382
  86.0 12.9 %copy-start.32 = (f32[128,1536]{1,0:T(8,128)}, f32[128,1536]{1,0:T(8,128)S(1)}, u32[]{:S(2)}) copy-start(f32[128,1536]{1,0:T(8,128)S(1)} %collective-permute-done.15.refs_1_) | copy-start | bytes 2359300
  86.0 36.0 %collective-permute-start.18 = (f32[128,1536]{1,0:T(8,128)S(1)}, f32[128,1536]{1,0:T(8,128)S(1)}, u32[]{:S(2)}, u32[]{:S(2)}) collective-permute-start(f32[128,1536]{1,0:T(8,128)S(1)} %collective-permute-done.15.refs_1_), channel_id=1, source_target_pairs={{0,2},{1,3},{2,6},{3,7},{6,4},{7,5},{4,0},{5,1},{8,10},{9,11},{10,... | collective-permute-start | bytes 2359304 | tf_op jit(solution)/shard_map/ppermute | solution.py:382
  98.9 23.1 %copy-start.30 = (f32[128,1536]{1,0:T(8,128)}, f32[128,1536]{1,0:T(8,128)S(1)}, u32[]{:S(2)}) copy-start(f32[128,1536]{1,0:T(8,128)S(1)} %collective-permute-done.16.refs_0_) | copy-start | bytes 2359300
  98.9 48.7 %collective-permute-start.17 = (f32[128,1536]{1,0:T(8,128)S(1)}, f32[128,1536]{1,0:T(8,128)S(1)}, u32[]{:S(2)}, u32[]{:S(2)}) collective-permute-start(f32[128,1536]{1,0:T(8,128)S(1)} %collective-permute-done.16.refs_0_), channel_id=1, source_target_pairs={{0,2},{1,3},{2,6},{3,7},{6,4},{7,5},{4,0},{5,1},{8,10},{9,11},{10,... | collective-permute-start | bytes 2359304 | tf_op jit(solution)/shard_map/ppermute | solution.py:382
  122.0 25.6 %copy-start.27 = (f32[128,1536]{1,0:T(8,128)S(1)}, f32[128,1536]{1,0:T(8,128)}, u32[]{:S(2)}) copy-start(f32[128,1536]{1,0:T(8,128)} %get-tuple-element.142) | copy-start | bytes 2359300
  122.0 26.3 %copy-start.28 = (f32[128,1536]{1,0:T(8,128)S(1)}, f32[128,1536]{1,0:T(8,128)}, u32[]{:S(2)}) copy-start(f32[128,1536]{1,0:T(8,128)} %get-tuple-element.137) | copy-start | bytes 2359300
  122.0 2.7 copy-start.31
  122.0 27.9 %collective-permute-start.20 = (f32[128,1536]{1,0:T(8,128)S(1)}, f32[128,1536]{1,0:T(8,128)S(1)}, u32[]{:S(2)}, u32[]{:S(2)}) collective-permute-start(f32[128,1536]{1,0:T(8,128)S(1)} %collective-permute-done.18.refs_1_), channel_id=1, source_target_pairs={{0,2},{1,3},{2,6},{3,7},{6,4},{7,5},{4,0},{5,1},{8,10},{9,11},{10,... | collective-permute-start | bytes 2359304 | tf_op jit(solution)/shard_map/ppermute | solution.py:382
  147.6 2.3 copy-start.29
  147.6 34.9 %collective-permute-start.23 = (f32[128,1536]{1,0:T(8,128)S(1)}, f32[128,1536]{1,0:T(8,128)S(1)}, u32[]{:S(2)}, u32[]{:S(2)}) collective-permute-start(f32[128,1536]{1,0:T(8,128)S(1)} %copy-done.27), channel_id=1, source_target_pairs={{0,2},{1,3},{2,6},{3,7},{6,4},{7,5},{4,0},{5,1},{8,10},{9,11},{10,... | collective-permute-start | bytes 2359304 | tf_op jit(solution)/shard_map/ppermute | solution.py:382
  148.3 33.8 %copy-start.6 = (f32[128,1536]{1,0:T(8,128)S(1)}, f32[128,1536]{1,0:T(8,128)}, u32[]{:S(2)}) copy-start(f32[128,1536]{1,0:T(8,128)} %get-tuple-element.135) | copy-start | bytes 2359300
  148.3 34.3 %copy-start.5 = (f32[128,1536]{1,0:T(8,128)S(1)}, f32[128,1536]{1,0:T(8,128)}, u32[]{:S(2)}) copy-start(f32[128,1536]{1,0:T(8,128)} %get-tuple-element.136) | copy-start | bytes 2359300
  148.3 33.8 %collective-permute-start.19 = (f32[128,1536]{1,0:T(8,128)S(1)}, f32[128,1536]{1,0:T(8,128)S(1)}, u32[]{:S(2)}, u32[]{:S(2)}) collective-permute-start(f32[128,1536]{1,0:T(8,128)S(1)} %copy-done.28), channel_id=1, source_target_pairs={{0,2},{1,3},{2,6},{3,7},{6,4},{7,5},{4,0},{5,1},{8,10},{9,11},{10,... | collective-permute-start | bytes 2359304 | tf_op jit(solution)/shard_map/ppermute | solution.py:382
  182.2 21.4 %collective-permute-start.21 = (f32[128,1536]{1,0:T(8,128)S(1)}, f32[128,1536]{1,0:T(8,128)S(1)}, u32[]{:S(2)}, u32[]{:S(2)}) collective-permute-start(f32[128,1536]{1,0:T(8,128)S(1)} %add.26), channel_id=1, source_target_pairs={{0,2},{1,3},{2,6},{3,7},{6,4},{7,5},{4,0},{5,1},{8,10},{9,11},{10,... | collective-permute-start | bytes 2359304 | tf_op jit(solution)/shard_map/ppermute | solution.py:382
  183.6 32.4 %collective-permute-start.24 = (f32[128,1536]{1,0:T(8,128)}, f32[128,1536]{1,0:T(8,128)S(1)}, u32[]{:S(2)}, u32[]{:S(2)}) collective-permute-start(f32[128,1536]{1,0:T(8,128)} %add.29), channel_id=1, source_target_pairs={{0,2},{1,3},{2,6},{3,7},{6,4},{7,5},{4,0},{5,1},{8,10},{9,11},{10,... | collective-permute-start | bytes 2359304 | tf_op jit(solution)/shard_map/ppermute | solution.py:382
  198.0 46.7 %collective-permute-start.26 = (f32[768,1536]{1,0:T(8,128)}, f32[768,1536]{1,0:T(8,128)S(1)}, u32[]{:S(2)}, u32[]{:S(2)}) collective-permute-start(f32[768,1536]{1,0:T(8,128)} %shard_map.65), channel_id=1, source_target_pairs={{0,1},{1,0},{2,3},{3,2},{4,5},{5,4},{6,7},{7,6},{8,9},{9,8},{10,11... | collective-permute-start | bytes 14155784 | tf_op jit(solution)/shard_map/ppermute | solution.py:384
  215.9 4.1 %copy-start.4 = (f32[128,1536]{1,0:T(8,128)S(1)}, f32[128,1536]{1,0:T(8,128)}, u32[]{:S(2)}) copy-start(f32[128,1536]{1,0:T(8,128)} %get-tuple-element.138) | copy-start | bytes 2359300
  215.9 5.1 %copy-start.3 = (f32[128,1536]{1,0:T(8,128)S(1)}, f32[128,1536]{1,0:T(8,128)}, u32[]{:S(2)}) copy-start(f32[128,1536]{1,0:T(8,128)} %get-tuple-element.139) | copy-start | bytes 2359300
  220.0 24.7 %collective-permute-start.27 = (f32[768,1536]{1,0:T(8,128)}, f32[768,1536]{1,0:T(8,128)}, u32[]{:S(2)}, u32[]{:S(2)}) collective-permute-start(f32[768,1536]{1,0:T(8,128)} %shard_map.67), channel_id=1, source_target_pairs={{0,1},{1,0},{2,3},{3,2},{4,5},{5,4},{6,7},{7,6},{8,9},{9,8},{10,11... | collective-permute-start | bytes 14155784 | tf_op jit(solution)/shard_map/ppermute | solution.py:384
  221.0 21.6 %collective-permute-start.22 = (f32[128,1536]{1,0:T(8,128)}, f32[128,1536]{1,0:T(8,128)}, u32[]{:S(2)}, u32[]{:S(2)}) collective-permute-start(f32[128,1536]{1,0:T(8,128)} %add.27), channel_id=1, source_target_pairs={{0,2},{1,3},{2,6},{3,7},{6,4},{7,5},{4,0},{5,1},{8,10},{9,11},{10,... | collective-permute-start | bytes 2359304 | tf_op jit(solution)/shard_map/ppermute | solution.py:382
  221.1 21.5 %copy-start.2 = (f32[128,1536]{1,0:T(8,128)S(1)}, f32[128,1536]{1,0:T(8,128)}, u32[]{:S(2)}) copy-start(f32[128,1536]{1,0:T(8,128)} %get-tuple-element.130) | copy-start | bytes 2359300
  221.1 37.8 %copy-start.1 = (f32[128,1536]{1,0:T(8,128)S(1)}, f32[128,1536]{1,0:T(8,128)}, u32[]{:S(2)}) copy-start(f32[128,1536]{1,0:T(8,128)} %get-tuple-element.131) | copy-start | bytes 2359300
  221.1 37.8 %collective-permute-start.25 = (f32[128,1536]{1,0:T(8,128)S(1)}, f32[128,1536]{1,0:T(8,128)S(1)}, u32[]{:S(2)}, u32[]{:S(2)}) collective-permute-start(f32[128,1536]{1,0:T(8,128)S(1)} %add.30), channel_id=1, source_target_pairs={{0,2},{1,3},{2,6},{3,7},{6,4},{7,5},{4,0},{5,1},{8,10},{9,11},{10,... | collective-permute-start | bytes 2359304 | tf_op jit(solution)/shard_map/ppermute | solution.py:382
  244.7 30.2 %copy-start = (f32[768,1536]{1,0:T(8,128)}, f32[768,1536]{1,0:T(8,128)S(1)}, u32[]{:S(2)}) copy-start(f32[768,1536]{1,0:T(8,128)S(1)} %collective-permute-done.26.refs_5_) | copy-start | bytes 14155780
  248.5 12.3 %collective-permute-start.28 = (f32[64,1536]{1,0:T(8,128)}, f32[64,1536]{1,0:T(8,128)S(1)}, u32[]{:S(2)}, u32[]{:S(2)}) collective-permute-start(f32[64,1536]{1,0:T(8,128)} %get-tuple-element.208), channel_id=1, source_target_pairs={{0,8},{8,0},{16,24},{24,16},{1,9},{9,1},{17,25},{25,17},{2,10},{10... | collective-permute-start | bytes 1179656 | tf_op jit(solution)/shard_map/ppermute | solution.py:385
  249.4 18.7 %collective-permute-start.29 = (f32[64,1536]{1,0:T(8,128)}, f32[64,1536]{1,0:T(8,128)S(1)}, u32[]{:S(2)}, u32[]{:S(2)}) collective-permute-start(f32[64,1536]{1,0:T(8,128)} %get-tuple-element.209), channel_id=1, source_target_pairs={{0,16},{8,24},{16,0},{24,8},{1,17},{9,25},{17,1},{25,9},{2,18},{10... | collective-permute-start | bytes 1179656 | tf_op jit(solution)/shard_map/ppermute | solution.py:385
  250.1 18.0 %collective-permute-start.30 = (f32[64,1536]{1,0:T(8,128)}, f32[64,1536]{1,0:T(8,128)S(1)}, u32[]{:S(2)}, u32[]{:S(2)}) collective-permute-start(f32[64,1536]{1,0:T(8,128)} %get-tuple-element.210), channel_id=1, source_target_pairs={{0,24},{8,16},{16,8},{24,0},{1,25},{9,17},{17,9},{25,1},{2,26},{10... | collective-permute-start | bytes 1179656 | tf_op jit(solution)/shard_map/ppermute | solution.py:385
  260.9 29.3 %copy-start.13 = (f32[64,1536]{1,0:T(8,128)}, f32[64,1536]{1,0:T(8,128)S(1)}, u32[]{:S(2)}) copy-start(f32[64,1536]{1,0:T(8,128)S(1)} %collective-permute-done.28.refs_6_) | copy-start | bytes 1179652
  268.1 22.1 %copy-start.14 = (f32[64,1536]{1,0:T(8,128)}, f32[64,1536]{1,0:T(8,128)S(1)}, u32[]{:S(2)}) copy-start(f32[64,1536]{1,0:T(8,128)S(1)} %collective-permute-done.29.refs_7_) | copy-start | bytes 1179652
  268.1 22.1 %copy-start.15 = (f32[64,1536]{1,0:T(8,128)}, f32[64,1536]{1,0:T(8,128)S(1)}, u32[]{:S(2)}) copy-start(f32[64,1536]{1,0:T(8,128)S(1)} %collective-permute-done.30.refs_8_) | copy-start | bytes 1179652
  271.3 18.9 %collective-permute-start.31 = (f32[64,1536]{1,0:T(8,128)}, f32[64,1536]{1,0:T(8,128)S(1)}, u32[]{:S(2)}, u32[]{:S(2)}) collective-permute-start(f32[64,1536]{1,0:T(8,128)} %get-tuple-element.212), channel_id=1, source_target_pairs={{0,8},{8,0},{16,24},{24,16},{1,9},{9,1},{17,25},{25,17},{2,10},{10... | collective-permute-start | bytes 1179656 | tf_op jit(solution)/shard_map/ppermute | solution.py:385
  272.5 17.7 %collective-permute-start.32 = (f32[64,1536]{1,0:T(8,128)}, f32[64,1536]{1,0:T(8,128)S(1)}, u32[]{:S(2)}, u32[]{:S(2)}) collective-permute-start(f32[64,1536]{1,0:T(8,128)} %get-tuple-element.213), channel_id=1, source_target_pairs={{0,16},{8,24},{16,0},{24,8},{1,17},{9,25},{17,1},{25,9},{2,18},{10... | collective-permute-start | bytes 1179656 | tf_op jit(solution)/shard_map/ppermute | solution.py:385
  273.0 17.3 %collective-permute-start.33 = (f32[64,1536]{1,0:T(8,128)}, f32[64,1536]{1,0:T(8,128)S(1)}, u32[]{:S(2)}, u32[]{:S(2)}) collective-permute-start(f32[64,1536]{1,0:T(8,128)} %get-tuple-element.214), channel_id=1, source_target_pairs={{0,24},{8,16},{16,8},{24,0},{1,25},{9,17},{17,9},{25,1},{2,26},{10... | collective-permute-start | bytes 1179656 | tf_op jit(solution)/shard_map/ppermute | solution.py:385
  290.3 1.0 copy-start.18
  (6 other events, 4.7 us)

commit v8 on v7

--- a/solution.py
+++ b/solution.py
@@ -392,8 +392,6 @@
     part_width = width // PIECES
     blocks = [pick(me_ref, packets, slots, integrals, p * part_width, part_width) for p in range(PIECES)]
 
-    own_half = split_rows(after(own_rows, *blocks[-1]))
-
     ids = lax.broadcasted_iota(jnp.int32, (groups, own_count, occ_energy.shape[0]), 2)
     orbitals = jnp.stack(packets)[:, slots:]
     row_energies = jnp.sum(jnp.where(orbitals[:, :, None] == ids, occ_energy, 0.0), axis=2)
@@ -415,12 +413,12 @@
         sent = blocks[p]
         got = [to_group(block, k + 1) for k, block in enumerate(sent)]
         if p == 1:
-            halves = (own_half, split_rows(after(sib_rows, pieces[0][0])))
-        got = after(got, halves, pieces[-1][0]) if p else after(got, own_half, early_energies)
+            own_half = split_rows(after(own_rows, pieces[0][0]))
+        got = after(got, own_half, sib_rows, pieces[-1][0]) if p else after(got, early_energies)
         part = choose(me_ref, packet, slots, integrals, got, p * part_width)
         pieces.append([part, hop(part)])
-        if p == 1:
-            pieces[0][1] = after(pieces[0][1], halves)
+    halves = (own_half, split_rows(after(sib_rows, pieces[1][0])))
+    pieces[0][1] = after(pieces[0][1], halves)
     parts = [piece[0] for piece in pieces]
     first = [piece[1] for piece in pieces]
 

time: 295 us -> 290 us (0.983)
  waiting for transfers between devices: 46.8 us -> 39.6 us
    ppermute x15, waiting for transfers between devices: 36 us -> 26.1 us  [body(): along = lambda x, s: lax.ppermute(x, 'blk', ring(s))]
  transfers between devices with their start and end apart: 34 -> 34, of which waited for: 10 -> 10; matrix products, arithmetic and copies ran while one was open for 4% -> 4% of each run, Pallas kernels for 63% -> 64%
where the time goes in v8:
time: 290 us
  Pallas kernels  191 us (66%)
  starting transfers between devices  41.5 us (14%)
  waiting for transfers between devices  39.6 us (14%)
  local copies, waits for them, and re-layouts  9.4 us (3%)
  other arithmetic  7.22 us (2%)
    pallas_call x4, Pallas kernels, unit(): pl.pallas_call(functools.partial(unit_kernel, steps), grid=(2 * steps,),...  91.3 us
    pallas_call x4, Pallas kernels, forward(): pl.pallas_call(functools.partial(forward_kernel, len(units), spans, parti...  56.4 us
    ppermute x15, waiting for transfers between devices, body(): along = lambda x, s: lax.ppermute(x, 'blk', ring(s))  26.1 us
    ppermute x15, starting transfers between devices, body(): along = lambda x, s: lax.ppermute(x, 'blk', ring(s))  23.3 us
    ppermute x15, starting transfers between devices, body(): lax.ppermute(x, 'grp', [(g, g ^ k) for g in range(groups)])  17.7 us
    pallas_call x2, Pallas kernels, split_rows(): pl.pallas_call(split_kernel, grid=(rows // step,), in_specs=[spec], out_s...  17.2 us
    ppermute x15, waiting for transfers between devices, body(): lax.ppermute(x, 'grp', [(g, g ^ k) for g in range(groups)])  12.5 us
    pallas_call x2, Pallas kernels, back(): pl.pallas_call(functools.partial(back_kernel, groups, slots, own_count),...  6.9 us
  transfers between devices with their start and end apart: 34, of which 10 were waited for; matrix products, arithmetic and copies ran while one was open for 4% of the time, Pallas kernels for 64%

profile of v8, /device:TPU:0, one launch (start us, length us, event | category | flops | bytes accessed | tf_op | source)
XLA Modules:
  0.0 289.7 jit_solution(763671643135351486)
XLA Ops:
  0.5 0.7 pad_add_fusion.1.refs_0_.lists
  1.2 2.5 collective-permute-start
  3.7 1.5 collective-permute-start.1
  5.2 2.0 collective-permute-start.7
  7.3 0.7 stack.47
  8.1 1.5 collective-permute-done.2.refs_3_
  10.2 3.1 %shard_map.55 = (f32[64,1536]{1,0:T(8,128)}, f32[64,1536]{1,0:T(8,128)}, f32[64,1536]{1,0:T(8,128)}) custom-call(s32[1]{0:T(128)} %bitcast.me_ref, s32[14]{0:T(128)} %copy-done.19, s32[14]{0:T(128)} %copy-done.20, s32[14]{0:T(128)} %copy-done.21, s32[14]{0:T(128)} %copy-done.22, f32[12,128,1536]{2,1,0:T(8,128)} %x_ref.3), custom_call_target="tpu_custom_call" | custom-call | bytes 3145728 | tf_op jit(solution)/shard_map/pallas_call | solution.py:94
  13.9 1.1 collective-permute-start.4
  15.0 1.8 collective-permute-start.5
  18.0 3.6 %collective-permute-start.8 = (f32[128]{0:T(128)S(1)}, f32[128]{0:T(128)S(1)}, u32[]{:S(2)}, u32[]{:S(2)}) collective-permute-start(f32[128]{0:T(128)S(1)} %copy-done.25), channel_id=1, source_target_pairs={{0,6},{1,7},{2,4},{3,5},{6,0},{7,1},{4,2},{5,3},{8,14},{9,15},{10,... | collective-permute-start | bytes 1544 | tf_op jit(solution)/shard_map/ppermute | solution.py:382
  21.8 1.6 collective-permute-done.8
  23.4 0.8 collective-permute-start.9
  24.3 3.0 %shard_map.58 = (f32[64,1536]{1,0:T(8,128)}, f32[64,1536]{1,0:T(8,128)}, f32[64,1536]{1,0:T(8,128)}) custom-call(s32[1]{0:T(128)} %bitcast.me_ref, s32[14]{0:T(128)} %copy-done.19, s32[14]{0:T(128)} %copy-done.20, s32[14]{0:T(128)} %copy-done.21, s32[14]{0:T(128)} %copy-done.22, f32[12,128,1536]{2,1,0:T(8,128)} %x_ref.3), custom_call_target="tpu_custom_call" | custom-call | bytes 3145728 | tf_op jit(solution)/shard_map/pallas_call | solution.py:94
  27.5 1.0 collective-permute-done.6
  29.1 0.8 collective-permute-start.12
  29.9 2.2 collective-permute-done.4.refs_1_
  32.1 1.6 collective-permute-start.13
  33.7 0.7 copy-done.9
  34.5 2.7 shard_map.56.refs_0_
  37.2 2.4 collective-permute-start.14
  39.7 0.8 unstack.34.col_ref
  41.2 0.8 unstack.33.col_ref
  42.0 0.8 unstack.32.col_ref
  42.8 0.8 unstack.35.col_ref
  43.6 8.6 %shard_map.57 = (bf16[1536,1536]{1,0:T(8,128)(2,1)}, bf16[1536,1536]{1,0:T(8,128)(2,1)}) custom-call(f32[1536,1536]{1,0:T(8,128)} %bitcast.13), custom_call_target="tpu_custom_call" | custom-call | flops 4718592 | bytes 18874368 | tf_op jit(solution)/shard_map/pallas_call | solution.py:54
  52.3 0.7 copy-done.10
  53.2 2.7 shard_map.59.refs_1_
  55.9 1.1 collective-permute-start.15
  57.1 8.6 %shard_map.60 = (bf16[1536,1536]{1,0:T(8,128)(2,1)}, bf16[1536,1536]{1,0:T(8,128)(2,1)}) custom-call(f32[1536,1536]{1,0:T(8,128)} %collective-permute-done.10.x_ref), custom_call_target="tpu_custom_call" | custom-call | flops 4718592 | bytes 18874368 | tf_op jit(solution)/shard_map/pallas_call | solution.py:54
  65.7 1.0 collective-permute-start.16
  66.7 22.8 %shard_map.61 = (bf16[256,3072]{1,0:T(8,128)(2,1)}, bf16[256,3072]{1,0:T(8,128)(2,1)}, bf16[256,1536]{1,0:T(8,128)(2,1)}, bf16[256,1536]{1,0:T(8,128)(2,1)}, f32[128,1536]{1,0:T(8,128)}, /*index=5*/f32[128,1536]{1,0:T(8,128)}) custom-call(bf16[1536,1536]{1,0:T(8,128)(2,1)} %get-tuple-element.117.own_high, bf16[1536,1536]{1,0:T(8,128)(2,1)} %get-tuple-element.118.own_low, ...), custom_call_target="tpu_custom_call" | custom-call | flops 14495514624 | bytes 25165824 | tf_op jit(solution)/shard_map/pallas_call | solution.py:285
  90.1 2.4 collective-permute-start.17
  92.5 22.8 %shard_map.62 = (bf16[256,3072]{1,0:T(8,128)(2,1)}, bf16[256,3072]{1,0:T(8,128)(2,1)}, bf16[256,1536]{1,0:T(8,128)(2,1)}, bf16[256,1536]{1,0:T(8,128)(2,1)}, f32[128,1536]{1,0:T(8,128)}, /*index=5*/f32[128,1536]{1,0:T(8,128)}) custom-call(bf16[1536,1536]{1,0:T(8,128)(2,1)} %get-tuple-element.117.own_high, bf16[1536,1536]{1,0:T(8,128)(2,1)} %get-tuple-element.118.own_low, ...), custom_call_target="tpu_custom_call" | custom-call | flops 14495514624 | bytes 25165824 | tf_op jit(solution)/shard_map/pallas_call | solution.py:285
  115.4 3.3 %collective-permute-start.20 = (f32[128,1536]{1,0:T(8,128)S(1)}, f32[128,1536]{1,0:T(8,128)S(1)}, u32[]{:S(2)}, u32[]{:S(2)}) collective-permute-start(f32[128,1536]{1,0:T(8,128)S(1)} %collective-permute-done.18.refs_1_), channel_id=1, source_target_pairs={{0,2},{1,3},{2,6},{3,7},{6,4},{7,5},{4,0},{5,1},{8,10},{9,11},{10,... | collective-permute-start | bytes 2359304 | tf_op jit(solution)/shard_map/ppermute | solution.py:382
  118.7 22.9 %shard_map.63 = (bf16[256,3072]{1,0:T(8,128)(2,1)}, bf16[256,3072]{1,0:T(8,128)(2,1)}, bf16[256,1536]{1,0:T(8,128)(2,1)}, bf16[256,1536]{1,0:T(8,128)(2,1)}, f32[128,1536]{1,0:T(8,128)}, /*index=5*/f32[128,1536]{1,0:T(8,128)}) custom-call(bf16[1536,1536]{1,0:T(8,128)(2,1)} %get-tuple-element.117.own_high, bf16[1536,1536]{1,0:T(8,128)(2,1)} %get-tuple-element.118.own_low, ...), custom_call_target="tpu_custom_call" | custom-call | flops 14495514624 | bytes 25165824 | tf_op jit(solution)/shard_map/pallas_call | solution.py:285
  141.6 0.7 collective-permute-start.23
  142.6 0.9 copy-done.33
  143.5 22.8 %shard_map.64 = (bf16[256,3072]{1,0:T(8,128)(2,1)}, bf16[256,3072]{1,0:T(8,128)(2,1)}, bf16[256,1536]{1,0:T(8,128)(2,1)}, bf16[256,1536]{1,0:T(8,128)(2,1)}, f32[128,1536]{1,0:T(8,128)}, /*index=5*/f32[128,1536]{1,0:T(8,128)}) custom-call(bf16[1536,1536]{1,0:T(8,128)(2,1)} %get-tuple-element.117.own_high, bf16[1536,1536]{1,0:T(8,128)(2,1)} %get-tuple-element.118.own_low, ...), custom_call_target="tpu_custom_call" | custom-call | flops 14495514624 | bytes 25165824 | tf_op jit(solution)/shard_map/pallas_call | solution.py:285
  166.3 9.7 %collective-permute-done.19 = f32[128,1536]{1,0:T(8,128)S(1)} collective-permute-done((f32[128,1536]{1,0:T(8,128)S(1)}, f32[128,1536]{1,0:T(8,128)S(1)}, u32[]{:S(2)}, u32[]{:S(2)}) %collective-permute-start.19) | collective-permute-done | bytes 786464 | tf_op jit(solution)/shard_map/ppermute | solution.py:382
  176.3 1.0 add.29
  177.2 2.0 collective-permute-start.24
  179.3 12.5 %shard_map.65 = f32[768,1536]{1,0:T(8,128)} custom-call(bf16[256,3072]{1,0:T(8,128)(2,1)} %get-tuple-element.195.refs_0_, bf16[256,3072]{1,0:T(8,128)(2,1)} %get-tuple-element.196.refs_1_, bf16[256,1536]{1,0:T(8,128)(2,1)} %get-tuple-element.197.refs_2_, bf16[256,1536]{1,0:T(8,128)(2,1)} %get-tuple-element.198.refs_3_, ...), custom_call_target="tpu_custom_call" | custom-call | flops 7247757312 | bytes 9437184 | tf_op jit(solution)/shard_map/pallas_call | solution.py:331
  191.9 5.7 %collective-permute-done.21 = f32[128,1536]{1,0:T(8,128)S(1)} collective-permute-done((f32[128,1536]{1,0:T(8,128)S(1)}, f32[128,1536]{1,0:T(8,128)S(1)}, u32[]{:S(2)}, u32[]{:S(2)}) %collective-permute-start.21) | collective-permute-done | bytes 786464 | tf_op jit(solution)/shard_map/ppermute | solution.py:382
  197.6 12.3 %shard_map.66.known = f32[768,1536]{1,0:T(8,128)} custom-call(bf16[256,3072]{1,0:T(8,128)(2,1)} %get-tuple-element.195.refs_0_, bf16[256,3072]{1,0:T(8,128)(2,1)} %get-tuple-element.196.refs_1_, bf16[256,1536]{1,0:T(8,128)(2,1)} %get-tuple-element.197.refs_2_, bf16[256,1536]{1,0:T(8,128)(2,1)} %get-tuple-element.198.refs_3_, ...), custom_call_target="tpu_custom_call" | custom-call | flops 7247757312 | bytes 9437184 | tf_op jit(solution)/shard_map/pallas_call | solution.py:331
  210.0 4.1 %shard_map.67 = f32[768,1536]{1,0:T(8,128)} custom-call(bf16[256,3072]{1,0:T(8,128)(2,1)} %get-tuple-element.191.refs_12_.t_high.refs_0_, bf16[256,3072]{1,0:T(8,128)(2,1)} %get-tuple-element.192.refs_13_.t_low.refs_1_, bf16[256,1536]{1,0:T(8,128)(2,1)} %get-tuple-element.193.refs_14_.r_high.refs_2_, ...), custom_call_target="tpu_custom_call", output_to_operand_aliasing={{}: (4, {})} | custom-call | flops 1811939328 | bytes 9437184 | tf_op jit(solution)/shard_map/pallas_call | solution.py:354
  214.0 1.0 add.27
  215.1 2.9 %collective-permute-start.25 = (f32[128,1536]{1,0:T(8,128)S(1)}, f32[128,1536]{1,0:T(8,128)S(1)}, u32[]{:S(2)}, u32[]{:S(2)}) collective-permute-start(f32[128,1536]{1,0:T(8,128)S(1)} %add.30), channel_id=1, source_target_pairs={{0,2},{1,3},{2,6},{3,7},{6,4},{7,5},{4,0},{5,1},{8,10},{9,11},{10,... | collective-permute-start | bytes 2359304 | tf_op jit(solution)/shard_map/ppermute | solution.py:382
  218.0 16.2 %shard_map.68.refs_4_ = f32[1536,1536]{1,0:T(8,128)} custom-call(bf16[256,3072]{1,0:T(8,128)(2,1)} %get-tuple-element.195.refs_0_, bf16[256,3072]{1,0:T(8,128)(2,1)} %get-tuple-element.196.refs_1_, bf16[256,1536]{1,0:T(8,128)(2,1)} %get-tuple-element.197.refs_2_, bf16[256,1536]{1,0:T(8,128)(2,1)} %get-tuple-element.198.refs_3_, ...), custom_call_target="tpu_custom_call" | custom-call | flops 10871635968 | bytes 18874368 | tf_op jit(solution)/shard_map/pallas_call | solution.py:331
  234.3 2.3 collective-permute-done.22
  236.6 2.1 add.28.share.refs_4_
  238.7 3.9 %shard_map.69 = (f32[64,1536]{1,0:T(8,128)}, f32[64,1536]{1,0:T(8,128)}, f32[64,1536]{1,0:T(8,128)}) custom-call(s32[1]{0:T(128)} %bitcast.me_ref, s32[14]{0:T(128)} %copy-done.19, f32[128,1536]{1,0:T(8,128)} %add.28.share.refs_4_), custom_call_target="tpu_custom_call" | custom-call | bytes 3145728 | tf_op jit(solution)/shard_map/pallas_call | solution.py:165
  242.5 1.4 collective-permute-start.28
  243.9 2.2 collective-permute-start.30
  246.1 6.8 %collective-permute-done.25 = f32[128,1536]{1,0:T(8,128)S(1)} collective-permute-done((f32[128,1536]{1,0:T(8,128)S(1)}, f32[128,1536]{1,0:T(8,128)S(1)}, u32[]{:S(2)}, u32[]{:S(2)}) %collective-permute-start.25) | collective-permute-done | bytes 786464 | tf_op jit(solution)/shard_map/ppermute | solution.py:382
  252.9 1.0 add.31.share.refs_5_
  253.9 0.9 collective-permute-done.28.refs_6_
  254.9 7.8 %collective-permute-done.29.refs_7_ = f32[64,1536]{1,0:T(8,128)S(1)} collective-permute-done((f32[64,1536]{1,0:T(8,128)}, f32[64,1536]{1,0:T(8,128)S(1)}, u32[]{:S(2)}, u32[]{:S(2)}) %collective-permute-start.29) | collective-permute-done | bytes 393248 | tf_op jit(solution)/shard_map/ppermute | solution.py:385
  262.6 3.0 %shard_map.70 = (f32[64,1536]{1,0:T(8,128)}, f32[64,1536]{1,0:T(8,128)}, f32[64,1536]{1,0:T(8,128)}) custom-call(s32[1]{0:T(128)} %bitcast.me_ref, s32[14]{0:T(128)} %copy-done.19, f32[128,1536]{1,0:T(8,128)} %add.31.share.refs_5_), custom_call_target="tpu_custom_call" | custom-call | bytes 3145728 | tf_op jit(solution)/shard_map/pallas_call | solution.py:165
  265.7 0.7 collective-permute-start.31
  266.4 1.1 collective-permute-start.32
  267.5 1.8 collective-permute-start.33
  269.3 15.3 %shard_map.71 = f32[1536,1536]{1,0:T(8,128)} custom-call(bf16[256,3072]{1,0:T(8,128)(2,1)} %get-tuple-element.191.refs_12_.t_high.refs_0_, bf16[256,3072]{1,0:T(8,128)(2,1)} %get-tuple-element.192.refs_13_.t_low.refs_1_, bf16[256,1536]{1,0:T(8,128)(2,1)} %get-tuple-element.193.refs_14_.r_high.refs_2_, ...), custom_call_target="tpu_custom_call" | custom-call | flops 3623878656 | bytes 18874368 | tf_op jit(solution)/shard_map/pallas_call | solution.py:331
  284.7 0.7 copy-done.16
  285.6 3.9 %shard_map.72 = f32[12,128,1536]{2,1,0:T(8,128)} custom-call(s32[1]{0:T(128)} %bitcast.me_ref, s32[14]{0:T(128)} %copy-done.19, s32[14]{0:T(128)} %copy-done.20, s32[14]{0:T(128)} %copy-done.21, s32[14]{0:T(128)} %copy-done.22, f32[128,1536]{1,0:T(8,128)} %add.28.share.refs_4_, f32[128,1536]{1,0:T(8,128)} %add.31.share.refs_5_, ...), custom_call_target="tpu_custom_call", output_to_operand_aliasing={{}: (13, {})} | custom-call | bytes 9437184 | tf_op jit(solution)/shard_map/pallas_call | solution.py:227
  (120 shorter events, 6.5 us)
Async XLA Ops:
  0.0 52.2 %collective-permute-start.10 = (f32[1536,1536]{1,0:T(8,128)}, f32[1536,1536]{1,0:T(8,128)}, u32[]{:S(2)}, u32[]{:S(2)}) collective-permute-start(f32[1536,1536]{1,0:T(8,128)} %bitcast.12), channel_id=1, source_target_pairs={{0,1},{1,0},{2,3},{3,2},{4,5},{5,4},{6,7},{7,6},{8,9},{9,8},{10,11... | collective-permute-start | bytes 28311560 | tf_op jit(solution)/shard_map/ppermute | solution.py:384
  1.2 8.5 %copy-start.19 = (s32[14]{0:T(128)}, s32[14]{0:T(128)S(1)}, u32[]{:S(2)}) copy-start(s32[14]{0:T(128)S(1)} %pad_add_fusion.1.refs_0_.lists) | copy-start | bytes 172
  1.2 6.9 %collective-permute-start = (s32[14]{0:T(128)S(1)}, s32[14]{0:T(128)S(1)}, u32[]{:S(2)}, u32[]{:S(2)}) collective-permute-start(s32[14]{0:T(128)S(1)} %pad_add_fusion.1.refs_0_.lists), channel_id=1, source_target_pairs={{0,8},{8,0},{16,24},{24,16},{1,9},{9,1},{17,25},{25,17},{2,10},{10... | collective-permute-start | bytes 176 | tf_op jit(solution)/shard_map/ppermute | solution.py:385
  3.7 4.4 %collective-permute-start.1 = (s32[14]{0:T(128)S(1)}, s32[14]{0:T(128)S(1)}, u32[]{:S(2)}, u32[]{:S(2)}) collective-permute-start(s32[14]{0:T(128)S(1)} %pad_add_fusion.1.refs_0_.lists), channel_id=1, source_target_pairs={{0,16},{8,24},{16,0},{24,8},{1,17},{9,25},{17,1},{25,9},{2,18},{10... | collective-permute-start | bytes 176 | tf_op jit(solution)/shard_map/ppermute | solution.py:385
  5.2 4.4 %collective-permute-start.2 = (s32[14]{0:T(128)S(1)}, s32[14]{0:T(128)S(1)}, u32[]{:S(2)}, u32[]{:S(2)}) collective-permute-start(s32[14]{0:T(128)S(1)} %pad_add_fusion.1.refs_0_.lists), channel_id=1, source_target_pairs={{0,24},{8,16},{16,8},{24,0},{1,25},{9,17},{17,9},{25,1},{2,26},{10... | collective-permute-start | bytes 176 | tf_op jit(solution)/shard_map/ppermute | solution.py:385
  5.2 12.7 %collective-permute-start.7 = (f32[128]{0:T(128)}, f32[128]{0:T(128)S(1)}, u32[]{:S(2)}, u32[]{:S(2)}) collective-permute-start(f32[128]{0:T(128)} %param.9), channel_id=1, source_target_pairs={{0,2},{1,3},{2,6},{3,7},{6,4},{7,5},{4,0},{5,1},{8,10},{9,11},{10,... | collective-permute-start | bytes 1544 | tf_op jit(solution)/shard_map/ppermute | solution.py:382
  8.1 1.6 copy-start.20
  8.1 1.6 copy-start.21
  10.2 7.5 %copy-start.23 = (f32[48]{0:T(128)S(1)}, f32[48]{0:T(128)}, u32[]{:S(2)}) copy-start(f32[48]{0:T(128)} %param.8) | copy-start | bytes 580
  10.2 7.8 %copy-start.25 = (f32[128]{0:T(128)S(1)}, f32[128]{0:T(128)}, u32[]{:S(2)}) copy-start(f32[128]{0:T(128)} %param.9) | copy-start | bytes 1540
  10.2 11.4 %copy-start.24 = (s32[1,2]{1,0:T(1,128)S(1)}, s32[1,2]{1,0:T(1,128)}, u32[]{:S(2)}) copy-start(s32[1,2]{1,0:T(1,128)} %param.6) | copy-start | bytes 28
  13.3 15.8 %collective-permute-start.3 = (f32[64,1536]{1,0:T(8,128)}, f32[64,1536]{1,0:T(8,128)S(1)}, u32[]{:S(2)}, u32[]{:S(2)}) collective-permute-start(f32[64,1536]{1,0:T(8,128)} %get-tuple-element.110), channel_id=1, source_target_pairs={{0,8},{8,0},{16,24},{24,16},{1,9},{9,1},{17,25},{25,17},{2,10},{10... | collective-permute-start | bytes 1179656 | tf_op jit(solution)/shard_map/ppermute | solution.py:385
  13.9 18.2 %collective-permute-start.4 = (f32[64,1536]{1,0:T(8,128)}, f32[64,1536]{1,0:T(8,128)S(1)}, u32[]{:S(2)}, u32[]{:S(2)}) collective-permute-start(f32[64,1536]{1,0:T(8,128)} %get-tuple-element.111), channel_id=1, source_target_pairs={{0,16},{8,24},{16,0},{24,8},{1,17},{9,25},{17,1},{25,9},{2,18},{10... | collective-permute-start | bytes 1179656 | tf_op jit(solution)/shard_map/ppermute | solution.py:385
  15.0 18.7 %collective-permute-start.5 = (f32[64,1536]{1,0:T(8,128)}, f32[64,1536]{1,0:T(8,128)S(1)}, u32[]{:S(2)}, u32[]{:S(2)}) collective-permute-start(f32[64,1536]{1,0:T(8,128)} %get-tuple-element.112), channel_id=1, source_target_pairs={{0,24},{8,16},{16,8},{24,0},{1,25},{9,17},{17,9},{25,1},{2,26},{10... | collective-permute-start | bytes 1179656 | tf_op jit(solution)/shard_map/ppermute | solution.py:385
  18.0 5.4 %collective-permute-start.8 = (f32[128]{0:T(128)S(1)}, f32[128]{0:T(128)S(1)}, u32[]{:S(2)}, u32[]{:S(2)}) collective-permute-start(f32[128]{0:T(128)S(1)} %copy-done.25), channel_id=1, source_target_pairs={{0,6},{1,7},{2,4},{3,5},{6,0},{7,1},{4,2},{5,3},{8,14},{9,15},{10,... | collective-permute-start | bytes 1544 | tf_op jit(solution)/shard_map/ppermute | solution.py:382
  23.4 4.1 %collective-permute-start.9 = (f32[128]{0:T(128)S(1)}, f32[128]{0:T(128)S(1)}, u32[]{:S(2)}, u32[]{:S(2)}) collective-permute-start(f32[128]{0:T(128)S(1)} %copy-done.25), channel_id=1, source_target_pairs={{0,4},{1,5},{2,0},{3,1},{6,2},{7,3},{4,6},{5,7},{8,12},{9,13},{10,... | collective-permute-start | bytes 1544 | tf_op jit(solution)/shard_map/ppermute | solution.py:382
  27.4 1.1 collective-permute-start.6
  28.6 23.6 %collective-permute-start.11 = (f32[64,1536]{1,0:T(8,128)}, f32[64,1536]{1,0:T(8,128)S(1)}, u32[]{:S(2)}, u32[]{:S(2)}) collective-permute-start(f32[64,1536]{1,0:T(8,128)} %get-tuple-element.119), channel_id=1, source_target_pairs={{0,8},{8,0},{16,24},{24,16},{1,9},{9,1},{17,25},{25,17},{2,10},{10... | collective-permute-start | bytes 1179656 | tf_op jit(solution)/shard_map/ppermute | solution.py:385
  29.1 4.6 %copy-start.7 = (f32[64,1536]{1,0:T(8,128)}, f32[64,1536]{1,0:T(8,128)S(1)}, u32[]{:S(2)}) copy-start(f32[64,1536]{1,0:T(8,128)S(1)} %collective-permute-done.3.refs_0_) | copy-start | bytes 1179652
  29.1 23.1 %collective-permute-start.12 = (f32[64,1536]{1,0:T(8,128)}, f32[64,1536]{1,0:T(8,128)S(1)}, u32[]{:S(2)}, u32[]{:S(2)}) collective-permute-start(f32[64,1536]{1,0:T(8,128)} %get-tuple-element.120), channel_id=1, source_target_pairs={{0,16},{8,24},{16,0},{24,8},{1,17},{9,25},{17,1},{25,9},{2,18},{10... | collective-permute-start | bytes 1179656 | tf_op jit(solution)/shard_map/ppermute | solution.py:385
  32.1 1.6 copy-start.8
  32.1 20.2 %collective-permute-start.13 = (f32[64,1536]{1,0:T(8,128)}, f32[64,1536]{1,0:T(8,128)S(1)}, u32[]{:S(2)}, u32[]{:S(2)}) collective-permute-start(f32[64,1536]{1,0:T(8,128)} %get-tuple-element.121), channel_id=1, source_target_pairs={{0,24},{8,16},{16,8},{24,0},{1,25},{9,17},{17,9},{25,1},{2,26},{10... | collective-permute-start | bytes 1179656 | tf_op jit(solution)/shard_map/ppermute | solution.py:385
  37.2 28.5 %collective-permute-start.14 = (f32[128,1536]{1,0:T(8,128)}, f32[128,1536]{1,0:T(8,128)S(1)}, u32[]{:S(2)}, u32[]{:S(2)}) collective-permute-start(f32[128,1536]{1,0:T(8,128)} %shard_map.56.refs_0_), channel_id=1, source_target_pairs={{0,2},{1,3},{2,6},{3,7},{6,4},{7,5},{4,0},{5,1},{8,10},{9,11},{10,... | collective-permute-start | bytes 2359304 | tf_op jit(solution)/shard_map/ppermute | solution.py:382
  52.2 0.9 copy-start.11
  52.2 1.0 copy-start.12
  55.9 33.6 %collective-permute-start.15 = (f32[128,1536]{1,0:T(8,128)}, f32[128,1536]{1,0:T(8,128)S(1)}, u32[]{:S(2)}, u32[]{:S(2)}) collective-permute-start(f32[128,1536]{1,0:T(8,128)} %shard_map.59.refs_1_), channel_id=1, source_target_pairs={{0,2},{1,3},{2,6},{3,7},{6,4},{7,5},{4,0},{5,1},{8,10},{9,11},{10,... | collective-permute-start | bytes 2359304 | tf_op jit(solution)/shard_map/ppermute | solution.py:382
  65.7 23.8 %copy-start.26 = (f32[128,1536]{1,0:T(8,128)}, f32[128,1536]{1,0:T(8,128)S(1)}, u32[]{:S(2)}) copy-start(f32[128,1536]{1,0:T(8,128)S(1)} %collective-permute-done.14.refs_0_) | copy-start | bytes 2359300
  65.7 24.4 %collective-permute-start.16 = (f32[128,1536]{1,0:T(8,128)S(1)}, f32[128,1536]{1,0:T(8,128)S(1)}, u32[]{:S(2)}, u32[]{:S(2)}) collective-permute-start(f32[128,1536]{1,0:T(8,128)S(1)} %collective-permute-done.14.refs_0_), channel_id=1, source_target_pairs={{0,2},{1,3},{2,6},{3,7},{6,4},{7,5},{4,0},{5,1},{8,10},{9,11},{10,... | collective-permute-start | bytes 2359304 | tf_op jit(solution)/shard_map/ppermute | solution.py:382
  89.5 3.0 %copy-start.31 = (f32[128,1536]{1,0:T(8,128)}, f32[128,1536]{1,0:T(8,128)S(1)}, u32[]{:S(2)}) copy-start(f32[128,1536]{1,0:T(8,128)S(1)} %collective-permute-done.15.refs_1_) | copy-start | bytes 2359300
  89.5 25.8 %collective-permute-start.18 = (f32[128,1536]{1,0:T(8,128)S(1)}, f32[128,1536]{1,0:T(8,128)S(1)}, u32[]{:S(2)}, u32[]{:S(2)}) collective-permute-start(f32[128,1536]{1,0:T(8,128)S(1)} %collective-permute-done.15.refs_1_), channel_id=1, source_target_pairs={{0,2},{1,3},{2,6},{3,7},{6,4},{7,5},{4,0},{5,1},{8,10},{9,11},{10,... | collective-permute-start | bytes 2359304 | tf_op jit(solution)/shard_map/ppermute | solution.py:382
  90.1 25.2 %copy-start.30 = (f32[128,1536]{1,0:T(8,128)}, f32[128,1536]{1,0:T(8,128)S(1)}, u32[]{:S(2)}) copy-start(f32[128,1536]{1,0:T(8,128)S(1)} %collective-permute-done.16.refs_0_) | copy-start | bytes 2359300
  90.1 51.4 %collective-permute-start.17 = (f32[128,1536]{1,0:T(8,128)S(1)}, f32[128,1536]{1,0:T(8,128)S(1)}, u32[]{:S(2)}, u32[]{:S(2)}) collective-permute-start(f32[128,1536]{1,0:T(8,128)S(1)} %collective-permute-done.16.refs_0_), channel_id=1, source_target_pairs={{0,2},{1,3},{2,6},{3,7},{6,4},{7,5},{4,0},{5,1},{8,10},{9,11},{10,... | collective-permute-start | bytes 2359304 | tf_op jit(solution)/shard_map/ppermute | solution.py:382
  115.3 26.3 %copy-start.27 = (f32[128,1536]{1,0:T(8,128)S(1)}, f32[128,1536]{1,0:T(8,128)}, u32[]{:S(2)}) copy-start(f32[128,1536]{1,0:T(8,128)} %get-tuple-element.142) | copy-start | bytes 2359300
  115.3 27.0 %copy-start.28 = (f32[128,1536]{1,0:T(8,128)S(1)}, f32[128,1536]{1,0:T(8,128)}, u32[]{:S(2)}) copy-start(f32[128,1536]{1,0:T(8,128)} %get-tuple-element.137) | copy-start | bytes 2359300
  115.4 3.3 %copy-start.32 = (f32[128,1536]{1,0:T(8,128)}, f32[128,1536]{1,0:T(8,128)S(1)}, u32[]{:S(2)}) copy-start(f32[128,1536]{1,0:T(8,128)S(1)} %collective-permute-done.18.refs_1_) | copy-start | bytes 2359300
  115.4 27.2 %collective-permute-start.20 = (f32[128,1536]{1,0:T(8,128)S(1)}, f32[128,1536]{1,0:T(8,128)S(1)}, u32[]{:S(2)}, u32[]{:S(2)}) collective-permute-start(f32[128,1536]{1,0:T(8,128)S(1)} %collective-permute-done.18.refs_1_), channel_id=1, source_target_pairs={{0,2},{1,3},{2,6},{3,7},{6,4},{7,5},{4,0},{5,1},{8,10},{9,11},{10,... | collective-permute-start | bytes 2359304 | tf_op jit(solution)/shard_map/ppermute | solution.py:382
  141.6 1.0 copy-start.29
  141.6 34.6 %collective-permute-start.23 = (f32[128,1536]{1,0:T(8,128)S(1)}, f32[128,1536]{1,0:T(8,128)S(1)}, u32[]{:S(2)}, u32[]{:S(2)}) collective-permute-start(f32[128,1536]{1,0:T(8,128)S(1)} %copy-done.27), channel_id=1, source_target_pairs={{0,2},{1,3},{2,6},{3,7},{6,4},{7,5},{4,0},{5,1},{8,10},{9,11},{10,... | collective-permute-start | bytes 2359304 | tf_op jit(solution)/shard_map/ppermute | solution.py:382
  142.3 33.7 %copy-start.6 = (f32[128,1536]{1,0:T(8,128)S(1)}, f32[128,1536]{1,0:T(8,128)}, u32[]{:S(2)}) copy-start(f32[128,1536]{1,0:T(8,128)} %get-tuple-element.135) | copy-start | bytes 2359300
  142.3 33.9 %copy-start.5 = (f32[128,1536]{1,0:T(8,128)S(1)}, f32[128,1536]{1,0:T(8,128)}, u32[]{:S(2)}) copy-start(f32[128,1536]{1,0:T(8,128)} %get-tuple-element.136) | copy-start | bytes 2359300
  142.3 33.7 %collective-permute-start.19 = (f32[128,1536]{1,0:T(8,128)S(1)}, f32[128,1536]{1,0:T(8,128)S(1)}, u32[]{:S(2)}, u32[]{:S(2)}) collective-permute-start(f32[128,1536]{1,0:T(8,128)S(1)} %copy-done.28), channel_id=1, source_target_pairs={{0,2},{1,3},{2,6},{3,7},{6,4},{7,5},{4,0},{5,1},{8,10},{9,11},{10,... | collective-permute-start | bytes 2359304 | tf_op jit(solution)/shard_map/ppermute | solution.py:382
  142.6 0.9 copy-start.33
  176.2 21.4 %collective-permute-start.21 = (f32[128,1536]{1,0:T(8,128)S(1)}, f32[128,1536]{1,0:T(8,128)S(1)}, u32[]{:S(2)}, u32[]{:S(2)}) collective-permute-start(f32[128,1536]{1,0:T(8,128)S(1)} %add.26), channel_id=1, source_target_pairs={{0,2},{1,3},{2,6},{3,7},{6,4},{7,5},{4,0},{5,1},{8,10},{9,11},{10,... | collective-permute-start | bytes 2359304 | tf_op jit(solution)/shard_map/ppermute | solution.py:382
  177.2 32.7 %collective-permute-start.24 = (f32[128,1536]{1,0:T(8,128)}, f32[128,1536]{1,0:T(8,128)S(1)}, u32[]{:S(2)}, u32[]{:S(2)}) collective-permute-start(f32[128,1536]{1,0:T(8,128)} %add.29), channel_id=1, source_target_pairs={{0,2},{1,3},{2,6},{3,7},{6,4},{7,5},{4,0},{5,1},{8,10},{9,11},{10,... | collective-permute-start | bytes 2359304 | tf_op jit(solution)/shard_map/ppermute | solution.py:382
  191.8 46.9 %collective-permute-start.26 = (f32[768,1536]{1,0:T(8,128)}, f32[768,1536]{1,0:T(8,128)S(1)}, u32[]{:S(2)}, u32[]{:S(2)}) collective-permute-start(f32[768,1536]{1,0:T(8,128)} %shard_map.65), channel_id=1, source_target_pairs={{0,1},{1,0},{2,3},{3,2},{4,5},{5,4},{6,7},{7,6},{8,9},{9,8},{10,11... | collective-permute-start | bytes 14155784 | tf_op jit(solution)/shard_map/ppermute | solution.py:384
  209.9 4.1 %copy-start.4 = (f32[128,1536]{1,0:T(8,128)S(1)}, f32[128,1536]{1,0:T(8,128)}, u32[]{:S(2)}) copy-start(f32[128,1536]{1,0:T(8,128)} %get-tuple-element.138) | copy-start | bytes 2359300
  209.9 5.1 %copy-start.3 = (f32[128,1536]{1,0:T(8,128)S(1)}, f32[128,1536]{1,0:T(8,128)}, u32[]{:S(2)}) copy-start(f32[128,1536]{1,0:T(8,128)} %get-tuple-element.139) | copy-start | bytes 2359300
  214.0 24.6 %collective-permute-start.27 = (f32[768,1536]{1,0:T(8,128)}, f32[768,1536]{1,0:T(8,128)}, u32[]{:S(2)}, u32[]{:S(2)}) collective-permute-start(f32[768,1536]{1,0:T(8,128)} %shard_map.67), channel_id=1, source_target_pairs={{0,1},{1,0},{2,3},{3,2},{4,5},{5,4},{6,7},{7,6},{8,9},{9,8},{10,11... | collective-permute-start | bytes 14155784 | tf_op jit(solution)/shard_map/ppermute | solution.py:384
  215.0 21.6 %collective-permute-start.22 = (f32[128,1536]{1,0:T(8,128)}, f32[128,1536]{1,0:T(8,128)}, u32[]{:S(2)}, u32[]{:S(2)}) collective-permute-start(f32[128,1536]{1,0:T(8,128)} %add.27), channel_id=1, source_target_pairs={{0,2},{1,3},{2,6},{3,7},{6,4},{7,5},{4,0},{5,1},{8,10},{9,11},{10,... | collective-permute-start | bytes 2359304 | tf_op jit(solution)/shard_map/ppermute | solution.py:382
  215.1 21.5 %copy-start.2 = (f32[128,1536]{1,0:T(8,128)S(1)}, f32[128,1536]{1,0:T(8,128)}, u32[]{:S(2)}) copy-start(f32[128,1536]{1,0:T(8,128)} %get-tuple-element.130) | copy-start | bytes 2359300
  215.1 37.8 %copy-start.1 = (f32[128,1536]{1,0:T(8,128)S(1)}, f32[128,1536]{1,0:T(8,128)}, u32[]{:S(2)}) copy-start(f32[128,1536]{1,0:T(8,128)} %get-tuple-element.131) | copy-start | bytes 2359300
  215.1 37.8 %collective-permute-start.25 = (f32[128,1536]{1,0:T(8,128)S(1)}, f32[128,1536]{1,0:T(8,128)S(1)}, u32[]{:S(2)}, u32[]{:S(2)}) collective-permute-start(f32[128,1536]{1,0:T(8,128)S(1)} %add.30), channel_id=1, source_target_pairs={{0,2},{1,3},{2,6},{3,7},{6,4},{7,5},{4,0},{5,1},{8,10},{9,11},{10,... | collective-permute-start | bytes 2359304 | tf_op jit(solution)/shard_map/ppermute | solution.py:382
  238.7 30.6 %copy-start = (f32[768,1536]{1,0:T(8,128)}, f32[768,1536]{1,0:T(8,128)S(1)}, u32[]{:S(2)}) copy-start(f32[768,1536]{1,0:T(8,128)S(1)} %collective-permute-done.26.refs_5_) | copy-start | bytes 14155780
  242.5 12.3 %collective-permute-start.28 = (f32[64,1536]{1,0:T(8,128)}, f32[64,1536]{1,0:T(8,128)S(1)}, u32[]{:S(2)}, u32[]{:S(2)}) collective-permute-start(f32[64,1536]{1,0:T(8,128)} %get-tuple-element.208), channel_id=1, source_target_pairs={{0,8},{8,0},{16,24},{24,16},{1,9},{9,1},{17,25},{25,17},{2,10},{10... | collective-permute-start | bytes 1179656 | tf_op jit(solution)/shard_map/ppermute | solution.py:385
  243.9 18.7 %collective-permute-start.29 = (f32[64,1536]{1,0:T(8,128)}, f32[64,1536]{1,0:T(8,128)S(1)}, u32[]{:S(2)}, u32[]{:S(2)}) collective-permute-start(f32[64,1536]{1,0:T(8,128)} %get-tuple-element.209), channel_id=1, source_target_pairs={{0,16},{8,24},{16,0},{24,8},{1,17},{9,25},{17,1},{25,9},{2,18},{10... | collective-permute-start | bytes 1179656 | tf_op jit(solution)/shard_map/ppermute | solution.py:385
  243.9 18.7 %collective-permute-start.30 = (f32[64,1536]{1,0:T(8,128)}, f32[64,1536]{1,0:T(8,128)S(1)}, u32[]{:S(2)}, u32[]{:S(2)}) collective-permute-start(f32[64,1536]{1,0:T(8,128)} %get-tuple-element.210), channel_id=1, source_target_pairs={{0,24},{8,16},{16,8},{24,0},{1,25},{9,17},{17,9},{25,1},{2,26},{10... | collective-permute-start | bytes 1179656 | tf_op jit(solution)/shard_map/ppermute | solution.py:385
  254.9 29.7 %copy-start.13 = (f32[64,1536]{1,0:T(8,128)}, f32[64,1536]{1,0:T(8,128)S(1)}, u32[]{:S(2)}) copy-start(f32[64,1536]{1,0:T(8,128)S(1)} %collective-permute-done.28.refs_6_) | copy-start | bytes 1179652
  262.6 22.0 %copy-start.14 = (f32[64,1536]{1,0:T(8,128)}, f32[64,1536]{1,0:T(8,128)S(1)}, u32[]{:S(2)}) copy-start(f32[64,1536]{1,0:T(8,128)S(1)} %collective-permute-done.29.refs_7_) | copy-start | bytes 1179652
  262.6 22.0 %copy-start.15 = (f32[64,1536]{1,0:T(8,128)}, f32[64,1536]{1,0:T(8,128)S(1)}, u32[]{:S(2)}) copy-start(f32[64,1536]{1,0:T(8,128)S(1)} %collective-permute-done.30.refs_8_) | copy-start | bytes 1179652
  265.7 18.9 %collective-permute-start.31 = (f32[64,1536]{1,0:T(8,128)}, f32[64,1536]{1,0:T(8,128)S(1)}, u32[]{:S(2)}, u32[]{:S(2)}) collective-permute-start(f32[64,1536]{1,0:T(8,128)} %get-tuple-element.212), channel_id=1, source_target_pairs={{0,8},{8,0},{16,24},{24,16},{1,9},{9,1},{17,25},{25,17},{2,10},{10... | collective-permute-start | bytes 1179656 | tf_op jit(solution)/shard_map/ppermute | solution.py:385
  266.4 18.2 %collective-permute-start.32 = (f32[64,1536]{1,0:T(8,128)}, f32[64,1536]{1,0:T(8,128)S(1)}, u32[]{:S(2)}, u32[]{:S(2)}) collective-permute-start(f32[64,1536]{1,0:T(8,128)} %get-tuple-element.213), channel_id=1, source_target_pairs={{0,16},{8,24},{16,0},{24,8},{1,17},{9,25},{17,1},{25,9},{2,18},{10... | collective-permute-start | bytes 1179656 | tf_op jit(solution)/shard_map/ppermute | solution.py:385
  267.5 17.1 %collective-permute-start.33 = (f32[64,1536]{1,0:T(8,128)}, f32[64,1536]{1,0:T(8,128)S(1)}, u32[]{:S(2)}, u32[]{:S(2)}) collective-permute-start(f32[64,1536]{1,0:T(8,128)} %get-tuple-element.214), channel_id=1, source_target_pairs={{0,24},{8,16},{16,8},{24,0},{1,25},{9,17},{17,9},{25,1},{2,26},{10... | collective-permute-start | bytes 1179656 | tf_op jit(solution)/shard_map/ppermute | solution.py:385
  284.6 0.9 copy-start.17
  284.7 1.0 copy-start.18
  (4 other events, 2.8 us)

commit v9 on v8

--- a/solution.py
+++ b/solution.py
@@ -77,15 +77,19 @@
 
 
 def pick_kernel(groups, slots, own_count, first, me_ref, *refs):
-    lists, x_ref, outs, sem = refs[:groups], refs[groups], refs[groups + 1:-1], refs[-1]
+    lists, x_ref, outs, (held, sem, sent) = refs[:groups], refs[groups], refs[groups + 1:-3], refs[-3:]
     rows = outs[0].shape[0]
     copies = []
     for k in range(1, groups):
         _, row = asked_row(lists[k], me_ref[0], slots, own_count)
-        copies.append(pltpu.make_async_copy(x_ref.at[row, pl.ds(first, rows)], outs[k - 1], sem.at[k - 1]))
+        copies.append(pltpu.make_async_copy(x_ref.at[row, pl.ds(first, rows)], held.at[k - 1], sem.at[k - 1]))
         copies[-1].start()
-    for copy in copies:
+    leaving = [pltpu.make_async_copy(held.at[n], out, sent.at[n]) for n, out in enumerate(outs)]
+    for copy, leave in zip(copies, leaving):
         copy.wait()
+        leave.start()
+    for leave in leaving:
+        leave.wait()
 
 
 def pick(me, lists, slots, integrals, first, rows):
@@ -94,9 +98,10 @@
     return pl.pallas_call(
         functools.partial(pick_kernel, groups, slots, own_count, first),
         in_specs=[SMEM] * (groups + 1) + [ANY],
-        out_specs=[LOCAL] * (groups - 1),
+        out_specs=[ANY] * (groups - 1),
         out_shape=[jax.ShapeDtypeStruct((rows, aux), jnp.float32)] * (groups - 1),
-        scratch_shapes=[pltpu.SemaphoreType.DMA((groups - 1,))],
+        scratch_shapes=[pltpu.VMEM((groups - 1, rows, aux), jnp.float32)]
+        + [pltpu.SemaphoreType.DMA((groups - 1,))] * 2,
         cost_estimate=cost(0, 8 * rows * aux * groups),
         compiler_params=PARAMS,
     )(me, *lists, integrals)
@@ -146,7 +151,7 @@
 
 
 def back_kernel(groups, slots, own_count, me_ref, lists, share, *refs):
-    outs, sem = refs[:-1], refs[-1]
+    outs, (held, sem, sent) = refs[:-3], refs[-3:]
     rows = outs[0].shape[0]
     copies = []
     for k in range(1, groups):
@@ -154,10 +159,14 @@
         for s in range(slots):
             slot = jnp.where(slot_holder(lists, me_ref[0], s, own_count) == k, s, slot)
         start = pl.multiple_of(slot * rows, rows)
-        copies.append(pltpu.make_async_copy(share.at[pl.ds(start, rows)], outs[k - 1], sem.at[k - 1]))
+        copies.append(pltpu.make_async_copy(share.at[pl.ds(start, rows)], held.at[k - 1], sem.at[k - 1]))
         copies[-1].start()
-    for copy in copies:
+    leaving = [pltpu.make_async_copy(held.at[n], out, sent.at[n]) for n, out in enumerate(outs)]
+    for copy, leave in zip(copies, leaving):
         copy.wait()
+        leave.start()
+    for leave in leaving:
+        leave.wait()
 
 
 def back(me, lists, slots, own_count, share, groups):
@@ -165,9 +174,10 @@
     return pl.pallas_call(
         functools.partial(back_kernel, groups, slots, own_count),
         in_specs=[SMEM, SMEM, ANY],
-        out_specs=[LOCAL] * (groups - 1),
+        out_specs=[ANY] * (groups - 1),
         out_shape=[jax.ShapeDtypeStruct((rows, aux), jnp.float32)] * (groups - 1),
-        scratch_shapes=[pltpu.SemaphoreType.DMA((groups - 1,))],
+        scratch_shapes=[pltpu.VMEM((groups - 1, rows, aux), jnp.float32)]
+        + [pltpu.SemaphoreType.DMA((groups - 1,))] * 2,
         cost_estimate=cost(0, 8 * rows * aux * groups),
         compiler_params=PARAMS,
     )(me, lists, share)

time: 290 us -> 290 us (level)
  transfers between devices with their start and end apart: 34 -> 34, of which waited for: 10 -> 11; matrix products, arithmetic and copies ran while one was open for 4% -> 4% of each run, Pallas kernels for 64% -> 64%
where the time goes in v9:
time: 290 us; the launch traced here: 289 us
  Pallas kernels  191 us (66%)
  waiting for transfers between devices  40.7 us (14%)
  starting transfers between devices  39.9 us (14%)
  local copies, waits for them, and re-layouts  10.2 us (4%)
  other arithmetic  7.22 us (2%)
    pallas_call x4, Pallas kernels, unit(): pl.pallas_call(functools.partial(unit_kernel, steps), grid=(2 * steps,),...  91.3 us
    pallas_call x4, Pallas kernels, forward(): pl.pallas_call(functools.partial(forward_kernel, len(units), spans, parti...  56.4 us
    ppermute x15, waiting for transfers between devices, body(): along = lambda x, s: lax.ppermute(x, 'blk', ring(s))  27.3 us
    ppermute x15, starting transfers between devices, body(): along = lambda x, s: lax.ppermute(x, 'blk', ring(s))  23.4 us
    pallas_call x2, Pallas kernels, split_rows(): pl.pallas_call(split_kernel, grid=(rows // step,), in_specs=[spec], out_s...  17.2 us
    ppermute x15, starting transfers between devices, body(): lax.ppermute(x, 'grp', [(g, g ^ k) for g in range(groups)])  15.9 us
    ppermute x15, waiting for transfers between devices, body(): lax.ppermute(x, 'grp', [(g, g ^ k) for g in range(groups)])  12.4 us
    pallas_call x2, Pallas kernels, back(): pl.pallas_call(functools.partial(back_kernel, groups, slots, own_count),...  6.54 us
  transfers between devices with their start and end apart: 34, of which 11 were waited for; matrix products, arithmetic and copies ran while one was open for 4% of the time, Pallas kernels for 64%

profile of v9, /device:TPU:0, one launch (start us, length us, event | category | flops | bytes accessed | tf_op | source)
XLA Modules:
  0.0 289.4 jit_solution(18042178066317311197)
XLA Ops:
  0.5 0.7 pad_add_fusion.1.refs_0_.lists
  1.2 2.5 collective-permute-start
  3.7 1.5 collective-permute-start.1
  5.2 2.0 collective-permute-start.7
  7.3 0.7 stack.47
  8.1 1.5 collective-permute-done.2.refs_3_
  10.2 3.1 %shard_map.55 = (f32[64,1536]{1,0:T(8,128)}, f32[64,1536]{1,0:T(8,128)}, f32[64,1536]{1,0:T(8,128)}) custom-call(s32[1]{0:T(128)} %bitcast.me_ref, s32[14]{0:T(128)} %copy-done.19, s32[14]{0:T(128)} %copy-done.20, s32[14]{0:T(128)} %copy-done.21, s32[14]{0:T(128)} %copy-done.22, f32[12,128,1536]{2,1,0:T(8,128)} %x_ref.3), custom_call_target="tpu_custom_call" | custom-call | bytes 3145728 | tf_op jit(solution)/shard_map/pallas_call | solution.py:98
  13.3 0.8 collective-permute-start.3
  14.1 0.8 collective-permute-start.4
  14.9 2.0 collective-permute-start.5
  16.9 0.7 pad_add_fusion
  18.0 3.6 %collective-permute-start.8 = (f32[128]{0:T(128)S(1)}, f32[128]{0:T(128)S(1)}, u32[]{:S(2)}, u32[]{:S(2)}) collective-permute-start(f32[128]{0:T(128)S(1)} %copy-done.25), channel_id=1, source_target_pairs={{0,6},{1,7},{2,4},{3,5},{6,0},{7,1},{4,2},{5,3},{8,14},{9,15},{10,... | collective-permute-start | bytes 1544 | tf_op jit(solution)/shard_map/ppermute | solution.py:392
  21.8 1.6 collective-permute-done.8
  23.4 0.8 collective-permute-start.9
  24.3 2.8 shard_map.58
  27.3 1.0 collective-permute-done.6
  28.4 1.0 collective-permute-start.11
  29.6 2.7 collective-permute-done.4.refs_1_
  32.4 0.8 copy-done.8
  33.1 0.7 copy-done.9
  33.9 2.7 shard_map.56.refs_0_
  36.6 2.6 collective-permute-start.14
  39.3 0.8 unstack.34.col_ref
  40.8 0.8 unstack.33.col_ref
  41.6 0.8 unstack.32.col_ref
  42.4 0.8 unstack.35.col_ref
  43.2 8.6 %shard_map.57 = (bf16[1536,1536]{1,0:T(8,128)(2,1)}, bf16[1536,1536]{1,0:T(8,128)(2,1)}) custom-call(f32[1536,1536]{1,0:T(8,128)} %bitcast.13), custom_call_target="tpu_custom_call" | custom-call | flops 4718592 | bytes 18874368 | tf_op jit(solution)/shard_map/pallas_call | solution.py:54
  51.9 0.7 copy-done.10
  52.8 2.7 shard_map.59.refs_1_
  55.6 1.8 collective-permute-start.15
  57.4 8.6 %shard_map.60 = (bf16[1536,1536]{1,0:T(8,128)(2,1)}, bf16[1536,1536]{1,0:T(8,128)(2,1)}) custom-call(f32[1536,1536]{1,0:T(8,128)} %collective-permute-done.10.x_ref), custom_call_target="tpu_custom_call" | custom-call | flops 4718592 | bytes 18874368 | tf_op jit(solution)/shard_map/pallas_call | solution.py:54
  66.2 22.8 %shard_map.61 = (bf16[256,3072]{1,0:T(8,128)(2,1)}, bf16[256,3072]{1,0:T(8,128)(2,1)}, bf16[256,1536]{1,0:T(8,128)(2,1)}, bf16[256,1536]{1,0:T(8,128)(2,1)}, f32[128,1536]{1,0:T(8,128)}, /*index=5*/f32[128,1536]{1,0:T(8,128)}) custom-call(bf16[1536,1536]{1,0:T(8,128)(2,1)} %get-tuple-element.117.own_high, bf16[1536,1536]{1,0:T(8,128)(2,1)} %get-tuple-element.118.own_low, ...), custom_call_target="tpu_custom_call" | custom-call | flops 14495514624 | bytes 25165824 | tf_op jit(solution)/shard_map/pallas_call | solution.py:295
  90.1 2.5 collective-permute-start.17
  92.6 22.8 %shard_map.62 = (bf16[256,3072]{1,0:T(8,128)(2,1)}, bf16[256,3072]{1,0:T(8,128)(2,1)}, bf16[256,1536]{1,0:T(8,128)(2,1)}, bf16[256,1536]{1,0:T(8,128)(2,1)}, f32[128,1536]{1,0:T(8,128)}, /*index=5*/f32[128,1536]{1,0:T(8,128)}) custom-call(bf16[1536,1536]{1,0:T(8,128)(2,1)} %get-tuple-element.117.own_high, bf16[1536,1536]{1,0:T(8,128)(2,1)} %get-tuple-element.118.own_low, ...), custom_call_target="tpu_custom_call" | custom-call | flops 14495514624 | bytes 25165824 | tf_op jit(solution)/shard_map/pallas_call | solution.py:295
  115.5 3.6 %collective-permute-start.20 = (f32[128,1536]{1,0:T(8,128)S(1)}, f32[128,1536]{1,0:T(8,128)S(1)}, u32[]{:S(2)}, u32[]{:S(2)}) collective-permute-start(f32[128,1536]{1,0:T(8,128)S(1)} %collective-permute-done.18.refs_1_), channel_id=1, source_target_pairs={{0,2},{1,3},{2,6},{3,7},{6,4},{7,5},{4,0},{5,1},{8,10},{9,11},{10,... | collective-permute-start | bytes 2359304 | tf_op jit(solution)/shard_map/ppermute | solution.py:392
  119.1 22.9 %shard_map.63 = (bf16[256,3072]{1,0:T(8,128)(2,1)}, bf16[256,3072]{1,0:T(8,128)(2,1)}, bf16[256,1536]{1,0:T(8,128)(2,1)}, bf16[256,1536]{1,0:T(8,128)(2,1)}, f32[128,1536]{1,0:T(8,128)}, /*index=5*/f32[128,1536]{1,0:T(8,128)}) custom-call(bf16[1536,1536]{1,0:T(8,128)(2,1)} %get-tuple-element.117.own_high, bf16[1536,1536]{1,0:T(8,128)(2,1)} %get-tuple-element.118.own_low, ...), custom_call_target="tpu_custom_call" | custom-call | flops 14495514624 | bytes 25165824 | tf_op jit(solution)/shard_map/pallas_call | solution.py:295
  142.0 0.7 collective-permute-start.23
  143.0 0.9 copy-done.33
  143.9 22.8 %shard_map.64 = (bf16[256,3072]{1,0:T(8,128)(2,1)}, bf16[256,3072]{1,0:T(8,128)(2,1)}, bf16[256,1536]{1,0:T(8,128)(2,1)}, bf16[256,1536]{1,0:T(8,128)(2,1)}, f32[128,1536]{1,0:T(8,128)}, /*index=5*/f32[128,1536]{1,0:T(8,128)}) custom-call(bf16[1536,1536]{1,0:T(8,128)(2,1)} %get-tuple-element.117.own_high, bf16[1536,1536]{1,0:T(8,128)(2,1)} %get-tuple-element.118.own_low, ...), custom_call_target="tpu_custom_call" | custom-call | flops 14495514624 | bytes 25165824 | tf_op jit(solution)/shard_map/pallas_call | solution.py:295
  166.8 9.7 %collective-permute-done.19 = f32[128,1536]{1,0:T(8,128)S(1)} collective-permute-done((f32[128,1536]{1,0:T(8,128)S(1)}, f32[128,1536]{1,0:T(8,128)S(1)}, u32[]{:S(2)}, u32[]{:S(2)}) %collective-permute-start.19) | collective-permute-done | bytes 786464 | tf_op jit(solution)/shard_map/ppermute | solution.py:392
  177.0 1.0 add.29
  178.0 1.6 collective-permute-start.24
  179.6 12.5 %shard_map.65 = f32[768,1536]{1,0:T(8,128)} custom-call(bf16[256,3072]{1,0:T(8,128)(2,1)} %get-tuple-element.195.refs_0_, bf16[256,3072]{1,0:T(8,128)(2,1)} %get-tuple-element.196.refs_1_, bf16[256,1536]{1,0:T(8,128)(2,1)} %get-tuple-element.197.refs_2_, bf16[256,1536]{1,0:T(8,128)(2,1)} %get-tuple-element.198.refs_3_, ...), custom_call_target="tpu_custom_call" | custom-call | flops 7247757312 | bytes 9437184 | tf_op jit(solution)/shard_map/pallas_call | solution.py:341
  192.2 5.9 %collective-permute-done.21 = f32[128,1536]{1,0:T(8,128)S(1)} collective-permute-done((f32[128,1536]{1,0:T(8,128)S(1)}, f32[128,1536]{1,0:T(8,128)S(1)}, u32[]{:S(2)}, u32[]{:S(2)}) %collective-permute-start.21) | collective-permute-done | bytes 786464 | tf_op jit(solution)/shard_map/ppermute | solution.py:392
  198.0 12.3 %shard_map.66.known = f32[768,1536]{1,0:T(8,128)} custom-call(bf16[256,3072]{1,0:T(8,128)(2,1)} %get-tuple-element.195.refs_0_, bf16[256,3072]{1,0:T(8,128)(2,1)} %get-tuple-element.196.refs_1_, bf16[256,1536]{1,0:T(8,128)(2,1)} %get-tuple-element.197.refs_2_, bf16[256,1536]{1,0:T(8,128)(2,1)} %get-tuple-element.198.refs_3_, ...), custom_call_target="tpu_custom_call" | custom-call | flops 7247757312 | bytes 9437184 | tf_op jit(solution)/shard_map/pallas_call | solution.py:341
  210.4 4.1 %shard_map.67 = f32[768,1536]{1,0:T(8,128)} custom-call(bf16[256,3072]{1,0:T(8,128)(2,1)} %get-tuple-element.191.refs_12_.t_high.refs_0_, bf16[256,3072]{1,0:T(8,128)(2,1)} %get-tuple-element.192.refs_13_.t_low.refs_1_, bf16[256,1536]{1,0:T(8,128)(2,1)} %get-tuple-element.193.refs_14_.r_high.refs_2_, ...), custom_call_target="tpu_custom_call", output_to_operand_aliasing={{}: (4, {})} | custom-call | flops 1811939328 | bytes 9437184 | tf_op jit(solution)/shard_map/pallas_call | solution.py:364
  214.4 1.0 add.27
  215.5 2.7 collective-permute-start.25
  218.2 16.2 %shard_map.68.refs_4_ = f32[1536,1536]{1,0:T(8,128)} custom-call(bf16[256,3072]{1,0:T(8,128)(2,1)} %get-tuple-element.195.refs_0_, bf16[256,3072]{1,0:T(8,128)(2,1)} %get-tuple-element.196.refs_1_, bf16[256,1536]{1,0:T(8,128)(2,1)} %get-tuple-element.197.refs_2_, bf16[256,1536]{1,0:T(8,128)(2,1)} %get-tuple-element.198.refs_3_, ...), custom_call_target="tpu_custom_call" | custom-call | flops 10871635968 | bytes 18874368 | tf_op jit(solution)/shard_map/pallas_call | solution.py:341
  234.5 2.5 collective-permute-done.22
  237.0 2.1 add.28.share.refs_4_
  239.1 3.6 %shard_map.69 = (f32[64,1536]{1,0:T(8,128)}, f32[64,1536]{1,0:T(8,128)}, f32[64,1536]{1,0:T(8,128)}) custom-call(s32[1]{0:T(128)} %bitcast.me_ref, s32[14]{0:T(128)} %copy-done.19, f32[128,1536]{1,0:T(8,128)} %add.28.share.refs_4_), custom_call_target="tpu_custom_call" | custom-call | bytes 3145728 | tf_op jit(solution)/shard_map/pallas_call | solution.py:174
  242.7 1.0 collective-permute-start.28
  243.7 2.6 collective-permute-start.30
  246.3 7.1 %collective-permute-done.25 = f32[128,1536]{1,0:T(8,128)S(1)} collective-permute-done((f32[128,1536]{1,0:T(8,128)S(1)}, f32[128,1536]{1,0:T(8,128)S(1)}, u32[]{:S(2)}, u32[]{:S(2)}) %collective-permute-start.25) | collective-permute-done | bytes 786464 | tf_op jit(solution)/shard_map/ppermute | solution.py:392
  253.3 1.0 add.31.share.refs_5_
  254.3 0.7 collective-permute-done.28.refs_6_
  255.0 7.4 %collective-permute-done.29.refs_7_ = f32[64,1536]{1,0:T(8,128)S(1)} collective-permute-done((f32[64,1536]{1,0:T(8,128)}, f32[64,1536]{1,0:T(8,128)S(1)}, u32[]{:S(2)}, u32[]{:S(2)}) %collective-permute-start.29) | collective-permute-done | bytes 393248 | tf_op jit(solution)/shard_map/ppermute | solution.py:395
  262.4 2.9 %shard_map.70 = (f32[64,1536]{1,0:T(8,128)}, f32[64,1536]{1,0:T(8,128)}, f32[64,1536]{1,0:T(8,128)}) custom-call(s32[1]{0:T(128)} %bitcast.me_ref, s32[14]{0:T(128)} %copy-done.19, f32[128,1536]{1,0:T(8,128)} %add.31.share.refs_5_), custom_call_target="tpu_custom_call" | custom-call | bytes 3145728 | tf_op jit(solution)/shard_map/pallas_call | solution.py:174
  265.4 1.3 collective-permute-start.31
  267.2 1.7 collective-permute-start.33
  268.9 15.3 %shard_map.71 = f32[1536,1536]{1,0:T(8,128)} custom-call(bf16[256,3072]{1,0:T(8,128)(2,1)} %get-tuple-element.191.refs_12_.t_high.refs_0_, bf16[256,3072]{1,0:T(8,128)(2,1)} %get-tuple-element.192.refs_13_.t_low.refs_1_, bf16[256,1536]{1,0:T(8,128)(2,1)} %get-tuple-element.193.refs_14_.r_high.refs_2_, ...), custom_call_target="tpu_custom_call" | custom-call | flops 3623878656 | bytes 18874368 | tf_op jit(solution)/shard_map/pallas_call | solution.py:341
  284.3 0.7 copy-done.16
  285.3 3.9 %shard_map.72 = f32[12,128,1536]{2,1,0:T(8,128)} custom-call(s32[1]{0:T(128)} %bitcast.me_ref, s32[14]{0:T(128)} %copy-done.19, s32[14]{0:T(128)} %copy-done.20, s32[14]{0:T(128)} %copy-done.21, s32[14]{0:T(128)} %copy-done.22, f32[128,1536]{1,0:T(8,128)} %add.28.share.refs_4_, f32[128,1536]{1,0:T(8,128)} %add.31.share.refs_5_, ...), custom_call_target="tpu_custom_call", output_to_operand_aliasing={{}: (13, {})} | custom-call | bytes 9437184 | tf_op jit(solution)/shard_map/pallas_call | solution.py:237
  (120 shorter events, 6.6 us)
Async XLA Ops:
  0.0 51.9 %collective-permute-start.10 = (f32[1536,1536]{1,0:T(8,128)}, f32[1536,1536]{1,0:T(8,128)}, u32[]{:S(2)}, u32[]{:S(2)}) collective-permute-start(f32[1536,1536]{1,0:T(8,128)} %bitcast.12), channel_id=1, source_target_pairs={{0,1},{1,0},{2,3},{3,2},{4,5},{5,4},{6,7},{7,6},{8,9},{9,8},{10,11... | collective-permute-start | bytes 28311560 | tf_op jit(solution)/shard_map/ppermute | solution.py:394
  1.2 8.5 %copy-start.19 = (s32[14]{0:T(128)}, s32[14]{0:T(128)S(1)}, u32[]{:S(2)}) copy-start(s32[14]{0:T(128)S(1)} %pad_add_fusion.1.refs_0_.lists) | copy-start | bytes 172
  1.2 6.9 %collective-permute-start = (s32[14]{0:T(128)S(1)}, s32[14]{0:T(128)S(1)}, u32[]{:S(2)}, u32[]{:S(2)}) collective-permute-start(s32[14]{0:T(128)S(1)} %pad_add_fusion.1.refs_0_.lists), channel_id=1, source_target_pairs={{0,8},{8,0},{16,24},{24,16},{1,9},{9,1},{17,25},{25,17},{2,10},{10... | collective-permute-start | bytes 176 | tf_op jit(solution)/shard_map/ppermute | solution.py:395
  3.7 4.4 %collective-permute-start.1 = (s32[14]{0:T(128)S(1)}, s32[14]{0:T(128)S(1)}, u32[]{:S(2)}, u32[]{:S(2)}) collective-permute-start(s32[14]{0:T(128)S(1)} %pad_add_fusion.1.refs_0_.lists), channel_id=1, source_target_pairs={{0,16},{8,24},{16,0},{24,8},{1,17},{9,25},{17,1},{25,9},{2,18},{10... | collective-permute-start | bytes 176 | tf_op jit(solution)/shard_map/ppermute | solution.py:395
  5.2 4.4 %collective-permute-start.2 = (s32[14]{0:T(128)S(1)}, s32[14]{0:T(128)S(1)}, u32[]{:S(2)}, u32[]{:S(2)}) collective-permute-start(s32[14]{0:T(128)S(1)} %pad_add_fusion.1.refs_0_.lists), channel_id=1, source_target_pairs={{0,24},{8,16},{16,8},{24,0},{1,25},{9,17},{17,9},{25,1},{2,26},{10... | collective-permute-start | bytes 176 | tf_op jit(solution)/shard_map/ppermute | solution.py:395
  5.2 12.8 %collective-permute-start.7 = (f32[128]{0:T(128)}, f32[128]{0:T(128)S(1)}, u32[]{:S(2)}, u32[]{:S(2)}) collective-permute-start(f32[128]{0:T(128)} %param.9), channel_id=1, source_target_pairs={{0,2},{1,3},{2,6},{3,7},{6,4},{7,5},{4,0},{5,1},{8,10},{9,11},{10,... | collective-permute-start | bytes 1544 | tf_op jit(solution)/shard_map/ppermute | solution.py:392
  8.1 1.6 copy-start.20
  8.1 1.6 copy-start.21
  10.2 7.6 %copy-start.23 = (f32[48]{0:T(128)S(1)}, f32[48]{0:T(128)}, u32[]{:S(2)}) copy-start(f32[48]{0:T(128)} %param.8) | copy-start | bytes 580
  10.2 7.8 %copy-start.25 = (f32[128]{0:T(128)S(1)}, f32[128]{0:T(128)}, u32[]{:S(2)}) copy-start(f32[128]{0:T(128)} %param.9) | copy-start | bytes 1540
  10.2 11.5 %copy-start.24 = (s32[1,2]{1,0:T(1,128)S(1)}, s32[1,2]{1,0:T(1,128)}, u32[]{:S(2)}) copy-start(s32[1,2]{1,0:T(1,128)} %param.6) | copy-start | bytes 28
  13.3 16.0 %collective-permute-start.3 = (f32[64,1536]{1,0:T(8,128)}, f32[64,1536]{1,0:T(8,128)S(1)}, u32[]{:S(2)}, u32[]{:S(2)}) collective-permute-start(f32[64,1536]{1,0:T(8,128)} %get-tuple-element.110), channel_id=1, source_target_pairs={{0,8},{8,0},{16,24},{24,16},{1,9},{9,1},{17,25},{25,17},{2,10},{10... | collective-permute-start | bytes 1179656 | tf_op jit(solution)/shard_map/ppermute | solution.py:395
  14.1 18.3 %collective-permute-start.4 = (f32[64,1536]{1,0:T(8,128)}, f32[64,1536]{1,0:T(8,128)S(1)}, u32[]{:S(2)}, u32[]{:S(2)}) collective-permute-start(f32[64,1536]{1,0:T(8,128)} %get-tuple-element.111), channel_id=1, source_target_pairs={{0,16},{8,24},{16,0},{24,8},{1,17},{9,25},{17,1},{25,9},{2,18},{10... | collective-permute-start | bytes 1179656 | tf_op jit(solution)/shard_map/ppermute | solution.py:395
  14.9 17.5 %collective-permute-start.5 = (f32[64,1536]{1,0:T(8,128)}, f32[64,1536]{1,0:T(8,128)S(1)}, u32[]{:S(2)}, u32[]{:S(2)}) collective-permute-start(f32[64,1536]{1,0:T(8,128)} %get-tuple-element.112), channel_id=1, source_target_pairs={{0,24},{8,16},{16,8},{24,0},{1,25},{9,17},{17,9},{25,1},{2,26},{10... | collective-permute-start | bytes 1179656 | tf_op jit(solution)/shard_map/ppermute | solution.py:395
  18.0 5.4 %collective-permute-start.8 = (f32[128]{0:T(128)S(1)}, f32[128]{0:T(128)S(1)}, u32[]{:S(2)}, u32[]{:S(2)}) collective-permute-start(f32[128]{0:T(128)S(1)} %copy-done.25), channel_id=1, source_target_pairs={{0,6},{1,7},{2,4},{3,5},{6,0},{7,1},{4,2},{5,3},{8,14},{9,15},{10,... | collective-permute-start | bytes 1544 | tf_op jit(solution)/shard_map/ppermute | solution.py:392
  23.4 3.9 %collective-permute-start.9 = (f32[128]{0:T(128)S(1)}, f32[128]{0:T(128)S(1)}, u32[]{:S(2)}, u32[]{:S(2)}) collective-permute-start(f32[128]{0:T(128)S(1)} %copy-done.25), channel_id=1, source_target_pairs={{0,4},{1,5},{2,0},{3,1},{6,2},{7,3},{4,6},{5,7},{8,12},{9,13},{10,... | collective-permute-start | bytes 1544 | tf_op jit(solution)/shard_map/ppermute | solution.py:392
  27.3 1.1 collective-permute-start.6
  28.4 23.4 %collective-permute-start.11 = (f32[64,1536]{1,0:T(8,128)}, f32[64,1536]{1,0:T(8,128)S(1)}, u32[]{:S(2)}, u32[]{:S(2)}) collective-permute-start(f32[64,1536]{1,0:T(8,128)} %get-tuple-element.119), channel_id=1, source_target_pairs={{0,8},{8,0},{16,24},{24,16},{1,9},{9,1},{17,25},{25,17},{2,10},{10... | collective-permute-start | bytes 1179656 | tf_op jit(solution)/shard_map/ppermute | solution.py:395
  29.4 3.0 %copy-start.7 = (f32[64,1536]{1,0:T(8,128)}, f32[64,1536]{1,0:T(8,128)S(1)}, u32[]{:S(2)}) copy-start(f32[64,1536]{1,0:T(8,128)S(1)} %collective-permute-done.3.refs_0_) | copy-start | bytes 1179652
  29.4 22.5 %collective-permute-start.12 = (f32[64,1536]{1,0:T(8,128)}, f32[64,1536]{1,0:T(8,128)S(1)}, u32[]{:S(2)}, u32[]{:S(2)}) collective-permute-start(f32[64,1536]{1,0:T(8,128)} %get-tuple-element.120), channel_id=1, source_target_pairs={{0,16},{8,24},{16,0},{24,8},{1,17},{9,25},{17,1},{25,9},{2,18},{10... | collective-permute-start | bytes 1179656 | tf_op jit(solution)/shard_map/ppermute | solution.py:395
  32.3 0.8 copy-start.8
  32.3 19.5 %collective-permute-start.13 = (f32[64,1536]{1,0:T(8,128)}, f32[64,1536]{1,0:T(8,128)S(1)}, u32[]{:S(2)}, u32[]{:S(2)}) collective-permute-start(f32[64,1536]{1,0:T(8,128)} %get-tuple-element.121), channel_id=1, source_target_pairs={{0,24},{8,16},{16,8},{24,0},{1,25},{9,17},{17,9},{25,1},{2,26},{10... | collective-permute-start | bytes 1179656 | tf_op jit(solution)/shard_map/ppermute | solution.py:395
  36.6 29.4 %collective-permute-start.14 = (f32[128,1536]{1,0:T(8,128)}, f32[128,1536]{1,0:T(8,128)S(1)}, u32[]{:S(2)}, u32[]{:S(2)}) collective-permute-start(f32[128,1536]{1,0:T(8,128)} %shard_map.56.refs_0_), channel_id=1, source_target_pairs={{0,2},{1,3},{2,6},{3,7},{6,4},{7,5},{4,0},{5,1},{8,10},{9,11},{10,... | collective-permute-start | bytes 2359304 | tf_op jit(solution)/shard_map/ppermute | solution.py:392
  51.8 0.9 copy-start.11
  51.9 1.0 copy-start.12
  55.6 33.5 %collective-permute-start.15 = (f32[128,1536]{1,0:T(8,128)}, f32[128,1536]{1,0:T(8,128)S(1)}, u32[]{:S(2)}, u32[]{:S(2)}) collective-permute-start(f32[128,1536]{1,0:T(8,128)} %shard_map.59.refs_1_), channel_id=1, source_target_pairs={{0,2},{1,3},{2,6},{3,7},{6,4},{7,5},{4,0},{5,1},{8,10},{9,11},{10,... | collective-permute-start | bytes 2359304 | tf_op jit(solution)/shard_map/ppermute | solution.py:392
  66.0 23.0 %copy-start.26 = (f32[128,1536]{1,0:T(8,128)}, f32[128,1536]{1,0:T(8,128)S(1)}, u32[]{:S(2)}) copy-start(f32[128,1536]{1,0:T(8,128)S(1)} %collective-permute-done.14.refs_0_) | copy-start | bytes 2359300
  66.0 24.1 %collective-permute-start.16 = (f32[128,1536]{1,0:T(8,128)S(1)}, f32[128,1536]{1,0:T(8,128)S(1)}, u32[]{:S(2)}, u32[]{:S(2)}) collective-permute-start(f32[128,1536]{1,0:T(8,128)S(1)} %collective-permute-done.14.refs_0_), channel_id=1, source_target_pairs={{0,2},{1,3},{2,6},{3,7},{6,4},{7,5},{4,0},{5,1},{8,10},{9,11},{10,... | collective-permute-start | bytes 2359304 | tf_op jit(solution)/shard_map/ppermute | solution.py:392
  89.1 3.6 %copy-start.31 = (f32[128,1536]{1,0:T(8,128)}, f32[128,1536]{1,0:T(8,128)S(1)}, u32[]{:S(2)}) copy-start(f32[128,1536]{1,0:T(8,128)S(1)} %collective-permute-done.15.refs_1_) | copy-start | bytes 2359300
  89.1 26.4 %collective-permute-start.18 = (f32[128,1536]{1,0:T(8,128)S(1)}, f32[128,1536]{1,0:T(8,128)S(1)}, u32[]{:S(2)}, u32[]{:S(2)}) collective-permute-start(f32[128,1536]{1,0:T(8,128)S(1)} %collective-permute-done.15.refs_1_), channel_id=1, source_target_pairs={{0,2},{1,3},{2,6},{3,7},{6,4},{7,5},{4,0},{5,1},{8,10},{9,11},{10,... | collective-permute-start | bytes 2359304 | tf_op jit(solution)/shard_map/ppermute | solution.py:392
  90.1 25.3 %copy-start.30 = (f32[128,1536]{1,0:T(8,128)}, f32[128,1536]{1,0:T(8,128)S(1)}, u32[]{:S(2)}) copy-start(f32[128,1536]{1,0:T(8,128)S(1)} %collective-permute-done.16.refs_0_) | copy-start | bytes 2359300
  90.1 51.9 %collective-permute-start.17 = (f32[128,1536]{1,0:T(8,128)S(1)}, f32[128,1536]{1,0:T(8,128)S(1)}, u32[]{:S(2)}, u32[]{:S(2)}) collective-permute-start(f32[128,1536]{1,0:T(8,128)S(1)} %collective-permute-done.16.refs_0_), channel_id=1, source_target_pairs={{0,2},{1,3},{2,6},{3,7},{6,4},{7,5},{4,0},{5,1},{8,10},{9,11},{10,... | collective-permute-start | bytes 2359304 | tf_op jit(solution)/shard_map/ppermute | solution.py:392
  115.5 26.6 %copy-start.27 = (f32[128,1536]{1,0:T(8,128)S(1)}, f32[128,1536]{1,0:T(8,128)}, u32[]{:S(2)}) copy-start(f32[128,1536]{1,0:T(8,128)} %get-tuple-element.142) | copy-start | bytes 2359300
  115.5 27.3 %copy-start.28 = (f32[128,1536]{1,0:T(8,128)S(1)}, f32[128,1536]{1,0:T(8,128)}, u32[]{:S(2)}) copy-start(f32[128,1536]{1,0:T(8,128)} %get-tuple-element.137) | copy-start | bytes 2359300
  115.5 3.6 %copy-start.32 = (f32[128,1536]{1,0:T(8,128)}, f32[128,1536]{1,0:T(8,128)S(1)}, u32[]{:S(2)}) copy-start(f32[128,1536]{1,0:T(8,128)S(1)} %collective-permute-done.18.refs_1_) | copy-start | bytes 2359300
  115.5 27.5 %collective-permute-start.20 = (f32[128,1536]{1,0:T(8,128)S(1)}, f32[128,1536]{1,0:T(8,128)S(1)}, u32[]{:S(2)}, u32[]{:S(2)}) collective-permute-start(f32[128,1536]{1,0:T(8,128)S(1)} %collective-permute-done.18.refs_1_), channel_id=1, source_target_pairs={{0,2},{1,3},{2,6},{3,7},{6,4},{7,5},{4,0},{5,1},{8,10},{9,11},{10,... | collective-permute-start | bytes 2359304 | tf_op jit(solution)/shard_map/ppermute | solution.py:392
  142.0 1.0 copy-start.29
  142.0 35.0 %collective-permute-start.23 = (f32[128,1536]{1,0:T(8,128)S(1)}, f32[128,1536]{1,0:T(8,128)S(1)}, u32[]{:S(2)}, u32[]{:S(2)}) collective-permute-start(f32[128,1536]{1,0:T(8,128)S(1)} %copy-done.27), channel_id=1, source_target_pairs={{0,2},{1,3},{2,6},{3,7},{6,4},{7,5},{4,0},{5,1},{8,10},{9,11},{10,... | collective-permute-start | bytes 2359304 | tf_op jit(solution)/shard_map/ppermute | solution.py:392
  142.7 33.7 %copy-start.6 = (f32[128,1536]{1,0:T(8,128)S(1)}, f32[128,1536]{1,0:T(8,128)}, u32[]{:S(2)}) copy-start(f32[128,1536]{1,0:T(8,128)} %get-tuple-element.135) | copy-start | bytes 2359300
  142.7 34.2 %copy-start.5 = (f32[128,1536]{1,0:T(8,128)S(1)}, f32[128,1536]{1,0:T(8,128)}, u32[]{:S(2)}) copy-start(f32[128,1536]{1,0:T(8,128)} %get-tuple-element.136) | copy-start | bytes 2359300
  142.7 33.7 %collective-permute-start.19 = (f32[128,1536]{1,0:T(8,128)S(1)}, f32[128,1536]{1,0:T(8,128)S(1)}, u32[]{:S(2)}, u32[]{:S(2)}) collective-permute-start(f32[128,1536]{1,0:T(8,128)S(1)} %copy-done.28), channel_id=1, source_target_pairs={{0,2},{1,3},{2,6},{3,7},{6,4},{7,5},{4,0},{5,1},{8,10},{9,11},{10,... | collective-permute-start | bytes 2359304 | tf_op jit(solution)/shard_map/ppermute | solution.py:392
  143.0 0.9 copy-start.33
  176.6 21.4 %collective-permute-start.21 = (f32[128,1536]{1,0:T(8,128)S(1)}, f32[128,1536]{1,0:T(8,128)S(1)}, u32[]{:S(2)}, u32[]{:S(2)}) collective-permute-start(f32[128,1536]{1,0:T(8,128)S(1)} %add.26), channel_id=1, source_target_pairs={{0,2},{1,3},{2,6},{3,7},{6,4},{7,5},{4,0},{5,1},{8,10},{9,11},{10,... | collective-permute-start | bytes 2359304 | tf_op jit(solution)/shard_map/ppermute | solution.py:392
  178.0 32.4 %collective-permute-start.24 = (f32[128,1536]{1,0:T(8,128)}, f32[128,1536]{1,0:T(8,128)S(1)}, u32[]{:S(2)}, u32[]{:S(2)}) collective-permute-start(f32[128,1536]{1,0:T(8,128)} %add.29), channel_id=1, source_target_pairs={{0,2},{1,3},{2,6},{3,7},{6,4},{7,5},{4,0},{5,1},{8,10},{9,11},{10,... | collective-permute-start | bytes 2359304 | tf_op jit(solution)/shard_map/ppermute | solution.py:392
  192.1 47.0 %collective-permute-start.26 = (f32[768,1536]{1,0:T(8,128)}, f32[768,1536]{1,0:T(8,128)S(1)}, u32[]{:S(2)}, u32[]{:S(2)}) collective-permute-start(f32[768,1536]{1,0:T(8,128)} %shard_map.65), channel_id=1, source_target_pairs={{0,1},{1,0},{2,3},{3,2},{4,5},{5,4},{6,7},{7,6},{8,9},{9,8},{10,11... | collective-permute-start | bytes 14155784 | tf_op jit(solution)/shard_map/ppermute | solution.py:394
  210.3 4.1 %copy-start.4 = (f32[128,1536]{1,0:T(8,128)S(1)}, f32[128,1536]{1,0:T(8,128)}, u32[]{:S(2)}) copy-start(f32[128,1536]{1,0:T(8,128)} %get-tuple-element.138) | copy-start | bytes 2359300
  210.3 5.1 %copy-start.3 = (f32[128,1536]{1,0:T(8,128)S(1)}, f32[128,1536]{1,0:T(8,128)}, u32[]{:S(2)}) copy-start(f32[128,1536]{1,0:T(8,128)} %get-tuple-element.139) | copy-start | bytes 2359300
  214.4 24.6 %collective-permute-start.27 = (f32[768,1536]{1,0:T(8,128)}, f32[768,1536]{1,0:T(8,128)}, u32[]{:S(2)}, u32[]{:S(2)}) collective-permute-start(f32[768,1536]{1,0:T(8,128)} %shard_map.67), channel_id=1, source_target_pairs={{0,1},{1,0},{2,3},{3,2},{4,5},{5,4},{6,7},{7,6},{8,9},{9,8},{10,11... | collective-permute-start | bytes 14155784 | tf_op jit(solution)/shard_map/ppermute | solution.py:394
  215.4 21.6 %collective-permute-start.22 = (f32[128,1536]{1,0:T(8,128)}, f32[128,1536]{1,0:T(8,128)}, u32[]{:S(2)}, u32[]{:S(2)}) collective-permute-start(f32[128,1536]{1,0:T(8,128)} %add.27), channel_id=1, source_target_pairs={{0,2},{1,3},{2,6},{3,7},{6,4},{7,5},{4,0},{5,1},{8,10},{9,11},{10,... | collective-permute-start | bytes 2359304 | tf_op jit(solution)/shard_map/ppermute | solution.py:392
  215.5 21.5 %copy-start.2 = (f32[128,1536]{1,0:T(8,128)S(1)}, f32[128,1536]{1,0:T(8,128)}, u32[]{:S(2)}) copy-start(f32[128,1536]{1,0:T(8,128)} %get-tuple-element.130) | copy-start | bytes 2359300
  215.5 37.8 %copy-start.1 = (f32[128,1536]{1,0:T(8,128)S(1)}, f32[128,1536]{1,0:T(8,128)}, u32[]{:S(2)}) copy-start(f32[128,1536]{1,0:T(8,128)} %get-tuple-element.131) | copy-start | bytes 2359300
  215.5 37.8 %collective-permute-start.25 = (f32[128,1536]{1,0:T(8,128)S(1)}, f32[128,1536]{1,0:T(8,128)S(1)}, u32[]{:S(2)}, u32[]{:S(2)}) collective-permute-start(f32[128,1536]{1,0:T(8,128)S(1)} %add.30), channel_id=1, source_target_pairs={{0,2},{1,3},{2,6},{3,7},{6,4},{7,5},{4,0},{5,1},{8,10},{9,11},{10,... | collective-permute-start | bytes 2359304 | tf_op jit(solution)/shard_map/ppermute | solution.py:392
  239.1 29.8 %copy-start = (f32[768,1536]{1,0:T(8,128)}, f32[768,1536]{1,0:T(8,128)S(1)}, u32[]{:S(2)}) copy-start(f32[768,1536]{1,0:T(8,128)S(1)} %collective-permute-done.26.refs_5_) | copy-start | bytes 14155780
  242.7 12.3 %collective-permute-start.28 = (f32[64,1536]{1,0:T(8,128)}, f32[64,1536]{1,0:T(8,128)S(1)}, u32[]{:S(2)}, u32[]{:S(2)}) collective-permute-start(f32[64,1536]{1,0:T(8,128)} %get-tuple-element.208), channel_id=1, source_target_pairs={{0,8},{8,0},{16,24},{24,16},{1,9},{9,1},{17,25},{25,17},{2,10},{10... | collective-permute-start | bytes 1179656 | tf_op jit(solution)/shard_map/ppermute | solution.py:395
  243.7 18.7 %collective-permute-start.29 = (f32[64,1536]{1,0:T(8,128)}, f32[64,1536]{1,0:T(8,128)S(1)}, u32[]{:S(2)}, u32[]{:S(2)}) collective-permute-start(f32[64,1536]{1,0:T(8,128)} %get-tuple-element.209), channel_id=1, source_target_pairs={{0,16},{8,24},{16,0},{24,8},{1,17},{9,25},{17,1},{25,9},{2,18},{10... | collective-permute-start | bytes 1179656 | tf_op jit(solution)/shard_map/ppermute | solution.py:395
  243.7 18.7 %collective-permute-start.30 = (f32[64,1536]{1,0:T(8,128)}, f32[64,1536]{1,0:T(8,128)S(1)}, u32[]{:S(2)}, u32[]{:S(2)}) collective-permute-start(f32[64,1536]{1,0:T(8,128)} %get-tuple-element.210), channel_id=1, source_target_pairs={{0,24},{8,16},{16,8},{24,0},{1,25},{9,17},{17,9},{25,1},{2,26},{10... | collective-permute-start | bytes 1179656 | tf_op jit(solution)/shard_map/ppermute | solution.py:395
  255.0 29.2 %copy-start.13 = (f32[64,1536]{1,0:T(8,128)}, f32[64,1536]{1,0:T(8,128)S(1)}, u32[]{:S(2)}) copy-start(f32[64,1536]{1,0:T(8,128)S(1)} %collective-permute-done.28.refs_6_) | copy-start | bytes 1179652
  262.4 21.8 %copy-start.14 = (f32[64,1536]{1,0:T(8,128)}, f32[64,1536]{1,0:T(8,128)S(1)}, u32[]{:S(2)}) copy-start(f32[64,1536]{1,0:T(8,128)S(1)} %collective-permute-done.29.refs_7_) | copy-start | bytes 1179652
  262.4 21.8 %copy-start.15 = (f32[64,1536]{1,0:T(8,128)}, f32[64,1536]{1,0:T(8,128)S(1)}, u32[]{:S(2)}) copy-start(f32[64,1536]{1,0:T(8,128)S(1)} %collective-permute-done.30.refs_8_) | copy-start | bytes 1179652
  265.4 18.9 %collective-permute-start.31 = (f32[64,1536]{1,0:T(8,128)}, f32[64,1536]{1,0:T(8,128)S(1)}, u32[]{:S(2)}, u32[]{:S(2)}) collective-permute-start(f32[64,1536]{1,0:T(8,128)} %get-tuple-element.212), channel_id=1, source_target_pairs={{0,8},{8,0},{16,24},{24,16},{1,9},{9,1},{17,25},{25,17},{2,10},{10... | collective-permute-start | bytes 1179656 | tf_op jit(solution)/shard_map/ppermute | solution.py:395
  266.6 17.7 %collective-permute-start.32 = (f32[64,1536]{1,0:T(8,128)}, f32[64,1536]{1,0:T(8,128)S(1)}, u32[]{:S(2)}, u32[]{:S(2)}) collective-permute-start(f32[64,1536]{1,0:T(8,128)} %get-tuple-element.213), channel_id=1, source_target_pairs={{0,16},{8,24},{16,0},{24,8},{1,17},{9,25},{17,1},{25,9},{2,18},{10... | collective-permute-start | bytes 1179656 | tf_op jit(solution)/shard_map/ppermute | solution.py:395
  267.2 17.1 %collective-permute-start.33 = (f32[64,1536]{1,0:T(8,128)}, f32[64,1536]{1,0:T(8,128)S(1)}, u32[]{:S(2)}, u32[]{:S(2)}) collective-permute-start(f32[64,1536]{1,0:T(8,128)} %get-tuple-element.214), channel_id=1, source_target_pairs={{0,24},{8,16},{16,8},{24,0},{1,25},{9,17},{17,9},{25,1},{2,26},{10... | collective-permute-start | bytes 1179656 | tf_op jit(solution)/shard_map/ppermute | solution.py:395
  284.3 0.9 copy-start.17
  284.3 1.0 copy-start.18
  (4 other events, 2.8 us)
